TPU v7x, 32 devices: a whole 2x2x4 slice. The times are simulated.
32 devices in a mesh: parts: 2 (over x), row: 16 (over z, y, core).
Axes of the slice: x: 2, y: 2, z: 4, core: 2. Of those that a mesh axis runs over, the one named last changes fastest.
Arguments:
- adj_rows: bfloat16 [6144, 32768], P(('parts', 'row')), parts along dimension 0, may hold values from 0 to 1
- adj_panel: bfloat16 [2, 32768, 384], P(None, ('parts', 'row')), parts along dimension 1, may hold values from 0 to 1
- adj_tile: bfloat16 [6144, 384], P(('parts', 'row')), parts along dimension 0, may hold values from 0 to 1
Outputs:
- intersection: float32 [6144, 384], P(('parts', 'row')), parts along dimension 0
- degree: float32 [6144], P(('parts', 'row')), parts along dimension 0
There are 2 independent parts, one for each index of `parts`. A program takes and returns all parts, laid end to end along the dimension named above; each array names one. Nothing has to cross between parts.
All inputs are finite; a program needn't handle non-finite values.
Results may differ from a plain program's by a relative error of at most 0.0003.
Values may be sent and summed in bfloat16 or wider, within the bound.
No kernel may reach another device: no remote copies, remote signals or barrier semaphores. Data moves between devices by JAX's collectives and lax.ppermute only.
A program may use at most 128 MiB of HBM per device.

v0:
```python
import jax
import jax.numpy as jnp
from jax import lax
from jax.sharding import PartitionSpec as P

PANEL = 16384
SECTIONS = 2


def shards(adj_rows, adj_panel, adj_tile):
    width = adj_panel.shape[2]
    degree = jnp.sum(adj_rows, axis=1, dtype=jnp.float32)
    col_degree = lax.psum(jnp.sum(adj_panel, axis=(0, 1), dtype=jnp.float32), "row")
    empty = (jnp.zeros((adj_rows.shape[0], width), jnp.float32), jnp.zeros((width,), jnp.float32))

    def add_slab(total, piece, offset):
        columns = lax.dynamic_slice_in_dim(adj_rows, offset, piece.shape[0], 1)
        product = total[0] + jnp.dot(columns, piece, preferred_element_type=jnp.float32)
        return (product, total[1])

    carried = empty
    for section in range(SECTIONS):

        def add_section(total, piece, start, section=section):
            return add_slab(total, piece, section * PANEL + start)

        carried = add_section(
            carried, lax.all_gather(adj_panel[section], "row", axis=0, tiled=True), jnp.int32(0)
        )
    square = carried[0]
    tile = adj_tile.astype(jnp.float32)
    lower = jnp.minimum(degree[:, None], col_degree[None, :])
    intersection = (square + tile) / (lower + 1.0 - tile)
    return (intersection, degree)


def solution(mesh):
    in_specs = (
        P(("parts", "row"), None),
        P(None, ("parts", "row"), None),
        P(("parts", "row"), None),
    )
    out_specs = (P(("parts", "row"), None), P(("parts", "row")))
    return jax.shard_map(shards, mesh=mesh, in_specs=in_specs, out_specs=out_specs, check_vma=False)
```

profile of v0, /device:TPU:0, one launch (start us, length us, event | category | flops | bytes accessed | tf_op | source)
XLA Modules:
  0.0 232.7 jit_solution(4948636650736569729)
XLA Ops:
  7.2 0.0 all-gather.7.cloned.1.call-start
  7.2 2.8 %fusion.21 = (bf16[1,1024,384]{2,1,0:T(8,128)(2,1)}, bf16[1,1024,384]{2,1,0:T(8,128)(2,1)}) fusion(bf16[2,1024,384]{2,1,0:T(8,128)(2,1)} %param.4), kind=kLoop, calls=%fused_computation.12 | loop fusion | bytes 3145728 | tf_op jit(solution)/shard_map/slice | solution.py:28
  10.0 0.0 all-gather.7.cloned.1.call-update
  10.0 0.0 all-gather.5.cloned.1.call-start
  10.0 0.7 all-gather.5.cloned.1.call-update
  10.7 1.7 convert_reduce_fusion.1
  12.5 36.1 %psum.7 = f32[384]{0:T(512)S(1)} all-reduce(f32[384]{0:T(512)S(1)} %convert_reduce_fusion.1), channel_id=1, replica_groups=mesh['parts'=2,'row'=16] {'row'}, use_global_device_ids=true, to_apply=%region_2.0 | all-reduce | flops 384 | bytes 3072 | tf_op jit(solution)/shard_map/psum | solution.py:13
  48.5 6.4 %convert_reduce_fusion = f32[192]{0:T(256)S(1)} fusion(bf16[192,32768]{1,0:T(8,128)(2,1)} %param.3), kind=kLoop, calls=%fused_computation | loop fusion | flops 12582720 | bytes 12583680 | tf_op jit(solution)/shard_map/reduce_sum | solution.py:12
  55.0 0.0 copy-start
  55.0 0.0 copy-start.1
  55.0 59.0 %all-gather.7.cloned.1.call-done = bf16[1,16384,384]{2,1,0:T(8,128)(2,1)} async-done(((bf16[1,1024,384]{2,1,0:T(8,128)(2,1)}), bf16[1,16384,384]{2,1,0:T(8,128)(2,1)}) %all-gather.7.cloned.1.call-update) | async-done | bytes 12582928 | tf_op jit(solution)/shard_map/all_gather | solution.py:28
  114.0 9.8 %fusion = f32[192,384]{1,0:T(8,128)S(1)} fusion(bf16[1,16384,384]{2,1,0:T(8,128)(2,1)} %all-gather.7.cloned.1.call-done, bf16[192,32768]{1,0:T(8,128)(2,1)} %param.3), kind=kOutput, calls=%fused_computation.1 | convolution fusion | flops 2415919104 | bytes 19169280 | tf_op jit(solution)/shard_map/dot_general | solution.py:18
  123.9 91.4 %all-gather.5.cloned.1.call-done = bf16[1,16384,384]{2,1,0:T(8,128)(2,1)} async-done(((bf16[1,1024,384]{2,1,0:T(8,128)(2,1)}), bf16[1,16384,384]{2,1,0:T(8,128)(2,1)}) %all-gather.5.cloned.1.call-update) | async-done | bytes 12582928 | tf_op jit(solution)/shard_map/all_gather | solution.py:28
  215.3 0.0 copy-done
  215.3 0.0 copy-done.1
  215.3 10.6 %fusion.16 = f32[192,384]{1,0:T(8,128)} fusion(f32[192,384]{1,0:T(8,128)S(1)} %fusion, bf16[1,16384,384]{2,1,0:T(8,128)(2,1)} %all-gather.5.cloned.1.call-done, bf16[192,32768]{1,0:T(8,128)(2,1)} %param.3, bf16[192,384]{1,0:T(8,128)(2,1)S(1)} %copy-done.1, f32[384]{0:T(512)S(1)} %psum.7, f32[192]{0:T(256)S(1)} %convert_reduce_fusion), kind=kOutput, calls=%fused_computation.10 | convolution fusion | flops 2416435200 | bytes 19613952 | tf_op jit(solution)/shard_map/dot_general | solution.py:18
Async XLA Ops:
  7.2 106.9 %all-gather.7.cloned.1.call-start = ((), (), s32[]{:S(2)}) async-start(), calls=%async_computation.1 | async-start | bytes 13369344 | tf_op jit(solution)/shard_map/all_gather | solution.py:28
  10.0 205.3 %all-gather.5.cloned.1.call-start = ((), (), s32[]{:S(2)}) async-start(), calls=%async_computation | async-start | bytes 13369344 | tf_op jit(solution)/shard_map/all_gather | solution.py:28
  55.0 160.3 %copy-start = (f32[192]{0:T(256)}, f32[192]{0:T(256)S(1)}, u32[]{:S(2)}) copy-start(f32[192]{0:T(256)S(1)} %convert_reduce_fusion) | copy-start | bytes 2308
  55.0 160.3 %copy-start.1 = (bf16[192,384]{1,0:T(8,128)(2,1)S(1)}, bf16[192,384]{1,0:T(8,128)(2,1)}, u32[]{:S(2)}) copy-start(bf16[192,384]{1,0:T(8,128)(2,1)} %param.5) | copy-start | bytes 442372
Sparse Core Ops, SparseCore 0:
  10.3 103.7 all-gather.6
  116.3 98.9 all-gather.4
where the time goes:
time: 233 us
  waiting for transfers between devices  151 us (65%)
  blocking collectives  36.1 us (15%)
  matrix products  20.4 us (9%)
  between operations  14.1 us (6%)
  other arithmetic  8.16 us (4%)
  local copies, waits for them, and re-layouts  2.77 us (1%)
    all_gather x2, waiting for transfers between devices, shards(): lax.all_gather(adj_panel[section], 'row', axis=0, tiled=True)  150 us
    psum x1, blocking collectives, shards(): lax.psum(jnp.sum(adj_panel, axis=(0, 1), dtype=jnp.float32), 'row')  36.1 us
    dot_general x2, matrix products, add_slab(): jnp.dot(columns, piece, preferred_element_type=jnp.float32)  20.4 us
    reduce_sum x1, other arithmetic, shards(): degree = jnp.sum(adj_rows, axis=1, dtype=jnp.float32)  6.44 us
  transfers between devices with their start and end apart: 2, of which 2 were waited for; matrix products, arithmetic and copies ran while one was open for 8% of the time, Pallas kernels for 0%

commit v1 on v0

v1 whole, which is shorter than its diff:
```python
import jax
import jax.numpy as jnp
import numpy as np
from jax import lax
from jax.sharding import PartitionSpec as P

CORES = 2


def chip_cycle(chips):
    wide = 1
    while (2 * wide) ** 2 <= chips:
        wide *= 2
    high = chips // wide
    if wide == 1 or high % 2 or wide * high != chips:
        return list(range(chips))
    walk = [(0, 0)]
    for i in range(high):
        line = range(1, wide)
        walk += [(i, j) for j in (line if i % 2 == 0 else reversed(line))]
    walk += [(i, 0) for i in range(high - 1, 0, -1)]
    return [i * wide + j for i, j in walk]


def make_shards(n_row):
    chips = n_row // CORES
    cycle = chip_cycle(chips)
    place = {chip: k for k, chip in enumerate(cycle)}

    def ring(step):
        return [
            (cycle[k] * CORES + c, cycle[(k + step) % chips] * CORES + c)
            for k in range(chips)
            for c in range(CORES)
        ]

    swap = [(d, d ^ 1) for d in range(n_row)]

    def owners(distance):
        return np.array([cycle[(place[d // CORES] - distance) % chips] for d in range(n_row)], np.int32)

    def shards(adj_rows, adj_panel, adj_tile):
        rows = adj_rows.shape[0]
        sections, depth, width = adj_panel.shape
        panel = n_row * depth
        me = lax.axis_index("row")
        core = lax.rem(me, CORES)

        pieces = [adj_panel[s] for s in range(sections)]
        lent = jnp.concatenate(
            [
                lax.dynamic_slice_in_dim(adj_rows, s * panel + (chip * CORES + 1 - core) * depth, depth, 1)
                for s in range(sections)
                for chip in range(chips)
            ],
            axis=1,
        )
        borrowed = lax.ppermute(lent, "row", swap)
        degree = jnp.sum(adj_rows, axis=1, dtype=jnp.float32)

        mine = jnp.zeros((rows, width), jnp.float32)
        theirs = jnp.zeros((rows, width), jnp.float32)
        col = jnp.zeros((1, width), jnp.float32)
        for step in range(chips):
            following = pieces
            if step < chips - 1:
                following = [
                    lax.ppermute(piece, "row", ring(1 if s % 2 == 0 else -1)) for s, piece in enumerate(pieces)
                ]
            for s, piece in enumerate(pieces):
                chip = jnp.asarray(owners(step if s % 2 == 0 else -step))[me]
                own = lax.dynamic_slice_in_dim(adj_rows, s * panel + (chip * CORES + core) * depth, depth, 1)
                other = lax.dynamic_slice_in_dim(borrowed, (s * chips + chip) * depth, depth, 1)
                mine = mine + jnp.dot(own, piece, preferred_element_type=jnp.float32)
                theirs = theirs + jnp.dot(other, piece, preferred_element_type=jnp.float32)
                col = col + jnp.sum(piece, axis=0, dtype=jnp.float32, keepdims=True)
            pieces = following

        partner = lax.ppermute(jnp.concatenate([theirs, jnp.broadcast_to(col, (8, width))], axis=0), "row", swap)
        square = mine + partner[:rows]
        col_degree = col + partner[rows : rows + 1]
        tile = adj_tile.astype(jnp.float32)
        lower = jnp.minimum(degree[:, None], col_degree)
        intersection = (square + tile) / (lower + 1.0 - tile)
        return (intersection, degree)

    return shards


def solution(mesh):
    in_specs = (
        P(("parts", "row"), None),
        P(None, ("parts", "row"), None),
        P(("parts", "row"), None),
    )
    out_specs = (P(("parts", "row"), None), P(("parts", "row")))
    return jax.shard_map(
        make_shards(mesh.shape["row"]), mesh=mesh, in_specs=in_specs, out_specs=out_specs, check_vma=False
    )
```

time: 233 us -> 210 us (0.901); the launches traced: 233 us -> 207 us
  waiting for transfers between devices: 151 us -> 82.7 us
  blocking collectives: 36.1 us -> 0 us
  local copies, waits for them, and re-layouts: 2.77 us -> 35.5 us
  matrix products: 20.4 us -> 45.8 us
  starting transfers between devices: 0.08 us -> 16 us
  between operations: 14.1 us -> 16.9 us
    all_gather x2 -> x0, waiting for transfers between devices: 150 us -> none  [shards(): lax.all_gather(adj_panel[section], 'row', axis=0, tiled=True)]
    ppermute x0 -> x16, waiting for transfers between devices: none -> 82.7 us  [the longest x14 82.7 us: shards(): lax.ppermute(piece, 'row', ring(1 if s % 2 == 0 else -1))]
    psum x1 -> x0, blocking collectives: 36.1 us -> none  [shards(): lax.psum(jnp.sum(adj_panel, axis=(0, 1), dtype=jnp.float32), 'row')]
    unnamed x4 -> x39, local copies, waits for them, and re-layouts: 0.01 us -> 27.2 us
    dot_general x2 -> x32, matrix products: 20.4 us -> 45.8 us  [the longest x16 23.6 us: shards(): mine = mine + jnp.dot(own, piece, preferred_element_type=jnp.float32)]
    ppermute x0 -> x16, starting transfers between devices: none -> 16 us  [the longest x14 15.4 us: shards(): lax.ppermute(piece, 'row', ring(1 if s % 2 == 0 else -1))]
    dynamic_slice x0 -> x8, local copies, waits for them, and re-layouts: none -> 5.12 us  [shards(): chip = jnp.asarray(owners(step if s % 2 == 0 else -step))[me]]
    slice x1 -> x0, local copies, waits for them, and re-layouts: 2.76 us -> none  [shards(): adj_panel[section]]
  transfers between devices with their start and end apart: 2 -> 16, of which waited for: 2 -> 7; matrix products, arithmetic and copies ran while one was open for 8% -> 18% of each run, Pallas kernels for 0% -> 0%
where the time goes in v1:
time: 210 us; the launch traced here: 207 us
  waiting for transfers between devices  82.7 us (39%)
  matrix products  45.8 us (22%)
  local copies, waits for them, and re-layouts  35.5 us (17%)
  between operations  16.9 us (8%)
  starting transfers between devices  16 us (8%)
  other arithmetic  10.4 us (5%)
    ppermute x14, waiting for transfers between devices, shards(): lax.ppermute(piece, 'row', ring(1 if s % 2 == 0 else -1))  82.7 us
    unnamed x39, local copies, waits for them, and re-layouts  27.2 us
    dot_general x16, matrix products, shards(): mine = mine + jnp.dot(own, piece, preferred_element_type=jnp.float32)  23.6 us
    dot_general x16, matrix products, shards(): theirs = theirs + jnp.dot(other, piece, preferred_element_type=jnp.float32)  22.2 us
    ppermute x14, starting transfers between devices, shards(): lax.ppermute(piece, 'row', ring(1 if s % 2 == 0 else -1))  15.4 us
    reduce_sum x1, other arithmetic, shards(): degree = jnp.sum(adj_rows, axis=1, dtype=jnp.float32)  6.58 us
    dynamic_slice x8, local copies, waits for them, and re-layouts, shards(): chip = jnp.asarray(owners(step if s % 2 == 0 else -step))[me]  5.12 us
  transfers between devices with their start and end apart: 16, of which 7 were waited for; matrix products, arithmetic and copies ran while one was open for 18% of the time, Pallas kernels for 0%

profile of v1, /device:TPU:0, one launch (start us, length us, event | category | flops | bytes accessed | tf_op | source)
XLA Modules:
  0.0 207.3 jit_solution(11167900094046057500)
XLA Ops:
  0.7 1.9 dynamic-slice_dynamic-update-slice_fusion.15
  2.6 1.8 dynamic-slice_dynamic-update-slice_fusion.14
  4.4 1.8 dynamic-slice_dynamic-update-slice_fusion.13
  6.2 1.8 dynamic-slice_dynamic-update-slice_fusion.12
  8.0 1.8 dynamic-slice_dynamic-update-slice_fusion.11
  9.8 1.8 dynamic-slice_dynamic-update-slice_fusion.10
  11.6 1.8 dynamic-slice_dynamic-update-slice_fusion.9
  13.4 1.8 dynamic-slice_dynamic-update-slice_fusion.8
  15.2 1.8 dynamic-slice_dynamic-update-slice_fusion.7
  17.0 1.8 dynamic-slice_dynamic-update-slice_fusion.6
  18.8 1.8 dynamic-slice_dynamic-update-slice_fusion.5
  20.6 1.8 dynamic-slice_dynamic-update-slice_fusion.4
  22.4 1.8 dynamic-slice_dynamic-update-slice_fusion.3
  24.2 1.8 dynamic-slice_dynamic-update-slice_fusion.2
  26.0 1.8 dynamic-slice_dynamic-update-slice_fusion.1
  27.8 1.8 dynamic-slice_dynamic-update-slice_fusion
  31.5 2.6 %collective-permute-start.1 = (bf16[1024,384]{1,0:T(8,128)(2,1)}, bf16[1024,384]{1,0:T(8,128)(2,1)S(1)}, u32[]{:S(2)}, u32[]{:S(2)}) collective-permute-start(bf16[1024,384]{1,0:T(8,128)(2,1)} %get-tuple-element.5), channel_id=1, source_target_pairs={{0,4},{1,5},{2,0},{3,1},{6,2},{7,3},{10,6},{11,7},{14,10},{15,11},... | collective-permute-start | bytes 2359304 | tf_op jit(solution)/shard_map/ppermute | solution.py:68
  35.4 2.1 %fusion.65 = f32[192,384]{1,0:T(8,128)} fusion(bf16[192,32768]{1,0:T(8,128)(2,1)} %param.19, s32[]{:T(128)S(6)} %select_n.163, bf16[2,1024,384]{2,1,0:T(8,128)(2,1)S(1)} %copy-done), kind=kOutput, calls=%fused_computation.115 | convolution fusion | flops 150994944 | bytes 1474564 | tf_op jit(solution)/shard_map/dot_general | solution.py:74
  37.6 6.6 %convert_reduce_fusion = f32[192]{0:T(256)S(1)} fusion(bf16[192,32768]{1,0:T(8,128)(2,1)} %param.19), kind=kLoop, calls=%fused_computation | loop fusion | flops 12582720 | bytes 12583680 | tf_op jit(solution)/shard_map/reduce_sum | solution.py:59
  44.1 8.3 %collective-permute-done.1 = bf16[1024,384]{1,0:T(8,128)(2,1)S(1)} collective-permute-done((bf16[1024,384]{1,0:T(8,128)(2,1)}, bf16[1024,384]{1,0:T(8,128)(2,1)S(1)}, u32[]{:S(2)}, u32[]{:S(2)}) %collective-permute-start.1) | collective-permute-done | bytes 786464 | tf_op jit(solution)/shard_map/ppermute | solution.py:68
  52.4 1.8 collective-permute-start.3
  77.2 1.4 fusion.17
  78.6 1.9 collective-permute-start.5
  80.6 13.6 %collective-permute-done.2 = bf16[1024,384]{1,0:T(8,128)(2,1)S(1)} collective-permute-done((bf16[1024,384]{1,0:T(8,128)(2,1)S(1)}, bf16[1024,384]{1,0:T(8,128)(2,1)S(1)}, u32[]{:S(2)}, u32[]{:S(2)}) %collective-permute-start.2) | collective-permute-done | bytes 786464 | tf_op jit(solution)/shard_map/ppermute | solution.py:68
  94.8 1.6 fusion.58
  96.4 1.4 fusion.16
  97.8 1.6 collective-permute-start.7
  100.8 11.4 %collective-permute-done.4 = bf16[1024,384]{1,0:T(8,128)(2,1)S(1)} collective-permute-done((bf16[1024,384]{1,0:T(8,128)(2,1)S(1)}, bf16[1024,384]{1,0:T(8,128)(2,1)S(1)}, u32[]{:S(2)}, u32[]{:S(2)}) %collective-permute-start.4) | collective-permute-done | bytes 786464 | tf_op jit(solution)/shard_map/ppermute | solution.py:68
  114.4 1.4 fusion.15
  115.8 1.4 collective-permute-start.9
  117.4 12.5 %collective-permute-done.6 = bf16[1024,384]{1,0:T(8,128)(2,1)S(1)} collective-permute-done((bf16[1024,384]{1,0:T(8,128)(2,1)S(1)}, bf16[1024,384]{1,0:T(8,128)(2,1)S(1)}, u32[]{:S(2)}, u32[]{:S(2)}) %collective-permute-start.6) | collective-permute-done | bytes 786464 | tf_op jit(solution)/shard_map/ppermute | solution.py:68
  132.1 1.4 fusion.14
  133.5 1.4 collective-permute-start.11
  135.1 12.5 %collective-permute-done.8 = bf16[1024,384]{1,0:T(8,128)(2,1)S(1)} collective-permute-done((bf16[1024,384]{1,0:T(8,128)(2,1)S(1)}, bf16[1024,384]{1,0:T(8,128)(2,1)S(1)}, u32[]{:S(2)}, u32[]{:S(2)}) %collective-permute-start.8) | collective-permute-done | bytes 786464 | tf_op jit(solution)/shard_map/ppermute | solution.py:68
  149.8 1.4 fusion.13
  151.2 1.4 collective-permute-start.13
  152.8 12.5 %collective-permute-done.10 = bf16[1024,384]{1,0:T(8,128)(2,1)S(1)} collective-permute-done((bf16[1024,384]{1,0:T(8,128)(2,1)S(1)}, bf16[1024,384]{1,0:T(8,128)(2,1)S(1)}, u32[]{:S(2)}, u32[]{:S(2)}) %collective-permute-start.10) | collective-permute-done | bytes 786464 | tf_op jit(solution)/shard_map/ppermute | solution.py:68
  168.0 11.8 %collective-permute-done.12 = bf16[1024,384]{1,0:T(8,128)(2,1)S(1)} collective-permute-done((bf16[1024,384]{1,0:T(8,128)(2,1)S(1)}, bf16[1024,384]{1,0:T(8,128)(2,1)S(1)}, u32[]{:S(2)}, u32[]{:S(2)}) %collective-permute-start.12) | collective-permute-done | bytes 786464 | tf_op jit(solution)/shard_map/ppermute | solution.py:68
  184.1 1.6 fusion.33
  185.7 1.4 fusion.30
  192.6 1.4 fusion.7
  195.3 1.4 fusion.4
  196.7 1.4 fusion.3
  198.1 1.4 fusion.2
  199.5 1.4 fusion.1
  200.9 1.4 fusion
  202.4 1.4 fusion.12
  205.2 2.1 %fusion.11 = f32[192,384]{1,0:T(8,128)} fusion(f32[192,384]{1,0:T(8,128)S(1)} %fusion.43, f32[192,384]{1,0:T(8,128)S(1)} %fusion.12, bf16[1024,384]{1,0:T(8,128)(2,1)S(1)} %collective-permute-done.12, bf16[192,32768]{1,0:T(8,128)(2,1)} %param.19, s32[]{:T(128)S(6)} %select_n.177, bf16[192,384]{1,0:T(8,128)(2,1)S(1)} %copy-done.3, ...), kind=kOutput, calls=%fused_computation.36 | convolution fusion | flops 151658496 | bytes 2509060 | tf_op jit(solution)/shard_map/dot_general | solution.py:74
  (85 shorter events, 34.8 us)
Async XLA Ops:
  0.6 29.5 %copy-start = (bf16[2,1024,384]{2,1,0:T(8,128)(2,1)S(1)}, bf16[2,1024,384]{2,1,0:T(8,128)(2,1)}, u32[]{:S(2)}) copy-start(bf16[2,1024,384]{2,1,0:T(8,128)(2,1)} %param.20) | copy-start | bytes 4718596
  8.0 26.1 %copy-start.11 = (s32[16]{0:T(128)S(1)}, s32[16]{0:T(128)}, u32[]{:S(2)}) copy-start(s32[16]{0:T(128)} %constant.114.clone) | copy-start | bytes 196
  29.7 150.3 %collective-permute-start.14 = (bf16[192,16384]{1,0:T(8,128)(2,1)}, bf16[192,16384]{1,0:T(8,128)(2,1)}, u32[]{:S(2)}, u32[]{:S(2)}) collective-permute-start(bf16[192,16384]{1,0:T(8,128)(2,1)} %dynamic-slice_dynamic-update-slice_fusion), channel_id=1, source_target_pairs={{0,1},{1,0},{2,3},{3,2},{4,5},{5,4},{6,7},{7,6},{8,9},{9,8},{10,11... | collective-permute-start | bytes 18874376 | tf_op jit(solution)/shard_map/ppermute | solution.py:58
  31.5 20.9 %collective-permute-start.1 = (bf16[1024,384]{1,0:T(8,128)(2,1)}, bf16[1024,384]{1,0:T(8,128)(2,1)S(1)}, u32[]{:S(2)}, u32[]{:S(2)}) collective-permute-start(bf16[1024,384]{1,0:T(8,128)(2,1)} %get-tuple-element.5), channel_id=1, source_target_pairs={{0,4},{1,5},{2,0},{3,1},{6,2},{7,3},{10,6},{11,7},{14,10},{15,11},... | collective-permute-start | bytes 2359304 | tf_op jit(solution)/shard_map/ppermute | solution.py:68
  34.0 41.2 %collective-permute-start = (bf16[1024,384]{1,0:T(8,128)(2,1)}, bf16[1024,384]{1,0:T(8,128)(2,1)S(1)}, u32[]{:S(2)}, u32[]{:S(2)}) collective-permute-start(bf16[1024,384]{1,0:T(8,128)(2,1)} %get-tuple-element.4), channel_id=1, source_target_pairs={{0,2},{1,3},{2,6},{3,7},{6,10},{7,11},{10,14},{11,15},{14,12},{15,... | collective-permute-start | bytes 2359304 | tf_op jit(solution)/shard_map/ppermute | solution.py:68
  37.5 16.7 %copy-start.1 = (f32[192,384]{1,0:T(8,128)S(1)}, f32[192,384]{1,0:T(8,128)}, u32[]{:S(2)}) copy-start(f32[192,384]{1,0:T(8,128)} %fusion.65) | copy-start | bytes 884740
  37.5 18.1 %copy-start.10 = (s32[16]{0:T(128)S(1)}, s32[16]{0:T(128)}, u32[]{:S(2)}) copy-start(s32[16]{0:T(128)} %constant.116.clone) | copy-start | bytes 196
  37.5 19.3 %copy-start.9 = (s32[16]{0:T(128)S(1)}, s32[16]{0:T(128)}, u32[]{:S(2)}) copy-start(s32[16]{0:T(128)} %constant.115.clone) | copy-start | bytes 196
  37.5 21.9 %copy-start.8 = (s32[16]{0:T(128)S(1)}, s32[16]{0:T(128)}, u32[]{:S(2)}) copy-start(s32[16]{0:T(128)} %constant.118.clone) | copy-start | bytes 196
  37.5 23.3 %copy-start.7 = (s32[16]{0:T(128)S(1)}, s32[16]{0:T(128)}, u32[]{:S(2)}) copy-start(s32[16]{0:T(128)} %constant.117.clone) | copy-start | bytes 196
  37.5 24.7 %copy-start.6 = (s32[16]{0:T(128)S(1)}, s32[16]{0:T(128)}, u32[]{:S(2)}) copy-start(s32[16]{0:T(128)} %constant.120.clone) | copy-start | bytes 196
  37.5 25.9 %copy-start.5 = (s32[16]{0:T(128)S(1)}, s32[16]{0:T(128)}, u32[]{:S(2)}) copy-start(s32[16]{0:T(128)} %constant.119.clone) | copy-start | bytes 196
  37.6 27.2 %copy-start.4 = (s32[16]{0:T(128)S(1)}, s32[16]{0:T(128)}, u32[]{:S(2)}) copy-start(s32[16]{0:T(128)} %constant.121.clone) | copy-start | bytes 196
  44.1 161.0 %copy-start.2 = (f32[192]{0:T(256)}, f32[192]{0:T(256)S(1)}, u32[]{:S(2)}) copy-start(f32[192]{0:T(256)S(1)} %convert_reduce_fusion) | copy-start | bytes 2308
  52.4 26.2 %collective-permute-start.3 = (bf16[1024,384]{1,0:T(8,128)(2,1)S(1)}, bf16[1024,384]{1,0:T(8,128)(2,1)}, u32[]{:S(2)}, u32[]{:S(2)}) collective-permute-start(bf16[1024,384]{1,0:T(8,128)(2,1)S(1)} %collective-permute-done.1), channel_id=1, source_target_pairs={{0,4},{1,5},{2,0},{3,1},{6,2},{7,3},{10,6},{11,7},{14,10},{15,11},... | collective-permute-start | bytes 2359304 | tf_op jit(solution)/shard_map/ppermute | solution.py:68
  75.3 18.9 %collective-permute-start.2 = (bf16[1024,384]{1,0:T(8,128)(2,1)S(1)}, bf16[1024,384]{1,0:T(8,128)(2,1)S(1)}, u32[]{:S(2)}, u32[]{:S(2)}) collective-permute-start(bf16[1024,384]{1,0:T(8,128)(2,1)S(1)} %collective-permute-done), channel_id=1, source_target_pairs={{0,2},{1,3},{2,6},{3,7},{6,10},{7,11},{10,14},{11,15},{14,12},{15,... | collective-permute-start | bytes 2359304 | tf_op jit(solution)/shard_map/ppermute | solution.py:68
  78.6 19.3 %collective-permute-start.5 = (bf16[1024,384]{1,0:T(8,128)(2,1)}, bf16[1024,384]{1,0:T(8,128)(2,1)S(1)}, u32[]{:S(2)}, u32[]{:S(2)}) collective-permute-start(bf16[1024,384]{1,0:T(8,128)(2,1)} %collective-permute-done.3), channel_id=1, source_target_pairs={{0,4},{1,5},{2,0},{3,1},{6,2},{7,3},{10,6},{11,7},{14,10},{15,11},... | collective-permute-start | bytes 2359304 | tf_op jit(solution)/shard_map/ppermute | solution.py:68
  94.2 18.0 %collective-permute-start.4 = (bf16[1024,384]{1,0:T(8,128)(2,1)S(1)}, bf16[1024,384]{1,0:T(8,128)(2,1)S(1)}, u32[]{:S(2)}, u32[]{:S(2)}) collective-permute-start(bf16[1024,384]{1,0:T(8,128)(2,1)S(1)} %collective-permute-done.2), channel_id=1, source_target_pairs={{0,2},{1,3},{2,6},{3,7},{6,10},{7,11},{10,14},{11,15},{14,12},{15,... | collective-permute-start | bytes 2359304 | tf_op jit(solution)/shard_map/ppermute | solution.py:68
  97.8 18.0 %collective-permute-start.7 = (bf16[1024,384]{1,0:T(8,128)(2,1)S(1)}, bf16[1024,384]{1,0:T(8,128)(2,1)S(1)}, u32[]{:S(2)}, u32[]{:S(2)}) collective-permute-start(bf16[1024,384]{1,0:T(8,128)(2,1)S(1)} %collective-permute-done.5), channel_id=1, source_target_pairs={{0,4},{1,5},{2,0},{3,1},{6,2},{7,3},{10,6},{11,7},{14,10},{15,11},... | collective-permute-start | bytes 2359304 | tf_op jit(solution)/shard_map/ppermute | solution.py:68
  112.2 17.7 %collective-permute-start.6 = (bf16[1024,384]{1,0:T(8,128)(2,1)S(1)}, bf16[1024,384]{1,0:T(8,128)(2,1)S(1)}, u32[]{:S(2)}, u32[]{:S(2)}) collective-permute-start(bf16[1024,384]{1,0:T(8,128)(2,1)S(1)} %collective-permute-done.4), channel_id=1, source_target_pairs={{0,2},{1,3},{2,6},{3,7},{6,10},{7,11},{10,14},{11,15},{14,12},{15,... | collective-permute-start | bytes 2359304 | tf_op jit(solution)/shard_map/ppermute | solution.py:68
  115.8 17.7 %collective-permute-start.9 = (bf16[1024,384]{1,0:T(8,128)(2,1)S(1)}, bf16[1024,384]{1,0:T(8,128)(2,1)S(1)}, u32[]{:S(2)}, u32[]{:S(2)}) collective-permute-start(bf16[1024,384]{1,0:T(8,128)(2,1)S(1)} %collective-permute-done.7), channel_id=1, source_target_pairs={{0,4},{1,5},{2,0},{3,1},{6,2},{7,3},{10,6},{11,7},{14,10},{15,11},... | collective-permute-start | bytes 2359304 | tf_op jit(solution)/shard_map/ppermute | solution.py:68
  129.9 17.7 %collective-permute-start.8 = (bf16[1024,384]{1,0:T(8,128)(2,1)S(1)}, bf16[1024,384]{1,0:T(8,128)(2,1)S(1)}, u32[]{:S(2)}, u32[]{:S(2)}) collective-permute-start(bf16[1024,384]{1,0:T(8,128)(2,1)S(1)} %collective-permute-done.6), channel_id=1, source_target_pairs={{0,2},{1,3},{2,6},{3,7},{6,10},{7,11},{10,14},{11,15},{14,12},{15,... | collective-permute-start | bytes 2359304 | tf_op jit(solution)/shard_map/ppermute | solution.py:68
  133.5 17.7 %collective-permute-start.11 = (bf16[1024,384]{1,0:T(8,128)(2,1)S(1)}, bf16[1024,384]{1,0:T(8,128)(2,1)S(1)}, u32[]{:S(2)}, u32[]{:S(2)}) collective-permute-start(bf16[1024,384]{1,0:T(8,128)(2,1)S(1)} %collective-permute-done.9), channel_id=1, source_target_pairs={{0,4},{1,5},{2,0},{3,1},{6,2},{7,3},{10,6},{11,7},{14,10},{15,11},... | collective-permute-start | bytes 2359304 | tf_op jit(solution)/shard_map/ppermute | solution.py:68
  147.6 17.7 %collective-permute-start.10 = (bf16[1024,384]{1,0:T(8,128)(2,1)S(1)}, bf16[1024,384]{1,0:T(8,128)(2,1)S(1)}, u32[]{:S(2)}, u32[]{:S(2)}) collective-permute-start(bf16[1024,384]{1,0:T(8,128)(2,1)S(1)} %collective-permute-done.8), channel_id=1, source_target_pairs={{0,2},{1,3},{2,6},{3,7},{6,10},{7,11},{10,14},{11,15},{14,12},{15,... | collective-permute-start | bytes 2359304 | tf_op jit(solution)/shard_map/ppermute | solution.py:68
  151.2 16.7 %collective-permute-start.13 = (bf16[1024,384]{1,0:T(8,128)(2,1)S(1)}, bf16[1024,384]{1,0:T(8,128)(2,1)S(1)}, u32[]{:S(2)}, u32[]{:S(2)}) collective-permute-start(bf16[1024,384]{1,0:T(8,128)(2,1)S(1)} %collective-permute-done.11), channel_id=1, source_target_pairs={{0,4},{1,5},{2,0},{3,1},{6,2},{7,3},{10,6},{11,7},{14,10},{15,11},... | collective-permute-start | bytes 2359304 | tf_op jit(solution)/shard_map/ppermute | solution.py:68
  165.3 14.5 %collective-permute-start.12 = (bf16[1024,384]{1,0:T(8,128)(2,1)S(1)}, bf16[1024,384]{1,0:T(8,128)(2,1)S(1)}, u32[]{:S(2)}, u32[]{:S(2)}) collective-permute-start(bf16[1024,384]{1,0:T(8,128)(2,1)S(1)} %collective-permute-done.10), channel_id=1, source_target_pairs={{0,2},{1,3},{2,6},{3,7},{6,10},{7,11},{10,14},{11,15},{14,12},{15,... | collective-permute-start | bytes 2359304 | tf_op jit(solution)/shard_map/ppermute | solution.py:68
  196.7 8.5 %copy-start.3 = (bf16[192,384]{1,0:T(8,128)(2,1)S(1)}, bf16[192,384]{1,0:T(8,128)(2,1)}, u32[]{:S(2)}) copy-start(bf16[192,384]{1,0:T(8,128)(2,1)} %param.21) | copy-start | bytes 442372
  202.3 2.8 %collective-permute-start.15 = (f32[200,384]{1,0:T(8,128)S(1)}, f32[200,384]{1,0:T(8,128)S(1)}, u32[]{:S(2)}, u32[]{:S(2)}) collective-permute-start(f32[200,384]{1,0:T(8,128)S(1)} %pad_maximum_fusion), channel_id=1, source_target_pairs={{0,1},{1,0},{2,3},{3,2},{4,5},{5,4},{6,7},{7,6},{8,9},{9,8},{10,11... | collective-permute-start | bytes 921608 | tf_op jit(solution)/shard_map/ppermute | solution.py:79

commit v2 on v1

v2 whole, which is shorter than its diff:
```python
import functools

import jax
import jax.numpy as jnp
import numpy as np
from jax import lax
from jax.experimental import pallas as pl
from jax.experimental.pallas import tpu as pltpu
from jax.sharding import PartitionSpec as P

CORES = 2
ONES = 16
MOST = 2
DEGREE_PARTS = 2
SHORT = pl.CostEstimate(flops=0, bytes_accessed=1024, transcendentals=0)
VMEM_LIMIT = 24 * 1024 * 1024


def chip_cycle(chips):
    wide = 1
    while (2 * wide) ** 2 <= chips:
        wide *= 2
    high = chips // wide
    if wide == 1 or high % 2 or wide * high != chips:
        return list(range(chips))
    walk = [(0, 0)]
    for i in range(high):
        line = range(1, wide)
        walk += [(i, j) for j in (line if i % 2 == 0 else reversed(line))]
    walk += [(i, 0) for i in range(high - 1, 0, -1)]
    return [i * wide + j for i, j in walk]


def lend_kernel(where, gate, *refs):
    out_ref = refs[-1]
    depth = refs[0].shape[1]
    for s, ref in enumerate(refs[:-1]):
        out_ref[:, s * depth : (s + 1) * depth] = ref[...]


def lend(where, gate, adj_rows, step, sections, n_row, depth):
    rows = adj_rows.shape[0]

    def block(s):
        return pl.BlockSpec(
            (rows, depth),
            lambda g, where: (0, s * n_row + where[1 + step * sections + s] * CORES + 1 - where[0]),
        )

    return pl.pallas_call(
        lend_kernel,
        grid_spec=pltpu.PrefetchScalarGridSpec(
            num_scalar_prefetch=1,
            grid=(1,),
            in_specs=[pl.BlockSpec(memory_space=pl.ANY)] + [block(s) for s in range(sections)],
            out_specs=pl.BlockSpec((rows, sections * depth), lambda g, where: (0, 0)),
        ),
        out_shape=jax.ShapeDtypeStruct((rows, sections * depth), adj_rows.dtype),
        compiler_params=pltpu.CompilerParams(vmem_limit_bytes=VMEM_LIMIT),
        cost_estimate=SHORT,
        name="lend",
    )(where, gate, *[adj_rows] * sections)


def absorb_kernel(sections, rows, first, where, *refs):
    own, other, slab = (refs[k * sections : (k + 1) * sections] for k in range(3))
    mine_out, theirs_out = refs[-2:]
    total = None
    for s in range(sections):
        ones = jnp.ones((ONES, own[s].shape[1]), own[s].dtype)
        left = jnp.concatenate([own[s][...], other[s][...], ones], axis=0)
        product = jnp.dot(left, slab[s][...], preferred_element_type=jnp.float32)
        total = product if total is None else total + product
    mine, theirs = total[:rows], total[rows:]
    if not first:
        mine_in, theirs_in = refs[3 * sections : 3 * sections + 2]
        mine, theirs = mine + mine_in[...], theirs + theirs_in[...]
    mine_out[...] = mine
    theirs_out[...] = theirs


def absorb(where, adj_rows, borrowed, slabs, sums, step, chunk, chunks, n_row):
    sections = len(slabs)
    rows = adj_rows.shape[0]
    deep, width = slabs[0].shape

    def own(s):
        return pl.BlockSpec(
            (rows, deep),
            lambda g, where: (
                0,
                (s * n_row + where[1 + step * sections + s] * CORES + where[0]) * chunks + chunk,
            ),
        )

    def other(s):
        return pl.BlockSpec(
            (rows, deep),
            lambda g, where: (0, s * chunks + chunk),
        )

    whole = lambda shape: pl.BlockSpec(shape, lambda g, where: (0, 0))
    shapes = [(rows, width), (rows + ONES, width)]
    first = sums is None
    operands = [adj_rows] * sections + [borrowed] * sections + list(slabs)
    in_specs = [own(s) for s in range(sections)] + [other(s) for s in range(sections)]
    in_specs += [whole((deep, width))] * sections
    if not first:
        operands += list(sums)
        in_specs += [whole(shape) for shape in shapes]
    at = 1 + 3 * sections
    return pl.pallas_call(
        functools.partial(absorb_kernel, sections, rows, first),
        grid_spec=pltpu.PrefetchScalarGridSpec(
            num_scalar_prefetch=1,
            grid=(1,),
            in_specs=in_specs,
            out_specs=[whole(shape) for shape in shapes],
        ),
        out_shape=[jax.ShapeDtypeStruct(shape, jnp.float32) for shape in shapes],
        input_output_aliases={} if first else {at: 0, at + 1: 1},
        compiler_params=pltpu.CompilerParams(vmem_limit_bytes=VMEM_LIMIT),
        cost_estimate=SHORT,
        name="absorb",
    )(where, *operands)


def make_shards(n_row):
    chips = n_row // CORES
    cycle = chip_cycle(chips)
    place = {chip: k for k, chip in enumerate(cycle)}

    def way(section):
        return 1 if section % 2 == 0 else -1

    def ring(step):
        return [
            (cycle[k] * CORES + c, cycle[(k + step) % chips] * CORES + c)
            for k in range(chips)
            for c in range(CORES)
        ]

    swap = [(d, d ^ 1) for d in range(n_row)]

    def shards(adj_rows, adj_panel, adj_tile):
        rows = adj_rows.shape[0]
        sections, depth, width = adj_panel.shape
        chunks = 2 if depth % 256 == 0 else 1
        deep = depth // chunks
        table = np.array(
            [
                [d % CORES]
                + [
                    cycle[(place[d // CORES] - way(s) * step) % chips]
                    for step in range(chips)
                    for s in range(sections)
                ]
                for d in range(n_row)
            ],
            np.int32,
        )
        where = jnp.asarray(table)[lax.axis_index("row")]

        held = [
            [adj_panel[s, j * deep : (j + 1) * deep] for s in range(sections)] for j in range(chunks)
        ]
        sums = None
        degree = []
        borrowed = {}
        due = [(0, j, held[j]) for j in range(chunks)]
        lends = list(range(chips))
        stretch = adj_rows.shape[1] // DEGREE_PARTS
        done = ()

        def tie(values, others):
            return lax.optimization_barrier((values, others))[0]

        for step in range(1, chips + 1):
            arrived = []
            for j in range(chunks):
                if step > 1:
                    held[j] = tie(held[j], done)
                if step < chips:
                    arrived.append([lax.ppermute(held[j][s], "row", ring(way(s))) for s in range(sections)])
                if step == 1:
                    continue
                now = tie(adj_rows, held[j])
                done = []
                at = step - 1
                while lends and lends[0] <= at + 1 and len(done) < MOST:
                    coming = lends.pop(0)
                    lent = lend(where, held[j][0], adj_rows, coming, sections, n_row, depth)
                    borrowed[coming] = lax.ppermute(lent, "row", swap)
                    done.append(lent)
                due.append((at, j, held[j]))
                if at > 1 or chips == 2:
                    for _ in range(MOST if step < chips else len(due)):
                        if due:
                            t, part, slabs = due.pop(0)
                            sums = absorb(
                                where, now, borrowed[t], tie(slabs, held[j]), sums, t, part, chunks, n_row
                            )
                            done.append(sums)
                if at > 2 and j == 0 and len(degree) < DEGREE_PARTS:
                    k = len(degree) * stretch
                    part = lax.slice_in_dim(now, k, k + stretch, axis=1)
                    degree.append(jnp.sum(part, axis=1, dtype=jnp.float32))
                    done.append(degree[-1])
            held = arrived
        degree = sum(degree)

        mine, theirs = sums
        partner = lax.ppermute(theirs, "row", swap)
        square = mine + partner[:rows]
        col_degree = theirs[rows : rows + 1] + partner[rows : rows + 1]
        tile = adj_tile.astype(jnp.float32)
        lower = jnp.minimum(degree[:, None], col_degree)
        intersection = (square + tile) / (lower + 1.0 - tile)
        return (intersection, degree)

    return shards


def solution(mesh):
    in_specs = (
        P(("parts", "row"), None),
        P(None, ("parts", "row"), None),
        P(("parts", "row"), None),
    )
    out_specs = (P(("parts", "row"), None), P(("parts", "row")))
    return jax.shard_map(
        make_shards(mesh.shape["row"]), mesh=mesh, in_specs=in_specs, out_specs=out_specs, check_vma=False
    )
```

time: 210 us -> 141 us (0.67); the launches traced: 207 us -> 141 us
  matrix products: 45.8 us -> 0 us
  local copies, waits for them, and re-layouts: 35.5 us -> 9.42 us
  Pallas kernels: 0 us -> 23 us
  between operations: 16.9 us -> 1.04 us
  starting transfers between devices: 16 us -> 31 us
  waiting for transfers between devices: 82.7 us -> 73.6 us
  other arithmetic: 10.4 us -> 2.81 us
    dot_general x32 -> x0, matrix products: 45.8 us -> none  [the longest x16 23.6 us: shards(): mine = mine + jnp.dot(own, piece, preferred_element_type=jnp.float32)]
    pallas_call x0 -> x24, Pallas kernels: none -> 23 us  [the longest x16 18.2 us: absorb(): pl.pallas_call(functools.partial(absorb_kernel, sections, rows, first), g...]
    unnamed x39 -> x20, local copies, waits for them, and re-layouts: 27.2 us -> 7.22 us
    ppermute x16 -> x37, starting transfers between devices: 16 us -> 31 us  [the longest x28 30.4 us: shards(): lax.ppermute(held[j][s], 'row', ring(way(s)))]
    ppermute x16 -> x37, waiting for transfers between devices: 82.7 us -> 73.6 us  [the longest x28 72 us: shards(): lax.ppermute(held[j][s], 'row', ring(way(s)))]
    reduce_sum x16 -> x2, other arithmetic: 10.4 us -> 1.93 us  [shards(): degree.append(jnp.sum(part, axis=1, dtype=jnp.float32))]
    dynamic_slice x8 -> x0, local copies, waits for them, and re-layouts: 5.12 us -> none  [shards(): chip = jnp.asarray(owners(step if s % 2 == 0 else -step))[me]]
  transfers between devices with their start and end apart: 16 -> 37, of which waited for: 7 -> 26; matrix products, arithmetic and copies ran while one was open for 18% -> 2% of each run, Pallas kernels for 0% -> 16%
where the time goes in v2:
time: 141 us
  waiting for transfers between devices  73.6 us (52%)
  starting transfers between devices  31 us (22%)
  Pallas kernels  23 us (16%)
  local copies, waits for them, and re-layouts  9.42 us (7%)
  other arithmetic  2.81 us (2%)
    ppermute x28, waiting for transfers between devices, shards(): lax.ppermute(held[j][s], 'row', ring(way(s)))  72 us
    ppermute x28, starting transfers between devices, shards(): lax.ppermute(held[j][s], 'row', ring(way(s)))  30.4 us
    pallas_call x16, Pallas kernels, absorb(): pl.pallas_call(functools.partial(absorb_kernel, sections, rows, first), g...  18.2 us
    unnamed x20, local copies, waits for them, and re-layouts  7.22 us
    pallas_call x8, Pallas kernels, lend(): pl.pallas_call(lend_kernel, grid_spec=pltpu.PrefetchScalarGridSpec(num_sc...  4.76 us
  transfers between devices with their start and end apart: 37, of which 26 were waited for; matrix products, arithmetic and copies ran while one was open for 2% of the time, Pallas kernels for 16%

profile of v2, /device:TPU:0, one launch (start us, length us, event | category | flops | bytes accessed | tf_op | source)
XLA Modules:
  0.0 140.8 jit_solution(9855522157785848267)
XLA Ops:
  0.6 1.5 %slice_bitcast_fusion = (bf16[512,384]{1,0:T(8,128)(2,1)S(1)}, bf16[512,384]{1,0:T(8,128)(2,1)S(1)}, bf16[512,384]{1,0:T(8,128)(2,1)S(1)}, bf16[512,384]{1,0:T(8,128)(2,1)S(1)}) fusion(bf16[2,1024,384]{2,1,0:T(8,128)(2,1)} %param.5), kind=kLoop, calls=%fused_computation.2 | loop fusion | bytes 3145728 | tf_op jit(solution)/shard_map/squeeze | solution.py:165
  2.1 3.0 %collective-permute-start.2 = (bf16[512,384]{1,0:T(8,128)(2,1)S(1)}, bf16[512,384]{1,0:T(8,128)(2,1)S(1)}, u32[]{:S(2)}, u32[]{:S(2)}) collective-permute-start(bf16[512,384]{1,0:T(8,128)(2,1)S(1)} %get-tuple-element.113.refs_4_), channel_id=1, source_target_pairs={{0,2},{1,3},{2,6},{3,7},{6,10},{7,11},{10,14},{11,15},{14,12},{15,... | collective-permute-start | bytes 1179656 | tf_op jit(solution)/shard_map/ppermute | solution.py:184
  5.3 1.9 %collective-permute-start = (bf16[512,384]{1,0:T(8,128)(2,1)S(1)}, bf16[512,384]{1,0:T(8,128)(2,1)S(1)}, u32[]{:S(2)}, u32[]{:S(2)}) collective-permute-start(bf16[512,384]{1,0:T(8,128)(2,1)S(1)} %get-tuple-element.117.refs_4_), channel_id=1, source_target_pairs={{0,2},{1,3},{2,6},{3,7},{6,10},{7,11},{10,14},{11,15},{14,12},{15,... | collective-permute-start | bytes 1179656 | tf_op jit(solution)/shard_map/ppermute | solution.py:184
  8.0 7.2 %collective-permute-done.2.gate.refs_4_ = bf16[512,384]{1,0:T(8,128)(2,1)S(1)} collective-permute-done((bf16[512,384]{1,0:T(8,128)(2,1)S(1)}, bf16[512,384]{1,0:T(8,128)(2,1)S(1)}, u32[]{:S(2)}, u32[]{:S(2)}) %collective-permute-start.2) | collective-permute-done | bytes 393248 | tf_op jit(solution)/shard_map/ppermute | solution.py:184
  15.2 2.0 %collective-permute-done.3.refs_5_ = bf16[512,384]{1,0:T(8,128)(2,1)S(1)} collective-permute-done((bf16[512,384]{1,0:T(8,128)(2,1)S(1)}, bf16[512,384]{1,0:T(8,128)(2,1)S(1)}, u32[]{:S(2)}, u32[]{:S(2)}) %collective-permute-start.3) | collective-permute-done | bytes 393248 | tf_op jit(solution)/shard_map/ppermute | solution.py:184
  17.2 4.6 %copy-done = bf16[192,32768]{1,0:T(8,128)(2,1)S(1)} copy-done((bf16[192,32768]{1,0:T(8,128)(2,1)S(1)}, bf16[192,32768]{1,0:T(8,128)(2,1)}, u32[]{:S(2)}) %copy-start) | copy-done | bytes 12582936
  22.5 1.6 %collective-permute-start.6 = (bf16[512,384]{1,0:T(8,128)(2,1)S(1)}, bf16[512,384]{1,0:T(8,128)(2,1)S(1)}, u32[]{:S(2)}, u32[]{:S(2)}) collective-permute-start(bf16[512,384]{1,0:T(8,128)(2,1)S(1)} %collective-permute-done.2.gate.refs_4_), channel_id=1, source_target_pairs={{0,2},{1,3},{2,6},{3,7},{6,10},{7,11},{10,14},{11,15},{14,12},{15,... | collective-permute-start | bytes 1179656 | tf_op jit(solution)/shard_map/ppermute | solution.py:184
  25.2 1.6 %collective-permute-start.4 = (bf16[512,384]{1,0:T(8,128)(2,1)S(1)}, bf16[512,384]{1,0:T(8,128)(2,1)S(1)}, u32[]{:S(2)}, u32[]{:S(2)}) collective-permute-start(bf16[512,384]{1,0:T(8,128)(2,1)S(1)} %collective-permute-done.gate.refs_4_), channel_id=1, source_target_pairs={{0,2},{1,3},{2,6},{3,7},{6,10},{7,11},{10,14},{11,15},{14,12},{15,... | collective-permute-start | bytes 1179656 | tf_op jit(solution)/shard_map/ppermute | solution.py:184
  27.5 7.0 %collective-permute-done.6.gate.refs_4_ = bf16[512,384]{1,0:T(8,128)(2,1)S(1)} collective-permute-done((bf16[512,384]{1,0:T(8,128)(2,1)S(1)}, bf16[512,384]{1,0:T(8,128)(2,1)S(1)}, u32[]{:S(2)}, u32[]{:S(2)}) %collective-permute-start.6) | collective-permute-done | bytes 393248 | tf_op jit(solution)/shard_map/ppermute | solution.py:184
  35.7 6.7 %collective-permute-done.4.refs_4_ = bf16[512,384]{1,0:T(8,128)(2,1)S(1)} collective-permute-done((bf16[512,384]{1,0:T(8,128)(2,1)S(1)}, bf16[512,384]{1,0:T(8,128)(2,1)S(1)}, u32[]{:S(2)}, u32[]{:S(2)}) %collective-permute-start.4) | collective-permute-done | bytes 393248 | tf_op jit(solution)/shard_map/ppermute | solution.py:184
  42.4 1.6 %collective-permute-start.11 = (bf16[512,384]{1,0:T(8,128)(2,1)S(1)}, bf16[512,384]{1,0:T(8,128)(2,1)S(1)}, u32[]{:S(2)}, u32[]{:S(2)}) collective-permute-start(bf16[512,384]{1,0:T(8,128)(2,1)S(1)} %collective-permute-done.6.gate.refs_4_), channel_id=1, source_target_pairs={{0,2},{1,3},{2,6},{3,7},{6,10},{7,11},{10,14},{11,15},{14,12},{15,... | collective-permute-start | bytes 1179656 | tf_op jit(solution)/shard_map/ppermute | solution.py:184
  46.2 1.1 absorb.17
  47.8 1.1 absorb.18
  49.0 1.1 absorb.19
  50.2 2.9 %collective-permute-done.11.gate.refs_4_ = bf16[512,384]{1,0:T(8,128)(2,1)S(1)} collective-permute-done((bf16[512,384]{1,0:T(8,128)(2,1)S(1)}, bf16[512,384]{1,0:T(8,128)(2,1)S(1)}, u32[]{:S(2)}, u32[]{:S(2)}) %collective-permute-start.11) | collective-permute-done | bytes 393248 | tf_op jit(solution)/shard_map/ppermute | solution.py:184
  53.1 3.0 %collective-permute-done.12.refs_5_ = bf16[512,384]{1,0:T(8,128)(2,1)S(1)} collective-permute-done((bf16[512,384]{1,0:T(8,128)(2,1)S(1)}, bf16[512,384]{1,0:T(8,128)(2,1)S(1)}, u32[]{:S(2)}, u32[]{:S(2)}) %collective-permute-start.12) | collective-permute-done | bytes 393248 | tf_op jit(solution)/shard_map/ppermute | solution.py:184
  56.6 1.6 %collective-permute-start.9 = (bf16[512,384]{1,0:T(8,128)(2,1)S(1)}, bf16[512,384]{1,0:T(8,128)(2,1)S(1)}, u32[]{:S(2)}, u32[]{:S(2)}) collective-permute-start(bf16[512,384]{1,0:T(8,128)(2,1)S(1)} %collective-permute-done.4.refs_4_), channel_id=1, source_target_pairs={{0,2},{1,3},{2,6},{3,7},{6,10},{7,11},{10,14},{11,15},{14,12},{15,... | collective-permute-start | bytes 1179656 | tf_op jit(solution)/shard_map/ppermute | solution.py:184
  58.3 1.6 %collective-permute-start.17 = (bf16[512,384]{1,0:T(8,128)(2,1)S(1)}, bf16[512,384]{1,0:T(8,128)(2,1)S(1)}, u32[]{:S(2)}, u32[]{:S(2)}) collective-permute-start(bf16[512,384]{1,0:T(8,128)(2,1)S(1)} %collective-permute-done.11.gate.refs_4_), channel_id=1, source_target_pairs={{0,2},{1,3},{2,6},{3,7},{6,10},{7,11},{10,14},{11,15},{14,12},{15,... | collective-permute-start | bytes 1179656 | tf_op jit(solution)/shard_map/ppermute | solution.py:184
  59.9 1.1 absorb.20
  61.2 1.1 absorb.21
  63.3 1.2 slice-done.1
  64.5 1.2 slice-done.2
  66.7 2.1 %collective-permute-done.9.refs_4_ = bf16[512,384]{1,0:T(8,128)(2,1)S(1)} collective-permute-done((bf16[512,384]{1,0:T(8,128)(2,1)S(1)}, bf16[512,384]{1,0:T(8,128)(2,1)S(1)}, u32[]{:S(2)}, u32[]{:S(2)}) %collective-permute-start.9) | collective-permute-done | bytes 393248 | tf_op jit(solution)/shard_map/ppermute | solution.py:184
  68.7 1.1 absorb.22
  70.0 1.1 absorb.23
  71.1 1.8 %collective-permute-done.17.gate.refs_4_ = bf16[512,384]{1,0:T(8,128)(2,1)S(1)} collective-permute-done((bf16[512,384]{1,0:T(8,128)(2,1)S(1)}, bf16[512,384]{1,0:T(8,128)(2,1)S(1)}, u32[]{:S(2)}, u32[]{:S(2)}) %collective-permute-start.17) | collective-permute-done | bytes 393248 | tf_op jit(solution)/shard_map/ppermute | solution.py:184
  75.3 1.4 collective-permute-start.16
  77.3 1.4 collective-permute-start.24
  79.7 1.1 absorb.24
  80.8 5.7 %collective-permute-done.15.refs_4_ = bf16[512,384]{1,0:T(8,128)(2,1)S(1)} collective-permute-done((bf16[512,384]{1,0:T(8,128)(2,1)S(1)}, bf16[512,384]{1,0:T(8,128)(2,1)S(1)}, u32[]{:S(2)}, u32[]{:S(2)}) %collective-permute-start.15) | collective-permute-done | bytes 393248 | tf_op jit(solution)/shard_map/ppermute | solution.py:184
  87.2 2.2 %collective-permute-start.21 = (bf16[512,384]{1,0:T(8,128)(2,1)S(1)}, bf16[512,384]{1,0:T(8,128)(2,1)S(1)}, u32[]{:S(2)}, u32[]{:S(2)}) collective-permute-start(bf16[512,384]{1,0:T(8,128)(2,1)S(1)} %collective-permute-done.15.refs_4_), channel_id=1, source_target_pairs={{0,2},{1,3},{2,6},{3,7},{6,10},{7,11},{10,14},{11,15},{14,12},{15,... | collective-permute-start | bytes 1179656 | tf_op jit(solution)/shard_map/ppermute | solution.py:184
  90.5 4.4 %collective-permute-done.23.gate.refs_4_ = bf16[512,384]{1,0:T(8,128)(2,1)S(1)} collective-permute-done((bf16[512,384]{1,0:T(8,128)(2,1)S(1)}, bf16[512,384]{1,0:T(8,128)(2,1)S(1)}, u32[]{:S(2)}, u32[]{:S(2)}) %collective-permute-start.23) | collective-permute-done | bytes 393248 | tf_op jit(solution)/shard_map/ppermute | solution.py:184
  96.3 2.2 %collective-permute-start.28 = (bf16[512,384]{1,0:T(8,128)(2,1)S(1)}, bf16[512,384]{1,0:T(8,128)(2,1)S(1)}, u32[]{:S(2)}, u32[]{:S(2)}) collective-permute-start(bf16[512,384]{1,0:T(8,128)(2,1)S(1)} %collective-permute-done.23.gate.refs_4_), channel_id=1, source_target_pairs={{0,2},{1,3},{2,6},{3,7},{6,10},{7,11},{10,14},{11,15},{14,12},{15,... | collective-permute-start | bytes 1179656 | tf_op jit(solution)/shard_map/ppermute | solution.py:184
  98.6 1.1 absorb.26
  99.7 3.7 %collective-permute-done.21.refs_4_ = bf16[512,384]{1,0:T(8,128)(2,1)S(1)} collective-permute-done((bf16[512,384]{1,0:T(8,128)(2,1)S(1)}, bf16[512,384]{1,0:T(8,128)(2,1)S(1)}, u32[]{:S(2)}, u32[]{:S(2)}) %collective-permute-start.21) | collective-permute-done | bytes 393248 | tf_op jit(solution)/shard_map/ppermute | solution.py:184
  104.1 2.2 %collective-permute-start.26 = (bf16[512,384]{1,0:T(8,128)(2,1)S(1)}, bf16[512,384]{1,0:T(8,128)(2,1)S(1)}, u32[]{:S(2)}, u32[]{:S(2)}) collective-permute-start(bf16[512,384]{1,0:T(8,128)(2,1)S(1)} %collective-permute-done.21.refs_4_), channel_id=1, source_target_pairs={{0,2},{1,3},{2,6},{3,7},{6,10},{7,11},{10,14},{11,15},{14,12},{15,... | collective-permute-start | bytes 1179656 | tf_op jit(solution)/shard_map/ppermute | solution.py:184
  106.2 1.1 absorb.27
  107.4 4.4 %collective-permute-done.28.gate.refs_4_ = bf16[512,384]{1,0:T(8,128)(2,1)S(1)} collective-permute-done((bf16[512,384]{1,0:T(8,128)(2,1)S(1)}, bf16[512,384]{1,0:T(8,128)(2,1)S(1)}, u32[]{:S(2)}, u32[]{:S(2)}) %collective-permute-start.28) | collective-permute-done | bytes 393248 | tf_op jit(solution)/shard_map/ppermute | solution.py:184
  113.2 2.2 %collective-permute-start.33 = (bf16[512,384]{1,0:T(8,128)(2,1)S(1)}, bf16[512,384]{1,0:T(8,128)(2,1)S(1)}, u32[]{:S(2)}, u32[]{:S(2)}) collective-permute-start(bf16[512,384]{1,0:T(8,128)(2,1)S(1)} %collective-permute-done.28.gate.refs_4_), channel_id=1, source_target_pairs={{0,2},{1,3},{2,6},{3,7},{6,10},{7,11},{10,14},{11,15},{14,12},{15,... | collective-permute-start | bytes 1179656 | tf_op jit(solution)/shard_map/ppermute | solution.py:184
  115.4 1.1 absorb.28
  116.6 3.7 %collective-permute-done.26.refs_4_ = bf16[512,384]{1,0:T(8,128)(2,1)S(1)} collective-permute-done((bf16[512,384]{1,0:T(8,128)(2,1)S(1)}, bf16[512,384]{1,0:T(8,128)(2,1)S(1)}, u32[]{:S(2)}, u32[]{:S(2)}) %collective-permute-start.26) | collective-permute-done | bytes 393248 | tf_op jit(solution)/shard_map/ppermute | solution.py:184
  120.9 2.2 %collective-permute-start.31 = (bf16[512,384]{1,0:T(8,128)(2,1)S(1)}, bf16[512,384]{1,0:T(8,128)(2,1)S(1)}, u32[]{:S(2)}, u32[]{:S(2)}) collective-permute-start(bf16[512,384]{1,0:T(8,128)(2,1)S(1)} %collective-permute-done.26.refs_4_), channel_id=1, source_target_pairs={{0,2},{1,3},{2,6},{3,7},{6,10},{7,11},{10,14},{11,15},{14,12},{15,... | collective-permute-start | bytes 1179656 | tf_op jit(solution)/shard_map/ppermute | solution.py:184
  123.1 1.1 absorb.29
  124.2 4.4 %collective-permute-done.33.refs_4_ = bf16[512,384]{1,0:T(8,128)(2,1)S(1)} collective-permute-done((bf16[512,384]{1,0:T(8,128)(2,1)S(1)}, bf16[512,384]{1,0:T(8,128)(2,1)S(1)}, u32[]{:S(2)}, u32[]{:S(2)}) %collective-permute-start.33) | collective-permute-done | bytes 393248 | tf_op jit(solution)/shard_map/ppermute | solution.py:184
  129.4 1.1 absorb.30
  130.5 6.2 %collective-permute-done.31.refs_4_ = bf16[512,384]{1,0:T(8,128)(2,1)S(1)} collective-permute-done((bf16[512,384]{1,0:T(8,128)(2,1)S(1)}, bf16[512,384]{1,0:T(8,128)(2,1)S(1)}, u32[]{:S(2)}, u32[]{:S(2)}) %collective-permute-start.31) | collective-permute-done | bytes 393248 | tf_op jit(solution)/shard_map/ppermute | solution.py:184
  137.1 1.1 absorb.31
  138.3 1.6 %collective-permute-done.36 = f32[208,384]{1,0:T(8,128)S(1)} collective-permute-done((f32[208,384]{1,0:T(8,128)S(1)}, f32[208,384]{1,0:T(8,128)S(1)}, u32[]{:S(2)}, u32[]{:S(2)}) %collective-permute-start.36) | collective-permute-done | bytes 319520 | tf_op jit(solution)/shard_map/ppermute | solution.py:213
  (78 shorter events, 21.7 us)
Async XLA Ops:
  2.1 13.0 %collective-permute-start.2 = (bf16[512,384]{1,0:T(8,128)(2,1)S(1)}, bf16[512,384]{1,0:T(8,128)(2,1)S(1)}, u32[]{:S(2)}, u32[]{:S(2)}) collective-permute-start(bf16[512,384]{1,0:T(8,128)(2,1)S(1)} %get-tuple-element.113.refs_4_), channel_id=1, source_target_pairs={{0,2},{1,3},{2,6},{3,7},{6,10},{7,11},{10,14},{11,15},{14,12},{15,... | collective-permute-start | bytes 1179656 | tf_op jit(solution)/shard_map/ppermute | solution.py:184
  5.2 12.0 %collective-permute-start.3 = (bf16[512,384]{1,0:T(8,128)(2,1)S(1)}, bf16[512,384]{1,0:T(8,128)(2,1)S(1)}, u32[]{:S(2)}, u32[]{:S(2)}) collective-permute-start(bf16[512,384]{1,0:T(8,128)(2,1)S(1)} %get-tuple-element.114.refs_5_), channel_id=1, source_target_pairs={{0,4},{1,5},{2,0},{3,1},{6,2},{7,3},{10,6},{11,7},{14,10},{15,11},... | collective-permute-start | bytes 1179656 | tf_op jit(solution)/shard_map/ppermute | solution.py:184
  5.3 19.9 %collective-permute-start = (bf16[512,384]{1,0:T(8,128)(2,1)S(1)}, bf16[512,384]{1,0:T(8,128)(2,1)S(1)}, u32[]{:S(2)}, u32[]{:S(2)}) collective-permute-start(bf16[512,384]{1,0:T(8,128)(2,1)S(1)} %get-tuple-element.117.refs_4_), channel_id=1, source_target_pairs={{0,2},{1,3},{2,6},{3,7},{6,10},{7,11},{10,14},{11,15},{14,12},{15,... | collective-permute-start | bytes 1179656 | tf_op jit(solution)/shard_map/ppermute | solution.py:184
  7.2 18.0 %collective-permute-start.1 = (bf16[512,384]{1,0:T(8,128)(2,1)S(1)}, bf16[512,384]{1,0:T(8,128)(2,1)S(1)}, u32[]{:S(2)}, u32[]{:S(2)}) collective-permute-start(bf16[512,384]{1,0:T(8,128)(2,1)S(1)} %get-tuple-element.118.refs_5_), channel_id=1, source_target_pairs={{0,4},{1,5},{2,0},{3,1},{6,2},{7,3},{10,6},{11,7},{14,10},{15,11},... | collective-permute-start | bytes 1179656 | tf_op jit(solution)/shard_map/ppermute | solution.py:184
  17.2 4.6 %copy-start = (bf16[192,32768]{1,0:T(8,128)(2,1)S(1)}, bf16[192,32768]{1,0:T(8,128)(2,1)}, u32[]{:S(2)}) copy-start(bf16[192,32768]{1,0:T(8,128)(2,1)} %refs_1_.31) | copy-start | bytes 37748740
  22.4 21.6 %collective-permute-start.8 = (bf16[192,2048]{1,0:T(8,128)(2,1)S(1)}, bf16[192,2048]{1,0:T(8,128)(2,1)S(1)}, u32[]{:S(2)}, u32[]{:S(2)}) collective-permute-start(bf16[192,2048]{1,0:T(8,128)(2,1)S(1)} %lend.8), channel_id=1, source_target_pairs={{0,1},{1,0},{2,3},{3,2},{4,5},{5,4},{6,7},{7,6},{8,9},{9,8},{10,11... | collective-permute-start | bytes 2359304 | tf_op jit(solution)/shard_map/ppermute | solution.py:193
  22.5 12.0 %collective-permute-start.6 = (bf16[512,384]{1,0:T(8,128)(2,1)S(1)}, bf16[512,384]{1,0:T(8,128)(2,1)S(1)}, u32[]{:S(2)}, u32[]{:S(2)}) collective-permute-start(bf16[512,384]{1,0:T(8,128)(2,1)S(1)} %collective-permute-done.2.gate.refs_4_), channel_id=1, source_target_pairs={{0,2},{1,3},{2,6},{3,7},{6,10},{7,11},{10,14},{11,15},{14,12},{15,... | collective-permute-start | bytes 1179656 | tf_op jit(solution)/shard_map/ppermute | solution.py:184
  24.1 11.2 %collective-permute-start.7 = (bf16[512,384]{1,0:T(8,128)(2,1)S(1)}, bf16[512,384]{1,0:T(8,128)(2,1)S(1)}, u32[]{:S(2)}, u32[]{:S(2)}) collective-permute-start(bf16[512,384]{1,0:T(8,128)(2,1)S(1)} %collective-permute-done.3.refs_5_), channel_id=1, source_target_pairs={{0,4},{1,5},{2,0},{3,1},{6,2},{7,3},{10,6},{11,7},{14,10},{15,11},... | collective-permute-start | bytes 1179656 | tf_op jit(solution)/shard_map/ppermute | solution.py:184
  25.2 22.6 %collective-permute-start.13 = (bf16[192,2048]{1,0:T(8,128)(2,1)S(1)}, bf16[192,2048]{1,0:T(8,128)(2,1)S(1)}, u32[]{:S(2)}, u32[]{:S(2)}) collective-permute-start(bf16[192,2048]{1,0:T(8,128)(2,1)S(1)} %lend.9), channel_id=1, source_target_pairs={{0,1},{1,0},{2,3},{3,2},{4,5},{5,4},{6,7},{7,6},{8,9},{9,8},{10,11... | collective-permute-start | bytes 2359304 | tf_op jit(solution)/shard_map/ppermute | solution.py:193
  25.2 17.2 %collective-permute-start.4 = (bf16[512,384]{1,0:T(8,128)(2,1)S(1)}, bf16[512,384]{1,0:T(8,128)(2,1)S(1)}, u32[]{:S(2)}, u32[]{:S(2)}) collective-permute-start(bf16[512,384]{1,0:T(8,128)(2,1)S(1)} %collective-permute-done.gate.refs_4_), channel_id=1, source_target_pairs={{0,2},{1,3},{2,6},{3,7},{6,10},{7,11},{10,14},{11,15},{14,12},{15,... | collective-permute-start | bytes 1179656 | tf_op jit(solution)/shard_map/ppermute | solution.py:184
  34.4 25.4 %collective-permute-start.14 = (bf16[192,2048]{1,0:T(8,128)(2,1)S(1)}, bf16[192,2048]{1,0:T(8,128)(2,1)S(1)}, u32[]{:S(2)}, u32[]{:S(2)}) collective-permute-start(bf16[192,2048]{1,0:T(8,128)(2,1)S(1)} %lend.10), channel_id=1, source_target_pairs={{0,1},{1,0},{2,3},{3,2},{4,5},{5,4},{6,7},{7,6},{8,9},{9,8},{10,11... | collective-permute-start | bytes 2359304 | tf_op jit(solution)/shard_map/ppermute | solution.py:193
  35.3 12.1 %collective-permute-start.5 = (bf16[512,384]{1,0:T(8,128)(2,1)S(1)}, bf16[512,384]{1,0:T(8,128)(2,1)S(1)}, u32[]{:S(2)}, u32[]{:S(2)}) collective-permute-start(bf16[512,384]{1,0:T(8,128)(2,1)S(1)} %collective-permute-done.1.refs_5_), channel_id=1, source_target_pairs={{0,4},{1,5},{2,0},{3,1},{6,2},{7,3},{10,6},{11,7},{14,10},{15,11},... | collective-permute-start | bytes 1179656 | tf_op jit(solution)/shard_map/ppermute | solution.py:184
  42.4 10.7 %collective-permute-start.11 = (bf16[512,384]{1,0:T(8,128)(2,1)S(1)}, bf16[512,384]{1,0:T(8,128)(2,1)S(1)}, u32[]{:S(2)}, u32[]{:S(2)}) collective-permute-start(bf16[512,384]{1,0:T(8,128)(2,1)S(1)} %collective-permute-done.6.gate.refs_4_), channel_id=1, source_target_pairs={{0,2},{1,3},{2,6},{3,7},{6,10},{7,11},{10,14},{11,15},{14,12},{15,... | collective-permute-start | bytes 1179656 | tf_op jit(solution)/shard_map/ppermute | solution.py:184
  44.0 12.1 %collective-permute-start.12 = (bf16[512,384]{1,0:T(8,128)(2,1)S(1)}, bf16[512,384]{1,0:T(8,128)(2,1)S(1)}, u32[]{:S(2)}, u32[]{:S(2)}) collective-permute-start(bf16[512,384]{1,0:T(8,128)(2,1)S(1)} %collective-permute-done.7.refs_5_), channel_id=1, source_target_pairs={{0,4},{1,5},{2,0},{3,1},{6,2},{7,3},{10,6},{11,7},{14,10},{15,11},... | collective-permute-start | bytes 1179656 | tf_op jit(solution)/shard_map/ppermute | solution.py:184
  47.4 15.4 %collective-permute-start.10 = (bf16[512,384]{1,0:T(8,128)(2,1)S(1)}, bf16[512,384]{1,0:T(8,128)(2,1)S(1)}, u32[]{:S(2)}, u32[]{:S(2)}) collective-permute-start(bf16[512,384]{1,0:T(8,128)(2,1)S(1)} %collective-permute-done.5.refs_5_), channel_id=1, source_target_pairs={{0,4},{1,5},{2,0},{3,1},{6,2},{7,3},{10,6},{11,7},{14,10},{15,11},... | collective-permute-start | bytes 1179656 | tf_op jit(solution)/shard_map/ppermute | solution.py:184
  47.8 20.9 %collective-permute-start.19 = (bf16[192,2048]{1,0:T(8,128)(2,1)S(1)}, bf16[192,2048]{1,0:T(8,128)(2,1)S(1)}, u32[]{:S(2)}, u32[]{:S(2)}) collective-permute-start(bf16[192,2048]{1,0:T(8,128)(2,1)S(1)} %lend.11), channel_id=1, source_target_pairs={{0,1},{1,0},{2,3},{3,2},{4,5},{5,4},{6,7},{7,6},{8,9},{9,8},{10,11... | collective-permute-start | bytes 2359304 | tf_op jit(solution)/shard_map/ppermute | solution.py:193
  56.6 12.1 %collective-permute-start.9 = (bf16[512,384]{1,0:T(8,128)(2,1)S(1)}, bf16[512,384]{1,0:T(8,128)(2,1)S(1)}, u32[]{:S(2)}, u32[]{:S(2)}) collective-permute-start(bf16[512,384]{1,0:T(8,128)(2,1)S(1)} %collective-permute-done.4.refs_4_), channel_id=1, source_target_pairs={{0,2},{1,3},{2,6},{3,7},{6,10},{7,11},{10,14},{11,15},{14,12},{15,... | collective-permute-start | bytes 1179656 | tf_op jit(solution)/shard_map/ppermute | solution.py:184
  58.3 14.7 %collective-permute-start.17 = (bf16[512,384]{1,0:T(8,128)(2,1)S(1)}, bf16[512,384]{1,0:T(8,128)(2,1)S(1)}, u32[]{:S(2)}, u32[]{:S(2)}) collective-permute-start(bf16[512,384]{1,0:T(8,128)(2,1)S(1)} %collective-permute-done.11.gate.refs_4_), channel_id=1, source_target_pairs={{0,2},{1,3},{2,6},{3,7},{6,10},{7,11},{10,14},{11,15},{14,12},{15,... | collective-permute-start | bytes 1179656 | tf_op jit(solution)/shard_map/ppermute | solution.py:184
  61.0 2.2 %slice-start = ((s8[12582912]{0:T(1024)(128)(4,1)}), s8[4194304]{0:T(1024)(128)(4,1)S(1)}, s32[]{:S(2)}) async-start(s8[12582912]{0:T(1024)(128)(4,1)} %bitcast.10), calls=%async_computation | async-start | bytes 8388608
  61.1 3.4 %slice-start.1 = ((s8[12582912]{0:T(1024)(128)(4,1)}), s8[4194304]{0:T(1024)(128)(4,1)S(1)}, s32[]{:S(2)}) async-start(s8[12582912]{0:T(1024)(128)(4,1)} %bitcast.10), calls=%async_computation.1 | async-start | bytes 8388608
  61.1 4.6 %slice-start.2 = ((s8[12582912]{0:T(1024)(128)(4,1)}), s8[4194304]{0:T(1024)(128)(4,1)S(1)}, s32[]{:S(2)}) async-start(s8[12582912]{0:T(1024)(128)(4,1)} %bitcast.10), calls=%async_computation.2 | async-start | bytes 8388608
  61.1 16.2 %collective-permute-start.20 = (bf16[192,2048]{1,0:T(8,128)(2,1)S(1)}, bf16[192,2048]{1,0:T(8,128)(2,1)S(1)}, u32[]{:S(2)}, u32[]{:S(2)}) collective-permute-start(bf16[192,2048]{1,0:T(8,128)(2,1)S(1)} %lend.12), channel_id=1, source_target_pairs={{0,1},{1,0},{2,3},{3,2},{4,5},{5,4},{6,7},{7,6},{8,9},{9,8},{10,11... | collective-permute-start | bytes 2359304 | tf_op jit(solution)/shard_map/ppermute | solution.py:193
  62.8 11.1 %collective-permute-start.18 = (bf16[512,384]{1,0:T(8,128)(2,1)S(1)}, bf16[512,384]{1,0:T(8,128)(2,1)S(1)}, u32[]{:S(2)}, u32[]{:S(2)}) collective-permute-start(bf16[512,384]{1,0:T(8,128)(2,1)S(1)} %collective-permute-done.12.refs_5_), channel_id=1, source_target_pairs={{0,4},{1,5},{2,0},{3,1},{6,2},{7,3},{10,6},{11,7},{14,10},{15,11},... | collective-permute-start | bytes 1179656 | tf_op jit(solution)/shard_map/ppermute | solution.py:184
  74.5 24.0 %collective-permute-start.25 = (bf16[192,2048]{1,0:T(8,128)(2,1)S(1)}, bf16[192,2048]{1,0:T(8,128)(2,1)S(1)}, u32[]{:S(2)}, u32[]{:S(2)}) collective-permute-start(bf16[192,2048]{1,0:T(8,128)(2,1)S(1)} %lend.13), channel_id=1, source_target_pairs={{0,1},{1,0},{2,3},{3,2},{4,5},{5,4},{6,7},{7,6},{8,9},{9,8},{10,11... | collective-permute-start | bytes 2359304 | tf_op jit(solution)/shard_map/ppermute | solution.py:193
  74.6 12.0 %collective-permute-start.15 = (bf16[512,384]{1,0:T(8,128)(2,1)S(1)}, bf16[512,384]{1,0:T(8,128)(2,1)S(1)}, u32[]{:S(2)}, u32[]{:S(2)}) collective-permute-start(bf16[512,384]{1,0:T(8,128)(2,1)S(1)} %collective-permute-done.9.refs_4_), channel_id=1, source_target_pairs={{0,2},{1,3},{2,6},{3,7},{6,10},{7,11},{10,14},{11,15},{14,12},{15,... | collective-permute-start | bytes 1179656 | tf_op jit(solution)/shard_map/ppermute | solution.py:184
  75.3 11.9 %collective-permute-start.16 = (bf16[512,384]{1,0:T(8,128)(2,1)S(1)}, bf16[512,384]{1,0:T(8,128)(2,1)S(1)}, u32[]{:S(2)}, u32[]{:S(2)}) collective-permute-start(bf16[512,384]{1,0:T(8,128)(2,1)S(1)} %collective-permute-done.10.refs_5_), channel_id=1, source_target_pairs={{0,4},{1,5},{2,0},{3,1},{6,2},{7,3},{10,6},{11,7},{14,10},{15,11},... | collective-permute-start | bytes 1179656 | tf_op jit(solution)/shard_map/ppermute | solution.py:184
  76.7 18.3 %collective-permute-start.23 = (bf16[512,384]{1,0:T(8,128)(2,1)S(1)}, bf16[512,384]{1,0:T(8,128)(2,1)S(1)}, u32[]{:S(2)}, u32[]{:S(2)}) collective-permute-start(bf16[512,384]{1,0:T(8,128)(2,1)S(1)} %collective-permute-done.17.gate.refs_4_), channel_id=1, source_target_pairs={{0,2},{1,3},{2,6},{3,7},{6,10},{7,11},{10,14},{11,15},{14,12},{15,... | collective-permute-start | bytes 1179656 | tf_op jit(solution)/shard_map/ppermute | solution.py:184
  77.3 18.3 %collective-permute-start.24 = (bf16[512,384]{1,0:T(8,128)(2,1)S(1)}, bf16[512,384]{1,0:T(8,128)(2,1)S(1)}, u32[]{:S(2)}, u32[]{:S(2)}) collective-permute-start(bf16[512,384]{1,0:T(8,128)(2,1)S(1)} %collective-permute-done.18.refs_5_), channel_id=1, source_target_pairs={{0,4},{1,5},{2,0},{3,1},{6,2},{7,3},{10,6},{11,7},{14,10},{15,11},... | collective-permute-start | bytes 1179656 | tf_op jit(solution)/shard_map/ppermute | solution.py:184
  87.2 16.2 %collective-permute-start.21 = (bf16[512,384]{1,0:T(8,128)(2,1)S(1)}, bf16[512,384]{1,0:T(8,128)(2,1)S(1)}, u32[]{:S(2)}, u32[]{:S(2)}) collective-permute-start(bf16[512,384]{1,0:T(8,128)(2,1)S(1)} %collective-permute-done.15.refs_4_), channel_id=1, source_target_pairs={{0,2},{1,3},{2,6},{3,7},{6,10},{7,11},{10,14},{11,15},{14,12},{15,... | collective-permute-start | bytes 1179656 | tf_op jit(solution)/shard_map/ppermute | solution.py:184
  89.4 14.7 %collective-permute-start.22 = (bf16[512,384]{1,0:T(8,128)(2,1)S(1)}, bf16[512,384]{1,0:T(8,128)(2,1)S(1)}, u32[]{:S(2)}, u32[]{:S(2)}) collective-permute-start(bf16[512,384]{1,0:T(8,128)(2,1)S(1)} %collective-permute-done.16.refs_5_), channel_id=1, source_target_pairs={{0,4},{1,5},{2,0},{3,1},{6,2},{7,3},{10,6},{11,7},{14,10},{15,11},... | collective-permute-start | bytes 1179656 | tf_op jit(solution)/shard_map/ppermute | solution.py:184
  96.2 19.2 %collective-permute-start.30 = (bf16[192,2048]{1,0:T(8,128)(2,1)S(1)}, bf16[192,2048]{1,0:T(8,128)(2,1)S(1)}, u32[]{:S(2)}, u32[]{:S(2)}) collective-permute-start(bf16[192,2048]{1,0:T(8,128)(2,1)S(1)} %lend.14), channel_id=1, source_target_pairs={{0,1},{1,0},{2,3},{3,2},{4,5},{5,4},{6,7},{7,6},{8,9},{9,8},{10,11... | collective-permute-start | bytes 2359304 | tf_op jit(solution)/shard_map/ppermute | solution.py:193
  96.3 15.5 %collective-permute-start.28 = (bf16[512,384]{1,0:T(8,128)(2,1)S(1)}, bf16[512,384]{1,0:T(8,128)(2,1)S(1)}, u32[]{:S(2)}, u32[]{:S(2)}) collective-permute-start(bf16[512,384]{1,0:T(8,128)(2,1)S(1)} %collective-permute-done.23.gate.refs_4_), channel_id=1, source_target_pairs={{0,2},{1,3},{2,6},{3,7},{6,10},{7,11},{10,14},{11,15},{14,12},{15,... | collective-permute-start | bytes 1179656 | tf_op jit(solution)/shard_map/ppermute | solution.py:184
  98.5 13.9 %collective-permute-start.29 = (bf16[512,384]{1,0:T(8,128)(2,1)S(1)}, bf16[512,384]{1,0:T(8,128)(2,1)S(1)}, u32[]{:S(2)}, u32[]{:S(2)}) collective-permute-start(bf16[512,384]{1,0:T(8,128)(2,1)S(1)} %collective-permute-done.24.refs_5_), channel_id=1, source_target_pairs={{0,4},{1,5},{2,0},{3,1},{6,2},{7,3},{10,6},{11,7},{14,10},{15,11},... | collective-permute-start | bytes 1179656 | tf_op jit(solution)/shard_map/ppermute | solution.py:184
  104.1 16.2 %collective-permute-start.26 = (bf16[512,384]{1,0:T(8,128)(2,1)S(1)}, bf16[512,384]{1,0:T(8,128)(2,1)S(1)}, u32[]{:S(2)}, u32[]{:S(2)}) collective-permute-start(bf16[512,384]{1,0:T(8,128)(2,1)S(1)} %collective-permute-done.21.refs_4_), channel_id=1, source_target_pairs={{0,2},{1,3},{2,6},{3,7},{6,10},{7,11},{10,14},{11,15},{14,12},{15,... | collective-permute-start | bytes 1179656 | tf_op jit(solution)/shard_map/ppermute | solution.py:184
  106.2 14.7 %collective-permute-start.27 = (bf16[512,384]{1,0:T(8,128)(2,1)S(1)}, bf16[512,384]{1,0:T(8,128)(2,1)S(1)}, u32[]{:S(2)}, u32[]{:S(2)}) collective-permute-start(bf16[512,384]{1,0:T(8,128)(2,1)S(1)} %collective-permute-done.22.refs_5_), channel_id=1, source_target_pairs={{0,4},{1,5},{2,0},{3,1},{6,2},{7,3},{10,6},{11,7},{14,10},{15,11},... | collective-permute-start | bytes 1179656 | tf_op jit(solution)/shard_map/ppermute | solution.py:184
  113.1 16.3 %collective-permute-start.35 = (bf16[192,2048]{1,0:T(8,128)(2,1)S(1)}, bf16[192,2048]{1,0:T(8,128)(2,1)S(1)}, u32[]{:S(2)}, u32[]{:S(2)}) collective-permute-start(bf16[192,2048]{1,0:T(8,128)(2,1)S(1)} %lend.15), channel_id=1, source_target_pairs={{0,1},{1,0},{2,3},{3,2},{4,5},{5,4},{6,7},{7,6},{8,9},{9,8},{10,11... | collective-permute-start | bytes 2359304 | tf_op jit(solution)/shard_map/ppermute | solution.py:193
  113.2 15.5 %collective-permute-start.33 = (bf16[512,384]{1,0:T(8,128)(2,1)S(1)}, bf16[512,384]{1,0:T(8,128)(2,1)S(1)}, u32[]{:S(2)}, u32[]{:S(2)}) collective-permute-start(bf16[512,384]{1,0:T(8,128)(2,1)S(1)} %collective-permute-done.28.gate.refs_4_), channel_id=1, source_target_pairs={{0,2},{1,3},{2,6},{3,7},{6,10},{7,11},{10,14},{11,15},{14,12},{15,... | collective-permute-start | bytes 1179656 | tf_op jit(solution)/shard_map/ppermute | solution.py:184
  115.4 13.9 %collective-permute-start.34 = (bf16[512,384]{1,0:T(8,128)(2,1)S(1)}, bf16[512,384]{1,0:T(8,128)(2,1)S(1)}, u32[]{:S(2)}, u32[]{:S(2)}) collective-permute-start(bf16[512,384]{1,0:T(8,128)(2,1)S(1)} %collective-permute-done.29.refs_5_), channel_id=1, source_target_pairs={{0,4},{1,5},{2,0},{3,1},{6,2},{7,3},{10,6},{11,7},{14,10},{15,11},... | collective-permute-start | bytes 1179656 | tf_op jit(solution)/shard_map/ppermute | solution.py:184
  120.9 15.7 %collective-permute-start.31 = (bf16[512,384]{1,0:T(8,128)(2,1)S(1)}, bf16[512,384]{1,0:T(8,128)(2,1)S(1)}, u32[]{:S(2)}, u32[]{:S(2)}) collective-permute-start(bf16[512,384]{1,0:T(8,128)(2,1)S(1)} %collective-permute-done.26.refs_4_), channel_id=1, source_target_pairs={{0,2},{1,3},{2,6},{3,7},{6,10},{7,11},{10,14},{11,15},{14,12},{15,... | collective-permute-start | bytes 1179656 | tf_op jit(solution)/shard_map/ppermute | solution.py:184
  123.1 14.0 %collective-permute-start.32 = (bf16[512,384]{1,0:T(8,128)(2,1)S(1)}, bf16[512,384]{1,0:T(8,128)(2,1)S(1)}, u32[]{:S(2)}, u32[]{:S(2)}) collective-permute-start(bf16[512,384]{1,0:T(8,128)(2,1)S(1)} %collective-permute-done.27.refs_5_), channel_id=1, source_target_pairs={{0,4},{1,5},{2,0},{3,1},{6,2},{7,3},{10,6},{11,7},{14,10},{15,11},... | collective-permute-start | bytes 1179656 | tf_op jit(solution)/shard_map/ppermute | solution.py:184
  137.1 2.9 %copy-start.1 = (bf16[192,384]{1,0:T(8,128)(2,1)S(1)}, bf16[192,384]{1,0:T(8,128)(2,1)}, u32[]{:S(2)}) copy-start(bf16[192,384]{1,0:T(8,128)(2,1)} %param.6) | copy-start | bytes 442372
  138.2 1.7 %collective-permute-start.36 = (f32[208,384]{1,0:T(8,128)S(1)}, f32[208,384]{1,0:T(8,128)S(1)}, u32[]{:S(2)}, u32[]{:S(2)}) collective-permute-start(f32[208,384]{1,0:T(8,128)S(1)} %get-tuple-element.209), channel_id=1, source_target_pairs={{0,1},{1,0},{2,3},{3,2},{4,5},{5,4},{6,7},{7,6},{8,9},{9,8},{10,11... | collective-permute-start | bytes 958472 | tf_op jit(solution)/shard_map/ppermute | solution.py:213
  138.3 2.5 %copy-start.2 = (f32[192]{0:T(256)}, f32[192]{0:T(256)S(1)}, u32[]{:S(2)}) copy-start(f32[192]{0:T(256)S(1)} %add.28) | copy-start | bytes 2308

commit v3 on v2

--- a/solution.py
+++ b/solution.py
@@ -14,6 +14,7 @@
 DEGREE_PARTS = 2
 SHORT = pl.CostEstimate(flops=0, bytes_accessed=1024, transcendentals=0)
 VMEM_LIMIT = 24 * 1024 * 1024
+LEND_LIMIT = 52 * 1024 * 1024
 
 
 def chip_cycle(chips):
@@ -31,38 +32,45 @@
     return [i * wide + j for i, j in walk]
 
 
-def lend_kernel(where, gate, *refs):
-    out_ref = refs[-1]
-    depth = refs[0].shape[1]
-    for s, ref in enumerate(refs[:-1]):
-        out_ref[:, s * depth : (s + 1) * depth] = ref[...]
+def lend_kernel(step, sections, n_row, depth, where, gate, rows_ref, own_ref, lent_ref, sems):
+    copies = []
+    for s in range(sections):
+        pair = (s * n_row + where[1 + step * sections + s] * CORES) * depth
+        for k, (ref, core) in enumerate(((own_ref, where[0]), (lent_ref, 1 - where[0]))):
+            start = pl.multiple_of(pair + core * depth, 128)
+            copies.append(
+                pltpu.make_async_copy(
+                    rows_ref.at[:, pl.ds(start, depth)],
+                    ref.at[:, pl.ds(s * depth, depth)],
+                    sems.at[s, k],
+                )
+            )
+    for copy in copies:
+        copy.start()
+    for copy in copies:
+        copy.wait()
 
 
 def lend(where, gate, adj_rows, step, sections, n_row, depth):
     rows = adj_rows.shape[0]
-
-    def block(s):
-        return pl.BlockSpec(
-            (rows, depth),
-            lambda g, where: (0, s * n_row + where[1 + step * sections + s] * CORES + 1 - where[0]),
-        )
-
+    shape = jax.ShapeDtypeStruct((rows, sections * depth), adj_rows.dtype)
     return pl.pallas_call(
-        lend_kernel,
-        grid_spec=pltpu.PrefetchScalarGridSpec(
-            num_scalar_prefetch=1,
-            grid=(1,),
-            in_specs=[pl.BlockSpec(memory_space=pl.ANY)] + [block(s) for s in range(sections)],
-            out_specs=pl.BlockSpec((rows, sections * depth), lambda g, where: (0, 0)),
-        ),
-        out_shape=jax.ShapeDtypeStruct((rows, sections * depth), adj_rows.dtype),
-        compiler_params=pltpu.CompilerParams(vmem_limit_bytes=VMEM_LIMIT),
+        functools.partial(lend_kernel, step, sections, n_row, depth),
+        in_specs=[
+            pl.BlockSpec(memory_space=pltpu.SMEM),
+            pl.BlockSpec(memory_space=pl.ANY),
+            pl.BlockSpec(memory_space=pltpu.HBM),
+        ],
+        out_specs=[pl.BlockSpec(memory_space=pltpu.VMEM)] * 2,
+        out_shape=[shape, shape],
+        scratch_shapes=[pltpu.SemaphoreType.DMA((sections, 2))],
+        compiler_params=pltpu.CompilerParams(vmem_limit_bytes=LEND_LIMIT),
         cost_estimate=SHORT,
         name="lend",
-    )(where, gate, *[adj_rows] * sections)
-
-
-def absorb_kernel(sections, rows, first, where, *refs):
+    )(where, gate, adj_rows)
+
+
+def absorb_kernel(sections, rows, first, *refs):
     own, other, slab = (refs[k * sections : (k + 1) * sections] for k in range(3))
     mine_out, theirs_out = refs[-2:]
     total = None
@@ -79,50 +87,36 @@
     theirs_out[...] = theirs
 
 
-def absorb(where, adj_rows, borrowed, slabs, sums, step, chunk, chunks, n_row):
+def absorb(own, borrowed, slabs, sums, chunk, chunks):
     sections = len(slabs)
-    rows = adj_rows.shape[0]
+    rows = own.shape[0]
     deep, width = slabs[0].shape
 
-    def own(s):
-        return pl.BlockSpec(
-            (rows, deep),
-            lambda g, where: (
-                0,
-                (s * n_row + where[1 + step * sections + s] * CORES + where[0]) * chunks + chunk,
-            ),
-        )
-
-    def other(s):
-        return pl.BlockSpec(
-            (rows, deep),
-            lambda g, where: (0, s * chunks + chunk),
-        )
-
-    whole = lambda shape: pl.BlockSpec(shape, lambda g, where: (0, 0))
+    def block(s):
+        return pl.BlockSpec((rows, deep), lambda g: (0, s * chunks + chunk))
+
+    def whole(shape):
+        return pl.BlockSpec(shape, lambda g: (0, 0))
+
     shapes = [(rows, width), (rows + ONES, width)]
     first = sums is None
-    operands = [adj_rows] * sections + [borrowed] * sections + list(slabs)
-    in_specs = [own(s) for s in range(sections)] + [other(s) for s in range(sections)]
-    in_specs += [whole((deep, width))] * sections
+    operands = [own] * sections + [borrowed] * sections + list(slabs)
+    in_specs = [block(s) for s in range(sections)] * 2 + [whole((deep, width))] * sections
     if not first:
         operands += list(sums)
         in_specs += [whole(shape) for shape in shapes]
-    at = 1 + 3 * sections
+    at = 3 * sections
     return pl.pallas_call(
         functools.partial(absorb_kernel, sections, rows, first),
-        grid_spec=pltpu.PrefetchScalarGridSpec(
-            num_scalar_prefetch=1,
-            grid=(1,),
-            in_specs=in_specs,
-            out_specs=[whole(shape) for shape in shapes],
-        ),
+        grid=(1,),
+        in_specs=in_specs,
+        out_specs=[whole(shape) for shape in shapes],
         out_shape=[jax.ShapeDtypeStruct(shape, jnp.float32) for shape in shapes],
         input_output_aliases={} if first else {at: 0, at + 1: 1},
         compiler_params=pltpu.CompilerParams(vmem_limit_bytes=VMEM_LIMIT),
         cost_estimate=SHORT,
         name="absorb",
-    )(where, *operands)
+    )(*operands)
 
 
 def make_shards(n_row):
@@ -166,6 +160,7 @@
         ]
         sums = None
         degree = []
+        own = {}
         borrowed = {}
         due = [(0, j, held[j]) for j in range(chunks)]
         lends = list(range(chips))
@@ -189,7 +184,7 @@
                 at = step - 1
                 while lends and lends[0] <= at + 1 and len(done) < MOST:
                     coming = lends.pop(0)
-                    lent = lend(where, held[j][0], adj_rows, coming, sections, n_row, depth)
+                    own[coming], lent = lend(where, held[j][0], adj_rows, coming, sections, n_row, depth)
                     borrowed[coming] = lax.ppermute(lent, "row", swap)
                     done.append(lent)
                 due.append((at, j, held[j]))
@@ -197,9 +192,7 @@
                     for _ in range(MOST if step < chips else len(due)):
                         if due:
                             t, part, slabs = due.pop(0)
-                            sums = absorb(
-                                where, now, borrowed[t], tie(slabs, held[j]), sums, t, part, chunks, n_row
-                            )
+                            sums = absorb(own[t], borrowed[t], tie(slabs, held[j]), sums, part, chunks)
                             done.append(sums)
                 if at > 2 and j == 0 and len(degree) < DEGREE_PARTS:
                     k = len(degree) * stretch

time: 141 us -> 142 us (level)
  waiting for transfers between devices: 73.6 us -> 63.4 us
  local copies, waits for them, and re-layouts: 9.42 us -> 3.13 us
  starting transfers between devices: 31 us -> 37.2 us
  other arithmetic: 2.81 us -> 8.38 us
  Pallas kernels: 23 us -> 27.8 us
    pallas_call x8, Pallas kernels: 4.76 us -> 18.2 us  [lend(): pl.pallas_call(functools.partial(lend_kernel, step, sections, n_row, dept...]
    ppermute x28, waiting for transfers between devices: 72 us -> 61.8 us  [shards(): lax.ppermute(held[j][s], 'row', ring(way(s)))]
    pallas_call x16, Pallas kernels: 18.2 us -> 9.6 us  [absorb(): pl.pallas_call(functools.partial(absorb_kernel, sections, rows, first), g...]
    ppermute x28, starting transfers between devices: 30.4 us -> 36.9 us  [shards(): lax.ppermute(held[j][s], 'row', ring(way(s)))]
    unnamed x20 -> x16, local copies, waits for them, and re-layouts: 7.22 us -> 0.92 us
    reduce_sum x2, other arithmetic: 1.93 us -> 7.5 us  [shards(): degree.append(jnp.sum(part, axis=1, dtype=jnp.float32))]
  transfers between devices with their start and end apart: 37 -> 37, of which waited for: 26 -> 23; matrix products, arithmetic and copies ran while one was open for 2% -> 6% of each run, Pallas kernels for 16% -> 19%
where the time goes in v3:
time: 142 us; the launch traced here: 141 us
  waiting for transfers between devices  63.4 us (45%)
  starting transfers between devices  37.2 us (26%)
  Pallas kernels  27.8 us (20%)
  other arithmetic  8.38 us (6%)
  local copies, waits for them, and re-layouts  3.13 us (2%)
    ppermute x28, waiting for transfers between devices, shards(): lax.ppermute(held[j][s], 'row', ring(way(s)))  61.8 us
    ppermute x28, starting transfers between devices, shards(): lax.ppermute(held[j][s], 'row', ring(way(s)))  36.9 us
    pallas_call x8, Pallas kernels, lend(): pl.pallas_call(functools.partial(lend_kernel, step, sections, n_row, dept...  18.2 us
    pallas_call x16, Pallas kernels, absorb(): pl.pallas_call(functools.partial(absorb_kernel, sections, rows, first), g...  9.6 us
    reduce_sum x2, other arithmetic, shards(): degree.append(jnp.sum(part, axis=1, dtype=jnp.float32))  7.5 us
  transfers between devices with their start and end apart: 37, of which 23 were waited for; matrix products, arithmetic and copies ran while one was open for 6% of the time, Pallas kernels for 19%

profile of v3, /device:TPU:0, one launch (start us, length us, event | category | flops | bytes accessed | tf_op | source)
XLA Modules:
  0.0 140.9 jit_solution(8897641633371551653)
XLA Ops:
  0.6 1.5 %slice_bitcast_fusion = (bf16[512,384]{1,0:T(8,128)(2,1)S(1)}, bf16[512,384]{1,0:T(8,128)(2,1)S(1)}, bf16[512,384]{1,0:T(8,128)(2,1)S(1)}, bf16[512,384]{1,0:T(8,128)(2,1)S(1)}) fusion(bf16[2,1024,384]{2,1,0:T(8,128)(2,1)} %param.5), kind=kLoop, calls=%fused_computation.2 | loop fusion | bytes 3145728 | tf_op jit(solution)/shard_map/squeeze | solution.py:159
  2.1 3.0 %collective-permute-start = (bf16[512,384]{1,0:T(8,128)(2,1)S(1)}, bf16[512,384]{1,0:T(8,128)(2,1)S(1)}, u32[]{:S(2)}, u32[]{:S(2)}) collective-permute-start(bf16[512,384]{1,0:T(8,128)(2,1)S(1)} %get-tuple-element.124.refs_4_), channel_id=1, source_target_pairs={{0,2},{1,3},{2,6},{3,7},{6,10},{7,11},{10,14},{11,15},{14,12},{15,... | collective-permute-start | bytes 1179656 | tf_op jit(solution)/shard_map/ppermute | solution.py:179
  5.3 1.9 %collective-permute-start.4 = (bf16[512,384]{1,0:T(8,128)(2,1)S(1)}, bf16[512,384]{1,0:T(8,128)(2,1)S(1)}, u32[]{:S(2)}, u32[]{:S(2)}) collective-permute-start(bf16[512,384]{1,0:T(8,128)(2,1)S(1)} %get-tuple-element.128.refs_4_), channel_id=1, source_target_pairs={{0,2},{1,3},{2,6},{3,7},{6,10},{7,11},{10,14},{11,15},{14,12},{15,... | collective-permute-start | bytes 1179656 | tf_op jit(solution)/shard_map/ppermute | solution.py:179
  7.3 0.7 dynamic-slice_bitcast_fusion.where
  8.0 7.2 %collective-permute-done.gate.refs_4_ = bf16[512,384]{1,0:T(8,128)(2,1)S(1)} collective-permute-done((bf16[512,384]{1,0:T(8,128)(2,1)S(1)}, bf16[512,384]{1,0:T(8,128)(2,1)S(1)}, u32[]{:S(2)}, u32[]{:S(2)}) %collective-permute-start) | collective-permute-done | bytes 393248 | tf_op jit(solution)/shard_map/ppermute | solution.py:179
  15.2 2.0 %collective-permute-done.1.refs_5_ = bf16[512,384]{1,0:T(8,128)(2,1)S(1)} collective-permute-done((bf16[512,384]{1,0:T(8,128)(2,1)S(1)}, bf16[512,384]{1,0:T(8,128)(2,1)S(1)}, u32[]{:S(2)}, u32[]{:S(2)}) %collective-permute-start.1) | collective-permute-done | bytes 393248 | tf_op jit(solution)/shard_map/ppermute | solution.py:179
  17.2 1.9 %lend.8 = (bf16[192,2048]{1,0:T(8,128)(2,1)S(1)}, bf16[192,2048]{1,0:T(8,128)(2,1)S(1)}) custom-call(s32[17]{0:T(128)S(1)} %dynamic-slice_bitcast_fusion.where, bf16[512,384]{1,0:T(8,128)(2,1)S(1)} %collective-permute-done.gate.refs_4_, bf16[192,32768]{1,0:T(8,128)(2,1)} %rows_ref.15), custom_call_target="tpu_custom_call" | custom-call | bytes 1024 | tf_op jit(solution)/shard_map/lend/pallas_call | solution.py:57
  19.2 1.6 %collective-permute-start.2 = (bf16[512,384]{1,0:T(8,128)(2,1)S(1)}, bf16[512,384]{1,0:T(8,128)(2,1)S(1)}, u32[]{:S(2)}, u32[]{:S(2)}) collective-permute-start(bf16[512,384]{1,0:T(8,128)(2,1)S(1)} %collective-permute-done.gate.refs_4_), channel_id=1, source_target_pairs={{0,2},{1,3},{2,6},{3,7},{6,10},{7,11},{10,14},{11,15},{14,12},{15,... | collective-permute-start | bytes 1179656 | tf_op jit(solution)/shard_map/ppermute | solution.py:179
  21.3 2.8 %lend.9 = (bf16[192,2048]{1,0:T(8,128)(2,1)S(1)}, bf16[192,2048]{1,0:T(8,128)(2,1)}) custom-call(s32[17]{0:T(128)S(1)} %dynamic-slice_bitcast_fusion.where, bf16[512,384]{1,0:T(8,128)(2,1)S(1)} %collective-permute-done.gate.refs_4_, bf16[192,32768]{1,0:T(8,128)(2,1)} %rows_ref.15), custom_call_target="tpu_custom_call" | custom-call | bytes 1024 | tf_op jit(solution)/shard_map/lend/pallas_call | solution.py:57
  24.6 1.6 %collective-permute-start.9 = (bf16[512,384]{1,0:T(8,128)(2,1)S(1)}, bf16[512,384]{1,0:T(8,128)(2,1)S(1)}, u32[]{:S(2)}, u32[]{:S(2)}) collective-permute-start(bf16[512,384]{1,0:T(8,128)(2,1)S(1)} %collective-permute-done.4.gate.refs_4_), channel_id=1, source_target_pairs={{0,2},{1,3},{2,6},{3,7},{6,10},{7,11},{10,14},{11,15},{14,12},{15,... | collective-permute-start | bytes 1179656 | tf_op jit(solution)/shard_map/ppermute | solution.py:179
  26.2 2.8 %lend.10 = (bf16[192,2048]{1,0:T(8,128)(2,1)S(1)}, bf16[192,2048]{1,0:T(8,128)(2,1)}) custom-call(s32[17]{0:T(128)S(1)} %dynamic-slice_bitcast_fusion.where, bf16[512,384]{1,0:T(8,128)(2,1)S(1)} %collective-permute-done.4.gate.refs_4_, bf16[192,32768]{1,0:T(8,128)(2,1)} %rows_ref.15), custom_call_target="tpu_custom_call" | custom-call | bytes 1024 | tf_op jit(solution)/shard_map/lend/pallas_call | solution.py:57
  29.0 2.5 %collective-permute-done.2.gate.refs_4_ = bf16[512,384]{1,0:T(8,128)(2,1)S(1)} collective-permute-done((bf16[512,384]{1,0:T(8,128)(2,1)S(1)}, bf16[512,384]{1,0:T(8,128)(2,1)S(1)}, u32[]{:S(2)}, u32[]{:S(2)}) %collective-permute-start.2) | collective-permute-done | bytes 393248 | tf_op jit(solution)/shard_map/ppermute | solution.py:179
  31.6 1.0 collective-permute-done.3.refs_5_
  32.6 1.5 %collective-permute-start.10 = (bf16[512,384]{1,0:T(8,128)(2,1)S(1)}, bf16[512,384]{1,0:T(8,128)(2,1)S(1)}, u32[]{:S(2)}, u32[]{:S(2)}) collective-permute-start(bf16[512,384]{1,0:T(8,128)(2,1)S(1)} %collective-permute-done.5.refs_5_), channel_id=1, source_target_pairs={{0,4},{1,5},{2,0},{3,1},{6,2},{7,3},{10,6},{11,7},{14,10},{15,11},... | collective-permute-start | bytes 1179656 | tf_op jit(solution)/shard_map/ppermute | solution.py:179
  34.1 5.5 %collective-permute-done.9.refs_4_ = bf16[512,384]{1,0:T(8,128)(2,1)S(1)} collective-permute-done((bf16[512,384]{1,0:T(8,128)(2,1)S(1)}, bf16[512,384]{1,0:T(8,128)(2,1)S(1)}, u32[]{:S(2)}, u32[]{:S(2)}) %collective-permute-start.9) | collective-permute-done | bytes 393248 | tf_op jit(solution)/shard_map/ppermute | solution.py:179
  39.6 1.7 %collective-permute-start.6 = (bf16[512,384]{1,0:T(8,128)(2,1)S(1)}, bf16[512,384]{1,0:T(8,128)(2,1)S(1)}, u32[]{:S(2)}, u32[]{:S(2)}) collective-permute-start(bf16[512,384]{1,0:T(8,128)(2,1)S(1)} %collective-permute-done.2.gate.refs_4_), channel_id=1, source_target_pairs={{0,2},{1,3},{2,6},{3,7},{6,10},{7,11},{10,14},{11,15},{14,12},{15,... | collective-permute-start | bytes 1179656 | tf_op jit(solution)/shard_map/ppermute | solution.py:179
  41.6 2.8 %lend.11 = (bf16[192,2048]{1,0:T(8,128)(2,1)S(1)}, bf16[192,2048]{1,0:T(8,128)(2,1)}) custom-call(s32[17]{0:T(128)S(1)} %dynamic-slice_bitcast_fusion.where, bf16[512,384]{1,0:T(8,128)(2,1)S(1)} %collective-permute-done.2.gate.refs_4_, bf16[192,32768]{1,0:T(8,128)(2,1)} %rows_ref.15), custom_call_target="tpu_custom_call" | custom-call | bytes 1024 | tf_op jit(solution)/shard_map/lend/pallas_call | solution.py:57
  45.2 0.6 absorb.17
  45.8 0.7 copy-done
  46.5 1.7 %collective-permute-start.15 = (bf16[512,384]{1,0:T(8,128)(2,1)S(1)}, bf16[512,384]{1,0:T(8,128)(2,1)S(1)}, u32[]{:S(2)}, u32[]{:S(2)}) collective-permute-start(bf16[512,384]{1,0:T(8,128)(2,1)S(1)} %collective-permute-done.9.refs_4_), channel_id=1, source_target_pairs={{0,2},{1,3},{2,6},{3,7},{6,10},{7,11},{10,14},{11,15},{14,12},{15,... | collective-permute-start | bytes 1179656 | tf_op jit(solution)/shard_map/ppermute | solution.py:179
  48.9 0.6 absorb.19
  49.5 2.1 %collective-permute-done.6.gate.refs_4_ = bf16[512,384]{1,0:T(8,128)(2,1)S(1)} collective-permute-done((bf16[512,384]{1,0:T(8,128)(2,1)S(1)}, bf16[512,384]{1,0:T(8,128)(2,1)S(1)}, u32[]{:S(2)}, u32[]{:S(2)}) %collective-permute-start.6) | collective-permute-done | bytes 393248 | tf_op jit(solution)/shard_map/ppermute | solution.py:179
  51.7 1.9 %lend.12 = (bf16[192,2048]{1,0:T(8,128)(2,1)S(1)}, bf16[192,2048]{1,0:T(8,128)(2,1)S(1)}) custom-call(s32[17]{0:T(128)S(1)} %dynamic-slice_bitcast_fusion.where, bf16[512,384]{1,0:T(8,128)(2,1)S(1)} %collective-permute-done.6.gate.refs_4_, bf16[192,32768]{1,0:T(8,128)(2,1)} %rows_ref.15), custom_call_target="tpu_custom_call" | custom-call | bytes 1024 | tf_op jit(solution)/shard_map/lend/pallas_call | solution.py:57
  53.6 2.4 %collective-permute-start.16 = (bf16[512,384]{1,0:T(8,128)(2,1)S(1)}, bf16[512,384]{1,0:T(8,128)(2,1)S(1)}, u32[]{:S(2)}, u32[]{:S(2)}) collective-permute-start(bf16[512,384]{1,0:T(8,128)(2,1)S(1)} %copy-done.1), channel_id=1, source_target_pairs={{0,4},{1,5},{2,0},{3,1},{6,2},{7,3},{10,6},{11,7},{14,10},{15,11},... | collective-permute-start | bytes 1179656 | tf_op jit(solution)/shard_map/ppermute | solution.py:179
  56.0 2.0 %collective-permute-start.13 = (bf16[512,384]{1,0:T(8,128)(2,1)S(1)}, bf16[512,384]{1,0:T(8,128)(2,1)S(1)}, u32[]{:S(2)}, u32[]{:S(2)}) collective-permute-start(bf16[512,384]{1,0:T(8,128)(2,1)S(1)} %collective-permute-done.7.refs_5_), channel_id=1, source_target_pairs={{0,4},{1,5},{2,0},{3,1},{6,2},{7,3},{10,6},{11,7},{14,10},{15,11},... | collective-permute-start | bytes 1179656 | tf_op jit(solution)/shard_map/ppermute | solution.py:179
  59.4 3.7 %convert_reduce_fusion.1 = f32[192]{0:T(256)S(1)} fusion(bf16[192,32768]{1,0:T(8,128)(2,1)} %rows_ref.15), kind=kLoop, calls=%fused_computation.1 | loop fusion | flops 6291264 | bytes 6292224 | tf_op jit(solution)/shard_map/reduce_sum | solution.py:200
  63.2 2.5 %collective-permute-done.16.refs_5_ = bf16[512,384]{1,0:T(8,128)(2,1)S(1)} collective-permute-done((bf16[512,384]{1,0:T(8,128)(2,1)S(1)}, bf16[512,384]{1,0:T(8,128)(2,1)S(1)}, u32[]{:S(2)}, u32[]{:S(2)}) %collective-permute-start.16) | collective-permute-done | bytes 393248 | tf_op jit(solution)/shard_map/ppermute | solution.py:179
  67.2 5.5 %collective-permute-done.13.refs_5_ = bf16[512,384]{1,0:T(8,128)(2,1)S(1)} collective-permute-done((bf16[512,384]{1,0:T(8,128)(2,1)S(1)}, bf16[512,384]{1,0:T(8,128)(2,1)S(1)}, u32[]{:S(2)}, u32[]{:S(2)}) %collective-permute-start.13) | collective-permute-done | bytes 393248 | tf_op jit(solution)/shard_map/ppermute | solution.py:179
  72.7 1.9 %lend.13 = (bf16[192,2048]{1,0:T(8,128)(2,1)S(1)}, bf16[192,2048]{1,0:T(8,128)(2,1)S(1)}) custom-call(s32[17]{0:T(128)S(1)} %dynamic-slice_bitcast_fusion.where, bf16[512,384]{1,0:T(8,128)(2,1)S(1)} %collective-permute-done.12.gate.refs_4_, bf16[192,32768]{1,0:T(8,128)(2,1)} %rows_ref.15), custom_call_target="tpu_custom_call" | custom-call | bytes 1024 | tf_op jit(solution)/shard_map/lend/pallas_call | solution.py:57
  75.3 2.0 %collective-permute-start.22 = (bf16[512,384]{1,0:T(8,128)(2,1)S(1)}, bf16[512,384]{1,0:T(8,128)(2,1)S(1)}, u32[]{:S(2)}, u32[]{:S(2)}) collective-permute-start(bf16[512,384]{1,0:T(8,128)(2,1)S(1)} %collective-permute-done.16.refs_5_), channel_id=1, source_target_pairs={{0,4},{1,5},{2,0},{3,1},{6,2},{7,3},{10,6},{11,7},{14,10},{15,11},... | collective-permute-start | bytes 1179656 | tf_op jit(solution)/shard_map/ppermute | solution.py:179
  77.8 1.7 %collective-permute-start.19 = (bf16[512,384]{1,0:T(8,128)(2,1)S(1)}, bf16[512,384]{1,0:T(8,128)(2,1)S(1)}, u32[]{:S(2)}, u32[]{:S(2)}) collective-permute-start(bf16[512,384]{1,0:T(8,128)(2,1)S(1)} %collective-permute-done.13.refs_5_), channel_id=1, source_target_pairs={{0,4},{1,5},{2,0},{3,1},{6,2},{7,3},{10,6},{11,7},{14,10},{15,11},... | collective-permute-start | bytes 1179656 | tf_op jit(solution)/shard_map/ppermute | solution.py:179
  79.4 3.7 %convert_reduce_fusion = f32[192]{0:T(256)S(1)} fusion(bf16[192,32768]{1,0:T(8,128)(2,1)} %rows_ref.15), kind=kLoop, calls=%fused_computation | loop fusion | flops 6291264 | bytes 6292224 | tf_op jit(solution)/shard_map/reduce_sum | solution.py:200
  83.8 3.5 %collective-permute-done.21.refs_4_ = bf16[512,384]{1,0:T(8,128)(2,1)S(1)} collective-permute-done((bf16[512,384]{1,0:T(8,128)(2,1)S(1)}, bf16[512,384]{1,0:T(8,128)(2,1)S(1)}, u32[]{:S(2)}, u32[]{:S(2)}) %collective-permute-start.21) | collective-permute-done | bytes 393248 | tf_op jit(solution)/shard_map/ppermute | solution.py:179
  87.6 2.5 %collective-permute-start.26 = (bf16[512,384]{1,0:T(8,128)(2,1)S(1)}, bf16[512,384]{1,0:T(8,128)(2,1)S(1)}, u32[]{:S(2)}, u32[]{:S(2)}) collective-permute-start(bf16[512,384]{1,0:T(8,128)(2,1)S(1)} %collective-permute-done.21.refs_4_), channel_id=1, source_target_pairs={{0,2},{1,3},{2,6},{3,7},{6,10},{7,11},{10,14},{11,15},{14,12},{15,... | collective-permute-start | bytes 1179656 | tf_op jit(solution)/shard_map/ppermute | solution.py:179
  90.7 5.0 %collective-permute-done.18.gate.refs_4_ = bf16[512,384]{1,0:T(8,128)(2,1)S(1)} collective-permute-done((bf16[512,384]{1,0:T(8,128)(2,1)S(1)}, bf16[512,384]{1,0:T(8,128)(2,1)S(1)}, u32[]{:S(2)}, u32[]{:S(2)}) %collective-permute-start.18) | collective-permute-done | bytes 393248 | tf_op jit(solution)/shard_map/ppermute | solution.py:179
  96.1 1.9 %lend.14 = (bf16[192,2048]{1,0:T(8,128)(2,1)S(1)}, bf16[192,2048]{1,0:T(8,128)(2,1)S(1)}) custom-call(s32[17]{0:T(128)S(1)} %dynamic-slice_bitcast_fusion.where, bf16[512,384]{1,0:T(8,128)(2,1)S(1)} %collective-permute-done.18.gate.refs_4_, bf16[192,32768]{1,0:T(8,128)(2,1)} %rows_ref.15), custom_call_target="tpu_custom_call" | custom-call | bytes 1024 | tf_op jit(solution)/shard_map/lend/pallas_call | solution.py:57
  98.0 2.5 %collective-permute-start.23 = (bf16[512,384]{1,0:T(8,128)(2,1)S(1)}, bf16[512,384]{1,0:T(8,128)(2,1)S(1)}, u32[]{:S(2)}, u32[]{:S(2)}) collective-permute-start(bf16[512,384]{1,0:T(8,128)(2,1)S(1)} %collective-permute-done.18.gate.refs_4_), channel_id=1, source_target_pairs={{0,2},{1,3},{2,6},{3,7},{6,10},{7,11},{10,14},{11,15},{14,12},{15,... | collective-permute-start | bytes 1179656 | tf_op jit(solution)/shard_map/ppermute | solution.py:179
  101.2 2.9 %collective-permute-done.26.refs_4_ = bf16[512,384]{1,0:T(8,128)(2,1)S(1)} collective-permute-done((bf16[512,384]{1,0:T(8,128)(2,1)S(1)}, bf16[512,384]{1,0:T(8,128)(2,1)S(1)}, u32[]{:S(2)}, u32[]{:S(2)}) %collective-permute-start.26) | collective-permute-done | bytes 393248 | tf_op jit(solution)/shard_map/ppermute | solution.py:179
  104.1 2.9 %collective-permute-start.29 = (bf16[512,384]{1,0:T(8,128)(2,1)S(1)}, bf16[512,384]{1,0:T(8,128)(2,1)S(1)}, u32[]{:S(2)}, u32[]{:S(2)}) collective-permute-start(bf16[512,384]{1,0:T(8,128)(2,1)S(1)} %collective-permute-done.26.refs_4_), channel_id=1, source_target_pairs={{0,2},{1,3},{2,6},{3,7},{6,10},{7,11},{10,14},{11,15},{14,12},{15,... | collective-permute-start | bytes 1179656 | tf_op jit(solution)/shard_map/ppermute | solution.py:179
  107.6 5.0 %collective-permute-done.23.gate.refs_4_ = bf16[512,384]{1,0:T(8,128)(2,1)S(1)} collective-permute-done((bf16[512,384]{1,0:T(8,128)(2,1)S(1)}, bf16[512,384]{1,0:T(8,128)(2,1)S(1)}, u32[]{:S(2)}, u32[]{:S(2)}) %collective-permute-start.23) | collective-permute-done | bytes 393248 | tf_op jit(solution)/shard_map/ppermute | solution.py:179
  112.6 1.9 %lend.15 = (bf16[192,2048]{1,0:T(8,128)(2,1)S(1)}, bf16[192,2048]{1,0:T(8,128)(2,1)S(1)}) custom-call(s32[17]{0:T(128)S(1)} %dynamic-slice_bitcast_fusion.where, bf16[512,384]{1,0:T(8,128)(2,1)S(1)} %collective-permute-done.23.gate.refs_4_, bf16[192,32768]{1,0:T(8,128)(2,1)} %rows_ref.15), custom_call_target="tpu_custom_call" | custom-call | bytes 1024 | tf_op jit(solution)/shard_map/lend/pallas_call | solution.py:57
  114.6 3.0 %collective-permute-start.34 = (bf16[512,384]{1,0:T(8,128)(2,1)S(1)}, bf16[512,384]{1,0:T(8,128)(2,1)S(1)}, u32[]{:S(2)}, u32[]{:S(2)}) collective-permute-start(bf16[512,384]{1,0:T(8,128)(2,1)S(1)} %collective-permute-done.23.gate.refs_4_), channel_id=1, source_target_pairs={{0,2},{1,3},{2,6},{3,7},{6,10},{7,11},{10,14},{11,15},{14,12},{15,... | collective-permute-start | bytes 1179656 | tf_op jit(solution)/shard_map/ppermute | solution.py:179
  118.3 2.7 %collective-permute-done.29.refs_4_ = bf16[512,384]{1,0:T(8,128)(2,1)S(1)} collective-permute-done((bf16[512,384]{1,0:T(8,128)(2,1)S(1)}, bf16[512,384]{1,0:T(8,128)(2,1)S(1)}, u32[]{:S(2)}, u32[]{:S(2)}) %collective-permute-start.29) | collective-permute-done | bytes 393248 | tf_op jit(solution)/shard_map/ppermute | solution.py:179
  121.0 2.8 %collective-permute-start.32 = (bf16[512,384]{1,0:T(8,128)(2,1)S(1)}, bf16[512,384]{1,0:T(8,128)(2,1)S(1)}, u32[]{:S(2)}, u32[]{:S(2)}) collective-permute-start(bf16[512,384]{1,0:T(8,128)(2,1)S(1)} %collective-permute-done.29.refs_4_), channel_id=1, source_target_pairs={{0,2},{1,3},{2,6},{3,7},{6,10},{7,11},{10,14},{11,15},{14,12},{15,... | collective-permute-start | bytes 1179656 | tf_op jit(solution)/shard_map/ppermute | solution.py:179
  124.4 5.0 %collective-permute-done.34.refs_4_ = bf16[512,384]{1,0:T(8,128)(2,1)S(1)} collective-permute-done((bf16[512,384]{1,0:T(8,128)(2,1)S(1)}, bf16[512,384]{1,0:T(8,128)(2,1)S(1)}, u32[]{:S(2)}, u32[]{:S(2)}) %collective-permute-start.34) | collective-permute-done | bytes 393248 | tf_op jit(solution)/shard_map/ppermute | solution.py:179
  130.4 7.2 %collective-permute-done.32.refs_4_ = bf16[512,384]{1,0:T(8,128)(2,1)S(1)} collective-permute-done((bf16[512,384]{1,0:T(8,128)(2,1)S(1)}, bf16[512,384]{1,0:T(8,128)(2,1)S(1)}, u32[]{:S(2)}, u32[]{:S(2)}) %collective-permute-start.32) | collective-permute-done | bytes 393248 | tf_op jit(solution)/shard_map/ppermute | solution.py:179
  138.5 1.6 %collective-permute-done.36 = f32[208,384]{1,0:T(8,128)S(1)} collective-permute-done((f32[208,384]{1,0:T(8,128)S(1)}, f32[208,384]{1,0:T(8,128)S(1)}, u32[]{:S(2)}, u32[]{:S(2)}) %collective-permute-start.36) | collective-permute-done | bytes 319520 | tf_op jit(solution)/shard_map/ppermute | solution.py:206
  140.1 0.9 fusion
  (73 shorter events, 13.2 us)
Async XLA Ops:
  2.1 13.0 %collective-permute-start = (bf16[512,384]{1,0:T(8,128)(2,1)S(1)}, bf16[512,384]{1,0:T(8,128)(2,1)S(1)}, u32[]{:S(2)}, u32[]{:S(2)}) collective-permute-start(bf16[512,384]{1,0:T(8,128)(2,1)S(1)} %get-tuple-element.124.refs_4_), channel_id=1, source_target_pairs={{0,2},{1,3},{2,6},{3,7},{6,10},{7,11},{10,14},{11,15},{14,12},{15,... | collective-permute-start | bytes 1179656 | tf_op jit(solution)/shard_map/ppermute | solution.py:179
  5.2 12.0 %collective-permute-start.1 = (bf16[512,384]{1,0:T(8,128)(2,1)S(1)}, bf16[512,384]{1,0:T(8,128)(2,1)S(1)}, u32[]{:S(2)}, u32[]{:S(2)}) collective-permute-start(bf16[512,384]{1,0:T(8,128)(2,1)S(1)} %get-tuple-element.125.refs_5_), channel_id=1, source_target_pairs={{0,4},{1,5},{2,0},{3,1},{6,2},{7,3},{10,6},{11,7},{14,10},{15,11},... | collective-permute-start | bytes 1179656 | tf_op jit(solution)/shard_map/ppermute | solution.py:179
  5.3 18.8 %collective-permute-start.4 = (bf16[512,384]{1,0:T(8,128)(2,1)S(1)}, bf16[512,384]{1,0:T(8,128)(2,1)S(1)}, u32[]{:S(2)}, u32[]{:S(2)}) collective-permute-start(bf16[512,384]{1,0:T(8,128)(2,1)S(1)} %get-tuple-element.128.refs_4_), channel_id=1, source_target_pairs={{0,2},{1,3},{2,6},{3,7},{6,10},{7,11},{10,14},{11,15},{14,12},{15,... | collective-permute-start | bytes 1179656 | tf_op jit(solution)/shard_map/ppermute | solution.py:179
  7.2 17.5 %collective-permute-start.5 = (bf16[512,384]{1,0:T(8,128)(2,1)S(1)}, bf16[512,384]{1,0:T(8,128)(2,1)S(1)}, u32[]{:S(2)}, u32[]{:S(2)}) collective-permute-start(bf16[512,384]{1,0:T(8,128)(2,1)S(1)} %get-tuple-element.129.refs_5_), channel_id=1, source_target_pairs={{0,4},{1,5},{2,0},{3,1},{6,2},{7,3},{10,6},{11,7},{14,10},{15,11},... | collective-permute-start | bytes 1179656 | tf_op jit(solution)/shard_map/ppermute | solution.py:179
  19.1 22.2 %collective-permute-start.11 = (bf16[192,2048]{1,0:T(8,128)(2,1)S(1)}, bf16[192,2048]{1,0:T(8,128)(2,1)S(1)}, u32[]{:S(2)}, u32[]{:S(2)}) collective-permute-start(bf16[192,2048]{1,0:T(8,128)(2,1)S(1)} %get-tuple-element.114), channel_id=1, source_target_pairs={{0,1},{1,0},{2,3},{3,2},{4,5},{5,4},{6,7},{7,6},{8,9},{9,8},{10,11... | collective-permute-start | bytes 2359304 | tf_op jit(solution)/shard_map/ppermute | solution.py:188
  19.2 12.3 %collective-permute-start.2 = (bf16[512,384]{1,0:T(8,128)(2,1)S(1)}, bf16[512,384]{1,0:T(8,128)(2,1)S(1)}, u32[]{:S(2)}, u32[]{:S(2)}) collective-permute-start(bf16[512,384]{1,0:T(8,128)(2,1)S(1)} %collective-permute-done.gate.refs_4_), channel_id=1, source_target_pairs={{0,2},{1,3},{2,6},{3,7},{6,10},{7,11},{10,14},{11,15},{14,12},{15,... | collective-permute-start | bytes 1179656 | tf_op jit(solution)/shard_map/ppermute | solution.py:179
  20.9 11.7 %collective-permute-start.3 = (bf16[512,384]{1,0:T(8,128)(2,1)S(1)}, bf16[512,384]{1,0:T(8,128)(2,1)S(1)}, u32[]{:S(2)}, u32[]{:S(2)}) collective-permute-start(bf16[512,384]{1,0:T(8,128)(2,1)S(1)} %collective-permute-done.1.refs_5_), channel_id=1, source_target_pairs={{0,4},{1,5},{2,0},{3,1},{6,2},{7,3},{10,6},{11,7},{14,10},{15,11},... | collective-permute-start | bytes 1179656 | tf_op jit(solution)/shard_map/ppermute | solution.py:179
  24.1 24.1 %collective-permute-start.8 = (bf16[192,2048]{1,0:T(8,128)(2,1)}, bf16[192,2048]{1,0:T(8,128)(2,1)S(1)}, u32[]{:S(2)}, u32[]{:S(2)}) collective-permute-start(bf16[192,2048]{1,0:T(8,128)(2,1)} %get-tuple-element.115), channel_id=1, source_target_pairs={{0,1},{1,0},{2,3},{3,2},{4,5},{5,4},{6,7},{7,6},{8,9},{9,8},{10,11... | collective-permute-start | bytes 2359304 | tf_op jit(solution)/shard_map/ppermute | solution.py:188
  24.6 15.0 %collective-permute-start.9 = (bf16[512,384]{1,0:T(8,128)(2,1)S(1)}, bf16[512,384]{1,0:T(8,128)(2,1)S(1)}, u32[]{:S(2)}, u32[]{:S(2)}) collective-permute-start(bf16[512,384]{1,0:T(8,128)(2,1)S(1)} %collective-permute-done.4.gate.refs_4_), channel_id=1, source_target_pairs={{0,2},{1,3},{2,6},{3,7},{6,10},{7,11},{10,14},{11,15},{14,12},{15,... | collective-permute-start | bytes 1179656 | tf_op jit(solution)/shard_map/ppermute | solution.py:179
  31.6 24.5 %collective-permute-start.17 = (bf16[192,2048]{1,0:T(8,128)(2,1)}, bf16[192,2048]{1,0:T(8,128)(2,1)S(1)}, u32[]{:S(2)}, u32[]{:S(2)}) collective-permute-start(bf16[192,2048]{1,0:T(8,128)(2,1)} %get-tuple-element.117), channel_id=1, source_target_pairs={{0,1},{1,0},{2,3},{3,2},{4,5},{5,4},{6,7},{7,6},{8,9},{9,8},{10,11... | collective-permute-start | bytes 2359304 | tf_op jit(solution)/shard_map/ppermute | solution.py:188
  32.6 13.2 %collective-permute-start.10 = (bf16[512,384]{1,0:T(8,128)(2,1)S(1)}, bf16[512,384]{1,0:T(8,128)(2,1)S(1)}, u32[]{:S(2)}, u32[]{:S(2)}) collective-permute-start(bf16[512,384]{1,0:T(8,128)(2,1)S(1)} %collective-permute-done.5.refs_5_), channel_id=1, source_target_pairs={{0,4},{1,5},{2,0},{3,1},{6,2},{7,3},{10,6},{11,7},{14,10},{15,11},... | collective-permute-start | bytes 1179656 | tf_op jit(solution)/shard_map/ppermute | solution.py:179
  39.6 12.0 %collective-permute-start.6 = (bf16[512,384]{1,0:T(8,128)(2,1)S(1)}, bf16[512,384]{1,0:T(8,128)(2,1)S(1)}, u32[]{:S(2)}, u32[]{:S(2)}) collective-permute-start(bf16[512,384]{1,0:T(8,128)(2,1)S(1)} %collective-permute-done.2.gate.refs_4_), channel_id=1, source_target_pairs={{0,2},{1,3},{2,6},{3,7},{6,10},{7,11},{10,14},{11,15},{14,12},{15,... | collective-permute-start | bytes 1179656 | tf_op jit(solution)/shard_map/ppermute | solution.py:179
  41.3 10.4 %collective-permute-start.7 = (bf16[512,384]{1,0:T(8,128)(2,1)S(1)}, bf16[512,384]{1,0:T(8,128)(2,1)S(1)}, u32[]{:S(2)}, u32[]{:S(2)}) collective-permute-start(bf16[512,384]{1,0:T(8,128)(2,1)S(1)} %collective-permute-done.3.refs_5_), channel_id=1, source_target_pairs={{0,4},{1,5},{2,0},{3,1},{6,2},{7,3},{10,6},{11,7},{14,10},{15,11},... | collective-permute-start | bytes 1179656 | tf_op jit(solution)/shard_map/ppermute | solution.py:179
  45.8 0.7 copy-start
  46.5 7.1 %copy-start.1 = (bf16[512,384]{1,0:T(8,128)(2,1)S(1)}, bf16[512,384]{1,0:T(8,128)(2,1)}, u32[]{:S(2)}) copy-start(bf16[512,384]{1,0:T(8,128)(2,1)} %copy-done) | copy-start | bytes 1179652
  46.5 12.9 %collective-permute-start.15 = (bf16[512,384]{1,0:T(8,128)(2,1)S(1)}, bf16[512,384]{1,0:T(8,128)(2,1)S(1)}, u32[]{:S(2)}, u32[]{:S(2)}) collective-permute-start(bf16[512,384]{1,0:T(8,128)(2,1)S(1)} %collective-permute-done.9.refs_4_), channel_id=1, source_target_pairs={{0,2},{1,3},{2,6},{3,7},{6,10},{7,11},{10,14},{11,15},{14,12},{15,... | collective-permute-start | bytes 1179656 | tf_op jit(solution)/shard_map/ppermute | solution.py:179
  48.2 17.5 %collective-permute-start.14 = (bf16[192,2048]{1,0:T(8,128)(2,1)}, bf16[192,2048]{1,0:T(8,128)(2,1)S(1)}, u32[]{:S(2)}, u32[]{:S(2)}) collective-permute-start(bf16[192,2048]{1,0:T(8,128)(2,1)} %get-tuple-element.122), channel_id=1, source_target_pairs={{0,1},{1,0},{2,3},{3,2},{4,5},{5,4},{6,7},{7,6},{8,9},{9,8},{10,11... | collective-permute-start | bytes 2359304 | tf_op jit(solution)/shard_map/ppermute | solution.py:188
  53.6 12.1 %collective-permute-start.16 = (bf16[512,384]{1,0:T(8,128)(2,1)S(1)}, bf16[512,384]{1,0:T(8,128)(2,1)S(1)}, u32[]{:S(2)}, u32[]{:S(2)}) collective-permute-start(bf16[512,384]{1,0:T(8,128)(2,1)S(1)} %copy-done.1), channel_id=1, source_target_pairs={{0,4},{1,5},{2,0},{3,1},{6,2},{7,3},{10,6},{11,7},{14,10},{15,11},... | collective-permute-start | bytes 1179656 | tf_op jit(solution)/shard_map/ppermute | solution.py:179
  56.0 11.2 %collective-permute-start.12 = (bf16[512,384]{1,0:T(8,128)(2,1)S(1)}, bf16[512,384]{1,0:T(8,128)(2,1)S(1)}, u32[]{:S(2)}, u32[]{:S(2)}) collective-permute-start(bf16[512,384]{1,0:T(8,128)(2,1)S(1)} %collective-permute-done.6.gate.refs_4_), channel_id=1, source_target_pairs={{0,2},{1,3},{2,6},{3,7},{6,10},{7,11},{10,14},{11,15},{14,12},{15,... | collective-permute-start | bytes 1179656 | tf_op jit(solution)/shard_map/ppermute | solution.py:179
  56.0 16.7 %collective-permute-start.13 = (bf16[512,384]{1,0:T(8,128)(2,1)S(1)}, bf16[512,384]{1,0:T(8,128)(2,1)S(1)}, u32[]{:S(2)}, u32[]{:S(2)}) collective-permute-start(bf16[512,384]{1,0:T(8,128)(2,1)S(1)} %collective-permute-done.7.refs_5_), channel_id=1, source_target_pairs={{0,4},{1,5},{2,0},{3,1},{6,2},{7,3},{10,6},{11,7},{14,10},{15,11},... | collective-permute-start | bytes 1179656 | tf_op jit(solution)/shard_map/ppermute | solution.py:179
  59.4 18.3 %collective-permute-start.20 = (bf16[192,2048]{1,0:T(8,128)(2,1)S(1)}, bf16[192,2048]{1,0:T(8,128)(2,1)S(1)}, u32[]{:S(2)}, u32[]{:S(2)}) collective-permute-start(bf16[192,2048]{1,0:T(8,128)(2,1)S(1)} %get-tuple-element.145), channel_id=1, source_target_pairs={{0,1},{1,0},{2,3},{3,2},{4,5},{5,4},{6,7},{7,6},{8,9},{9,8},{10,11... | collective-permute-start | bytes 2359304 | tf_op jit(solution)/shard_map/ppermute | solution.py:188
  74.7 25.9 %collective-permute-start.25 = (bf16[192,2048]{1,0:T(8,128)(2,1)S(1)}, bf16[192,2048]{1,0:T(8,128)(2,1)S(1)}, u32[]{:S(2)}, u32[]{:S(2)}) collective-permute-start(bf16[192,2048]{1,0:T(8,128)(2,1)S(1)} %get-tuple-element.169), channel_id=1, source_target_pairs={{0,1},{1,0},{2,3},{3,2},{4,5},{5,4},{6,7},{7,6},{8,9},{9,8},{10,11... | collective-permute-start | bytes 2359304 | tf_op jit(solution)/shard_map/ppermute | solution.py:188
  74.8 12.5 %collective-permute-start.21 = (bf16[512,384]{1,0:T(8,128)(2,1)S(1)}, bf16[512,384]{1,0:T(8,128)(2,1)S(1)}, u32[]{:S(2)}, u32[]{:S(2)}) collective-permute-start(bf16[512,384]{1,0:T(8,128)(2,1)S(1)} %collective-permute-done.15.refs_4_), channel_id=1, source_target_pairs={{0,2},{1,3},{2,6},{3,7},{6,10},{7,11},{10,14},{11,15},{14,12},{15,... | collective-permute-start | bytes 1179656 | tf_op jit(solution)/shard_map/ppermute | solution.py:179
  75.3 12.3 %collective-permute-start.22 = (bf16[512,384]{1,0:T(8,128)(2,1)S(1)}, bf16[512,384]{1,0:T(8,128)(2,1)S(1)}, u32[]{:S(2)}, u32[]{:S(2)}) collective-permute-start(bf16[512,384]{1,0:T(8,128)(2,1)S(1)} %collective-permute-done.16.refs_5_), channel_id=1, source_target_pairs={{0,4},{1,5},{2,0},{3,1},{6,2},{7,3},{10,6},{11,7},{14,10},{15,11},... | collective-permute-start | bytes 1179656 | tf_op jit(solution)/shard_map/ppermute | solution.py:179
  77.4 18.3 %collective-permute-start.18 = (bf16[512,384]{1,0:T(8,128)(2,1)S(1)}, bf16[512,384]{1,0:T(8,128)(2,1)S(1)}, u32[]{:S(2)}, u32[]{:S(2)}) collective-permute-start(bf16[512,384]{1,0:T(8,128)(2,1)S(1)} %collective-permute-done.12.gate.refs_4_), channel_id=1, source_target_pairs={{0,2},{1,3},{2,6},{3,7},{6,10},{7,11},{10,14},{11,15},{14,12},{15,... | collective-permute-start | bytes 1179656 | tf_op jit(solution)/shard_map/ppermute | solution.py:179
  77.8 18.3 %collective-permute-start.19 = (bf16[512,384]{1,0:T(8,128)(2,1)S(1)}, bf16[512,384]{1,0:T(8,128)(2,1)S(1)}, u32[]{:S(2)}, u32[]{:S(2)}) collective-permute-start(bf16[512,384]{1,0:T(8,128)(2,1)S(1)} %collective-permute-done.13.refs_5_), channel_id=1, source_target_pairs={{0,4},{1,5},{2,0},{3,1},{6,2},{7,3},{10,6},{11,7},{14,10},{15,11},... | collective-permute-start | bytes 1179656 | tf_op jit(solution)/shard_map/ppermute | solution.py:179
  87.6 16.5 %collective-permute-start.26 = (bf16[512,384]{1,0:T(8,128)(2,1)S(1)}, bf16[512,384]{1,0:T(8,128)(2,1)S(1)}, u32[]{:S(2)}, u32[]{:S(2)}) collective-permute-start(bf16[512,384]{1,0:T(8,128)(2,1)S(1)} %collective-permute-done.21.refs_4_), channel_id=1, source_target_pairs={{0,2},{1,3},{2,6},{3,7},{6,10},{7,11},{10,14},{11,15},{14,12},{15,... | collective-permute-start | bytes 1179656 | tf_op jit(solution)/shard_map/ppermute | solution.py:179
  90.1 14.0 %collective-permute-start.27 = (bf16[512,384]{1,0:T(8,128)(2,1)S(1)}, bf16[512,384]{1,0:T(8,128)(2,1)S(1)}, u32[]{:S(2)}, u32[]{:S(2)}) collective-permute-start(bf16[512,384]{1,0:T(8,128)(2,1)S(1)} %collective-permute-done.22.refs_5_), channel_id=1, source_target_pairs={{0,4},{1,5},{2,0},{3,1},{6,2},{7,3},{10,6},{11,7},{14,10},{15,11},... | collective-permute-start | bytes 1179656 | tf_op jit(solution)/shard_map/ppermute | solution.py:179
  98.0 14.5 %collective-permute-start.23 = (bf16[512,384]{1,0:T(8,128)(2,1)S(1)}, bf16[512,384]{1,0:T(8,128)(2,1)S(1)}, u32[]{:S(2)}, u32[]{:S(2)}) collective-permute-start(bf16[512,384]{1,0:T(8,128)(2,1)S(1)} %collective-permute-done.18.gate.refs_4_), channel_id=1, source_target_pairs={{0,2},{1,3},{2,6},{3,7},{6,10},{7,11},{10,14},{11,15},{14,12},{15,... | collective-permute-start | bytes 1179656 | tf_op jit(solution)/shard_map/ppermute | solution.py:179
  100.5 17.1 %collective-permute-start.31 = (bf16[192,2048]{1,0:T(8,128)(2,1)S(1)}, bf16[192,2048]{1,0:T(8,128)(2,1)S(1)}, u32[]{:S(2)}, u32[]{:S(2)}) collective-permute-start(bf16[192,2048]{1,0:T(8,128)(2,1)S(1)} %get-tuple-element.184), channel_id=1, source_target_pairs={{0,1},{1,0},{2,3},{3,2},{4,5},{5,4},{6,7},{7,6},{8,9},{9,8},{10,11... | collective-permute-start | bytes 2359304 | tf_op jit(solution)/shard_map/ppermute | solution.py:188
  100.5 12.0 %collective-permute-start.24 = (bf16[512,384]{1,0:T(8,128)(2,1)S(1)}, bf16[512,384]{1,0:T(8,128)(2,1)S(1)}, u32[]{:S(2)}, u32[]{:S(2)}) collective-permute-start(bf16[512,384]{1,0:T(8,128)(2,1)S(1)} %collective-permute-done.19.refs_5_), channel_id=1, source_target_pairs={{0,4},{1,5},{2,0},{3,1},{6,2},{7,3},{10,6},{11,7},{14,10},{15,11},... | collective-permute-start | bytes 1179656 | tf_op jit(solution)/shard_map/ppermute | solution.py:179
  104.1 16.8 %collective-permute-start.29 = (bf16[512,384]{1,0:T(8,128)(2,1)S(1)}, bf16[512,384]{1,0:T(8,128)(2,1)S(1)}, u32[]{:S(2)}, u32[]{:S(2)}) collective-permute-start(bf16[512,384]{1,0:T(8,128)(2,1)S(1)} %collective-permute-done.26.refs_4_), channel_id=1, source_target_pairs={{0,2},{1,3},{2,6},{3,7},{6,10},{7,11},{10,14},{11,15},{14,12},{15,... | collective-permute-start | bytes 1179656 | tf_op jit(solution)/shard_map/ppermute | solution.py:179
  107.0 14.0 %collective-permute-start.30 = (bf16[512,384]{1,0:T(8,128)(2,1)S(1)}, bf16[512,384]{1,0:T(8,128)(2,1)S(1)}, u32[]{:S(2)}, u32[]{:S(2)}) collective-permute-start(bf16[512,384]{1,0:T(8,128)(2,1)S(1)} %collective-permute-done.27.refs_5_), channel_id=1, source_target_pairs={{0,4},{1,5},{2,0},{3,1},{6,2},{7,3},{10,6},{11,7},{14,10},{15,11},... | collective-permute-start | bytes 1179656 | tf_op jit(solution)/shard_map/ppermute | solution.py:179
  112.6 27.5 %copy-start.2 = (bf16[192,384]{1,0:T(8,128)(2,1)S(1)}, bf16[192,384]{1,0:T(8,128)(2,1)}, u32[]{:S(2)}) copy-start(bf16[192,384]{1,0:T(8,128)(2,1)} %param.6) | copy-start | bytes 442372
  114.5 15.2 %collective-permute-start.28 = (bf16[192,2048]{1,0:T(8,128)(2,1)S(1)}, bf16[192,2048]{1,0:T(8,128)(2,1)S(1)}, u32[]{:S(2)}, u32[]{:S(2)}) collective-permute-start(bf16[192,2048]{1,0:T(8,128)(2,1)S(1)} %get-tuple-element.197), channel_id=1, source_target_pairs={{0,1},{1,0},{2,3},{3,2},{4,5},{5,4},{6,7},{7,6},{8,9},{9,8},{10,11... | collective-permute-start | bytes 2359304 | tf_op jit(solution)/shard_map/ppermute | solution.py:188
  114.6 14.8 %collective-permute-start.34 = (bf16[512,384]{1,0:T(8,128)(2,1)S(1)}, bf16[512,384]{1,0:T(8,128)(2,1)S(1)}, u32[]{:S(2)}, u32[]{:S(2)}) collective-permute-start(bf16[512,384]{1,0:T(8,128)(2,1)S(1)} %collective-permute-done.23.gate.refs_4_), channel_id=1, source_target_pairs={{0,2},{1,3},{2,6},{3,7},{6,10},{7,11},{10,14},{11,15},{14,12},{15,... | collective-permute-start | bytes 1179656 | tf_op jit(solution)/shard_map/ppermute | solution.py:179
  117.7 12.1 %collective-permute-start.35 = (bf16[512,384]{1,0:T(8,128)(2,1)S(1)}, bf16[512,384]{1,0:T(8,128)(2,1)S(1)}, u32[]{:S(2)}, u32[]{:S(2)}) collective-permute-start(bf16[512,384]{1,0:T(8,128)(2,1)S(1)} %collective-permute-done.24.refs_5_), channel_id=1, source_target_pairs={{0,4},{1,5},{2,0},{3,1},{6,2},{7,3},{10,6},{11,7},{14,10},{15,11},... | collective-permute-start | bytes 1179656 | tf_op jit(solution)/shard_map/ppermute | solution.py:179
  121.0 16.6 %collective-permute-start.32 = (bf16[512,384]{1,0:T(8,128)(2,1)S(1)}, bf16[512,384]{1,0:T(8,128)(2,1)S(1)}, u32[]{:S(2)}, u32[]{:S(2)}) collective-permute-start(bf16[512,384]{1,0:T(8,128)(2,1)S(1)} %collective-permute-done.29.refs_4_), channel_id=1, source_target_pairs={{0,2},{1,3},{2,6},{3,7},{6,10},{7,11},{10,14},{11,15},{14,12},{15,... | collective-permute-start | bytes 1179656 | tf_op jit(solution)/shard_map/ppermute | solution.py:179
  123.8 13.9 %collective-permute-start.33 = (bf16[512,384]{1,0:T(8,128)(2,1)S(1)}, bf16[512,384]{1,0:T(8,128)(2,1)S(1)}, u32[]{:S(2)}, u32[]{:S(2)}) collective-permute-start(bf16[512,384]{1,0:T(8,128)(2,1)S(1)} %collective-permute-done.30.refs_5_), channel_id=1, source_target_pairs={{0,4},{1,5},{2,0},{3,1},{6,2},{7,3},{10,6},{11,7},{14,10},{15,11},... | collective-permute-start | bytes 1179656 | tf_op jit(solution)/shard_map/ppermute | solution.py:179
  138.4 1.7 %collective-permute-start.36 = (f32[208,384]{1,0:T(8,128)S(1)}, f32[208,384]{1,0:T(8,128)S(1)}, u32[]{:S(2)}, u32[]{:S(2)}) collective-permute-start(f32[208,384]{1,0:T(8,128)S(1)} %get-tuple-element.221), channel_id=1, source_target_pairs={{0,1},{1,0},{2,3},{3,2},{4,5},{5,4},{6,7},{7,6},{8,9},{9,8},{10,11... | collective-permute-start | bytes 958472 | tf_op jit(solution)/shard_map/ppermute | solution.py:206
  138.4 2.5 %copy-start.3 = (f32[192]{0:T(256)}, f32[192]{0:T(256)S(1)}, u32[]{:S(2)}) copy-start(f32[192]{0:T(256)S(1)} %add.28) | copy-start | bytes 2308

commit v4 on v2

--- a/solution.py
+++ b/solution.py
@@ -10,10 +10,14 @@
 
 CORES = 2
 ONES = 16
-MOST = 2
+MOST = 3
+LENT = 4
+LEND_AT = 2
+ABSORB_FROM = 4
 DEGREE_PARTS = 2
 SHORT = pl.CostEstimate(flops=0, bytes_accessed=1024, transcendentals=0)
 VMEM_LIMIT = 24 * 1024 * 1024
+LEND_LIMIT = 52 * 1024 * 1024
 
 
 def chip_cycle(chips):
@@ -31,35 +35,42 @@
     return [i * wide + j for i, j in walk]
 
 
-def lend_kernel(where, gate, *refs):
-    out_ref = refs[-1]
-    depth = refs[0].shape[1]
-    for s, ref in enumerate(refs[:-1]):
-        out_ref[:, s * depth : (s + 1) * depth] = ref[...]
-
-
-def lend(where, gate, adj_rows, step, sections, n_row, depth):
-    rows = adj_rows.shape[0]
-
-    def block(s):
-        return pl.BlockSpec(
-            (rows, depth),
-            lambda g, where: (0, s * n_row + where[1 + step * sections + s] * CORES + 1 - where[0]),
+def lend_kernel(sections, n_row, depth, where, gate, rows_ref, *refs):
+    sems = refs[-1]
+    per = refs[0].shape[1] // depth
+    copies = []
+    for k in range(per * (len(refs) - 1)):
+        start = (k % sections * n_row + where[1 + k] * CORES + 1 - where[0]) * depth
+        copies.append(
+            pltpu.make_async_copy(
+                rows_ref.at[:, pl.ds(pl.multiple_of(start, 128), depth)],
+                refs[k // per].at[:, pl.ds(k % per * depth, depth)],
+                sems.at[k],
+            )
         )
-
+    for copy in copies:
+        copy.start()
+    for copy in copies:
+        copy.wait()
+
+
+def lend(where, gate, adj_rows, sections, n_row, depth):
+    blocks = sections * n_row // CORES
+    shape = jax.ShapeDtypeStruct((adj_rows.shape[0], blocks // LENT * depth), adj_rows.dtype)
     return pl.pallas_call(
-        lend_kernel,
-        grid_spec=pltpu.PrefetchScalarGridSpec(
-            num_scalar_prefetch=1,
-            grid=(1,),
-            in_specs=[pl.BlockSpec(memory_space=pl.ANY)] + [block(s) for s in range(sections)],
-            out_specs=pl.BlockSpec((rows, sections * depth), lambda g, where: (0, 0)),
-        ),
-        out_shape=jax.ShapeDtypeStruct((rows, sections * depth), adj_rows.dtype),
-        compiler_params=pltpu.CompilerParams(vmem_limit_bytes=VMEM_LIMIT),
+        functools.partial(lend_kernel, sections, n_row, depth),
+        in_specs=[
+            pl.BlockSpec(memory_space=pltpu.SMEM),
+            pl.BlockSpec(memory_space=pl.ANY),
+            pl.BlockSpec(memory_space=pl.ANY),
+        ],
+        out_specs=[pl.BlockSpec(memory_space=pl.ANY)] * LENT,
+        out_shape=[shape] * LENT,
+        scratch_shapes=[pltpu.SemaphoreType.DMA((blocks,))],
+        compiler_params=pltpu.CompilerParams(vmem_limit_bytes=LEND_LIMIT),
         cost_estimate=SHORT,
         name="lend",
-    )(where, gate, *[adj_rows] * sections)
+    )(where, gate, adj_rows)
 
 
 def absorb_kernel(sections, rows, first, where, *refs):
@@ -93,16 +104,17 @@
             ),
         )
 
+    per = n_row // CORES // LENT
+
     def other(s):
-        return pl.BlockSpec(
-            (rows, deep),
-            lambda g, where: (0, s * chunks + chunk),
-        )
-
-    whole = lambda shape: pl.BlockSpec(shape, lambda g, where: (0, 0))
+        return pl.BlockSpec((rows, deep), lambda g, where: (0, (step % per * sections + s) * chunks + chunk))
+
+    def whole(shape):
+        return pl.BlockSpec(shape, lambda g, where: (0, 0))
+
     shapes = [(rows, width), (rows + ONES, width)]
     first = sums is None
-    operands = [adj_rows] * sections + [borrowed] * sections + list(slabs)
+    operands = [adj_rows] * sections + [borrowed[step // per]] * sections + list(slabs)
     in_specs = [own(s) for s in range(sections)] + [other(s) for s in range(sections)]
     in_specs += [whole((deep, width))] * sections
     if not first:
@@ -166,9 +178,7 @@
         ]
         sums = None
         degree = []
-        borrowed = {}
         due = [(0, j, held[j]) for j in range(chunks)]
-        lends = list(range(chips))
         stretch = adj_rows.shape[1] // DEGREE_PARTS
         done = ()
 
@@ -184,28 +194,26 @@
                     arrived.append([lax.ppermute(held[j][s], "row", ring(way(s))) for s in range(sections)])
                 if step == 1:
                     continue
-                now = tie(adj_rows, held[j])
+                at = step - 1
                 done = []
-                at = step - 1
-                while lends and lends[0] <= at + 1 and len(done) < MOST:
-                    coming = lends.pop(0)
-                    lent = lend(where, held[j][0], adj_rows, coming, sections, n_row, depth)
-                    borrowed[coming] = lax.ppermute(lent, "row", swap)
+                due.append((at, j, held[j]))
+                if at == LEND_AT and j == chunks - 1:
+                    lent = lend(where, held[j][0], adj_rows, sections, n_row, depth)
+                    borrowed = [lax.ppermute(part, "row", swap) for part in lent]
                     done.append(lent)
-                due.append((at, j, held[j]))
-                if at > 1 or chips == 2:
+                if at >= ABSORB_FROM:
+                    now = tie(adj_rows, held[j])
                     for _ in range(MOST if step < chips else len(due)):
                         if due:
                             t, part, slabs = due.pop(0)
-                            sums = absorb(
-                                where, now, borrowed[t], tie(slabs, held[j]), sums, t, part, chunks, n_row
-                            )
+                            slabs = tie(slabs, held[j])
+                            sums = absorb(where, now, borrowed, slabs, sums, t, part, chunks, n_row)
                             done.append(sums)
-                if at > 2 and j == 0 and len(degree) < DEGREE_PARTS:
-                    k = len(degree) * stretch
-                    part = lax.slice_in_dim(now, k, k + stretch, axis=1)
-                    degree.append(jnp.sum(part, axis=1, dtype=jnp.float32))
-                    done.append(degree[-1])
+                    if at > ABSORB_FROM and j == 0 and len(degree) < DEGREE_PARTS:
+                        k = len(degree) * stretch
+                        part = lax.slice_in_dim(now, k, k + stretch, axis=1)
+                        degree.append(jnp.sum(part, axis=1, dtype=jnp.float32))
+                        done.append(degree[-1])
             held = arrived
         degree = sum(degree)
 

time: 141 us -> 294 us (2.09)
  Pallas kernels: 23 us -> 166 us
  waiting for transfers between devices: 73.6 us -> 81.4 us
    pallas_call x8 -> x1, Pallas kernels: 4.76 us -> 145 us  [lend(): pl.pallas_call(functools.partial(lend_kernel, sections, n_row, depth), in...]
    ppermute x28, waiting for transfers between devices: 72 us -> 79.8 us  [shards(): lax.ppermute(held[j][s], 'row', ring(way(s)))]
    pallas_call x16, Pallas kernels: 18.2 us -> 21.4 us  [absorb(): pl.pallas_call(functools.partial(absorb_kernel, sections, rows, first), g...]
    unnamed x20 -> x28, local copies, waits for them, and re-layouts: 7.22 us -> 8.34 us
  transfers between devices with their start and end apart: 37 -> 33, of which waited for: 26 -> 26; matrix products, arithmetic and copies ran while one was open for 2% -> 1% of each run, Pallas kernels for 16% -> 56%
where the time goes in v4:
time: 294 us
  Pallas kernels  166 us (56%)
  waiting for transfers between devices  81.4 us (28%)
  starting transfers between devices  31.9 us (11%)
  local copies, waits for them, and re-layouts  10.5 us (4%)
    pallas_call x1, Pallas kernels, lend(): pl.pallas_call(functools.partial(lend_kernel, sections, n_row, depth), in...  145 us
    ppermute x28, waiting for transfers between devices, shards(): lax.ppermute(held[j][s], 'row', ring(way(s)))  79.8 us
    ppermute x28, starting transfers between devices, shards(): lax.ppermute(held[j][s], 'row', ring(way(s)))  31.8 us
    pallas_call x16, Pallas kernels, absorb(): pl.pallas_call(functools.partial(absorb_kernel, sections, rows, first), g...  21.4 us
    unnamed x28, local copies, waits for them, and re-layouts  8.34 us
  transfers between devices with their start and end apart: 33, of which 26 were waited for; matrix products, arithmetic and copies ran while one was open for 1% of the time, Pallas kernels for 56%

profile of v4, /device:TPU:0, one launch (start us, length us, event | category | flops | bytes accessed | tf_op | source)
XLA Modules:
  0.0 293.8 jit_solution(7878484590993153947)
XLA Ops:
  0.6 1.5 slice_bitcast_fusion
  2.1 3.0 %collective-permute-start.8 = (bf16[512,384]{1,0:T(8,128)(2,1)S(1)}, bf16[512,384]{1,0:T(8,128)(2,1)S(1)}, u32[]{:S(2)}, u32[]{:S(2)}) collective-permute-start(bf16[512,384]{1,0:T(8,128)(2,1)S(1)} %get-tuple-element.125.refs_4_), channel_id=1, source_target_pairs={{0,2},{1,3},{2,6},{3,7},{6,10},{7,11},{10,14},{11,15},{14,12},{15,... | collective-permute-start | bytes 1179656 | tf_op jit(solution)/shard_map/ppermute | solution.py:194
  5.3 1.9 collective-permute-start
  7.3 7.8 %collective-permute-done.8.refs_4_ = bf16[512,384]{1,0:T(8,128)(2,1)S(1)} collective-permute-done((bf16[512,384]{1,0:T(8,128)(2,1)S(1)}, bf16[512,384]{1,0:T(8,128)(2,1)S(1)}, u32[]{:S(2)}, u32[]{:S(2)}) %collective-permute-start.8) | collective-permute-done | bytes 393248 | tf_op jit(solution)/shard_map/ppermute | solution.py:194
  15.2 2.1 collective-permute-done.9.refs_5_
  17.3 1.6 collective-permute-start.10
  19.3 4.3 %collective-permute-done.refs_4_ = bf16[512,384]{1,0:T(8,128)(2,1)S(1)} collective-permute-done((bf16[512,384]{1,0:T(8,128)(2,1)S(1)}, bf16[512,384]{1,0:T(8,128)(2,1)S(1)}, u32[]{:S(2)}, u32[]{:S(2)}) %collective-permute-start) | collective-permute-done | bytes 393248 | tf_op jit(solution)/shard_map/ppermute | solution.py:194
  23.6 2.1 collective-permute-done.1.refs_5_
  25.7 1.6 collective-permute-start.2
  27.8 4.3 %collective-permute-done.10.refs_4_ = bf16[512,384]{1,0:T(8,128)(2,1)S(1)} collective-permute-done((bf16[512,384]{1,0:T(8,128)(2,1)S(1)}, bf16[512,384]{1,0:T(8,128)(2,1)S(1)}, u32[]{:S(2)}, u32[]{:S(2)}) %collective-permute-start.10) | collective-permute-done | bytes 393248 | tf_op jit(solution)/shard_map/ppermute | solution.py:194
  32.0 2.0 collective-permute-done.11.refs_5_
  34.1 1.6 collective-permute-start.12
  36.3 4.1 %collective-permute-done.2.gate.refs_4_ = bf16[512,384]{1,0:T(8,128)(2,1)S(1)} collective-permute-done((bf16[512,384]{1,0:T(8,128)(2,1)S(1)}, bf16[512,384]{1,0:T(8,128)(2,1)S(1)}, u32[]{:S(2)}, u32[]{:S(2)}) %collective-permute-start.2) | collective-permute-done | bytes 393248 | tf_op jit(solution)/shard_map/ppermute | solution.py:194
  41.1 144.7 %lend.1 = (bf16[192,4096]{1,0:T(8,128)(2,1)S(1)}, bf16[192,4096]{1,0:T(8,128)(2,1)}, bf16[192,4096]{1,0:T(8,128)(2,1)}, bf16[192,4096]{1,0:T(8,128)(2,1)}) custom-call(s32[17]{0:T(128)S(1)} %dynamic-slice_bitcast_fusion.where, bf16[512,384]{1,0:T(8,128)(2,1)S(1)} %collective-permute-done.2.gate.refs_4_, bf16[192,32768]{1,0:T(8,128)(2,1)} %refs_1_.15), custom_call_target="tpu_custom_call" | custom-call | bytes 1024 | tf_op jit(solution)/shard_map/lend/pallas_call | solution.py:60
  186.0 1.4 collective-permute-start.13
  188.0 1.4 collective-permute-start.5
  189.4 8.5 %collective-permute-done.13.refs_5_ = bf16[512,384]{1,0:T(8,128)(2,1)S(1)} collective-permute-done((bf16[512,384]{1,0:T(8,128)(2,1)S(1)}, bf16[512,384]{1,0:T(8,128)(2,1)S(1)}, u32[]{:S(2)}, u32[]{:S(2)}) %collective-permute-start.13) | collective-permute-done | bytes 393248 | tf_op jit(solution)/shard_map/ppermute | solution.py:194
  199.5 6.4 %collective-permute-done.5.refs_5_ = bf16[512,384]{1,0:T(8,128)(2,1)S(1)} collective-permute-done((bf16[512,384]{1,0:T(8,128)(2,1)}, bf16[512,384]{1,0:T(8,128)(2,1)S(1)}, u32[]{:S(2)}, u32[]{:S(2)}) %collective-permute-start.5) | collective-permute-done | bytes 393248 | tf_op jit(solution)/shard_map/ppermute | solution.py:194
  205.9 1.4 collective-permute-start.15
  207.3 2.2 collective-permute-done.14.refs_4_
  209.5 1.6 collective-permute-start.6
  211.0 5.5 %collective-permute-done.15.refs_5_ = bf16[512,384]{1,0:T(8,128)(2,1)S(1)} collective-permute-done((bf16[512,384]{1,0:T(8,128)(2,1)S(1)}, bf16[512,384]{1,0:T(8,128)(2,1)S(1)}, u32[]{:S(2)}, u32[]{:S(2)}) %collective-permute-start.15) | collective-permute-done | bytes 393248 | tf_op jit(solution)/shard_map/ppermute | solution.py:194
  216.6 1.4 collective-permute-start.7
  218.0 1.5 collective-permute-done.6.refs_4_
  219.5 6.9 %collective-permute-done.7.refs_5_ = bf16[512,384]{1,0:T(8,128)(2,1)S(1)} collective-permute-done((bf16[512,384]{1,0:T(8,128)(2,1)S(1)}, bf16[512,384]{1,0:T(8,128)(2,1)S(1)}, u32[]{:S(2)}, u32[]{:S(2)}) %collective-permute-start.7) | collective-permute-done | bytes 393248 | tf_op jit(solution)/shard_map/ppermute | solution.py:194
  226.4 1.6 collective-permute-start.19
  228.4 4.6 %copy-done = bf16[192,32768]{1,0:T(8,128)(2,1)S(1)} copy-done((bf16[192,32768]{1,0:T(8,128)(2,1)S(1)}, bf16[192,32768]{1,0:T(8,128)(2,1)}, u32[]{:S(2)}) %copy-start) | copy-done | bytes 12582936
  235.4 2.2 absorb.18
  237.6 2.2 absorb.19
  242.0 1.3 slice-done.1
  243.3 1.2 slice-done.2
  244.5 2.2 absorb.21
  246.7 1.6 collective-permute-start.17
  248.8 1.6 collective-permute-start.25
  255.4 3.4 %collective-permute-done.17.refs_4_ = bf16[512,384]{1,0:T(8,128)(2,1)S(1)} collective-permute-done((bf16[512,384]{1,0:T(8,128)(2,1)S(1)}, bf16[512,384]{1,0:T(8,128)(2,1)S(1)}, u32[]{:S(2)}, u32[]{:S(2)}) %collective-permute-start.17) | collective-permute-done | bytes 393248 | tf_op jit(solution)/shard_map/ppermute | solution.py:194
  258.8 1.6 collective-permute-done.18.refs_5_
  260.4 1.6 collective-permute-start.23
  266.0 1.3 collective-permute-done.25.refs_4_
  267.2 1.6 collective-permute-done.26.refs_5_
  268.8 1.6 collective-permute-start.30
  272.9 2.7 collective-permute-done.23.refs_4_
  275.6 1.6 collective-permute-done.24.refs_5_
  277.2 1.6 collective-permute-start.28
  280.4 3.7 %collective-permute-done.30.refs_4_ = bf16[512,384]{1,0:T(8,128)(2,1)S(1)} collective-permute-done((bf16[512,384]{1,0:T(8,128)(2,1)S(1)}, bf16[512,384]{1,0:T(8,128)(2,1)S(1)}, u32[]{:S(2)}, u32[]{:S(2)}) %collective-permute-start.30) | collective-permute-done | bytes 393248 | tf_op jit(solution)/shard_map/ppermute | solution.py:194
  284.1 1.6 collective-permute-done.31.refs_5_
  286.8 2.0 collective-permute-done.28.refs_4_
  288.8 1.3 collective-permute-done.29.refs_5_
  291.3 1.6 collective-permute-done.32
  (71 shorter events, 26.5 us)
Async XLA Ops:
  2.1 13.0 %collective-permute-start.8 = (bf16[512,384]{1,0:T(8,128)(2,1)S(1)}, bf16[512,384]{1,0:T(8,128)(2,1)S(1)}, u32[]{:S(2)}, u32[]{:S(2)}) collective-permute-start(bf16[512,384]{1,0:T(8,128)(2,1)S(1)} %get-tuple-element.125.refs_4_), channel_id=1, source_target_pairs={{0,2},{1,3},{2,6},{3,7},{6,10},{7,11},{10,14},{11,15},{14,12},{15,... | collective-permute-start | bytes 1179656 | tf_op jit(solution)/shard_map/ppermute | solution.py:194
  5.2 12.1 %collective-permute-start.9 = (bf16[512,384]{1,0:T(8,128)(2,1)S(1)}, bf16[512,384]{1,0:T(8,128)(2,1)}, u32[]{:S(2)}, u32[]{:S(2)}) collective-permute-start(bf16[512,384]{1,0:T(8,128)(2,1)S(1)} %get-tuple-element.126.refs_5_), channel_id=1, source_target_pairs={{0,4},{1,5},{2,0},{3,1},{6,2},{7,3},{10,6},{11,7},{14,10},{15,11},... | collective-permute-start | bytes 1179656 | tf_op jit(solution)/shard_map/ppermute | solution.py:194
  5.3 18.3 %collective-permute-start = (bf16[512,384]{1,0:T(8,128)(2,1)S(1)}, bf16[512,384]{1,0:T(8,128)(2,1)S(1)}, u32[]{:S(2)}, u32[]{:S(2)}) collective-permute-start(bf16[512,384]{1,0:T(8,128)(2,1)S(1)} %get-tuple-element.129.refs_4_), channel_id=1, source_target_pairs={{0,2},{1,3},{2,6},{3,7},{6,10},{7,11},{10,14},{11,15},{14,12},{15,... | collective-permute-start | bytes 1179656 | tf_op jit(solution)/shard_map/ppermute | solution.py:194
  7.2 18.5 %collective-permute-start.1 = (bf16[512,384]{1,0:T(8,128)(2,1)S(1)}, bf16[512,384]{1,0:T(8,128)(2,1)}, u32[]{:S(2)}, u32[]{:S(2)}) collective-permute-start(bf16[512,384]{1,0:T(8,128)(2,1)S(1)} %get-tuple-element.130.refs_5_), channel_id=1, source_target_pairs={{0,4},{1,5},{2,0},{3,1},{6,2},{7,3},{10,6},{11,7},{14,10},{15,11},... | collective-permute-start | bytes 1179656 | tf_op jit(solution)/shard_map/ppermute | solution.py:194
  17.3 14.7 %collective-permute-start.10 = (bf16[512,384]{1,0:T(8,128)(2,1)S(1)}, bf16[512,384]{1,0:T(8,128)(2,1)S(1)}, u32[]{:S(2)}, u32[]{:S(2)}) collective-permute-start(bf16[512,384]{1,0:T(8,128)(2,1)S(1)} %collective-permute-done.8.refs_4_), channel_id=1, source_target_pairs={{0,2},{1,3},{2,6},{3,7},{6,10},{7,11},{10,14},{11,15},{14,12},{15,... | collective-permute-start | bytes 1179656 | tf_op jit(solution)/shard_map/ppermute | solution.py:194
  18.9 15.2 %collective-permute-start.11 = (bf16[512,384]{1,0:T(8,128)(2,1)}, bf16[512,384]{1,0:T(8,128)(2,1)S(1)}, u32[]{:S(2)}, u32[]{:S(2)}) collective-permute-start(bf16[512,384]{1,0:T(8,128)(2,1)} %collective-permute-done.9.refs_5_), channel_id=1, source_target_pairs={{0,4},{1,5},{2,0},{3,1},{6,2},{7,3},{10,6},{11,7},{14,10},{15,11},... | collective-permute-start | bytes 1179656 | tf_op jit(solution)/shard_map/ppermute | solution.py:194
  25.7 14.7 %collective-permute-start.2 = (bf16[512,384]{1,0:T(8,128)(2,1)S(1)}, bf16[512,384]{1,0:T(8,128)(2,1)S(1)}, u32[]{:S(2)}, u32[]{:S(2)}) collective-permute-start(bf16[512,384]{1,0:T(8,128)(2,1)S(1)} %collective-permute-done.refs_4_), channel_id=1, source_target_pairs={{0,2},{1,3},{2,6},{3,7},{6,10},{7,11},{10,14},{11,15},{14,12},{15,... | collective-permute-start | bytes 1179656 | tf_op jit(solution)/shard_map/ppermute | solution.py:194
  27.3 13.8 %collective-permute-start.3 = (bf16[512,384]{1,0:T(8,128)(2,1)}, bf16[512,384]{1,0:T(8,128)(2,1)}, u32[]{:S(2)}, u32[]{:S(2)}) collective-permute-start(bf16[512,384]{1,0:T(8,128)(2,1)} %collective-permute-done.1.refs_5_), channel_id=1, source_target_pairs={{0,4},{1,5},{2,0},{3,1},{6,2},{7,3},{10,6},{11,7},{14,10},{15,11},... | collective-permute-start | bytes 1179656 | tf_op jit(solution)/shard_map/ppermute | solution.py:194
  34.1 154.0 %collective-permute-start.12 = (bf16[512,384]{1,0:T(8,128)(2,1)S(1)}, bf16[512,384]{1,0:T(8,128)(2,1)S(1)}, u32[]{:S(2)}, u32[]{:S(2)}) collective-permute-start(bf16[512,384]{1,0:T(8,128)(2,1)S(1)} %collective-permute-done.10.refs_4_), channel_id=1, source_target_pairs={{0,2},{1,3},{2,6},{3,7},{6,10},{7,11},{10,14},{11,15},{14,12},{15,... | collective-permute-start | bytes 1179656 | tf_op jit(solution)/shard_map/ppermute | solution.py:194
  185.9 42.1 %collective-permute-start.16 = (bf16[192,4096]{1,0:T(8,128)(2,1)S(1)}, bf16[192,4096]{1,0:T(8,128)(2,1)S(1)}, u32[]{:S(2)}, u32[]{:S(2)}) collective-permute-start(bf16[192,4096]{1,0:T(8,128)(2,1)S(1)} %get-tuple-element.116), channel_id=1, source_target_pairs={{0,1},{1,0},{2,3},{3,2},{4,5},{5,4},{6,7},{7,6},{8,9},{9,8},{10,11... | collective-permute-start | bytes 4718600 | tf_op jit(solution)/shard_map/ppermute | solution.py:202
  186.0 12.0 %collective-permute-start.13 = (bf16[512,384]{1,0:T(8,128)(2,1)S(1)}, bf16[512,384]{1,0:T(8,128)(2,1)S(1)}, u32[]{:S(2)}, u32[]{:S(2)}) collective-permute-start(bf16[512,384]{1,0:T(8,128)(2,1)S(1)} %collective-permute-done.11.refs_5_), channel_id=1, source_target_pairs={{0,4},{1,5},{2,0},{3,1},{6,2},{7,3},{10,6},{11,7},{14,10},{15,11},... | collective-permute-start | bytes 1179656 | tf_op jit(solution)/shard_map/ppermute | solution.py:194
  187.4 11.2 %collective-permute-start.4 = (bf16[512,384]{1,0:T(8,128)(2,1)S(1)}, bf16[512,384]{1,0:T(8,128)(2,1)S(1)}, u32[]{:S(2)}, u32[]{:S(2)}) collective-permute-start(bf16[512,384]{1,0:T(8,128)(2,1)S(1)} %collective-permute-done.2.gate.refs_4_), channel_id=1, source_target_pairs={{0,2},{1,3},{2,6},{3,7},{6,10},{7,11},{10,14},{11,15},{14,12},{15,... | collective-permute-start | bytes 1179656 | tf_op jit(solution)/shard_map/ppermute | solution.py:194
  188.0 51.8 %collective-permute-start.21 = (bf16[192,4096]{1,0:T(8,128)(2,1)}, bf16[192,4096]{1,0:T(8,128)(2,1)S(1)}, u32[]{:S(2)}, u32[]{:S(2)}) collective-permute-start(bf16[192,4096]{1,0:T(8,128)(2,1)} %get-tuple-element.117), channel_id=1, source_target_pairs={{0,1},{1,0},{2,3},{3,2},{4,5},{5,4},{6,7},{7,6},{8,9},{9,8},{10,11... | collective-permute-start | bytes 4718600 | tf_op jit(solution)/shard_map/ppermute | solution.py:202
  188.0 17.9 %collective-permute-start.5 = (bf16[512,384]{1,0:T(8,128)(2,1)}, bf16[512,384]{1,0:T(8,128)(2,1)S(1)}, u32[]{:S(2)}, u32[]{:S(2)}) collective-permute-start(bf16[512,384]{1,0:T(8,128)(2,1)} %collective-permute-done.3.refs_5_), channel_id=1, source_target_pairs={{0,4},{1,5},{2,0},{3,1},{6,2},{7,3},{10,6},{11,7},{14,10},{15,11},... | collective-permute-start | bytes 1179656 | tf_op jit(solution)/shard_map/ppermute | solution.py:194
  197.9 54.8 %collective-permute-start.22 = (bf16[192,4096]{1,0:T(8,128)(2,1)}, bf16[192,4096]{1,0:T(8,128)(2,1)S(1)}, u32[]{:S(2)}, u32[]{:S(2)}) collective-permute-start(bf16[192,4096]{1,0:T(8,128)(2,1)} %get-tuple-element.118), channel_id=1, source_target_pairs={{0,1},{1,0},{2,3},{3,2},{4,5},{5,4},{6,7},{7,6},{8,9},{9,8},{10,11... | collective-permute-start | bytes 4718600 | tf_op jit(solution)/shard_map/ppermute | solution.py:202
  198.6 10.9 %collective-permute-start.14 = (bf16[512,384]{1,0:T(8,128)(2,1)S(1)}, bf16[512,384]{1,0:T(8,128)(2,1)S(1)}, u32[]{:S(2)}, u32[]{:S(2)}) collective-permute-start(bf16[512,384]{1,0:T(8,128)(2,1)S(1)} %collective-permute-done.12.refs_4_), channel_id=1, source_target_pairs={{0,2},{1,3},{2,6},{3,7},{6,10},{7,11},{10,14},{11,15},{14,12},{15,... | collective-permute-start | bytes 1179656 | tf_op jit(solution)/shard_map/ppermute | solution.py:194
  205.9 10.7 %collective-permute-start.15 = (bf16[512,384]{1,0:T(8,128)(2,1)S(1)}, bf16[512,384]{1,0:T(8,128)(2,1)S(1)}, u32[]{:S(2)}, u32[]{:S(2)}) collective-permute-start(bf16[512,384]{1,0:T(8,128)(2,1)S(1)} %collective-permute-done.13.refs_5_), channel_id=1, source_target_pairs={{0,4},{1,5},{2,0},{3,1},{6,2},{7,3},{10,6},{11,7},{14,10},{15,11},... | collective-permute-start | bytes 1179656 | tf_op jit(solution)/shard_map/ppermute | solution.py:194
  209.5 10.0 %collective-permute-start.6 = (bf16[512,384]{1,0:T(8,128)(2,1)S(1)}, bf16[512,384]{1,0:T(8,128)(2,1)S(1)}, u32[]{:S(2)}, u32[]{:S(2)}) collective-permute-start(bf16[512,384]{1,0:T(8,128)(2,1)S(1)} %collective-permute-done.4.refs_4_), channel_id=1, source_target_pairs={{0,2},{1,3},{2,6},{3,7},{6,10},{7,11},{10,14},{11,15},{14,12},{15,... | collective-permute-start | bytes 1179656 | tf_op jit(solution)/shard_map/ppermute | solution.py:194
  216.6 9.8 %collective-permute-start.7 = (bf16[512,384]{1,0:T(8,128)(2,1)S(1)}, bf16[512,384]{1,0:T(8,128)(2,1)S(1)}, u32[]{:S(2)}, u32[]{:S(2)}) collective-permute-start(bf16[512,384]{1,0:T(8,128)(2,1)S(1)} %collective-permute-done.5.refs_5_), channel_id=1, source_target_pairs={{0,4},{1,5},{2,0},{3,1},{6,2},{7,3},{10,6},{11,7},{14,10},{15,11},... | collective-permute-start | bytes 1179656 | tf_op jit(solution)/shard_map/ppermute | solution.py:194
  219.5 52.3 %collective-permute-start.27 = (bf16[192,4096]{1,0:T(8,128)(2,1)}, bf16[192,4096]{1,0:T(8,128)(2,1)S(1)}, u32[]{:S(2)}, u32[]{:S(2)}) collective-permute-start(bf16[192,4096]{1,0:T(8,128)(2,1)} %get-tuple-element.119), channel_id=1, source_target_pairs={{0,1},{1,0},{2,3},{3,2},{4,5},{5,4},{6,7},{7,6},{8,9},{9,8},{10,11... | collective-permute-start | bytes 4718600 | tf_op jit(solution)/shard_map/ppermute | solution.py:202
  226.4 20.3 %collective-permute-start.19 = (bf16[512,384]{1,0:T(8,128)(2,1)S(1)}, bf16[512,384]{1,0:T(8,128)(2,1)S(1)}, u32[]{:S(2)}, u32[]{:S(2)}) collective-permute-start(bf16[512,384]{1,0:T(8,128)(2,1)S(1)} %collective-permute-done.14.refs_4_), channel_id=1, source_target_pairs={{0,2},{1,3},{2,6},{3,7},{6,10},{7,11},{10,14},{11,15},{14,12},{15,... | collective-permute-start | bytes 1179656 | tf_op jit(solution)/shard_map/ppermute | solution.py:194
  227.9 18.7 %collective-permute-start.20 = (bf16[512,384]{1,0:T(8,128)(2,1)S(1)}, bf16[512,384]{1,0:T(8,128)(2,1)S(1)}, u32[]{:S(2)}, u32[]{:S(2)}) collective-permute-start(bf16[512,384]{1,0:T(8,128)(2,1)S(1)} %collective-permute-done.15.refs_5_), channel_id=1, source_target_pairs={{0,4},{1,5},{2,0},{3,1},{6,2},{7,3},{10,6},{11,7},{14,10},{15,11},... | collective-permute-start | bytes 1179656 | tf_op jit(solution)/shard_map/ppermute | solution.py:194
  228.4 4.6 %copy-start = (bf16[192,32768]{1,0:T(8,128)(2,1)S(1)}, bf16[192,32768]{1,0:T(8,128)(2,1)}, u32[]{:S(2)}) copy-start(bf16[192,32768]{1,0:T(8,128)(2,1)} %refs_1_.15) | copy-start | bytes 37748740
  239.8 2.2 slice-start
  239.8 3.4 %slice-start.1 = ((s8[12582912]{0:T(1024)(128)(4,1)}), s8[4194304]{0:T(1024)(128)(4,1)S(1)}, s32[]{:S(2)}) async-start(s8[12582912]{0:T(1024)(128)(4,1)} %bitcast.10), calls=%async_computation.1 | async-start | bytes 8388608
  239.9 4.6 %slice-start.2 = ((s8[12582912]{0:T(1024)(128)(4,1)}), s8[4194304]{0:T(1024)(128)(4,1)S(1)}, s32[]{:S(2)}) async-start(s8[12582912]{0:T(1024)(128)(4,1)} %bitcast.10), calls=%async_computation.2 | async-start | bytes 8388608
  246.7 12.1 %collective-permute-start.17 = (bf16[512,384]{1,0:T(8,128)(2,1)S(1)}, bf16[512,384]{1,0:T(8,128)(2,1)S(1)}, u32[]{:S(2)}, u32[]{:S(2)}) collective-permute-start(bf16[512,384]{1,0:T(8,128)(2,1)S(1)} %collective-permute-done.6.refs_4_), channel_id=1, source_target_pairs={{0,2},{1,3},{2,6},{3,7},{6,10},{7,11},{10,14},{11,15},{14,12},{15,... | collective-permute-start | bytes 1179656 | tf_op jit(solution)/shard_map/ppermute | solution.py:194
  248.3 12.1 %collective-permute-start.18 = (bf16[512,384]{1,0:T(8,128)(2,1)S(1)}, bf16[512,384]{1,0:T(8,128)(2,1)S(1)}, u32[]{:S(2)}, u32[]{:S(2)}) collective-permute-start(bf16[512,384]{1,0:T(8,128)(2,1)S(1)} %collective-permute-done.7.refs_5_), channel_id=1, source_target_pairs={{0,4},{1,5},{2,0},{3,1},{6,2},{7,3},{10,6},{11,7},{14,10},{15,11},... | collective-permute-start | bytes 1179656 | tf_op jit(solution)/shard_map/ppermute | solution.py:194
  248.8 18.5 %collective-permute-start.25 = (bf16[512,384]{1,0:T(8,128)(2,1)S(1)}, bf16[512,384]{1,0:T(8,128)(2,1)S(1)}, u32[]{:S(2)}, u32[]{:S(2)}) collective-permute-start(bf16[512,384]{1,0:T(8,128)(2,1)S(1)} %collective-permute-done.19.refs_4_), channel_id=1, source_target_pairs={{0,2},{1,3},{2,6},{3,7},{6,10},{7,11},{10,14},{11,15},{14,12},{15,... | collective-permute-start | bytes 1179656 | tf_op jit(solution)/shard_map/ppermute | solution.py:194
  252.8 16.0 %collective-permute-start.26 = (bf16[512,384]{1,0:T(8,128)(2,1)S(1)}, bf16[512,384]{1,0:T(8,128)(2,1)S(1)}, u32[]{:S(2)}, u32[]{:S(2)}) collective-permute-start(bf16[512,384]{1,0:T(8,128)(2,1)S(1)} %collective-permute-done.20.refs_5_), channel_id=1, source_target_pairs={{0,4},{1,5},{2,0},{3,1},{6,2},{7,3},{10,6},{11,7},{14,10},{15,11},... | collective-permute-start | bytes 1179656 | tf_op jit(solution)/shard_map/ppermute | solution.py:194
  260.4 15.3 %collective-permute-start.23 = (bf16[512,384]{1,0:T(8,128)(2,1)S(1)}, bf16[512,384]{1,0:T(8,128)(2,1)S(1)}, u32[]{:S(2)}, u32[]{:S(2)}) collective-permute-start(bf16[512,384]{1,0:T(8,128)(2,1)S(1)} %collective-permute-done.17.refs_4_), channel_id=1, source_target_pairs={{0,2},{1,3},{2,6},{3,7},{6,10},{7,11},{10,14},{11,15},{14,12},{15,... | collective-permute-start | bytes 1179656 | tf_op jit(solution)/shard_map/ppermute | solution.py:194
  262.0 15.3 %collective-permute-start.24 = (bf16[512,384]{1,0:T(8,128)(2,1)S(1)}, bf16[512,384]{1,0:T(8,128)(2,1)S(1)}, u32[]{:S(2)}, u32[]{:S(2)}) collective-permute-start(bf16[512,384]{1,0:T(8,128)(2,1)S(1)} %collective-permute-done.18.refs_5_), channel_id=1, source_target_pairs={{0,4},{1,5},{2,0},{3,1},{6,2},{7,3},{10,6},{11,7},{14,10},{15,11},... | collective-permute-start | bytes 1179656 | tf_op jit(solution)/shard_map/ppermute | solution.py:194
  268.8 15.3 %collective-permute-start.30 = (bf16[512,384]{1,0:T(8,128)(2,1)S(1)}, bf16[512,384]{1,0:T(8,128)(2,1)S(1)}, u32[]{:S(2)}, u32[]{:S(2)}) collective-permute-start(bf16[512,384]{1,0:T(8,128)(2,1)S(1)} %collective-permute-done.25.refs_4_), channel_id=1, source_target_pairs={{0,2},{1,3},{2,6},{3,7},{6,10},{7,11},{10,14},{11,15},{14,12},{15,... | collective-permute-start | bytes 1179656 | tf_op jit(solution)/shard_map/ppermute | solution.py:194
  270.4 15.3 %collective-permute-start.31 = (bf16[512,384]{1,0:T(8,128)(2,1)S(1)}, bf16[512,384]{1,0:T(8,128)(2,1)S(1)}, u32[]{:S(2)}, u32[]{:S(2)}) collective-permute-start(bf16[512,384]{1,0:T(8,128)(2,1)S(1)} %collective-permute-done.26.refs_5_), channel_id=1, source_target_pairs={{0,4},{1,5},{2,0},{3,1},{6,2},{7,3},{10,6},{11,7},{14,10},{15,11},... | collective-permute-start | bytes 1179656 | tf_op jit(solution)/shard_map/ppermute | solution.py:194
  277.2 11.5 %collective-permute-start.28 = (bf16[512,384]{1,0:T(8,128)(2,1)S(1)}, bf16[512,384]{1,0:T(8,128)(2,1)S(1)}, u32[]{:S(2)}, u32[]{:S(2)}) collective-permute-start(bf16[512,384]{1,0:T(8,128)(2,1)S(1)} %collective-permute-done.23.refs_4_), channel_id=1, source_target_pairs={{0,2},{1,3},{2,6},{3,7},{6,10},{7,11},{10,14},{11,15},{14,12},{15,... | collective-permute-start | bytes 1179656 | tf_op jit(solution)/shard_map/ppermute | solution.py:194
  278.8 11.2 %collective-permute-start.29 = (bf16[512,384]{1,0:T(8,128)(2,1)S(1)}, bf16[512,384]{1,0:T(8,128)(2,1)S(1)}, u32[]{:S(2)}, u32[]{:S(2)}) collective-permute-start(bf16[512,384]{1,0:T(8,128)(2,1)S(1)} %collective-permute-done.24.refs_5_), channel_id=1, source_target_pairs={{0,4},{1,5},{2,0},{3,1},{6,2},{7,3},{10,6},{11,7},{14,10},{15,11},... | collective-permute-start | bytes 1179656 | tf_op jit(solution)/shard_map/ppermute | solution.py:194
  290.1 2.9 copy-start.1
  291.2 1.7 collective-permute-start.32
  291.3 2.5 copy-start.2

commit v5 on v3

--- a/solution.py
+++ b/solution.py
@@ -10,11 +10,15 @@
 
 CORES = 2
 ONES = 16
-MOST = 2
+SLOTS = 1
+LENDS = 2
+MOST = 3
+LEND_FROM = 1
+ABSORB_FROM = 2
 DEGREE_PARTS = 2
 SHORT = pl.CostEstimate(flops=0, bytes_accessed=1024, transcendentals=0)
 VMEM_LIMIT = 24 * 1024 * 1024
-LEND_LIMIT = 52 * 1024 * 1024
+LEND_LIMIT = 48 * 1024 * 1024
 
 
 def chip_cycle(chips):
@@ -139,7 +143,7 @@
     def shards(adj_rows, adj_panel, adj_tile):
         rows = adj_rows.shape[0]
         sections, depth, width = adj_panel.shape
-        chunks = 2 if depth % 256 == 0 else 1
+        chunks = 1
         deep = depth // chunks
         table = np.array(
             [
@@ -165,7 +169,7 @@
         due = [(0, j, held[j]) for j in range(chunks)]
         lends = list(range(chips))
         stretch = adj_rows.shape[1] // DEGREE_PARTS
-        done = ()
+        past = []
 
         def tie(values, others):
             return lax.optimization_barrier((values, others))[0]
@@ -174,27 +178,28 @@
             arrived = []
             for j in range(chunks):
                 if step > 1:
-                    held[j] = tie(held[j], done)
+                    held[j] = tie(held[j], past[-SLOTS] if len(past) >= SLOTS else ())
                 if step < chips:
                     arrived.append([lax.ppermute(held[j][s], "row", ring(way(s))) for s in range(sections)])
                 if step == 1:
                     continue
                 now = tie(adj_rows, held[j])
                 done = []
+                past.append(done)
                 at = step - 1
-                while lends and lends[0] <= at + 1 and len(done) < MOST:
+                while at >= LEND_FROM and lends and lends[0] <= at + 1 and len(done) < LENDS:
                     coming = lends.pop(0)
                     own[coming], lent = lend(where, held[j][0], adj_rows, coming, sections, n_row, depth)
                     borrowed[coming] = lax.ppermute(lent, "row", swap)
                     done.append(lent)
                 due.append((at, j, held[j]))
-                if at > 1 or chips == 2:
+                if at >= ABSORB_FROM:
                     for _ in range(MOST if step < chips else len(due)):
                         if due:
                             t, part, slabs = due.pop(0)
                             sums = absorb(own[t], borrowed[t], tie(slabs, held[j]), sums, part, chunks)
                             done.append(sums)
-                if at > 2 and j == 0 and len(degree) < DEGREE_PARTS:
+                if at > ABSORB_FROM and j == 0 and len(degree) < DEGREE_PARTS:
                     k = len(degree) * stretch
                     part = lax.slice_in_dim(now, k, k + stretch, axis=1)
                     degree.append(jnp.sum(part, axis=1, dtype=jnp.float32))

time: 142 us -> 144 us (1.014)
  waiting for transfers between devices: 63.4 us -> 89.1 us
  starting transfers between devices: 37.2 us -> 16.5 us
  Pallas kernels: 27.8 us -> 26.2 us
    ppermute x28 -> x14, waiting for transfers between devices: 61.8 us -> 87.5 us  [shards(): lax.ppermute(held[j][s], 'row', ring(way(s)))]
    ppermute x28 -> x14, starting transfers between devices: 36.9 us -> 15.3 us  [shards(): lax.ppermute(held[j][s], 'row', ring(way(s)))]
    pallas_call x8, Pallas kernels: 18.2 us -> 15.5 us  [lend(): pl.pallas_call(functools.partial(lend_kernel, step, sections, n_row, dept...]
    pallas_call x16 -> x8, Pallas kernels: 9.6 us -> 10.7 us  [absorb(): pl.pallas_call(functools.partial(absorb_kernel, sections, rows, first), g...]
  transfers between devices with their start and end apart: 37 -> 23, of which waited for: 23 -> 15; matrix products, arithmetic and copies ran while one was open for 6% -> 6% of each run, Pallas kernels for 19% -> 18%
where the time goes in v5:
time: 144 us; the launch traced here: 143 us
  waiting for transfers between devices  89.1 us (62%)
  Pallas kernels  26.2 us (18%)
  starting transfers between devices  16.5 us (11%)
  other arithmetic  8.38 us (6%)
  local copies, waits for them, and re-layouts  2.32 us (2%)
    ppermute x14, waiting for transfers between devices, shards(): lax.ppermute(held[j][s], 'row', ring(way(s)))  87.5 us
    pallas_call x8, Pallas kernels, lend(): pl.pallas_call(functools.partial(lend_kernel, step, sections, n_row, dept...  15.5 us
    ppermute x14, starting transfers between devices, shards(): lax.ppermute(held[j][s], 'row', ring(way(s)))  15.3 us
    pallas_call x8, Pallas kernels, absorb(): pl.pallas_call(functools.partial(absorb_kernel, sections, rows, first), g...  10.7 us
    reduce_sum x2, other arithmetic, shards(): degree.append(jnp.sum(part, axis=1, dtype=jnp.float32))  7.5 us
  transfers between devices with their start and end apart: 23, of which 15 were waited for; matrix products, arithmetic and copies ran while one was open for 6% of the time, Pallas kernels for 18%

profile of v5, /device:TPU:0, one launch (start us, length us, event | category | flops | bytes accessed | tf_op | source)
XLA Modules:
  0.0 143.4 jit_solution(13270049555182781820)
XLA Ops:
  0.6 1.5 %slice_bitcast_fusion = (bf16[1024,384]{1,0:T(8,128)(2,1)S(1)}, bf16[1024,384]{1,0:T(8,128)(2,1)S(1)}) fusion(bf16[2,1024,384]{2,1,0:T(8,128)(2,1)} %param.5), kind=kLoop, calls=%fused_computation.2 | loop fusion | bytes 3145728 | tf_op jit(solution)/shard_map/squeeze | solution.py:163
  2.2 3.0 %collective-permute-start = (bf16[1024,384]{1,0:T(8,128)(2,1)S(1)}, bf16[1024,384]{1,0:T(8,128)(2,1)S(1)}, u32[]{:S(2)}, u32[]{:S(2)}) collective-permute-start(bf16[1024,384]{1,0:T(8,128)(2,1)S(1)} %get-tuple-element.75.refs_4_), channel_id=1, source_target_pairs={{0,2},{1,3},{2,6},{3,7},{6,10},{7,11},{10,14},{11,15},{14,12},{15,... | collective-permute-start | bytes 2359304 | tf_op jit(solution)/shard_map/ppermute | solution.py:183
  5.3 17.5 %collective-permute-done.gate.refs_4_ = bf16[1024,384]{1,0:T(8,128)(2,1)S(1)} collective-permute-done((bf16[1024,384]{1,0:T(8,128)(2,1)S(1)}, bf16[1024,384]{1,0:T(8,128)(2,1)S(1)}, u32[]{:S(2)}, u32[]{:S(2)}) %collective-permute-start) | collective-permute-done | bytes 786464 | tf_op jit(solution)/shard_map/ppermute | solution.py:183
  22.8 1.5 %collective-permute-done.1.refs_5_ = bf16[1024,384]{1,0:T(8,128)(2,1)} collective-permute-done((bf16[1024,384]{1,0:T(8,128)(2,1)S(1)}, bf16[1024,384]{1,0:T(8,128)(2,1)}, u32[]{:S(2)}, u32[]{:S(2)}) %collective-permute-start.1) | collective-permute-done | bytes 786464 | tf_op jit(solution)/shard_map/ppermute | solution.py:183
  24.3 1.6 %collective-permute-start.2 = (bf16[1024,384]{1,0:T(8,128)(2,1)S(1)}, bf16[1024,384]{1,0:T(8,128)(2,1)S(1)}, u32[]{:S(2)}, u32[]{:S(2)}) collective-permute-start(bf16[1024,384]{1,0:T(8,128)(2,1)S(1)} %collective-permute-done.gate.refs_4_), channel_id=1, source_target_pairs={{0,2},{1,3},{2,6},{3,7},{6,10},{7,11},{10,14},{11,15},{14,12},{15,... | collective-permute-start | bytes 2359304 | tf_op jit(solution)/shard_map/ppermute | solution.py:183
  25.9 0.4 collective-permute-start.3
  26.3 0.7 dynamic-slice_bitcast_fusion.where
  27.0 1.9 %lend.8 = (bf16[192,2048]{1,0:T(8,128)(2,1)S(1)}, bf16[192,2048]{1,0:T(8,128)(2,1)S(1)}) custom-call(s32[17]{0:T(128)S(1)} %dynamic-slice_bitcast_fusion.where, bf16[1024,384]{1,0:T(8,128)(2,1)S(1)} %collective-permute-done.gate.refs_4_, bf16[192,32768]{1,0:T(8,128)(2,1)} %rows_ref.15), custom_call_target="tpu_custom_call" | custom-call | bytes 1024 | tf_op jit(solution)/shard_map/lend/pallas_call | solution.py:61
  29.0 1.9 %lend.9 = (bf16[192,2048]{1,0:T(8,128)(2,1)S(1)}, bf16[192,2048]{1,0:T(8,128)(2,1)S(1)}) custom-call(s32[17]{0:T(128)S(1)} %dynamic-slice_bitcast_fusion.where, bf16[1024,384]{1,0:T(8,128)(2,1)S(1)} %collective-permute-done.gate.refs_4_, bf16[192,32768]{1,0:T(8,128)(2,1)} %rows_ref.15), custom_call_target="tpu_custom_call" | custom-call | bytes 1024 | tf_op jit(solution)/shard_map/lend/pallas_call | solution.py:61
  31.0 0.6 collective-permute-start.7
  31.5 10.8 %collective-permute-done.2.gate.refs_4_ = bf16[1024,384]{1,0:T(8,128)(2,1)S(1)} collective-permute-done((bf16[1024,384]{1,0:T(8,128)(2,1)S(1)}, bf16[1024,384]{1,0:T(8,128)(2,1)S(1)}, u32[]{:S(2)}, u32[]{:S(2)}) %collective-permute-start.2) | collective-permute-done | bytes 786464 | tf_op jit(solution)/shard_map/ppermute | solution.py:183
  42.4 1.6 %collective-permute-done.3.refs_5_ = bf16[1024,384]{1,0:T(8,128)(2,1)} collective-permute-done((bf16[1024,384]{1,0:T(8,128)(2,1)}, bf16[1024,384]{1,0:T(8,128)(2,1)}, u32[]{:S(2)}, u32[]{:S(2)}) %collective-permute-start.3) | collective-permute-done | bytes 786464 | tf_op jit(solution)/shard_map/ppermute | solution.py:183
  44.0 1.9 %lend.10 = (bf16[192,2048]{1,0:T(8,128)(2,1)S(1)}, bf16[192,2048]{1,0:T(8,128)(2,1)S(1)}) custom-call(s32[17]{0:T(128)S(1)} %dynamic-slice_bitcast_fusion.where, bf16[1024,384]{1,0:T(8,128)(2,1)S(1)} %collective-permute-done.2.gate.refs_4_, bf16[192,32768]{1,0:T(8,128)(2,1)} %rows_ref.15), custom_call_target="tpu_custom_call" | custom-call | bytes 1024 | tf_op jit(solution)/shard_map/lend/pallas_call | solution.py:61
  46.0 1.6 %collective-permute-start.4 = (bf16[1024,384]{1,0:T(8,128)(2,1)S(1)}, bf16[1024,384]{1,0:T(8,128)(2,1)S(1)}, u32[]{:S(2)}, u32[]{:S(2)}) collective-permute-start(bf16[1024,384]{1,0:T(8,128)(2,1)S(1)} %collective-permute-done.2.gate.refs_4_), channel_id=1, source_target_pairs={{0,2},{1,3},{2,6},{3,7},{6,10},{7,11},{10,14},{11,15},{14,12},{15,... | collective-permute-start | bytes 2359304 | tf_op jit(solution)/shard_map/ppermute | solution.py:183
  47.6 0.4 collective-permute-start.5
  48.1 1.9 %lend.11 = (bf16[192,2048]{1,0:T(8,128)(2,1)S(1)}, bf16[192,2048]{1,0:T(8,128)(2,1)S(1)}) custom-call(s32[17]{0:T(128)S(1)} %dynamic-slice_bitcast_fusion.where, bf16[1024,384]{1,0:T(8,128)(2,1)S(1)} %collective-permute-done.2.gate.refs_4_, bf16[192,32768]{1,0:T(8,128)(2,1)} %rows_ref.15), custom_call_target="tpu_custom_call" | custom-call | bytes 1024 | tf_op jit(solution)/shard_map/lend/pallas_call | solution.py:61
  50.1 1.0 absorb.8
  51.2 2.3 %absorb.9 = (f32[192,384]{1,0:T(8,128)S(1)}, f32[208,384]{1,0:T(8,128)S(1)}) custom-call(bf16[192,2048]{1,0:T(8,128)(2,1)S(1)} %get-tuple-element.79.refs_0_.refs_1_, bf16[192,2048]{1,0:T(8,128)(2,1)S(1)} %get-tuple-element.79.refs_0_.refs_1_, ...), custom_call_target="tpu_custom_call", output_to_operand_aliasing={{0}: (6, {}), {1}: (7, {})} | custom-call | bytes 1024 | tf_op jit(solution)/shard_map/absorb/pallas_call | solution.py:113
  53.6 2.3 %absorb.10 = (f32[192,384]{1,0:T(8,128)S(1)}, f32[208,384]{1,0:T(8,128)S(1)}) custom-call(bf16[192,2048]{1,0:T(8,128)(2,1)S(1)} %get-tuple-element.84.refs_0_.refs_1_, bf16[192,2048]{1,0:T(8,128)(2,1)S(1)} %get-tuple-element.84.refs_0_.refs_1_, ...), custom_call_target="tpu_custom_call", output_to_operand_aliasing={{0}: (6, {}), {1}: (7, {})} | custom-call | bytes 1024 | tf_op jit(solution)/shard_map/absorb/pallas_call | solution.py:113
  55.8 10.1 %collective-permute-done.4.gate.refs_4_ = bf16[1024,384]{1,0:T(8,128)(2,1)S(1)} collective-permute-done((bf16[1024,384]{1,0:T(8,128)(2,1)S(1)}, bf16[1024,384]{1,0:T(8,128)(2,1)S(1)}, u32[]{:S(2)}, u32[]{:S(2)}) %collective-permute-start.4) | collective-permute-done | bytes 786464 | tf_op jit(solution)/shard_map/ppermute | solution.py:183
  66.0 1.5 %collective-permute-done.5.refs_5_ = bf16[1024,384]{1,0:T(8,128)(2,1)S(1)} collective-permute-done((bf16[1024,384]{1,0:T(8,128)(2,1)}, bf16[1024,384]{1,0:T(8,128)(2,1)S(1)}, u32[]{:S(2)}, u32[]{:S(2)}) %collective-permute-start.5) | collective-permute-done | bytes 786464 | tf_op jit(solution)/shard_map/ppermute | solution.py:183
  67.5 0.4 collective-permute-start.10
  67.9 1.6 %collective-permute-start.9 = (bf16[1024,384]{1,0:T(8,128)(2,1)S(1)}, bf16[1024,384]{1,0:T(8,128)(2,1)S(1)}, u32[]{:S(2)}, u32[]{:S(2)}) collective-permute-start(bf16[1024,384]{1,0:T(8,128)(2,1)S(1)} %collective-permute-done.4.gate.refs_4_), channel_id=1, source_target_pairs={{0,2},{1,3},{2,6},{3,7},{6,10},{7,11},{10,14},{11,15},{14,12},{15,... | collective-permute-start | bytes 2359304 | tf_op jit(solution)/shard_map/ppermute | solution.py:183
  69.5 1.9 %lend.12 = (bf16[192,2048]{1,0:T(8,128)(2,1)S(1)}, bf16[192,2048]{1,0:T(8,128)(2,1)S(1)}) custom-call(s32[17]{0:T(128)S(1)} %dynamic-slice_bitcast_fusion.where, bf16[1024,384]{1,0:T(8,128)(2,1)S(1)} %collective-permute-done.4.gate.refs_4_, bf16[192,32768]{1,0:T(8,128)(2,1)} %rows_ref.15), custom_call_target="tpu_custom_call" | custom-call | bytes 1024 | tf_op jit(solution)/shard_map/lend/pallas_call | solution.py:61
  71.5 1.0 absorb.11
  72.6 3.8 %convert_reduce_fusion.1 = f32[192]{0:T(256)S(1)} fusion(bf16[192,32768]{1,0:T(8,128)(2,1)} %rows_ref.15), kind=kLoop, calls=%fused_computation.1 | loop fusion | flops 6291264 | bytes 6292224 | tf_op jit(solution)/shard_map/reduce_sum | solution.py:205
  76.3 9.9 %collective-permute-done.10.refs_5_ = bf16[1024,384]{1,0:T(8,128)(2,1)S(1)} collective-permute-done((bf16[1024,384]{1,0:T(8,128)(2,1)S(1)}, bf16[1024,384]{1,0:T(8,128)(2,1)S(1)}, u32[]{:S(2)}, u32[]{:S(2)}) %collective-permute-start.10) | collective-permute-done | bytes 786464 | tf_op jit(solution)/shard_map/ppermute | solution.py:183
  86.4 1.6 %collective-permute-start.12 = (bf16[1024,384]{1,0:T(8,128)(2,1)S(1)}, bf16[1024,384]{1,0:T(8,128)(2,1)S(1)}, u32[]{:S(2)}, u32[]{:S(2)}) collective-permute-start(bf16[1024,384]{1,0:T(8,128)(2,1)S(1)} %collective-permute-done.9.gate.refs_4_), channel_id=1, source_target_pairs={{0,2},{1,3},{2,6},{3,7},{6,10},{7,11},{10,14},{11,15},{14,12},{15,... | collective-permute-start | bytes 2359304 | tf_op jit(solution)/shard_map/ppermute | solution.py:183
  88.4 1.9 %lend.13 = (bf16[192,2048]{1,0:T(8,128)(2,1)S(1)}, bf16[192,2048]{1,0:T(8,128)(2,1)S(1)}) custom-call(s32[17]{0:T(128)S(1)} %dynamic-slice_bitcast_fusion.where, bf16[1024,384]{1,0:T(8,128)(2,1)S(1)} %collective-permute-done.9.gate.refs_4_, bf16[192,32768]{1,0:T(8,128)(2,1)} %rows_ref.15), custom_call_target="tpu_custom_call" | custom-call | bytes 1024 | tf_op jit(solution)/shard_map/lend/pallas_call | solution.py:61
  90.5 1.0 absorb.12
  91.5 3.8 %convert_reduce_fusion = f32[192]{0:T(256)S(1)} fusion(bf16[192,32768]{1,0:T(8,128)(2,1)} %rows_ref.15), kind=kLoop, calls=%fused_computation | loop fusion | flops 6291264 | bytes 6292224 | tf_op jit(solution)/shard_map/reduce_sum | solution.py:205
  95.3 8.8 %collective-permute-done.12.gate.refs_4_ = bf16[1024,384]{1,0:T(8,128)(2,1)S(1)} collective-permute-done((bf16[1024,384]{1,0:T(8,128)(2,1)S(1)}, bf16[1024,384]{1,0:T(8,128)(2,1)S(1)}, u32[]{:S(2)}, u32[]{:S(2)}) %collective-permute-start.12) | collective-permute-done | bytes 786464 | tf_op jit(solution)/shard_map/ppermute | solution.py:183
  104.1 1.3 collective-permute-done.13.refs_5_
  105.4 1.5 %collective-permute-start.15 = (bf16[1024,384]{1,0:T(8,128)(2,1)S(1)}, bf16[1024,384]{1,0:T(8,128)(2,1)S(1)}, u32[]{:S(2)}, u32[]{:S(2)}) collective-permute-start(bf16[1024,384]{1,0:T(8,128)(2,1)S(1)} %collective-permute-done.12.gate.refs_4_), channel_id=1, source_target_pairs={{0,2},{1,3},{2,6},{3,7},{6,10},{7,11},{10,14},{11,15},{14,12},{15,... | collective-permute-start | bytes 2359304 | tf_op jit(solution)/shard_map/ppermute | solution.py:183
  107.0 0.5 collective-permute-start.16
  107.4 1.9 %lend.14 = (bf16[192,2048]{1,0:T(8,128)(2,1)S(1)}, bf16[192,2048]{1,0:T(8,128)(2,1)S(1)}) custom-call(s32[17]{0:T(128)S(1)} %dynamic-slice_bitcast_fusion.where, bf16[1024,384]{1,0:T(8,128)(2,1)S(1)} %collective-permute-done.12.gate.refs_4_, bf16[192,32768]{1,0:T(8,128)(2,1)} %rows_ref.15), custom_call_target="tpu_custom_call" | custom-call | bytes 1024 | tf_op jit(solution)/shard_map/lend/pallas_call | solution.py:61
  109.5 1.0 absorb.13
  110.5 12.0 %collective-permute-done.15.gate.refs_4_ = bf16[1024,384]{1,0:T(8,128)(2,1)S(1)} collective-permute-done((bf16[1024,384]{1,0:T(8,128)(2,1)S(1)}, bf16[1024,384]{1,0:T(8,128)(2,1)S(1)}, u32[]{:S(2)}, u32[]{:S(2)}) %collective-permute-start.15) | collective-permute-done | bytes 786464 | tf_op jit(solution)/shard_map/ppermute | solution.py:183
  122.5 1.6 %collective-permute-done.16.refs_5_ = bf16[1024,384]{1,0:T(8,128)(2,1)S(1)} collective-permute-done((bf16[1024,384]{1,0:T(8,128)(2,1)S(1)}, bf16[1024,384]{1,0:T(8,128)(2,1)S(1)}, u32[]{:S(2)}, u32[]{:S(2)}) %collective-permute-start.16) | collective-permute-done | bytes 786464 | tf_op jit(solution)/shard_map/ppermute | solution.py:183
  124.1 0.8 collective-permute-start.19
  124.9 1.2 collective-permute-start.20
  126.1 1.9 %lend.15 = (bf16[192,2048]{1,0:T(8,128)(2,1)S(1)}, bf16[192,2048]{1,0:T(8,128)(2,1)S(1)}) custom-call(s32[17]{0:T(128)S(1)} %dynamic-slice_bitcast_fusion.where, bf16[1024,384]{1,0:T(8,128)(2,1)S(1)} %collective-permute-done.15.gate.refs_4_, bf16[192,32768]{1,0:T(8,128)(2,1)} %rows_ref.15), custom_call_target="tpu_custom_call" | custom-call | bytes 1024 | tf_op jit(solution)/shard_map/lend/pallas_call | solution.py:61
  128.1 1.0 absorb.14
  129.2 9.6 %collective-permute-done.19.refs_4_ = bf16[1024,384]{1,0:T(8,128)(2,1)S(1)} collective-permute-done((bf16[1024,384]{1,0:T(8,128)(2,1)S(1)}, bf16[1024,384]{1,0:T(8,128)(2,1)S(1)}, u32[]{:S(2)}, u32[]{:S(2)}) %collective-permute-start.19) | collective-permute-done | bytes 786464 | tf_op jit(solution)/shard_map/ppermute | solution.py:183
  138.8 1.1 collective-permute-done.20.refs_5_
  139.8 1.0 absorb.15
  141.0 1.6 %collective-permute-done.22 = f32[208,384]{1,0:T(8,128)S(1)} collective-permute-done((f32[208,384]{1,0:T(8,128)S(1)}, f32[208,384]{1,0:T(8,128)S(1)}, u32[]{:S(2)}, u32[]{:S(2)}) %collective-permute-start.22) | collective-permute-done | bytes 319520 | tf_op jit(solution)/shard_map/ppermute | solution.py:211
  142.6 0.9 fusion
  (29 shorter events, 1.5 us)
Async XLA Ops:
  2.2 20.6 %collective-permute-start = (bf16[1024,384]{1,0:T(8,128)(2,1)S(1)}, bf16[1024,384]{1,0:T(8,128)(2,1)S(1)}, u32[]{:S(2)}, u32[]{:S(2)}) collective-permute-start(bf16[1024,384]{1,0:T(8,128)(2,1)S(1)} %get-tuple-element.75.refs_4_), channel_id=1, source_target_pairs={{0,2},{1,3},{2,6},{3,7},{6,10},{7,11},{10,14},{11,15},{14,12},{15,... | collective-permute-start | bytes 2359304 | tf_op jit(solution)/shard_map/ppermute | solution.py:183
  5.2 19.1 %collective-permute-start.1 = (bf16[1024,384]{1,0:T(8,128)(2,1)S(1)}, bf16[1024,384]{1,0:T(8,128)(2,1)}, u32[]{:S(2)}, u32[]{:S(2)}) collective-permute-start(bf16[1024,384]{1,0:T(8,128)(2,1)S(1)} %get-tuple-element.76.refs_5_), channel_id=1, source_target_pairs={{0,4},{1,5},{2,0},{3,1},{6,2},{7,3},{10,6},{11,7},{14,10},{15,11},... | collective-permute-start | bytes 2359304 | tf_op jit(solution)/shard_map/ppermute | solution.py:183
  24.3 18.1 %collective-permute-start.2 = (bf16[1024,384]{1,0:T(8,128)(2,1)S(1)}, bf16[1024,384]{1,0:T(8,128)(2,1)S(1)}, u32[]{:S(2)}, u32[]{:S(2)}) collective-permute-start(bf16[1024,384]{1,0:T(8,128)(2,1)S(1)} %collective-permute-done.gate.refs_4_), channel_id=1, source_target_pairs={{0,2},{1,3},{2,6},{3,7},{6,10},{7,11},{10,14},{11,15},{14,12},{15,... | collective-permute-start | bytes 2359304 | tf_op jit(solution)/shard_map/ppermute | solution.py:183
  25.9 18.1 %collective-permute-start.3 = (bf16[1024,384]{1,0:T(8,128)(2,1)}, bf16[1024,384]{1,0:T(8,128)(2,1)}, u32[]{:S(2)}, u32[]{:S(2)}) collective-permute-start(bf16[1024,384]{1,0:T(8,128)(2,1)} %collective-permute-done.1.refs_5_), channel_id=1, source_target_pairs={{0,4},{1,5},{2,0},{3,1},{6,2},{7,3},{10,6},{11,7},{14,10},{15,11},... | collective-permute-start | bytes 2359304 | tf_op jit(solution)/shard_map/ppermute | solution.py:183
  29.0 21.1 %collective-permute-start.6 = (bf16[192,2048]{1,0:T(8,128)(2,1)S(1)}, bf16[192,2048]{1,0:T(8,128)(2,1)S(1)}, u32[]{:S(2)}, u32[]{:S(2)}) collective-permute-start(bf16[192,2048]{1,0:T(8,128)(2,1)S(1)} %get-tuple-element.68), channel_id=1, source_target_pairs={{0,1},{1,0},{2,3},{3,2},{4,5},{5,4},{6,7},{7,6},{8,9},{9,8},{10,11... | collective-permute-start | bytes 2359304 | tf_op jit(solution)/shard_map/ppermute | solution.py:193
  31.0 20.2 %collective-permute-start.7 = (bf16[192,2048]{1,0:T(8,128)(2,1)S(1)}, bf16[192,2048]{1,0:T(8,128)(2,1)S(1)}, u32[]{:S(2)}, u32[]{:S(2)}) collective-permute-start(bf16[192,2048]{1,0:T(8,128)(2,1)S(1)} %get-tuple-element.69), channel_id=1, source_target_pairs={{0,1},{1,0},{2,3},{3,2},{4,5},{5,4},{6,7},{7,6},{8,9},{9,8},{10,11... | collective-permute-start | bytes 2359304 | tf_op jit(solution)/shard_map/ppermute | solution.py:193
  45.9 7.6 %collective-permute-start.8 = (bf16[192,2048]{1,0:T(8,128)(2,1)S(1)}, bf16[192,2048]{1,0:T(8,128)(2,1)S(1)}, u32[]{:S(2)}, u32[]{:S(2)}) collective-permute-start(bf16[192,2048]{1,0:T(8,128)(2,1)S(1)} %get-tuple-element.72), channel_id=1, source_target_pairs={{0,1},{1,0},{2,3},{3,2},{4,5},{5,4},{6,7},{7,6},{8,9},{9,8},{10,11... | collective-permute-start | bytes 2359304 | tf_op jit(solution)/shard_map/ppermute | solution.py:193
  46.0 19.9 %collective-permute-start.4 = (bf16[1024,384]{1,0:T(8,128)(2,1)S(1)}, bf16[1024,384]{1,0:T(8,128)(2,1)S(1)}, u32[]{:S(2)}, u32[]{:S(2)}) collective-permute-start(bf16[1024,384]{1,0:T(8,128)(2,1)S(1)} %collective-permute-done.2.gate.refs_4_), channel_id=1, source_target_pairs={{0,2},{1,3},{2,6},{3,7},{6,10},{7,11},{10,14},{11,15},{14,12},{15,... | collective-permute-start | bytes 2359304 | tf_op jit(solution)/shard_map/ppermute | solution.py:183
  47.6 19.8 %collective-permute-start.5 = (bf16[1024,384]{1,0:T(8,128)(2,1)}, bf16[1024,384]{1,0:T(8,128)(2,1)S(1)}, u32[]{:S(2)}, u32[]{:S(2)}) collective-permute-start(bf16[1024,384]{1,0:T(8,128)(2,1)} %collective-permute-done.3.refs_5_), channel_id=1, source_target_pairs={{0,4},{1,5},{2,0},{3,1},{6,2},{7,3},{10,6},{11,7},{14,10},{15,11},... | collective-permute-start | bytes 2359304 | tf_op jit(solution)/shard_map/ppermute | solution.py:183
  50.0 21.5 %collective-permute-start.11 = (bf16[192,2048]{1,0:T(8,128)(2,1)S(1)}, bf16[192,2048]{1,0:T(8,128)(2,1)S(1)}, u32[]{:S(2)}, u32[]{:S(2)}) collective-permute-start(bf16[192,2048]{1,0:T(8,128)(2,1)S(1)} %get-tuple-element.73), channel_id=1, source_target_pairs={{0,1},{1,0},{2,3},{3,2},{4,5},{5,4},{6,7},{7,6},{8,9},{9,8},{10,11... | collective-permute-start | bytes 2359304 | tf_op jit(solution)/shard_map/ppermute | solution.py:193
  67.5 18.8 %collective-permute-start.10 = (bf16[1024,384]{1,0:T(8,128)(2,1)S(1)}, bf16[1024,384]{1,0:T(8,128)(2,1)S(1)}, u32[]{:S(2)}, u32[]{:S(2)}) collective-permute-start(bf16[1024,384]{1,0:T(8,128)(2,1)S(1)} %collective-permute-done.5.refs_5_), channel_id=1, source_target_pairs={{0,4},{1,5},{2,0},{3,1},{6,2},{7,3},{10,6},{11,7},{14,10},{15,11},... | collective-permute-start | bytes 2359304 | tf_op jit(solution)/shard_map/ppermute | solution.py:183
  67.9 18.5 %collective-permute-start.9 = (bf16[1024,384]{1,0:T(8,128)(2,1)S(1)}, bf16[1024,384]{1,0:T(8,128)(2,1)S(1)}, u32[]{:S(2)}, u32[]{:S(2)}) collective-permute-start(bf16[1024,384]{1,0:T(8,128)(2,1)S(1)} %collective-permute-done.4.gate.refs_4_), channel_id=1, source_target_pairs={{0,2},{1,3},{2,6},{3,7},{6,10},{7,11},{10,14},{11,15},{14,12},{15,... | collective-permute-start | bytes 2359304 | tf_op jit(solution)/shard_map/ppermute | solution.py:183
  71.4 19.0 %collective-permute-start.14 = (bf16[192,2048]{1,0:T(8,128)(2,1)S(1)}, bf16[192,2048]{1,0:T(8,128)(2,1)S(1)}, u32[]{:S(2)}, u32[]{:S(2)}) collective-permute-start(bf16[192,2048]{1,0:T(8,128)(2,1)S(1)} %get-tuple-element.91), channel_id=1, source_target_pairs={{0,1},{1,0},{2,3},{3,2},{4,5},{5,4},{6,7},{7,6},{8,9},{9,8},{10,11... | collective-permute-start | bytes 2359304 | tf_op jit(solution)/shard_map/ppermute | solution.py:193
  86.4 17.7 %collective-permute-start.12 = (bf16[1024,384]{1,0:T(8,128)(2,1)S(1)}, bf16[1024,384]{1,0:T(8,128)(2,1)S(1)}, u32[]{:S(2)}, u32[]{:S(2)}) collective-permute-start(bf16[1024,384]{1,0:T(8,128)(2,1)S(1)} %collective-permute-done.9.gate.refs_4_), channel_id=1, source_target_pairs={{0,2},{1,3},{2,6},{3,7},{6,10},{7,11},{10,14},{11,15},{14,12},{15,... | collective-permute-start | bytes 2359304 | tf_op jit(solution)/shard_map/ppermute | solution.py:183
  88.0 17.4 %collective-permute-start.13 = (bf16[1024,384]{1,0:T(8,128)(2,1)S(1)}, bf16[1024,384]{1,0:T(8,128)(2,1)S(1)}, u32[]{:S(2)}, u32[]{:S(2)}) collective-permute-start(bf16[1024,384]{1,0:T(8,128)(2,1)S(1)} %collective-permute-done.10.refs_5_), channel_id=1, source_target_pairs={{0,4},{1,5},{2,0},{3,1},{6,2},{7,3},{10,6},{11,7},{14,10},{15,11},... | collective-permute-start | bytes 2359304 | tf_op jit(solution)/shard_map/ppermute | solution.py:183
  90.4 19.1 %collective-permute-start.17 = (bf16[192,2048]{1,0:T(8,128)(2,1)S(1)}, bf16[192,2048]{1,0:T(8,128)(2,1)S(1)}, u32[]{:S(2)}, u32[]{:S(2)}) collective-permute-start(bf16[192,2048]{1,0:T(8,128)(2,1)S(1)} %get-tuple-element.100), channel_id=1, source_target_pairs={{0,1},{1,0},{2,3},{3,2},{4,5},{5,4},{6,7},{7,6},{8,9},{9,8},{10,11... | collective-permute-start | bytes 2359304 | tf_op jit(solution)/shard_map/ppermute | solution.py:193
  105.4 17.1 %collective-permute-start.15 = (bf16[1024,384]{1,0:T(8,128)(2,1)S(1)}, bf16[1024,384]{1,0:T(8,128)(2,1)S(1)}, u32[]{:S(2)}, u32[]{:S(2)}) collective-permute-start(bf16[1024,384]{1,0:T(8,128)(2,1)S(1)} %collective-permute-done.12.gate.refs_4_), channel_id=1, source_target_pairs={{0,2},{1,3},{2,6},{3,7},{6,10},{7,11},{10,14},{11,15},{14,12},{15,... | collective-permute-start | bytes 2359304 | tf_op jit(solution)/shard_map/ppermute | solution.py:183
  107.0 17.1 %collective-permute-start.16 = (bf16[1024,384]{1,0:T(8,128)(2,1)S(1)}, bf16[1024,384]{1,0:T(8,128)(2,1)S(1)}, u32[]{:S(2)}, u32[]{:S(2)}) collective-permute-start(bf16[1024,384]{1,0:T(8,128)(2,1)S(1)} %collective-permute-done.13.refs_5_), channel_id=1, source_target_pairs={{0,4},{1,5},{2,0},{3,1},{6,2},{7,3},{10,6},{11,7},{14,10},{15,11},... | collective-permute-start | bytes 2359304 | tf_op jit(solution)/shard_map/ppermute | solution.py:183
  109.4 18.8 %collective-permute-start.21 = (bf16[192,2048]{1,0:T(8,128)(2,1)S(1)}, bf16[192,2048]{1,0:T(8,128)(2,1)S(1)}, u32[]{:S(2)}, u32[]{:S(2)}) collective-permute-start(bf16[192,2048]{1,0:T(8,128)(2,1)S(1)} %get-tuple-element.109), channel_id=1, source_target_pairs={{0,1},{1,0},{2,3},{3,2},{4,5},{5,4},{6,7},{7,6},{8,9},{9,8},{10,11... | collective-permute-start | bytes 2359304 | tf_op jit(solution)/shard_map/ppermute | solution.py:193
  110.5 32.1 %copy-start = (bf16[192,384]{1,0:T(8,128)(2,1)S(1)}, bf16[192,384]{1,0:T(8,128)(2,1)}, u32[]{:S(2)}) copy-start(bf16[192,384]{1,0:T(8,128)(2,1)} %param.6) | copy-start | bytes 442372
  124.1 14.7 %collective-permute-start.19 = (bf16[1024,384]{1,0:T(8,128)(2,1)S(1)}, bf16[1024,384]{1,0:T(8,128)(2,1)S(1)}, u32[]{:S(2)}, u32[]{:S(2)}) collective-permute-start(bf16[1024,384]{1,0:T(8,128)(2,1)S(1)} %collective-permute-done.15.gate.refs_4_), channel_id=1, source_target_pairs={{0,2},{1,3},{2,6},{3,7},{6,10},{7,11},{10,14},{11,15},{14,12},{15,... | collective-permute-start | bytes 2359304 | tf_op jit(solution)/shard_map/ppermute | solution.py:183
  124.9 14.9 %collective-permute-start.20 = (bf16[1024,384]{1,0:T(8,128)(2,1)S(1)}, bf16[1024,384]{1,0:T(8,128)(2,1)S(1)}, u32[]{:S(2)}, u32[]{:S(2)}) collective-permute-start(bf16[1024,384]{1,0:T(8,128)(2,1)S(1)} %collective-permute-done.16.refs_5_), channel_id=1, source_target_pairs={{0,4},{1,5},{2,0},{3,1},{6,2},{7,3},{10,6},{11,7},{14,10},{15,11},... | collective-permute-start | bytes 2359304 | tf_op jit(solution)/shard_map/ppermute | solution.py:183
  128.1 11.8 %collective-permute-start.18 = (bf16[192,2048]{1,0:T(8,128)(2,1)S(1)}, bf16[192,2048]{1,0:T(8,128)(2,1)S(1)}, u32[]{:S(2)}, u32[]{:S(2)}) collective-permute-start(bf16[192,2048]{1,0:T(8,128)(2,1)S(1)} %get-tuple-element.117), channel_id=1, source_target_pairs={{0,1},{1,0},{2,3},{3,2},{4,5},{5,4},{6,7},{7,6},{8,9},{9,8},{10,11... | collective-permute-start | bytes 2359304 | tf_op jit(solution)/shard_map/ppermute | solution.py:193
  140.9 1.7 %collective-permute-start.22 = (f32[208,384]{1,0:T(8,128)S(1)}, f32[208,384]{1,0:T(8,128)S(1)}, u32[]{:S(2)}, u32[]{:S(2)}) collective-permute-start(f32[208,384]{1,0:T(8,128)S(1)} %get-tuple-element.129), channel_id=1, source_target_pairs={{0,1},{1,0},{2,3},{3,2},{4,5},{5,4},{6,7},{7,6},{8,9},{9,8},{10,11... | collective-permute-start | bytes 958472 | tf_op jit(solution)/shard_map/ppermute | solution.py:211
  141.0 2.5 %copy-start.1 = (f32[192]{0:T(256)}, f32[192]{0:T(256)S(1)}, u32[]{:S(2)}) copy-start(f32[192]{0:T(256)S(1)} %add.28) | copy-start | bytes 2308

commit v6 on v5

--- a/solution.py
+++ b/solution.py
@@ -10,7 +10,7 @@
 
 CORES = 2
 ONES = 16
-SLOTS = 1
+SLOTS = 3
 LENDS = 2
 MOST = 3
 LEND_FROM = 1
@@ -143,7 +143,7 @@
     def shards(adj_rows, adj_panel, adj_tile):
         rows = adj_rows.shape[0]
         sections, depth, width = adj_panel.shape
-        chunks = 1
+        chunks = 2 if depth % 256 == 0 else 1
         deep = depth // chunks
         table = np.array(
             [

time: 144 us -> 131 us (0.910)
  waiting for transfers between devices: 89.1 us -> 55.5 us
  starting transfers between devices: 16.5 us -> 37.4 us
    ppermute x14 -> x28, waiting for transfers between devices: 87.5 us -> 53.9 us  [shards(): lax.ppermute(held[j][s], 'row', ring(way(s)))]
    ppermute x14 -> x28, starting transfers between devices: 15.3 us -> 37 us  [shards(): lax.ppermute(held[j][s], 'row', ring(way(s)))]
    pallas_call x8 -> x16, Pallas kernels: 10.7 us -> 9.6 us  [absorb(): pl.pallas_call(functools.partial(absorb_kernel, sections, rows, first), g...]
  transfers between devices with their start and end apart: 23 -> 37, of which waited for: 15 -> 22; matrix products, arithmetic and copies ran while one was open for 6% -> 6% of each run, Pallas kernels for 18% -> 19%
where the time goes in v6:
time: 131 us
  waiting for transfers between devices  55.5 us (42%)
  starting transfers between devices  37.4 us (29%)
  Pallas kernels  26 us (20%)
  other arithmetic  8.38 us (6%)
  local copies, waits for them, and re-layouts  2.39 us (2%)
    ppermute x28, waiting for transfers between devices, shards(): lax.ppermute(held[j][s], 'row', ring(way(s)))  53.9 us
    ppermute x28, starting transfers between devices, shards(): lax.ppermute(held[j][s], 'row', ring(way(s)))  37 us
    pallas_call x8, Pallas kernels, lend(): pl.pallas_call(functools.partial(lend_kernel, step, sections, n_row, dept...  16.4 us
    pallas_call x16, Pallas kernels, absorb(): pl.pallas_call(functools.partial(absorb_kernel, sections, rows, first), g...  9.6 us
    reduce_sum x2, other arithmetic, shards(): degree.append(jnp.sum(part, axis=1, dtype=jnp.float32))  7.5 us
  transfers between devices with their start and end apart: 37, of which 22 were waited for; matrix products, arithmetic and copies ran while one was open for 6% of the time, Pallas kernels for 19%

profile of v6, /device:TPU:0, one launch (start us, length us, event | category | flops | bytes accessed | tf_op | source)
XLA Modules:
  0.0 130.8 jit_solution(8126717487025812354)
XLA Ops:
  0.6 1.5 %slice_bitcast_fusion = (bf16[512,384]{1,0:T(8,128)(2,1)S(1)}, bf16[512,384]{1,0:T(8,128)(2,1)S(1)}, bf16[512,384]{1,0:T(8,128)(2,1)S(1)}, bf16[512,384]{1,0:T(8,128)(2,1)S(1)}) fusion(bf16[2,1024,384]{2,1,0:T(8,128)(2,1)} %param.5), kind=kLoop, calls=%fused_computation.2 | loop fusion | bytes 3145728 | tf_op jit(solution)/shard_map/squeeze | solution.py:163
  2.1 3.0 %collective-permute-start = (bf16[512,384]{1,0:T(8,128)(2,1)S(1)}, bf16[512,384]{1,0:T(8,128)(2,1)S(1)}, u32[]{:S(2)}, u32[]{:S(2)}) collective-permute-start(bf16[512,384]{1,0:T(8,128)(2,1)S(1)} %get-tuple-element.133.refs_4_), channel_id=1, source_target_pairs={{0,2},{1,3},{2,6},{3,7},{6,10},{7,11},{10,14},{11,15},{14,12},{15,... | collective-permute-start | bytes 1179656 | tf_op jit(solution)/shard_map/ppermute | solution.py:183
  5.3 1.9 %collective-permute-start.6 = (bf16[512,384]{1,0:T(8,128)(2,1)S(1)}, bf16[512,384]{1,0:T(8,128)(2,1)S(1)}, u32[]{:S(2)}, u32[]{:S(2)}) collective-permute-start(bf16[512,384]{1,0:T(8,128)(2,1)S(1)} %get-tuple-element.131.refs_4_), channel_id=1, source_target_pairs={{0,2},{1,3},{2,6},{3,7},{6,10},{7,11},{10,14},{11,15},{14,12},{15,... | collective-permute-start | bytes 1179656 | tf_op jit(solution)/shard_map/ppermute | solution.py:183
  8.0 7.2 %collective-permute-done.gate.refs_4_ = bf16[512,384]{1,0:T(8,128)(2,1)S(1)} collective-permute-done((bf16[512,384]{1,0:T(8,128)(2,1)S(1)}, bf16[512,384]{1,0:T(8,128)(2,1)S(1)}, u32[]{:S(2)}, u32[]{:S(2)}) %collective-permute-start) | collective-permute-done | bytes 393248 | tf_op jit(solution)/shard_map/ppermute | solution.py:183
  15.2 2.0 %collective-permute-done.1.refs_5_ = bf16[512,384]{1,0:T(8,128)(2,1)S(1)} collective-permute-done((bf16[512,384]{1,0:T(8,128)(2,1)S(1)}, bf16[512,384]{1,0:T(8,128)(2,1)S(1)}, u32[]{:S(2)}, u32[]{:S(2)}) %collective-permute-start.1) | collective-permute-done | bytes 393248 | tf_op jit(solution)/shard_map/ppermute | solution.py:183
  17.2 1.6 %collective-permute-start.2 = (bf16[512,384]{1,0:T(8,128)(2,1)S(1)}, bf16[512,384]{1,0:T(8,128)(2,1)S(1)}, u32[]{:S(2)}, u32[]{:S(2)}) collective-permute-start(bf16[512,384]{1,0:T(8,128)(2,1)S(1)} %collective-permute-done.gate.refs_4_), channel_id=1, source_target_pairs={{0,2},{1,3},{2,6},{3,7},{6,10},{7,11},{10,14},{11,15},{14,12},{15,... | collective-permute-start | bytes 1179656 | tf_op jit(solution)/shard_map/ppermute | solution.py:183
  18.8 1.9 %lend.10 = (bf16[192,2048]{1,0:T(8,128)(2,1)S(1)}, bf16[192,2048]{1,0:T(8,128)(2,1)S(1)}) custom-call(s32[17]{0:T(128)S(1)} %dynamic-slice_bitcast_fusion.where, bf16[512,384]{1,0:T(8,128)(2,1)S(1)} %collective-permute-done.gate.refs_4_, bf16[192,32768]{1,0:T(8,128)(2,1)} %rows_ref.15), custom_call_target="tpu_custom_call" | custom-call | bytes 1024 | tf_op jit(solution)/shard_map/lend/pallas_call | solution.py:61
  21.3 2.3 %collective-permute-done.6.gate.refs_4_ = bf16[512,384]{1,0:T(8,128)(2,1)S(1)} collective-permute-done((bf16[512,384]{1,0:T(8,128)(2,1)S(1)}, bf16[512,384]{1,0:T(8,128)(2,1)S(1)}, u32[]{:S(2)}, u32[]{:S(2)}) %collective-permute-start.6) | collective-permute-done | bytes 393248 | tf_op jit(solution)/shard_map/ppermute | solution.py:183
  24.4 1.6 %collective-permute-start.11 = (bf16[512,384]{1,0:T(8,128)(2,1)S(1)}, bf16[512,384]{1,0:T(8,128)(2,1)S(1)}, u32[]{:S(2)}, u32[]{:S(2)}) collective-permute-start(bf16[512,384]{1,0:T(8,128)(2,1)S(1)} %collective-permute-done.6.gate.refs_4_), channel_id=1, source_target_pairs={{0,2},{1,3},{2,6},{3,7},{6,10},{7,11},{10,14},{11,15},{14,12},{15,... | collective-permute-start | bytes 1179656 | tf_op jit(solution)/shard_map/ppermute | solution.py:183
  26.4 2.8 %lend.9 = (bf16[192,2048]{1,0:T(8,128)(2,1)S(1)}, bf16[192,2048]{1,0:T(8,128)(2,1)}) custom-call(s32[17]{0:T(128)S(1)} %dynamic-slice_bitcast_fusion.where, bf16[512,384]{1,0:T(8,128)(2,1)S(1)} %collective-permute-done.gate.refs_4_, bf16[192,32768]{1,0:T(8,128)(2,1)} %rows_ref.15), custom_call_target="tpu_custom_call" | custom-call | bytes 1024 | tf_op jit(solution)/shard_map/lend/pallas_call | solution.py:61
  29.2 2.8 %collective-permute-done.2.refs_4_.gate = bf16[512,384]{1,0:T(8,128)(2,1)S(1)} collective-permute-done((bf16[512,384]{1,0:T(8,128)(2,1)S(1)}, bf16[512,384]{1,0:T(8,128)(2,1)S(1)}, u32[]{:S(2)}, u32[]{:S(2)}) %collective-permute-start.2) | collective-permute-done | bytes 393248 | tf_op jit(solution)/shard_map/ppermute | solution.py:183
  32.8 1.6 %collective-permute-start.4 = (bf16[512,384]{1,0:T(8,128)(2,1)S(1)}, bf16[512,384]{1,0:T(8,128)(2,1)S(1)}, u32[]{:S(2)}, u32[]{:S(2)}) collective-permute-start(bf16[512,384]{1,0:T(8,128)(2,1)S(1)} %collective-permute-done.2.refs_4_.gate), channel_id=1, source_target_pairs={{0,2},{1,3},{2,6},{3,7},{6,10},{7,11},{10,14},{11,15},{14,12},{15,... | collective-permute-start | bytes 1179656 | tf_op jit(solution)/shard_map/ppermute | solution.py:183
  34.4 6.0 %collective-permute-done.11.refs_4_ = bf16[512,384]{1,0:T(8,128)(2,1)S(1)} collective-permute-done((bf16[512,384]{1,0:T(8,128)(2,1)S(1)}, bf16[512,384]{1,0:T(8,128)(2,1)S(1)}, u32[]{:S(2)}, u32[]{:S(2)}) %collective-permute-start.11) | collective-permute-done | bytes 393248 | tf_op jit(solution)/shard_map/ppermute | solution.py:183
  40.4 2.1 %collective-permute-start.5 = (bf16[512,384]{1,0:T(8,128)(2,1)S(1)}, bf16[512,384]{1,0:T(8,128)(2,1)S(1)}, u32[]{:S(2)}, u32[]{:S(2)}) collective-permute-start(bf16[512,384]{1,0:T(8,128)(2,1)S(1)} %collective-permute-done.3.refs_5_), channel_id=1, source_target_pairs={{0,4},{1,5},{2,0},{3,1},{6,2},{7,3},{10,6},{11,7},{14,10},{15,11},... | collective-permute-start | bytes 1179656 | tf_op jit(solution)/shard_map/ppermute | solution.py:183
  42.5 1.9 %lend.8 = (bf16[192,2048]{1,0:T(8,128)(2,1)S(1)}, bf16[192,2048]{1,0:T(8,128)(2,1)S(1)}) custom-call(s32[17]{0:T(128)S(1)} %dynamic-slice_bitcast_fusion.where, bf16[512,384]{1,0:T(8,128)(2,1)S(1)} %collective-permute-done.6.gate.refs_4_, bf16[192,32768]{1,0:T(8,128)(2,1)} %rows_ref.15), custom_call_target="tpu_custom_call" | custom-call | bytes 1024 | tf_op jit(solution)/shard_map/lend/pallas_call | solution.py:61
  44.6 1.9 %lend.11 = (bf16[192,2048]{1,0:T(8,128)(2,1)S(1)}, bf16[192,2048]{1,0:T(8,128)(2,1)S(1)}) custom-call(s32[17]{0:T(128)S(1)} %dynamic-slice_bitcast_fusion.where, bf16[512,384]{1,0:T(8,128)(2,1)S(1)} %collective-permute-done.2.refs_4_.gate, bf16[192,32768]{1,0:T(8,128)(2,1)} %rows_ref.15), custom_call_target="tpu_custom_call" | custom-call | bytes 1024 | tf_op jit(solution)/shard_map/lend/pallas_call | solution.py:61
  46.6 1.8 %collective-permute-done.4.refs_4_.gate = bf16[512,384]{1,0:T(8,128)(2,1)S(1)} collective-permute-done((bf16[512,384]{1,0:T(8,128)(2,1)S(1)}, bf16[512,384]{1,0:T(8,128)(2,1)S(1)}, u32[]{:S(2)}, u32[]{:S(2)}) %collective-permute-start.4) | collective-permute-done | bytes 393248 | tf_op jit(solution)/shard_map/ppermute | solution.py:183
  48.4 1.9 %collective-permute-start.19 = (bf16[512,384]{1,0:T(8,128)(2,1)S(1)}, bf16[512,384]{1,0:T(8,128)(2,1)S(1)}, u32[]{:S(2)}, u32[]{:S(2)}) collective-permute-start(bf16[512,384]{1,0:T(8,128)(2,1)S(1)} %collective-permute-done.12.refs_5_), channel_id=1, source_target_pairs={{0,4},{1,5},{2,0},{3,1},{6,2},{7,3},{10,6},{11,7},{14,10},{15,11},... | collective-permute-start | bytes 1179656 | tf_op jit(solution)/shard_map/ppermute | solution.py:183
  51.6 1.0 collective-permute-start.8
  52.7 4.1 %collective-permute-done.18.refs_4_ = bf16[512,384]{1,0:T(8,128)(2,1)S(1)} collective-permute-done((bf16[512,384]{1,0:T(8,128)(2,1)S(1)}, bf16[512,384]{1,0:T(8,128)(2,1)S(1)}, u32[]{:S(2)}, u32[]{:S(2)}) %collective-permute-start.18) | collective-permute-done | bytes 393248 | tf_op jit(solution)/shard_map/ppermute | solution.py:183
  56.8 1.9 %collective-permute-start.9 = (bf16[512,384]{1,0:T(8,128)(2,1)S(1)}, bf16[512,384]{1,0:T(8,128)(2,1)S(1)}, u32[]{:S(2)}, u32[]{:S(2)}) collective-permute-start(bf16[512,384]{1,0:T(8,128)(2,1)S(1)} %collective-permute-done.5.refs_5_), channel_id=1, source_target_pairs={{0,4},{1,5},{2,0},{3,1},{6,2},{7,3},{10,6},{11,7},{14,10},{15,11},... | collective-permute-start | bytes 1179656 | tf_op jit(solution)/shard_map/ppermute | solution.py:183
  60.0 1.9 %lend.12 = (bf16[192,2048]{1,0:T(8,128)(2,1)S(1)}, bf16[192,2048]{1,0:T(8,128)(2,1)S(1)}) custom-call(s32[17]{0:T(128)S(1)} %dynamic-slice_bitcast_fusion.where, bf16[512,384]{1,0:T(8,128)(2,1)S(1)} %collective-permute-done.4.refs_4_.gate, bf16[192,32768]{1,0:T(8,128)(2,1)} %rows_ref.15), custom_call_target="tpu_custom_call" | custom-call | bytes 1024 | tf_op jit(solution)/shard_map/lend/pallas_call | solution.py:61
  64.0 1.3 collective-permute-done.8.refs_4_.gate
  65.2 1.9 %collective-permute-start.24 = (bf16[512,384]{1,0:T(8,128)(2,1)S(1)}, bf16[512,384]{1,0:T(8,128)(2,1)S(1)}, u32[]{:S(2)}, u32[]{:S(2)}) collective-permute-start(bf16[512,384]{1,0:T(8,128)(2,1)S(1)} %collective-permute-done.19.refs_5_), channel_id=1, source_target_pairs={{0,4},{1,5},{2,0},{3,1},{6,2},{7,3},{10,6},{11,7},{14,10},{15,11},... | collective-permute-start | bytes 1179656 | tf_op jit(solution)/shard_map/ppermute | solution.py:183
  67.3 0.9 collective-permute-start.15
  68.2 1.9 %lend.14 = (bf16[192,2048]{1,0:T(8,128)(2,1)S(1)}, bf16[192,2048]{1,0:T(8,128)(2,1)S(1)}) custom-call(s32[17]{0:T(128)S(1)} %dynamic-slice_bitcast_fusion.where, bf16[512,384]{1,0:T(8,128)(2,1)S(1)} %collective-permute-done.8.refs_4_.gate, bf16[192,32768]{1,0:T(8,128)(2,1)} %rows_ref.15), custom_call_target="tpu_custom_call" | custom-call | bytes 1024 | tf_op jit(solution)/shard_map/lend/pallas_call | solution.py:61
  70.1 1.2 collective-permute-start.16
  71.3 2.4 %collective-permute-done.23.refs_4_ = bf16[512,384]{1,0:T(8,128)(2,1)S(1)} collective-permute-done((bf16[512,384]{1,0:T(8,128)(2,1)S(1)}, bf16[512,384]{1,0:T(8,128)(2,1)S(1)}, u32[]{:S(2)}, u32[]{:S(2)}) %collective-permute-start.23) | collective-permute-done | bytes 393248 | tf_op jit(solution)/shard_map/ppermute | solution.py:183
  73.7 3.7 %convert_reduce_fusion.1 = f32[192]{0:T(256)S(1)} fusion(bf16[192,32768]{1,0:T(8,128)(2,1)} %rows_ref.15), kind=kLoop, calls=%fused_computation.1 | loop fusion | flops 6291264 | bytes 6292224 | tf_op jit(solution)/shard_map/reduce_sum | solution.py:205
  78.0 2.5 %collective-permute-start.26 = (bf16[512,384]{1,0:T(8,128)(2,1)S(1)}, bf16[512,384]{1,0:T(8,128)(2,1)S(1)}, u32[]{:S(2)}, u32[]{:S(2)}) collective-permute-start(bf16[512,384]{1,0:T(8,128)(2,1)S(1)} %collective-permute-done.23.refs_4_), channel_id=1, source_target_pairs={{0,2},{1,3},{2,6},{3,7},{6,10},{7,11},{10,14},{11,15},{14,12},{15,... | collective-permute-start | bytes 1179656 | tf_op jit(solution)/shard_map/ppermute | solution.py:183
  82.1 1.7 %collective-permute-start.27 = (bf16[512,384]{1,0:T(8,128)(2,1)S(1)}, bf16[512,384]{1,0:T(8,128)(2,1)S(1)}, u32[]{:S(2)}, u32[]{:S(2)}) collective-permute-start(bf16[512,384]{1,0:T(8,128)(2,1)S(1)} %collective-permute-done.24.refs_5_), channel_id=1, source_target_pairs={{0,4},{1,5},{2,0},{3,1},{6,2},{7,3},{10,6},{11,7},{14,10},{15,11},... | collective-permute-start | bytes 1179656 | tf_op jit(solution)/shard_map/ppermute | solution.py:183
  84.3 1.9 %collective-permute-start.20 = (bf16[512,384]{1,0:T(8,128)(2,1)S(1)}, bf16[512,384]{1,0:T(8,128)(2,1)S(1)}, u32[]{:S(2)}, u32[]{:S(2)}) collective-permute-start(bf16[512,384]{1,0:T(8,128)(2,1)S(1)} %collective-permute-done.15.gate.refs_4_), channel_id=1, source_target_pairs={{0,2},{1,3},{2,6},{3,7},{6,10},{7,11},{10,14},{11,15},{14,12},{15,... | collective-permute-start | bytes 1179656 | tf_op jit(solution)/shard_map/ppermute | solution.py:183
  86.3 3.7 %convert_reduce_fusion = f32[192]{0:T(256)S(1)} fusion(bf16[192,32768]{1,0:T(8,128)(2,1)} %rows_ref.15), kind=kLoop, calls=%fused_computation | loop fusion | flops 6291264 | bytes 6292224 | tf_op jit(solution)/shard_map/reduce_sum | solution.py:205
  90.1 1.9 %lend.15 = (bf16[192,2048]{1,0:T(8,128)(2,1)S(1)}, bf16[192,2048]{1,0:T(8,128)(2,1)S(1)}) custom-call(s32[17]{0:T(128)S(1)} %dynamic-slice_bitcast_fusion.where, bf16[512,384]{1,0:T(8,128)(2,1)S(1)} %collective-permute-done.15.gate.refs_4_, bf16[192,32768]{1,0:T(8,128)(2,1)} %rows_ref.15), custom_call_target="tpu_custom_call" | custom-call | bytes 1024 | tf_op jit(solution)/shard_map/lend/pallas_call | solution.py:61
  92.7 1.5 %collective-permute-done.27.refs_5_ = bf16[512,384]{1,0:T(8,128)(2,1)S(1)} collective-permute-done((bf16[512,384]{1,0:T(8,128)(2,1)S(1)}, bf16[512,384]{1,0:T(8,128)(2,1)S(1)}, u32[]{:S(2)}, u32[]{:S(2)}) %collective-permute-start.27) | collective-permute-done | bytes 393248 | tf_op jit(solution)/shard_map/ppermute | solution.py:183
  94.1 1.3 %collective-permute-start.28 = (bf16[512,384]{1,0:T(8,128)(2,1)S(1)}, bf16[512,384]{1,0:T(8,128)(2,1)S(1)}, u32[]{:S(2)}, u32[]{:S(2)}) collective-permute-start(bf16[512,384]{1,0:T(8,128)(2,1)S(1)} %collective-permute-done.26.refs_4_), channel_id=1, source_target_pairs={{0,2},{1,3},{2,6},{3,7},{6,10},{7,11},{10,14},{11,15},{14,12},{15,... | collective-permute-start | bytes 1179656 | tf_op jit(solution)/shard_map/ppermute | solution.py:183
  96.8 2.2 %collective-permute-done.20.gate.refs_4_ = bf16[512,384]{1,0:T(8,128)(2,1)S(1)} collective-permute-done((bf16[512,384]{1,0:T(8,128)(2,1)S(1)}, bf16[512,384]{1,0:T(8,128)(2,1)S(1)}, u32[]{:S(2)}, u32[]{:S(2)}) %collective-permute-start.20) | collective-permute-done | bytes 393248 | tf_op jit(solution)/shard_map/ppermute | solution.py:183
  99.0 3.6 %collective-permute-done.21.refs_5_ = bf16[512,384]{1,0:T(8,128)(2,1)S(1)} collective-permute-done((bf16[512,384]{1,0:T(8,128)(2,1)S(1)}, bf16[512,384]{1,0:T(8,128)(2,1)S(1)}, u32[]{:S(2)}, u32[]{:S(2)}) %collective-permute-start.21) | collective-permute-done | bytes 393248 | tf_op jit(solution)/shard_map/ppermute | solution.py:183
  102.6 1.3 %collective-permute-start.34 = (bf16[512,384]{1,0:T(8,128)(2,1)S(1)}, bf16[512,384]{1,0:T(8,128)(2,1)S(1)}, u32[]{:S(2)}, u32[]{:S(2)}) collective-permute-start(bf16[512,384]{1,0:T(8,128)(2,1)S(1)} %collective-permute-done.20.gate.refs_4_), channel_id=1, source_target_pairs={{0,2},{1,3},{2,6},{3,7},{6,10},{7,11},{10,14},{11,15},{14,12},{15,... | collective-permute-start | bytes 1179656 | tf_op jit(solution)/shard_map/ppermute | solution.py:183
  103.9 1.9 %lend.13 = (bf16[192,2048]{1,0:T(8,128)(2,1)S(1)}, bf16[192,2048]{1,0:T(8,128)(2,1)S(1)}) custom-call(s32[17]{0:T(128)S(1)} %dynamic-slice_bitcast_fusion.where, bf16[512,384]{1,0:T(8,128)(2,1)S(1)} %collective-permute-done.20.gate.refs_4_, bf16[192,32768]{1,0:T(8,128)(2,1)} %rows_ref.15), custom_call_target="tpu_custom_call" | custom-call | bytes 1024 | tf_op jit(solution)/shard_map/lend/pallas_call | solution.py:61
  105.9 1.4 %collective-permute-done.28.refs_4_ = bf16[512,384]{1,0:T(8,128)(2,1)S(1)} collective-permute-done((bf16[512,384]{1,0:T(8,128)(2,1)S(1)}, bf16[512,384]{1,0:T(8,128)(2,1)S(1)}, u32[]{:S(2)}, u32[]{:S(2)}) %collective-permute-start.28) | collective-permute-done | bytes 393248 | tf_op jit(solution)/shard_map/ppermute | solution.py:183
  107.4 1.7 %collective-permute-start.35 = (bf16[512,384]{1,0:T(8,128)(2,1)S(1)}, bf16[512,384]{1,0:T(8,128)(2,1)S(1)}, u32[]{:S(2)}, u32[]{:S(2)}) collective-permute-start(bf16[512,384]{1,0:T(8,128)(2,1)S(1)} %collective-permute-done.21.refs_5_), channel_id=1, source_target_pairs={{0,4},{1,5},{2,0},{3,1},{6,2},{7,3},{10,6},{11,7},{14,10},{15,11},... | collective-permute-start | bytes 1179656 | tf_op jit(solution)/shard_map/ppermute | solution.py:183
  109.7 1.6 %collective-permute-start.31 = (bf16[512,384]{1,0:T(8,128)(2,1)S(1)}, bf16[512,384]{1,0:T(8,128)(2,1)S(1)}, u32[]{:S(2)}, u32[]{:S(2)}) collective-permute-start(bf16[512,384]{1,0:T(8,128)(2,1)S(1)} %collective-permute-done.28.refs_4_), channel_id=1, source_target_pairs={{0,2},{1,3},{2,6},{3,7},{6,10},{7,11},{10,14},{11,15},{14,12},{15,... | collective-permute-start | bytes 1179656 | tf_op jit(solution)/shard_map/ppermute | solution.py:183
  111.3 4.5 %collective-permute-done.34.refs_4_ = bf16[512,384]{1,0:T(8,128)(2,1)S(1)} collective-permute-done((bf16[512,384]{1,0:T(8,128)(2,1)S(1)}, bf16[512,384]{1,0:T(8,128)(2,1)S(1)}, u32[]{:S(2)}, u32[]{:S(2)}) %collective-permute-start.34) | collective-permute-done | bytes 393248 | tf_op jit(solution)/shard_map/ppermute | solution.py:183
  115.8 1.7 %collective-permute-start.32 = (bf16[512,384]{1,0:T(8,128)(2,1)S(1)}, bf16[512,384]{1,0:T(8,128)(2,1)S(1)}, u32[]{:S(2)}, u32[]{:S(2)}) collective-permute-start(bf16[512,384]{1,0:T(8,128)(2,1)S(1)} %collective-permute-done.29.refs_5_), channel_id=1, source_target_pairs={{0,4},{1,5},{2,0},{3,1},{6,2},{7,3},{10,6},{11,7},{14,10},{15,11},... | collective-permute-start | bytes 1179656 | tf_op jit(solution)/shard_map/ppermute | solution.py:183
  118.8 5.1 %collective-permute-done.31.refs_4_ = bf16[512,384]{1,0:T(8,128)(2,1)S(1)} collective-permute-done((bf16[512,384]{1,0:T(8,128)(2,1)S(1)}, bf16[512,384]{1,0:T(8,128)(2,1)S(1)}, u32[]{:S(2)}, u32[]{:S(2)}) %collective-permute-start.31) | collective-permute-done | bytes 393248 | tf_op jit(solution)/shard_map/ppermute | solution.py:183
  123.9 2.5 %collective-permute-done.32.refs_5_ = bf16[512,384]{1,0:T(8,128)(2,1)S(1)} collective-permute-done((bf16[512,384]{1,0:T(8,128)(2,1)S(1)}, bf16[512,384]{1,0:T(8,128)(2,1)S(1)}, u32[]{:S(2)}, u32[]{:S(2)}) %collective-permute-start.32) | collective-permute-done | bytes 393248 | tf_op jit(solution)/shard_map/ppermute | solution.py:183
  128.3 1.6 %collective-permute-done.36 = f32[208,384]{1,0:T(8,128)S(1)} collective-permute-done((f32[208,384]{1,0:T(8,128)S(1)}, f32[208,384]{1,0:T(8,128)S(1)}, u32[]{:S(2)}, u32[]{:S(2)}) %collective-permute-start.36) | collective-permute-done | bytes 319520 | tf_op jit(solution)/shard_map/ppermute | solution.py:211
  (69 shorter events, 17.6 us)
Async XLA Ops:
  2.1 13.0 %collective-permute-start = (bf16[512,384]{1,0:T(8,128)(2,1)S(1)}, bf16[512,384]{1,0:T(8,128)(2,1)S(1)}, u32[]{:S(2)}, u32[]{:S(2)}) collective-permute-start(bf16[512,384]{1,0:T(8,128)(2,1)S(1)} %get-tuple-element.133.refs_4_), channel_id=1, source_target_pairs={{0,2},{1,3},{2,6},{3,7},{6,10},{7,11},{10,14},{11,15},{14,12},{15,... | collective-permute-start | bytes 1179656 | tf_op jit(solution)/shard_map/ppermute | solution.py:183
  5.2 12.0 %collective-permute-start.1 = (bf16[512,384]{1,0:T(8,128)(2,1)S(1)}, bf16[512,384]{1,0:T(8,128)(2,1)S(1)}, u32[]{:S(2)}, u32[]{:S(2)}) collective-permute-start(bf16[512,384]{1,0:T(8,128)(2,1)S(1)} %get-tuple-element.134.refs_5_), channel_id=1, source_target_pairs={{0,4},{1,5},{2,0},{3,1},{6,2},{7,3},{10,6},{11,7},{14,10},{15,11},... | collective-permute-start | bytes 1179656 | tf_op jit(solution)/shard_map/ppermute | solution.py:183
  5.3 18.3 %collective-permute-start.6 = (bf16[512,384]{1,0:T(8,128)(2,1)S(1)}, bf16[512,384]{1,0:T(8,128)(2,1)S(1)}, u32[]{:S(2)}, u32[]{:S(2)}) collective-permute-start(bf16[512,384]{1,0:T(8,128)(2,1)S(1)} %get-tuple-element.131.refs_4_), channel_id=1, source_target_pairs={{0,2},{1,3},{2,6},{3,7},{6,10},{7,11},{10,14},{11,15},{14,12},{15,... | collective-permute-start | bytes 1179656 | tf_op jit(solution)/shard_map/ppermute | solution.py:183
  7.2 17.2 %collective-permute-start.7 = (bf16[512,384]{1,0:T(8,128)(2,1)S(1)}, bf16[512,384]{1,0:T(8,128)(2,1)S(1)}, u32[]{:S(2)}, u32[]{:S(2)}) collective-permute-start(bf16[512,384]{1,0:T(8,128)(2,1)S(1)} %get-tuple-element.132.refs_5_), channel_id=1, source_target_pairs={{0,4},{1,5},{2,0},{3,1},{6,2},{7,3},{10,6},{11,7},{14,10},{15,11},... | collective-permute-start | bytes 1179656 | tf_op jit(solution)/shard_map/ppermute | solution.py:183
  17.2 14.8 %collective-permute-start.2 = (bf16[512,384]{1,0:T(8,128)(2,1)S(1)}, bf16[512,384]{1,0:T(8,128)(2,1)S(1)}, u32[]{:S(2)}, u32[]{:S(2)}) collective-permute-start(bf16[512,384]{1,0:T(8,128)(2,1)S(1)} %collective-permute-done.gate.refs_4_), channel_id=1, source_target_pairs={{0,2},{1,3},{2,6},{3,7},{6,10},{7,11},{10,14},{11,15},{14,12},{15,... | collective-permute-start | bytes 1179656 | tf_op jit(solution)/shard_map/ppermute | solution.py:183
  20.7 23.8 %collective-permute-start.13 = (bf16[192,2048]{1,0:T(8,128)(2,1)S(1)}, bf16[192,2048]{1,0:T(8,128)(2,1)S(1)}, u32[]{:S(2)}, u32[]{:S(2)}) collective-permute-start(bf16[192,2048]{1,0:T(8,128)(2,1)S(1)} %get-tuple-element.123), channel_id=1, source_target_pairs={{0,1},{1,0},{2,3},{3,2},{4,5},{5,4},{6,7},{7,6},{8,9},{9,8},{10,11... | collective-permute-start | bytes 2359304 | tf_op jit(solution)/shard_map/ppermute | solution.py:193
  20.8 12.0 %collective-permute-start.3 = (bf16[512,384]{1,0:T(8,128)(2,1)S(1)}, bf16[512,384]{1,0:T(8,128)(2,1)S(1)}, u32[]{:S(2)}, u32[]{:S(2)}) collective-permute-start(bf16[512,384]{1,0:T(8,128)(2,1)S(1)} %collective-permute-done.1.refs_5_), channel_id=1, source_target_pairs={{0,4},{1,5},{2,0},{3,1},{6,2},{7,3},{10,6},{11,7},{14,10},{15,11},... | collective-permute-start | bytes 1179656 | tf_op jit(solution)/shard_map/ppermute | solution.py:183
  24.4 16.1 %collective-permute-start.11 = (bf16[512,384]{1,0:T(8,128)(2,1)S(1)}, bf16[512,384]{1,0:T(8,128)(2,1)S(1)}, u32[]{:S(2)}, u32[]{:S(2)}) collective-permute-start(bf16[512,384]{1,0:T(8,128)(2,1)S(1)} %collective-permute-done.6.gate.refs_4_), channel_id=1, source_target_pairs={{0,2},{1,3},{2,6},{3,7},{6,10},{7,11},{10,14},{11,15},{14,12},{15,... | collective-permute-start | bytes 1179656 | tf_op jit(solution)/shard_map/ppermute | solution.py:183
  25.9 18.5 %collective-permute-start.12 = (bf16[512,384]{1,0:T(8,128)(2,1)S(1)}, bf16[512,384]{1,0:T(8,128)(2,1)S(1)}, u32[]{:S(2)}, u32[]{:S(2)}) collective-permute-start(bf16[512,384]{1,0:T(8,128)(2,1)S(1)} %collective-permute-done.7.refs_5_), channel_id=1, source_target_pairs={{0,4},{1,5},{2,0},{3,1},{6,2},{7,3},{10,6},{11,7},{14,10},{15,11},... | collective-permute-start | bytes 1179656 | tf_op jit(solution)/shard_map/ppermute | solution.py:183
  32.0 19.6 %collective-permute-start.10 = (bf16[192,2048]{1,0:T(8,128)(2,1)}, bf16[192,2048]{1,0:T(8,128)(2,1)S(1)}, u32[]{:S(2)}, u32[]{:S(2)}) collective-permute-start(bf16[192,2048]{1,0:T(8,128)(2,1)} %get-tuple-element.121), channel_id=1, source_target_pairs={{0,1},{1,0},{2,3},{3,2},{4,5},{5,4},{6,7},{7,6},{8,9},{9,8},{10,11... | collective-permute-start | bytes 2359304 | tf_op jit(solution)/shard_map/ppermute | solution.py:193
  32.8 15.5 %collective-permute-start.4 = (bf16[512,384]{1,0:T(8,128)(2,1)S(1)}, bf16[512,384]{1,0:T(8,128)(2,1)S(1)}, u32[]{:S(2)}, u32[]{:S(2)}) collective-permute-start(bf16[512,384]{1,0:T(8,128)(2,1)S(1)} %collective-permute-done.2.refs_4_.gate), channel_id=1, source_target_pairs={{0,2},{1,3},{2,6},{3,7},{6,10},{7,11},{10,14},{11,15},{14,12},{15,... | collective-permute-start | bytes 1179656 | tf_op jit(solution)/shard_map/ppermute | solution.py:183
  40.4 9.8 %collective-permute-start.5 = (bf16[512,384]{1,0:T(8,128)(2,1)S(1)}, bf16[512,384]{1,0:T(8,128)(2,1)S(1)}, u32[]{:S(2)}, u32[]{:S(2)}) collective-permute-start(bf16[512,384]{1,0:T(8,128)(2,1)S(1)} %collective-permute-done.3.refs_5_), channel_id=1, source_target_pairs={{0,4},{1,5},{2,0},{3,1},{6,2},{7,3},{10,6},{11,7},{14,10},{15,11},... | collective-permute-start | bytes 1179656 | tf_op jit(solution)/shard_map/ppermute | solution.py:183
  44.5 17.5 %collective-permute-start.14 = (bf16[192,2048]{1,0:T(8,128)(2,1)S(1)}, bf16[192,2048]{1,0:T(8,128)(2,1)S(1)}, u32[]{:S(2)}, u32[]{:S(2)}) collective-permute-start(bf16[192,2048]{1,0:T(8,128)(2,1)S(1)} %get-tuple-element.117), channel_id=1, source_target_pairs={{0,1},{1,0},{2,3},{3,2},{4,5},{5,4},{6,7},{7,6},{8,9},{9,8},{10,11... | collective-permute-start | bytes 2359304 | tf_op jit(solution)/shard_map/ppermute | solution.py:193
  44.5 12.3 %collective-permute-start.18 = (bf16[512,384]{1,0:T(8,128)(2,1)S(1)}, bf16[512,384]{1,0:T(8,128)(2,1)S(1)}, u32[]{:S(2)}, u32[]{:S(2)}) collective-permute-start(bf16[512,384]{1,0:T(8,128)(2,1)S(1)} %collective-permute-done.11.refs_4_), channel_id=1, source_target_pairs={{0,2},{1,3},{2,6},{3,7},{6,10},{7,11},{10,14},{11,15},{14,12},{15,... | collective-permute-start | bytes 1179656 | tf_op jit(solution)/shard_map/ppermute | solution.py:183
  48.4 10.9 %collective-permute-start.19 = (bf16[512,384]{1,0:T(8,128)(2,1)S(1)}, bf16[512,384]{1,0:T(8,128)(2,1)S(1)}, u32[]{:S(2)}, u32[]{:S(2)}) collective-permute-start(bf16[512,384]{1,0:T(8,128)(2,1)S(1)} %collective-permute-done.12.refs_5_), channel_id=1, source_target_pairs={{0,4},{1,5},{2,0},{3,1},{6,2},{7,3},{10,6},{11,7},{14,10},{15,11},... | collective-permute-start | bytes 1179656 | tf_op jit(solution)/shard_map/ppermute | solution.py:183
  50.3 19.8 %collective-permute-start.17 = (bf16[192,2048]{1,0:T(8,128)(2,1)S(1)}, bf16[192,2048]{1,0:T(8,128)(2,1)S(1)}, u32[]{:S(2)}, u32[]{:S(2)}) collective-permute-start(bf16[192,2048]{1,0:T(8,128)(2,1)S(1)} %get-tuple-element.155), channel_id=1, source_target_pairs={{0,1},{1,0},{2,3},{3,2},{4,5},{5,4},{6,7},{7,6},{8,9},{9,8},{10,11... | collective-permute-start | bytes 2359304 | tf_op jit(solution)/shard_map/ppermute | solution.py:193
  51.6 13.6 %collective-permute-start.8 = (bf16[512,384]{1,0:T(8,128)(2,1)S(1)}, bf16[512,384]{1,0:T(8,128)(2,1)S(1)}, u32[]{:S(2)}, u32[]{:S(2)}) collective-permute-start(bf16[512,384]{1,0:T(8,128)(2,1)S(1)} %collective-permute-done.4.refs_4_.gate), channel_id=1, source_target_pairs={{0,2},{1,3},{2,6},{3,7},{6,10},{7,11},{10,14},{11,15},{14,12},{15,... | collective-permute-start | bytes 1179656 | tf_op jit(solution)/shard_map/ppermute | solution.py:183
  56.8 10.4 %collective-permute-start.9 = (bf16[512,384]{1,0:T(8,128)(2,1)S(1)}, bf16[512,384]{1,0:T(8,128)(2,1)S(1)}, u32[]{:S(2)}, u32[]{:S(2)}) collective-permute-start(bf16[512,384]{1,0:T(8,128)(2,1)S(1)} %collective-permute-done.5.refs_5_), channel_id=1, source_target_pairs={{0,4},{1,5},{2,0},{3,1},{6,2},{7,3},{10,6},{11,7},{14,10},{15,11},... | collective-permute-start | bytes 1179656 | tf_op jit(solution)/shard_map/ppermute | solution.py:183
  59.3 14.3 %collective-permute-start.23 = (bf16[512,384]{1,0:T(8,128)(2,1)S(1)}, bf16[512,384]{1,0:T(8,128)(2,1)S(1)}, u32[]{:S(2)}, u32[]{:S(2)}) collective-permute-start(bf16[512,384]{1,0:T(8,128)(2,1)S(1)} %collective-permute-done.18.refs_4_), channel_id=1, source_target_pairs={{0,2},{1,3},{2,6},{3,7},{6,10},{7,11},{10,14},{11,15},{14,12},{15,... | collective-permute-start | bytes 1179656 | tf_op jit(solution)/shard_map/ppermute | solution.py:183
  61.9 24.3 %collective-permute-start.22 = (bf16[192,2048]{1,0:T(8,128)(2,1)S(1)}, bf16[192,2048]{1,0:T(8,128)(2,1)S(1)}, u32[]{:S(2)}, u32[]{:S(2)}) collective-permute-start(bf16[192,2048]{1,0:T(8,128)(2,1)S(1)} %get-tuple-element.169), channel_id=1, source_target_pairs={{0,1},{1,0},{2,3},{3,2},{4,5},{5,4},{6,7},{7,6},{8,9},{9,8},{10,11... | collective-permute-start | bytes 2359304 | tf_op jit(solution)/shard_map/ppermute | solution.py:193
  65.2 12.8 %collective-permute-start.24 = (bf16[512,384]{1,0:T(8,128)(2,1)S(1)}, bf16[512,384]{1,0:T(8,128)(2,1)S(1)}, u32[]{:S(2)}, u32[]{:S(2)}) collective-permute-start(bf16[512,384]{1,0:T(8,128)(2,1)S(1)} %collective-permute-done.19.refs_5_), channel_id=1, source_target_pairs={{0,4},{1,5},{2,0},{3,1},{6,2},{7,3},{10,6},{11,7},{14,10},{15,11},... | collective-permute-start | bytes 1179656 | tf_op jit(solution)/shard_map/ppermute | solution.py:183
  67.3 14.8 %collective-permute-start.15 = (bf16[512,384]{1,0:T(8,128)(2,1)S(1)}, bf16[512,384]{1,0:T(8,128)(2,1)S(1)}, u32[]{:S(2)}, u32[]{:S(2)}) collective-permute-start(bf16[512,384]{1,0:T(8,128)(2,1)S(1)} %collective-permute-done.8.refs_4_.gate), channel_id=1, source_target_pairs={{0,2},{1,3},{2,6},{3,7},{6,10},{7,11},{10,14},{11,15},{14,12},{15,... | collective-permute-start | bytes 1179656 | tf_op jit(solution)/shard_map/ppermute | solution.py:183
  70.1 14.2 %collective-permute-start.16 = (bf16[512,384]{1,0:T(8,128)(2,1)S(1)}, bf16[512,384]{1,0:T(8,128)(2,1)S(1)}, u32[]{:S(2)}, u32[]{:S(2)}) collective-permute-start(bf16[512,384]{1,0:T(8,128)(2,1)S(1)} %collective-permute-done.9.refs_5_), channel_id=1, source_target_pairs={{0,4},{1,5},{2,0},{3,1},{6,2},{7,3},{10,6},{11,7},{14,10},{15,11},... | collective-permute-start | bytes 1179656 | tf_op jit(solution)/shard_map/ppermute | solution.py:183
  73.7 32.2 %collective-permute-start.30 = (bf16[192,2048]{1,0:T(8,128)(2,1)S(1)}, bf16[192,2048]{1,0:T(8,128)(2,1)S(1)}, u32[]{:S(2)}, u32[]{:S(2)}) collective-permute-start(bf16[192,2048]{1,0:T(8,128)(2,1)S(1)} %get-tuple-element.184), channel_id=1, source_target_pairs={{0,1},{1,0},{2,3},{3,2},{4,5},{5,4},{6,7},{7,6},{8,9},{9,8},{10,11... | collective-permute-start | bytes 2359304 | tf_op jit(solution)/shard_map/ppermute | solution.py:193
  78.0 14.6 %collective-permute-start.26 = (bf16[512,384]{1,0:T(8,128)(2,1)S(1)}, bf16[512,384]{1,0:T(8,128)(2,1)S(1)}, u32[]{:S(2)}, u32[]{:S(2)}) collective-permute-start(bf16[512,384]{1,0:T(8,128)(2,1)S(1)} %collective-permute-done.23.refs_4_), channel_id=1, source_target_pairs={{0,2},{1,3},{2,6},{3,7},{6,10},{7,11},{10,14},{11,15},{14,12},{15,... | collective-permute-start | bytes 1179656 | tf_op jit(solution)/shard_map/ppermute | solution.py:183
  82.1 12.1 %collective-permute-start.27 = (bf16[512,384]{1,0:T(8,128)(2,1)S(1)}, bf16[512,384]{1,0:T(8,128)(2,1)S(1)}, u32[]{:S(2)}, u32[]{:S(2)}) collective-permute-start(bf16[512,384]{1,0:T(8,128)(2,1)S(1)} %collective-permute-done.24.refs_5_), channel_id=1, source_target_pairs={{0,4},{1,5},{2,0},{3,1},{6,2},{7,3},{10,6},{11,7},{14,10},{15,11},... | collective-permute-start | bytes 1179656 | tf_op jit(solution)/shard_map/ppermute | solution.py:183
  84.3 14.6 %collective-permute-start.20 = (bf16[512,384]{1,0:T(8,128)(2,1)S(1)}, bf16[512,384]{1,0:T(8,128)(2,1)S(1)}, u32[]{:S(2)}, u32[]{:S(2)}) collective-permute-start(bf16[512,384]{1,0:T(8,128)(2,1)S(1)} %collective-permute-done.15.gate.refs_4_), channel_id=1, source_target_pairs={{0,2},{1,3},{2,6},{3,7},{6,10},{7,11},{10,14},{11,15},{14,12},{15,... | collective-permute-start | bytes 1179656 | tf_op jit(solution)/shard_map/ppermute | solution.py:183
  86.3 16.3 %collective-permute-start.21 = (bf16[512,384]{1,0:T(8,128)(2,1)S(1)}, bf16[512,384]{1,0:T(8,128)(2,1)S(1)}, u32[]{:S(2)}, u32[]{:S(2)}) collective-permute-start(bf16[512,384]{1,0:T(8,128)(2,1)S(1)} %collective-permute-done.16.refs_5_), channel_id=1, source_target_pairs={{0,4},{1,5},{2,0},{3,1},{6,2},{7,3},{10,6},{11,7},{14,10},{15,11},... | collective-permute-start | bytes 1179656 | tf_op jit(solution)/shard_map/ppermute | solution.py:183
  94.1 13.2 %collective-permute-start.28 = (bf16[512,384]{1,0:T(8,128)(2,1)S(1)}, bf16[512,384]{1,0:T(8,128)(2,1)S(1)}, u32[]{:S(2)}, u32[]{:S(2)}) collective-permute-start(bf16[512,384]{1,0:T(8,128)(2,1)S(1)} %collective-permute-done.26.refs_4_), channel_id=1, source_target_pairs={{0,2},{1,3},{2,6},{3,7},{6,10},{7,11},{10,14},{11,15},{14,12},{15,... | collective-permute-start | bytes 1179656 | tf_op jit(solution)/shard_map/ppermute | solution.py:183
  95.5 14.2 %collective-permute-start.29 = (bf16[512,384]{1,0:T(8,128)(2,1)S(1)}, bf16[512,384]{1,0:T(8,128)(2,1)S(1)}, u32[]{:S(2)}, u32[]{:S(2)}) collective-permute-start(bf16[512,384]{1,0:T(8,128)(2,1)S(1)} %collective-permute-done.27.refs_5_), channel_id=1, source_target_pairs={{0,4},{1,5},{2,0},{3,1},{6,2},{7,3},{10,6},{11,7},{14,10},{15,11},... | collective-permute-start | bytes 1179656 | tf_op jit(solution)/shard_map/ppermute | solution.py:183
  98.9 19.2 %collective-permute-start.33 = (bf16[192,2048]{1,0:T(8,128)(2,1)S(1)}, bf16[192,2048]{1,0:T(8,128)(2,1)S(1)}, u32[]{:S(2)}, u32[]{:S(2)}) collective-permute-start(bf16[192,2048]{1,0:T(8,128)(2,1)S(1)} %get-tuple-element.188), channel_id=1, source_target_pairs={{0,1},{1,0},{2,3},{3,2},{4,5},{5,4},{6,7},{7,6},{8,9},{9,8},{10,11... | collective-permute-start | bytes 2359304 | tf_op jit(solution)/shard_map/ppermute | solution.py:193
  102.6 13.2 %collective-permute-start.34 = (bf16[512,384]{1,0:T(8,128)(2,1)S(1)}, bf16[512,384]{1,0:T(8,128)(2,1)S(1)}, u32[]{:S(2)}, u32[]{:S(2)}) collective-permute-start(bf16[512,384]{1,0:T(8,128)(2,1)S(1)} %collective-permute-done.20.gate.refs_4_), channel_id=1, source_target_pairs={{0,2},{1,3},{2,6},{3,7},{6,10},{7,11},{10,14},{11,15},{14,12},{15,... | collective-permute-start | bytes 1179656 | tf_op jit(solution)/shard_map/ppermute | solution.py:183
  105.8 21.1 %collective-permute-start.25 = (bf16[192,2048]{1,0:T(8,128)(2,1)S(1)}, bf16[192,2048]{1,0:T(8,128)(2,1)S(1)}, u32[]{:S(2)}, u32[]{:S(2)}) collective-permute-start(bf16[192,2048]{1,0:T(8,128)(2,1)S(1)} %get-tuple-element.183), channel_id=1, source_target_pairs={{0,1},{1,0},{2,3},{3,2},{4,5},{5,4},{6,7},{7,6},{8,9},{9,8},{10,11... | collective-permute-start | bytes 2359304 | tf_op jit(solution)/shard_map/ppermute | solution.py:193
  107.4 10.8 %collective-permute-start.35 = (bf16[512,384]{1,0:T(8,128)(2,1)S(1)}, bf16[512,384]{1,0:T(8,128)(2,1)S(1)}, u32[]{:S(2)}, u32[]{:S(2)}) collective-permute-start(bf16[512,384]{1,0:T(8,128)(2,1)S(1)} %collective-permute-done.21.refs_5_), channel_id=1, source_target_pairs={{0,4},{1,5},{2,0},{3,1},{6,2},{7,3},{10,6},{11,7},{14,10},{15,11},... | collective-permute-start | bytes 1179656 | tf_op jit(solution)/shard_map/ppermute | solution.py:183
  109.1 20.8 %copy-start = (bf16[192,384]{1,0:T(8,128)(2,1)S(1)}, bf16[192,384]{1,0:T(8,128)(2,1)}, u32[]{:S(2)}) copy-start(bf16[192,384]{1,0:T(8,128)(2,1)} %param.6) | copy-start | bytes 442372
  109.7 14.2 %collective-permute-start.31 = (bf16[512,384]{1,0:T(8,128)(2,1)S(1)}, bf16[512,384]{1,0:T(8,128)(2,1)S(1)}, u32[]{:S(2)}, u32[]{:S(2)}) collective-permute-start(bf16[512,384]{1,0:T(8,128)(2,1)S(1)} %collective-permute-done.28.refs_4_), channel_id=1, source_target_pairs={{0,2},{1,3},{2,6},{3,7},{6,10},{7,11},{10,14},{11,15},{14,12},{15,... | collective-permute-start | bytes 1179656 | tf_op jit(solution)/shard_map/ppermute | solution.py:183
  115.8 10.6 %collective-permute-start.32 = (bf16[512,384]{1,0:T(8,128)(2,1)S(1)}, bf16[512,384]{1,0:T(8,128)(2,1)S(1)}, u32[]{:S(2)}, u32[]{:S(2)}) collective-permute-start(bf16[512,384]{1,0:T(8,128)(2,1)S(1)} %collective-permute-done.29.refs_5_), channel_id=1, source_target_pairs={{0,4},{1,5},{2,0},{3,1},{6,2},{7,3},{10,6},{11,7},{14,10},{15,11},... | collective-permute-start | bytes 1179656 | tf_op jit(solution)/shard_map/ppermute | solution.py:183
  128.2 1.7 %collective-permute-start.36 = (f32[208,384]{1,0:T(8,128)S(1)}, f32[208,384]{1,0:T(8,128)S(1)}, u32[]{:S(2)}, u32[]{:S(2)}) collective-permute-start(f32[208,384]{1,0:T(8,128)S(1)} %get-tuple-element.221), channel_id=1, source_target_pairs={{0,1},{1,0},{2,3},{3,2},{4,5},{5,4},{6,7},{7,6},{8,9},{9,8},{10,11... | collective-permute-start | bytes 958472 | tf_op jit(solution)/shard_map/ppermute | solution.py:211
  128.3 2.5 %copy-start.1 = (f32[192]{0:T(256)}, f32[192]{0:T(256)S(1)}, u32[]{:S(2)}) copy-start(f32[192]{0:T(256)S(1)} %add.28) | copy-start | bytes 2308

commit v7 on v1

v7 whole, which is shorter than its diff:
```python
import functools

import jax
import jax.numpy as jnp
import numpy as np
from jax import lax
from jax.experimental import pallas as pl
from jax.experimental.pallas import tpu as pltpu
from jax.sharding import PartitionSpec as P

CORES = 2
ONES = 16
SHIPS = True
PER_LENT = 4
EARLY = 2
REST_AT = 3
MOST = 2
ABSORB_FROM = 2
DEGREE_PARTS = 8
DEGREE_AT = 3
HELP_AT = (3, 4)
TILE = 128
SHORT = pl.CostEstimate(flops=0, bytes_accessed=1024, transcendentals=0)
VMEM_LIMIT = 40 * 1024 * 1024
LEND_LIMIT = 44 * 1024 * 1024


def chip_cycle(chips):
    wide = 1
    while (2 * wide) ** 2 <= chips:
        wide *= 2
    high = chips // wide
    if wide == 1 or high % 2 or wide * high != chips:
        return list(range(chips))
    walk = [(0, 0)]
    for i in range(high):
        line = range(1, wide)
        walk += [(i, j) for j in (line if i % 2 == 0 else reversed(line))]
    walk += [(i, 0) for i in range(high - 1, 0, -1)]
    walk = walk[:1] + walk[:0:-1]
    return [i * wide + j for i, j in walk]


def make_rounds(chips, ships):
    if not ships:
        turns = [{"up": [("own", 0)] * 4, "down": [("own", 1)] * 4}]
        for r in range(1, chips - 1):
            turns.append({"up": [("up", r)] * 4, "down": [("down", r)] * 4})
        return turns
    up = [[("up", r)] * 4 for r in range(6)]
    down = [[("down", r)] * 4 for r in range(6)]
    up[0], down[0] = [("own", 0)] * 4, [("own", 1)] * 4
    up[1][3], down[1][0] = ("own", 1), ("own", 0)
    up[2][0], down[2][3] = ("ship", 0), ("ship", 0)
    up[3][0], down[3][3] = ("ship", 1), ("ship", 1)
    up[3][1], down[3][2] = ("ch", 2), ("ch", 2)
    up[4][1], down[4][2] = ("ch", 3), ("ch", 3)
    turns = [{"up": up[r], "down": down[r]} for r in range(6)]
    for r, inner in {
        1: (("own", 1), ("own", 0)),
        2: (("down", 1), ("up", 1)),
        3: (("up", 2), ("down", 2)),
        4: (("down", 4), ("up", 4)),
    }.items():
        turns[r]["ch"] = [inner[0], inner[0], inner[1], inner[1]]
    return turns


def make_routes(chips):
    return {
        "up": {p: (p + 1) % chips for p in range(chips)},
        "down": {p: (p - 1) % chips for p in range(chips)},
        "ch": {1: 6, 6: 1, 2: 5, 5: 2},
    }


def shipped(p, which):
    if p % 4 == 0:
        return ((p + 1) % 8 if which == 0 else (p + 6) % 8), 0
    return ((p - 1) % 8 if which == 0 else (p - 6) % 8), 1


def trace_blocks(chips, turns):
    routes = make_routes(chips)
    held = {("own", s): [(p, s) for p in range(chips)] for s in range(2)}
    held |= {("ship", k): [None] * chips for k in range(2)}
    for r, turn in enumerate(turns, 1):
        for port, sources in turn.items():
            held[port, r] = [None] * chips
            for p, q in routes[port].items():
                held[port, r][q] = held[sources[p % 4]][p]
    return held


def lend_kernel(starts, depth, where, rows_ref, *refs):
    sems = refs[-1]
    copies = []
    for k, slot in enumerate(starts):
        start = pl.multiple_of((where[slot] + 1 - where[0]) * depth, 128)
        copies.append(
            pltpu.make_async_copy(
                rows_ref.at[:, pl.ds(start, depth)],
                refs[k // PER_LENT].at[:, pl.ds(k % PER_LENT * depth, depth)],
                sems.at[k],
            )
        )
    for copy in copies:
        copy.start()
    for copy in copies:
        copy.wait()


def lend(where, adj_rows, starts, depth):
    rows = adj_rows.shape[0]
    parts = len(starts) // PER_LENT
    shape = jax.ShapeDtypeStruct((rows, PER_LENT * depth), adj_rows.dtype)
    return pl.pallas_call(
        functools.partial(lend_kernel, starts, depth),
        in_specs=[pl.BlockSpec(memory_space=pltpu.SMEM), pl.BlockSpec(memory_space=pl.ANY)],
        out_specs=[pl.BlockSpec(memory_space=pltpu.VMEM)] * parts,
        out_shape=[shape] * parts,
        scratch_shapes=[pltpu.SemaphoreType.DMA((len(starts),))],
        compiler_params=pltpu.CompilerParams(vmem_limit_bytes=LEND_LIMIT),
        cost_estimate=SHORT,
        name="lend",
    )(where, adj_rows)


def degree_kernel(core, first, where, rows_ref, *refs):
    out_ref = refs[-1]
    g = pl.program_id(0)

    @pl.when(g == 0)
    def _():
        out_ref[...] = jnp.zeros_like(out_ref) if first else refs[0][...]

    @pl.when(where[0] == core)
    def _():
        for k in range(rows_ref.shape[1] // 128):
            out_ref[...] += rows_ref[:, k * 128 : (k + 1) * 128].astype(jnp.float32)


def row_sums(where, adj_rows, core, sums):
    rows, columns = adj_rows.shape
    block = columns // DEGREE_PARTS
    lanes = pl.BlockSpec((rows, 128), lambda g, where: (0, 0))
    first = sums is None
    return pl.pallas_call(
        functools.partial(degree_kernel, core, first),
        grid_spec=pltpu.PrefetchScalarGridSpec(
            num_scalar_prefetch=1,
            grid=(DEGREE_PARTS,),
            in_specs=[
                pl.BlockSpec((rows, block), lambda g, where: (0, jnp.where(where[0] == core, g, 0))),
            ]
            + ([] if first else [lanes]),
            out_specs=lanes,
        ),
        out_shape=jax.ShapeDtypeStruct((rows, 128), jnp.float32),
        compiler_params=pltpu.CompilerParams(vmem_limit_bytes=LEND_LIMIT),
        cost_estimate=SHORT,
        name="degree",
    )(where, adj_rows, *([] if first else [sums]))


def absorb_kernel(count, flags, rows, first, where, *refs):
    own, other, slab = (refs[k * count : (k + 1) * count] for k in range(3))
    mine_out, theirs_out = refs[-2:]
    total = None
    for k in range(count):
        ones = jnp.ones((ONES, own[k].shape[1]), own[k].dtype)
        left = jnp.concatenate([own[k][...], other[k][...], ones], axis=0)
        product = jnp.dot(left, slab[k][...], preferred_element_type=jnp.float32)
        if flags[k] is not None:
            product = jnp.where(where[flags[k]] > 0, product, 0.0)
        total = product if total is None else total + product
    mine, theirs = total[:rows], total[rows:]
    if not first:
        mine_in, theirs_in = refs[3 * count : 3 * count + 2]
        mine, theirs = mine + mine_in[...], theirs + theirs_in[...]
    mine_out[...] = mine
    theirs_out[...] = theirs


def absorb(where, adj_rows, borrowed, slabs, slots, columns, flags, sums):
    count = len(slabs)
    rows = adj_rows.shape[0]
    depth, width = slabs[0].shape

    def own(k):
        return pl.BlockSpec((rows, depth), lambda g, where: (0, where[slots[k]] + where[0]))

    def other(k):
        return pl.BlockSpec((rows, depth), lambda g, where: (0, columns[k] % PER_LENT))

    def whole(shape):
        return pl.BlockSpec(shape, lambda g, where: (0, 0))

    shapes = [(rows, width), (rows + ONES, width)]
    first = sums is None
    operands = [adj_rows] * count + [borrowed[column // PER_LENT] for column in columns] + list(slabs)
    in_specs = [own(k) for k in range(count)] + [other(k) for k in range(count)]
    in_specs += [whole((depth, width))] * count
    if not first:
        operands += list(sums)
        in_specs += [whole(shape) for shape in shapes]
    at = 1 + 3 * count
    return pl.pallas_call(
        functools.partial(absorb_kernel, count, flags, rows, first),
        grid_spec=pltpu.PrefetchScalarGridSpec(
            num_scalar_prefetch=1,
            grid=(1,),
            in_specs=in_specs,
            out_specs=[whole(shape) for shape in shapes],
        ),
        out_shape=[jax.ShapeDtypeStruct(shape, jnp.float32) for shape in shapes],
        input_output_aliases={} if first else {at: 0, at + 1: 1},
        compiler_params=pltpu.CompilerParams(vmem_limit_bytes=VMEM_LIMIT),
        cost_estimate=SHORT,
        name="absorb",
    )(where, *operands)


def pick_kernel(choices, n_in, where, *refs):
    outs = refs[n_in:]
    for out, by_kind in zip(outs, choices):
        for source in sorted(set(by_kind), key=str):
            kinds = [kind for kind, chosen in enumerate(by_kind) if chosen == source]
            here = where[1] == kinds[0]
            for kind in kinds[1:]:
                here = here | (where[1] == kind)

            def send(out=out, source=source):
                if isinstance(source, int):
                    out[...] = refs[source][...]
                    return
                left = jnp.concatenate([refs[source[0]][...], refs[source[1]][...]], axis=0)
                for i in range(left.shape[0] // TILE):
                    for k in range(left.shape[1] // TILE):
                        out[k * TILE : (k + 1) * TILE, i * TILE : (i + 1) * TILE] = left[
                            i * TILE : (i + 1) * TILE, k * TILE : (k + 1) * TILE
                        ]

            pl.when(here)(send)


def pick(where, operands, specs, choices, shape):
    return pl.pallas_call(
        functools.partial(pick_kernel, choices, len(operands)),
        grid_spec=pltpu.PrefetchScalarGridSpec(
            num_scalar_prefetch=1,
            grid=(1,),
            in_specs=specs,
            out_specs=[pl.BlockSpec(shape.shape, lambda g, where: (0, 0))] * len(choices),
        ),
        out_shape=[shape] * len(choices),
        compiler_params=pltpu.CompilerParams(vmem_limit_bytes=VMEM_LIMIT),
        cost_estimate=SHORT,
        name="pick",
    )(where, *operands)


def help_kernel(rows, first, where, *refs):
    mine_out, theirs_out, left = refs[-3:]
    if first:
        mine_out[...] = jnp.zeros_like(mine_out)
        theirs_out[...] = jnp.zeros_like(theirs_out)
    else:
        mine_out[...] = refs[4][...]
        theirs_out[...] = refs[5][...]
    for kind in (1, 2):
        packed, slab = refs[kind - 1], refs[kind + 1]

        @pl.when(where[1] == kind)
        def _(packed=packed, slab=slab):
            depth, width = packed.shape
            for i in range(width // TILE):
                for k in range(depth // TILE):
                    left[i * TILE : (i + 1) * TILE, k * TILE : (k + 1) * TILE] = packed[
                        k * TILE : (k + 1) * TILE, i * TILE : (i + 1) * TILE
                    ]
            left[width:, :] = jnp.ones((ONES, depth), left.dtype)
            product = jnp.dot(left[...], slab[...], preferred_element_type=jnp.float32)
            mine_out[...] += product[:rows]
            theirs_out[...] += product[rows:]


def help_corner(where, up, down, slabs, rows, sums):
    depth, width = up.shape
    shapes = [(rows, width), (rows + ONES, width)]
    first = sums is None
    operands = [up, down, *slabs] + ([] if first else list(sums))

    def whole(shape):
        return pl.BlockSpec(shape, lambda g, where: (0, 0))

    return pl.pallas_call(
        functools.partial(help_kernel, rows, first),
        grid_spec=pltpu.PrefetchScalarGridSpec(
            num_scalar_prefetch=1,
            grid=(1,),
            in_specs=[whole((depth, width))] * 4 + ([] if first else [whole(s) for s in shapes]),
            out_specs=[whole(shape) for shape in shapes],
            scratch_shapes=[pltpu.VMEM((width + ONES, depth), up.dtype)],
        ),
        out_shape=[jax.ShapeDtypeStruct(shape, jnp.float32) for shape in shapes],
        compiler_params=pltpu.CompilerParams(vmem_limit_bytes=VMEM_LIMIT),
        cost_estimate=SHORT,
        name="help",
    )(where, *operands)


def make_shards(n_row):
    chips = n_row // CORES
    cycle = chip_cycle(chips)
    place = {chip: k for k, chip in enumerate(cycle)}
    routes = make_routes(chips)

    def pairs(route):
        return [(cycle[p] * CORES + c, cycle[q] * CORES + c) for p, q in route.items() for c in range(CORES)]

    swap = [(d, d ^ 1) for d in range(n_row)]

    def shards(adj_rows, adj_panel, adj_tile):
        rows = adj_rows.shape[0]
        sections, depth, width = adj_panel.shape
        ships = SHIPS and chips == 8 and 2 * rows == width and width % TILE == 0 and depth % TILE == 0
        turns = make_rounds(chips, ships)
        blocks = trace_blocks(chips, turns)
        rounds = len(turns)

        groups = [[("own", 0), ("own", 1)]] + [[(port, r) for port in turn] for r, turn in enumerate(turns, 1)]
        sources = [source for group in groups for source in group]
        if ships:
            sources = [("ship", 0), ("ship", 1)] + sources
        slots, flags, columns = {}, {}, {}
        table = [[d % CORES, place[d // CORES] % 4] for d in range(n_row)]
        for k, source in enumerate(sources):
            columns[source], slots[source] = k, 2 + 2 * k
            masked = source[0] in ("up", "down") and None in blocks[source]
            flags[source] = 3 + 2 * k if masked else None
            for d in range(n_row):
                p = place[d // CORES]
                block = blocks[source][p]
                if source[0] == "ship" and p % 4 in (0, 3):
                    block = shipped(p, source[1])
                owner, s = block or (p, 0)
                table[d] += [s * n_row + cycle[owner] * CORES, int(block is not None)]
        where = jnp.asarray(np.array(table, np.int32))[lax.axis_index("row")]

        def tie(values, others):
            return lax.optimization_barrier((values, others))[0]

        def depart(turn):
            sending, mixed = {}, {}
            for port, chosen in turn.items():
                if len(set(chosen)) == 1:
                    sending[port] = slab[chosen[0]]
                else:
                    mixed[port] = chosen
            if not mixed:
                return sending
            operands, specs, index = [], [], {}
            for source in sorted({source for chosen in mixed.values() for source in chosen}):
                if source[0] == "ship":
                    spec = pl.BlockSpec((rows, depth), lambda g, where, slot=slots[source]: (0, where[slot] + where[0]))
                    lent = pl.BlockSpec((rows, depth), lambda g, where, column=columns[source]: (0, column % PER_LENT))
                    index[source] = (len(operands), len(operands) + 1)
                    operands += [adj_rows, borrowed[columns[source] // PER_LENT]]
                    specs += [spec, lent]
                else:
                    index[source] = len(operands)
                    operands.append(slab[source])
                    specs.append(pl.BlockSpec((depth, width), lambda g, where: (0, 0)))
            choices = [[index[source] for source in chosen] for chosen in mixed.values()]
            shape = jax.ShapeDtypeStruct((depth, width), adj_panel.dtype)
            sending.update(zip(mixed, pick(where, operands, specs, choices, shape)))
            return sending

        slab = {("own", s): adj_panel[s] for s in range(sections)}
        lent = lend(where, tie(adj_rows, list(slab.values())), [slots[source] for source in sources], depth)
        borrowed = [lax.ppermute(part, "row", swap) for part in lent[:EARLY]]
        sums, helped = None, None
        due = [0]
        done = ()
        for r in range(1, rounds + 2):
            at = r - 1
            if at > 0:
                arrived = tie([slab[port, at] for port in turns[at - 1]], done)
                slab |= {(port, at): piece for port, piece in zip(turns[at - 1], arrived)}
                due.append(at)
            if at == 1:
                lanes = row_sums(where, tie(adj_rows, arrived), 1, None)
                arrived, lanes = lax.optimization_barrier((arrived, lanes))
                slab |= {(port, at): piece for port, piece in zip(turns[at - 1], arrived)}
            if r <= rounds:
                sending = depart(turns[r - 1])
                for port, piece in sending.items():
                    slab[port, r] = lax.ppermute(piece, "row", pairs(routes[port]))
                if r == REST_AT:
                    rest = tie(lent[EARLY:], list(sending.values()))
                    borrowed += [lax.ppermute(part, "row", swap) for part in rest]
            if at == 0:
                continue
            gate = arrived[0]
            now = tie(adj_rows, arrived)
            done = []
            if ships and at in HELP_AT:
                held = [slab["ch", 2]] * 2 if helped else [slab["own", 0], slab["own", 1]]
                helped = help_corner(where, slab["up", at], slab["down", at], tie(held, gate), rows, helped)
                done.append(helped)
            if at >= ABSORB_FROM:
                for _ in range(MOST if r <= rounds else len(due)):
                    if due:
                        t = due.pop(0)
                        slabs = tie([slab[source] for source in groups[t]], gate)
                        sums = absorb(
                            where,
                            now,
                            borrowed,
                            slabs,
                            [slots[source] for source in groups[t]],
                            [columns[source] for source in groups[t]],
                            [flags[source] for source in groups[t]],
                            sums,
                        )
                        done.append(sums)
            if at == DEGREE_AT:
                lanes = row_sums(where, now, 0, lanes)
                done.append(lanes)
        degree = jnp.sum(lanes, axis=1)

        mine, theirs = sums
        if ships:
            other = lax.ppermute(helped[1], "row", swap)
            joined = jnp.concatenate([helped[0] + other[:rows], helped[1][rows:] + other[rows:]], axis=0)
            returned = lax.ppermute(joined, "row", pairs({1: 0, 2: 3, 5: 4, 6: 7}))
        partner = lax.ppermute(theirs, "row", swap)
        square = mine + partner[:rows]
        col_degree = theirs[rows : rows + 1] + partner[rows : rows + 1]
        if ships:
            square = square + returned[:rows]
            col_degree = col_degree + returned[rows : rows + 1]
        tile = adj_tile.astype(jnp.float32)
        lower = jnp.minimum(degree[:, None], col_degree)
        intersection = (square + tile) / (lower + 1.0 - tile)
        return (intersection, degree)

    return shards


def solution(mesh):
    in_specs = (
        P(("parts", "row"), None),
        P(None, ("parts", "row"), None),
        P(("parts", "row"), None),
    )
    out_specs = (P(("parts", "row"), None), P(("parts", "row")))
    return jax.shard_map(
        make_shards(mesh.shape["row"]), mesh=mesh, in_specs=in_specs, out_specs=out_specs, check_vma=False
    )
```

time: 210 us -> 147 us (0.70)
  matrix products: 45.8 us -> 0 us
  Pallas kernels: 0 us -> 44 us
  local copies, waits for them, and re-layouts: 35.5 us -> 2.32 us
  between operations: 16.9 us -> 0.94 us
  waiting for transfers between devices: 82.7 us -> 67.8 us
  starting transfers between devices: 16 us -> 30.2 us
  other arithmetic: 10.4 us -> 1.06 us
    dot_general x32 -> x0, matrix products: 45.8 us -> none  [the longest x16 23.6 us: shards(): mine = mine + jnp.dot(own, piece, preferred_element_type=jnp.float32)]
    pallas_call x0 -> x16, Pallas kernels: none -> 44 us  [the longest x7 21.1 us: absorb(): pl.pallas_call(functools.partial(absorb_kernel, count, flags, rows, first...]
    unnamed x39 -> x8, local copies, waits for them, and re-layouts: 27.2 us -> 0.1 us
    ppermute x16 -> x24, waiting for transfers between devices: 82.7 us -> 67.8 us  [the longest x16 66.4 us: shards(): slab[port, r] = lax.ppermute(piece, 'row', pairs(routes[port]))]
    ppermute x16 -> x24, starting transfers between devices: 16 us -> 30.2 us  [the longest x16 24.2 us: shards(): slab[port, r] = lax.ppermute(piece, 'row', pairs(routes[port]))]
    reduce_sum x16 -> x1, other arithmetic: 10.4 us -> 0.11 us  [shards(): degree = jnp.sum(lanes, axis=1)]
    dynamic_slice x8 -> x0, local copies, waits for them, and re-layouts: 5.12 us -> none  [shards(): chip = jnp.asarray(owners(step if s % 2 == 0 else -step))[me]]
  transfers between devices with their start and end apart: 16 -> 24, of which waited for: 7 -> 13; matrix products, arithmetic and copies ran while one was open for 18% -> 1% of each run, Pallas kernels for 0% -> 30%
where the time goes in v7:
time: 147 us; the launch traced here: 146 us
  waiting for transfers between devices  67.8 us (46%)
  Pallas kernels  44 us (30%)
  starting transfers between devices  30.2 us (21%)
  local copies, waits for them, and re-layouts  2.32 us (2%)
    ppermute x16, waiting for transfers between devices, shards(): slab[port, r] = lax.ppermute(piece, 'row', pairs(routes[port]))  66.4 us
    ppermute x16, starting transfers between devices, shards(): slab[port, r] = lax.ppermute(piece, 'row', pairs(routes[port]))  24.2 us
    pallas_call x7, Pallas kernels, absorb(): pl.pallas_call(functools.partial(absorb_kernel, count, flags, rows, first...  21.1 us
    pallas_call x2, Pallas kernels, row_sums(): pl.pallas_call(functools.partial(degree_kernel, core, first), grid_spec=p...  10.2 us
    pallas_call x1, Pallas kernels, lend(): pl.pallas_call(functools.partial(lend_kernel, starts, depth), in_specs=[p...  6.11 us
    pallas_call x4, Pallas kernels, pick(): pl.pallas_call(functools.partial(pick_kernel, choices, len(operands)), gr...  5.2 us
    ppermute x3, starting transfers between devices, shards(): borrowed += [lax.ppermute(part, 'row', swap) for part in rest]  3.48 us
  transfers between devices with their start and end apart: 24, of which 13 were waited for; matrix products, arithmetic and copies ran while one was open for 1% of the time, Pallas kernels for 30%

profile of v7, /device:TPU:0, one launch (start us, length us, event | category | flops | bytes accessed | tf_op | source)
XLA Modules:
  0.0 146.3 jit_solution(8207993063272254114)
XLA Ops:
  0.6 1.5 %slice_bitcast_fusion = (bf16[1024,384]{1,0:T(8,128)(2,1)S(1)}, bf16[1024,384]{1,0:T(8,128)(2,1)S(1)}) fusion(bf16[2,1024,384]{2,1,0:T(8,128)(2,1)} %param.5), kind=kLoop, calls=%fused_computation | loop fusion | bytes 3145728 | tf_op jit(solution)/shard_map/squeeze | solution.py:380
  2.2 3.0 %collective-permute-start.1 = (bf16[1024,384]{1,0:T(8,128)(2,1)S(1)}, bf16[1024,384]{1,0:T(8,128)(2,1)S(1)}, u32[]{:S(2)}, u32[]{:S(2)}) collective-permute-start(bf16[1024,384]{1,0:T(8,128)(2,1)S(1)} %get-tuple-element.121.refs_2_.refs_5_.refs_3_), channel_id=1, source_target_pairs={{0,2},{1,3},{4,0},{5,1},{8,4},{9,5},{12,8},{13,9},{14,12},{15,13},... | collective-permute-start | bytes 2359304 | tf_op jit(solution)/shard_map/ppermute | solution.py:399
  5.2 0.1 collective-permute-start
  5.3 0.7 dynamic-slice_bitcast_fusion.where
  6.0 6.1 %lend.1 = (bf16[192,4096]{1,0:T(8,128)(2,1)S(1)}, bf16[192,4096]{1,0:T(8,128)(2,1)}, bf16[192,4096]{1,0:T(8,128)(2,1)}, bf16[192,4096]{1,0:T(8,128)(2,1)}, bf16[192,4096]{1,0:T(8,128)(2,1)S(1)}) custom-call(s32[42]{0:T(128)S(1)} %dynamic-slice_bitcast_fusion.where, bf16[192,32768]{1,0:T(8,128)(2,1)} %refs_1_.6), custom_call_target="tpu_custom_call" | custom-call | bytes 1024 | tf_op jit(solution)/shard_map/lend/pallas_call | solution.py:117
  12.2 0.5 collective-permute-start.9
  12.7 10.1 %collective-permute-done.1.refs_0_.refs_5_ = bf16[1024,384]{1,0:T(8,128)(2,1)S(1)} collective-permute-done((bf16[1024,384]{1,0:T(8,128)(2,1)S(1)}, bf16[1024,384]{1,0:T(8,128)(2,1)S(1)}, u32[]{:S(2)}, u32[]{:S(2)}) %collective-permute-start.1) | collective-permute-done | bytes 786464 | tf_op jit(solution)/shard_map/ppermute | solution.py:399
  22.8 1.4 collective-permute-done.refs_3_.refs_4_
  24.2 2.0 %degree.2.refs_0_ = f32[192,128]{1,0:T(8,128)S(1)} custom-call(s32[42]{0:T(128)S(1)} %dynamic-slice_bitcast_fusion.where, bf16[192,32768]{1,0:T(8,128)(2,1)} %refs_1_.6), custom_call_target="tpu_custom_call" | custom-call | bytes 1024 | tf_op jit(solution)/shard_map/degree/pallas_call | solution.py:148
  26.1 0.8 pick.4
  26.9 0.5 collective-permute-start.2
  27.4 1.6 %collective-permute-start.3 = (bf16[1024,384]{1,0:T(8,128)(2,1)S(1)}, bf16[1024,384]{1,0:T(8,128)(2,1)S(1)}, u32[]{:S(2)}, u32[]{:S(2)}) collective-permute-start(bf16[1024,384]{1,0:T(8,128)(2,1)S(1)} %get-tuple-element.94), channel_id=1, source_target_pairs={{0,2},{1,3},{4,0},{5,1},{8,4},{9,5},{12,8},{13,9},{14,12},{15,13},... | collective-permute-start | bytes 2359304 | tf_op jit(solution)/shard_map/ppermute | solution.py:399
  29.0 0.7 collective-permute-start.4
  29.7 13.6 %collective-permute-done.2.refs_5_.refs_6_ = bf16[1024,384]{1,0:T(8,128)(2,1)S(1)} collective-permute-done((bf16[1024,384]{1,0:T(8,128)(2,1)S(1)}, bf16[1024,384]{1,0:T(8,128)(2,1)S(1)}, u32[]{:S(2)}, u32[]{:S(2)}) %collective-permute-start.2) | collective-permute-done | bytes 786464 | tf_op jit(solution)/shard_map/ppermute | solution.py:399
  43.3 0.4 collective-permute-done.3.refs_1_.refs_7_
  43.7 1.8 %pick.5 = (bf16[1024,384]{1,0:T(8,128)(2,1)S(1)}, bf16[1024,384]{1,0:T(8,128)(2,1)S(1)}, bf16[1024,384]{1,0:T(8,128)(2,1)S(1)}) custom-call(s32[42]{0:T(128)S(1)} %dynamic-slice_bitcast_fusion.where, bf16[1024,384]{1,0:T(8,128)(2,1)S(1)} %collective-permute-done.1.refs_0_.refs_5_, bf16[1024,384]{1,0:T(8,128)(2,1)S(1)} %collective-permute-done.3.refs_1_.refs_7_, ...), custom_call_target="tpu_custom_call" | custom-call | bytes 1024 | tf_op jit(solution)/shard_map/pick/pallas_call | solution.py:248
  45.5 5.0 %collective-permute-start.6 = (bf16[1024,384]{1,0:T(8,128)(2,1)S(1)}, bf16[1024,384]{1,0:T(8,128)(2,1)S(1)}, u32[]{:S(2)}, u32[]{:S(2)}) collective-permute-start(bf16[1024,384]{1,0:T(8,128)(2,1)S(1)} %get-tuple-element.100), channel_id=1, source_target_pairs={{0,4},{1,5},{4,8},{5,9},{8,12},{9,13},{12,14},{13,15},{14,10},{15,... | collective-permute-start | bytes 2359304 | tf_op jit(solution)/shard_map/ppermute | solution.py:399
  50.5 3.3 %collective-permute-start.13 = (bf16[192,4096]{1,0:T(8,128)(2,1)}, bf16[192,4096]{1,0:T(8,128)(2,1)S(1)}, u32[]{:S(2)}, u32[]{:S(2)}) collective-permute-start(bf16[192,4096]{1,0:T(8,128)(2,1)} %get-tuple-element.128), channel_id=1, source_target_pairs={{0,1},{1,0},{2,3},{3,2},{4,5},{5,4},{6,7},{7,6},{8,9},{9,8},{10,11... | collective-permute-start | bytes 4718600 | tf_op jit(solution)/shard_map/ppermute | solution.py:402
  53.8 0.7 collective-permute-start.8
  54.6 2.7 %absorb.7 = (f32[192,384]{1,0:T(8,128)S(1)}, f32[208,384]{1,0:T(8,128)S(1)}) custom-call(s32[42]{0:T(128)S(1)} %dynamic-slice_bitcast_fusion.where, bf16[192,32768]{1,0:T(8,128)(2,1)} %refs_1_.6, bf16[192,32768]{1,0:T(8,128)(2,1)} %refs_1_.6, bf16[192,4096]{1,0:T(8,128)(2,1)S(1)} %collective-permute-done.5.refs_3_.refs_2_.refs_4_, ...), custom_call_target="tpu_custom_call" | custom-call | bytes 1024 | tf_op jit(solution)/shard_map/absorb/pallas_call | solution.py:208
  57.4 2.7 %absorb.8 = (f32[192,384]{1,0:T(8,128)S(1)}, f32[208,384]{1,0:T(8,128)S(1)}) custom-call(s32[42]{0:T(128)S(1)} %dynamic-slice_bitcast_fusion.where, bf16[192,32768]{1,0:T(8,128)(2,1)} %refs_1_.6, bf16[192,32768]{1,0:T(8,128)(2,1)} %refs_1_.6, ...), custom_call_target="tpu_custom_call", output_to_operand_aliasing={{0}: (7, {}), {1}: (8, {})} | custom-call | bytes 1024 | tf_op jit(solution)/shard_map/absorb/pallas_call | solution.py:208
  60.1 5.7 %collective-permute-done.6.refs_6_.refs_0_ = bf16[1024,384]{1,0:T(8,128)(2,1)S(1)} collective-permute-done((bf16[1024,384]{1,0:T(8,128)(2,1)S(1)}, bf16[1024,384]{1,0:T(8,128)(2,1)S(1)}, u32[]{:S(2)}, u32[]{:S(2)}) %collective-permute-start.6) | collective-permute-done | bytes 786464 | tf_op jit(solution)/shard_map/ppermute | solution.py:399
  65.7 7.6 %collective-permute-done.7.refs_2_.refs_1_.refs_7_ = bf16[1024,384]{1,0:T(8,128)(2,1)S(1)} collective-permute-done((bf16[1024,384]{1,0:T(8,128)(2,1)S(1)}, bf16[1024,384]{1,0:T(8,128)(2,1)S(1)}, u32[]{:S(2)}, u32[]{:S(2)}) %collective-permute-start.7) | collective-permute-done | bytes 786464 | tf_op jit(solution)/shard_map/ppermute | solution.py:399
  73.3 1.8 %pick.6 = (bf16[1024,384]{1,0:T(8,128)(2,1)S(1)}, bf16[1024,384]{1,0:T(8,128)(2,1)S(1)}, bf16[1024,384]{1,0:T(8,128)(2,1)S(1)}) custom-call(s32[42]{0:T(128)S(1)} %dynamic-slice_bitcast_fusion.where, bf16[1024,384]{1,0:T(8,128)(2,1)S(1)} %collective-permute-done.4.refs_0_.refs_8_.refs_2_.refs_3_, ...), custom_call_target="tpu_custom_call" | custom-call | bytes 1024 | tf_op jit(solution)/shard_map/pick/pallas_call | solution.py:248
  75.1 3.9 %collective-permute-start.10 = (bf16[1024,384]{1,0:T(8,128)(2,1)S(1)}, bf16[1024,384]{1,0:T(8,128)(2,1)S(1)}, u32[]{:S(2)}, u32[]{:S(2)}) collective-permute-start(bf16[1024,384]{1,0:T(8,128)(2,1)S(1)} %get-tuple-element.117), channel_id=1, source_target_pairs={{0,4},{1,5},{4,8},{5,9},{8,12},{9,13},{12,14},{13,15},{14,10},{15,... | collective-permute-start | bytes 2359304 | tf_op jit(solution)/shard_map/ppermute | solution.py:399
  79.0 0.7 collective-permute-start.12
  79.7 8.3 %degree.3 = f32[192,128]{1,0:T(8,128)S(1)} custom-call(s32[42]{0:T(128)S(1)} %dynamic-slice_bitcast_fusion.where, bf16[192,32768]{1,0:T(8,128)(2,1)} %refs_1_.6, f32[192,128]{1,0:T(8,128)S(1)} %degree.2.refs_0_), custom_call_target="tpu_custom_call" | custom-call | bytes 1024 | tf_op jit(solution)/shard_map/degree/pallas_call | solution.py:148
  88.0 0.6 help.2
  88.6 3.3 %absorb.9 = (f32[192,384]{1,0:T(8,128)S(1)}, f32[208,384]{1,0:T(8,128)S(1)}) custom-call(s32[42]{0:T(128)S(1)} %dynamic-slice_bitcast_fusion.where, bf16[192,32768]{1,0:T(8,128)(2,1)} %refs_1_.6, bf16[192,32768]{1,0:T(8,128)(2,1)} %refs_1_.6, bf16[192,32768]{1,0:T(8,128)(2,1)} %refs_1_.6, ...), custom_call_target="tpu_custom_call", output_to_operand_aliasing={{0}: (10, {}), {1}: (11, {})} | custom-call | bytes 1024 | tf_op jit(solution)/shard_map/absorb/pallas_call | solution.py:208
  92.0 3.2 %absorb.10 = (f32[192,384]{1,0:T(8,128)S(1)}, f32[208,384]{1,0:T(8,128)S(1)}) custom-call(s32[42]{0:T(128)S(1)} %dynamic-slice_bitcast_fusion.where, bf16[192,32768]{1,0:T(8,128)(2,1)} %refs_1_.6, bf16[192,32768]{1,0:T(8,128)(2,1)} %refs_1_.6, bf16[192,32768]{1,0:T(8,128)(2,1)} %refs_1_.6, ...), custom_call_target="tpu_custom_call", output_to_operand_aliasing={{0}: (10, {}), {1}: (11, {})} | custom-call | bytes 1024 | tf_op jit(solution)/shard_map/absorb/pallas_call | solution.py:208
  95.2 2.1 %collective-permute-done.11.refs_1_.refs_7_ = bf16[1024,384]{1,0:T(8,128)(2,1)S(1)} collective-permute-done((bf16[1024,384]{1,0:T(8,128)(2,1)S(1)}, bf16[1024,384]{1,0:T(8,128)(2,1)S(1)}, u32[]{:S(2)}, u32[]{:S(2)}) %collective-permute-start.11) | collective-permute-done | bytes 786464 | tf_op jit(solution)/shard_map/ppermute | solution.py:399
  97.3 0.8 pick.7
  98.1 3.7 %collective-permute-start.14 = (bf16[1024,384]{1,0:T(8,128)(2,1)S(1)}, bf16[1024,384]{1,0:T(8,128)(2,1)S(1)}, u32[]{:S(2)}, u32[]{:S(2)}) collective-permute-start(bf16[1024,384]{1,0:T(8,128)(2,1)S(1)} %get-tuple-element.142), channel_id=1, source_target_pairs={{0,4},{1,5},{4,8},{5,9},{8,12},{9,13},{12,14},{13,15},{14,10},{15,... | collective-permute-start | bytes 2359304 | tf_op jit(solution)/shard_map/ppermute | solution.py:399
  101.8 0.7 collective-permute-start.16
  102.6 0.8 help.3
  103.4 0.6 collective-permute-start.22
  103.9 3.2 %absorb.11 = (f32[192,384]{1,0:T(8,128)S(1)}, f32[208,384]{1,0:T(8,128)S(1)}) custom-call(s32[42]{0:T(128)S(1)} %dynamic-slice_bitcast_fusion.where, bf16[192,32768]{1,0:T(8,128)(2,1)} %refs_1_.6, bf16[192,32768]{1,0:T(8,128)(2,1)} %refs_1_.6, bf16[192,32768]{1,0:T(8,128)(2,1)} %refs_1_.6, ...), custom_call_target="tpu_custom_call", output_to_operand_aliasing={{0}: (10, {}), {1}: (11, {})} | custom-call | bytes 1024 | tf_op jit(solution)/shard_map/absorb/pallas_call | solution.py:208
  107.2 9.3 %collective-permute-done.14.refs_6_ = bf16[1024,384]{1,0:T(8,128)(2,1)S(1)} collective-permute-done((bf16[1024,384]{1,0:T(8,128)(2,1)S(1)}, bf16[1024,384]{1,0:T(8,128)(2,1)S(1)}, u32[]{:S(2)}, u32[]{:S(2)}) %collective-permute-start.14) | collective-permute-done | bytes 786464 | tf_op jit(solution)/shard_map/ppermute | solution.py:399
  116.4 2.2 %collective-permute-done.15.refs_7_ = bf16[1024,384]{1,0:T(8,128)(2,1)S(1)} collective-permute-done((bf16[1024,384]{1,0:T(8,128)(2,1)S(1)}, bf16[1024,384]{1,0:T(8,128)(2,1)S(1)}, u32[]{:S(2)}, u32[]{:S(2)}) %collective-permute-start.15) | collective-permute-done | bytes 786464 | tf_op jit(solution)/shard_map/ppermute | solution.py:399
  118.6 3.6 %collective-permute-start.18 = (bf16[1024,384]{1,0:T(8,128)(2,1)S(1)}, bf16[1024,384]{1,0:T(8,128)(2,1)S(1)}, u32[]{:S(2)}, u32[]{:S(2)}) collective-permute-start(bf16[1024,384]{1,0:T(8,128)(2,1)S(1)} %collective-permute-done.14.refs_6_), channel_id=1, source_target_pairs={{0,4},{1,5},{4,8},{5,9},{8,12},{9,13},{12,14},{13,15},{14,10},{15,... | collective-permute-start | bytes 2359304 | tf_op jit(solution)/shard_map/ppermute | solution.py:399
  122.4 1.3 collective-permute-start.23
  123.7 3.3 %absorb.12 = (f32[192,384]{1,0:T(8,128)S(1)}, f32[208,384]{1,0:T(8,128)S(1)}) custom-call(s32[42]{0:T(128)S(1)} %dynamic-slice_bitcast_fusion.where, bf16[192,32768]{1,0:T(8,128)(2,1)} %refs_1_.6, bf16[192,32768]{1,0:T(8,128)(2,1)} %refs_1_.6, bf16[192,32768]{1,0:T(8,128)(2,1)} %refs_1_.6, ...), custom_call_target="tpu_custom_call", output_to_operand_aliasing={{0}: (10, {}), {1}: (11, {})} | custom-call | bytes 1024 | tf_op jit(solution)/shard_map/absorb/pallas_call | solution.py:208
  127.0 8.5 %collective-permute-done.18.refs_4_ = bf16[1024,384]{1,0:T(8,128)(2,1)S(1)} collective-permute-done((bf16[1024,384]{1,0:T(8,128)(2,1)S(1)}, bf16[1024,384]{1,0:T(8,128)(2,1)S(1)}, u32[]{:S(2)}, u32[]{:S(2)}) %collective-permute-start.18) | collective-permute-done | bytes 786464 | tf_op jit(solution)/shard_map/ppermute | solution.py:399
  135.4 5.6 %collective-permute-done.19.refs_5_ = bf16[1024,384]{1,0:T(8,128)(2,1)S(1)} collective-permute-done((bf16[1024,384]{1,0:T(8,128)(2,1)S(1)}, bf16[1024,384]{1,0:T(8,128)(2,1)S(1)}, u32[]{:S(2)}, u32[]{:S(2)}) %collective-permute-start.19) | collective-permute-done | bytes 786464 | tf_op jit(solution)/shard_map/ppermute | solution.py:399
  141.1 2.7 %absorb.13 = (f32[192,384]{1,0:T(8,128)S(1)}, f32[208,384]{1,0:T(8,128)S(1)}) custom-call(s32[42]{0:T(128)S(1)} %dynamic-slice_bitcast_fusion.where, bf16[192,32768]{1,0:T(8,128)(2,1)} %refs_1_.6, bf16[192,32768]{1,0:T(8,128)(2,1)} %refs_1_.6, ...), custom_call_target="tpu_custom_call", output_to_operand_aliasing={{0}: (7, {}), {1}: (8, {})} | custom-call | bytes 1024 | tf_op jit(solution)/shard_map/absorb/pallas_call | solution.py:208
  144.0 0.5 collective-permute-done.23
  144.5 1.0 collective-permute-done.21
  145.5 0.9 fusion
  (32 shorter events, 0.6 us)
Async XLA Ops:
  2.2 20.6 %collective-permute-start.1 = (bf16[1024,384]{1,0:T(8,128)(2,1)S(1)}, bf16[1024,384]{1,0:T(8,128)(2,1)S(1)}, u32[]{:S(2)}, u32[]{:S(2)}) collective-permute-start(bf16[1024,384]{1,0:T(8,128)(2,1)S(1)} %get-tuple-element.121.refs_2_.refs_5_.refs_3_), channel_id=1, source_target_pairs={{0,2},{1,3},{4,0},{5,1},{8,4},{9,5},{12,8},{13,9},{14,12},{15,13},... | collective-permute-start | bytes 2359304 | tf_op jit(solution)/shard_map/ppermute | solution.py:399
  5.2 19.0 %collective-permute-start = (bf16[1024,384]{1,0:T(8,128)(2,1)S(1)}, bf16[1024,384]{1,0:T(8,128)(2,1)S(1)}, u32[]{:S(2)}, u32[]{:S(2)}) collective-permute-start(bf16[1024,384]{1,0:T(8,128)(2,1)S(1)} %get-tuple-element.120.refs_1_.refs_4_.refs_2_), channel_id=1, source_target_pairs={{0,4},{1,5},{4,8},{5,9},{8,12},{9,13},{12,14},{13,15},{14,10},{15,... | collective-permute-start | bytes 2359304 | tf_op jit(solution)/shard_map/ppermute | solution.py:399
  12.1 31.6 %collective-permute-start.5 = (bf16[192,4096]{1,0:T(8,128)(2,1)S(1)}, bf16[192,4096]{1,0:T(8,128)(2,1)S(1)}, u32[]{:S(2)}, u32[]{:S(2)}) collective-permute-start(bf16[192,4096]{1,0:T(8,128)(2,1)S(1)} %get-tuple-element.98), channel_id=1, source_target_pairs={{0,1},{1,0},{2,3},{3,2},{4,5},{5,4},{6,7},{7,6},{8,9},{9,8},{10,11... | collective-permute-start | bytes 4718600 | tf_op jit(solution)/shard_map/ppermute | solution.py:382
  12.2 42.3 %collective-permute-start.9 = (bf16[192,4096]{1,0:T(8,128)(2,1)}, bf16[192,4096]{1,0:T(8,128)(2,1)S(1)}, u32[]{:S(2)}, u32[]{:S(2)}) collective-permute-start(bf16[192,4096]{1,0:T(8,128)(2,1)} %get-tuple-element.109), channel_id=1, source_target_pairs={{0,1},{1,0},{2,3},{3,2},{4,5},{5,4},{6,7},{7,6},{8,9},{9,8},{10,11... | collective-permute-start | bytes 4718600 | tf_op jit(solution)/shard_map/ppermute | solution.py:382
  26.9 16.4 %collective-permute-start.2 = (bf16[1024,384]{1,0:T(8,128)(2,1)S(1)}, bf16[1024,384]{1,0:T(8,128)(2,1)S(1)}, u32[]{:S(2)}, u32[]{:S(2)}) collective-permute-start(bf16[1024,384]{1,0:T(8,128)(2,1)S(1)} %get-tuple-element.93), channel_id=1, source_target_pairs={{0,4},{1,5},{4,8},{5,9},{8,12},{9,13},{12,14},{13,15},{14,10},{15,... | collective-permute-start | bytes 2359304 | tf_op jit(solution)/shard_map/ppermute | solution.py:399
  27.4 16.3 %collective-permute-start.3 = (bf16[1024,384]{1,0:T(8,128)(2,1)S(1)}, bf16[1024,384]{1,0:T(8,128)(2,1)S(1)}, u32[]{:S(2)}, u32[]{:S(2)}) collective-permute-start(bf16[1024,384]{1,0:T(8,128)(2,1)S(1)} %get-tuple-element.94), channel_id=1, source_target_pairs={{0,2},{1,3},{4,0},{5,1},{8,4},{9,5},{12,8},{13,9},{14,12},{15,13},... | collective-permute-start | bytes 2359304 | tf_op jit(solution)/shard_map/ppermute | solution.py:399
  29.0 14.7 %collective-permute-start.4 = (bf16[1024,384]{1,0:T(8,128)(2,1)S(1)}, bf16[1024,384]{1,0:T(8,128)(2,1)S(1)}, u32[]{:S(2)}, u32[]{:S(2)}) collective-permute-start(bf16[1024,384]{1,0:T(8,128)(2,1)S(1)} %get-tuple-element.95), channel_id=1, source_target_pairs={{4,6},{5,7},{6,4},{7,5},{8,10},{9,11},{10,8},{11,9},{20,22},{21,23... | collective-permute-start | bytes 2359304 | tf_op jit(solution)/shard_map/ppermute | solution.py:399
  45.5 20.2 %collective-permute-start.6 = (bf16[1024,384]{1,0:T(8,128)(2,1)S(1)}, bf16[1024,384]{1,0:T(8,128)(2,1)S(1)}, u32[]{:S(2)}, u32[]{:S(2)}) collective-permute-start(bf16[1024,384]{1,0:T(8,128)(2,1)S(1)} %get-tuple-element.100), channel_id=1, source_target_pairs={{0,4},{1,5},{4,8},{5,9},{8,12},{9,13},{12,14},{13,15},{14,10},{15,... | collective-permute-start | bytes 2359304 | tf_op jit(solution)/shard_map/ppermute | solution.py:399
  50.5 38.1 %collective-permute-start.13 = (bf16[192,4096]{1,0:T(8,128)(2,1)}, bf16[192,4096]{1,0:T(8,128)(2,1)S(1)}, u32[]{:S(2)}, u32[]{:S(2)}) collective-permute-start(bf16[192,4096]{1,0:T(8,128)(2,1)} %get-tuple-element.128), channel_id=1, source_target_pairs={{0,1},{1,0},{2,3},{3,2},{4,5},{5,4},{6,7},{7,6},{8,9},{9,8},{10,11... | collective-permute-start | bytes 4718600 | tf_op jit(solution)/shard_map/ppermute | solution.py:402
  53.8 19.4 %collective-permute-start.7 = (bf16[1024,384]{1,0:T(8,128)(2,1)S(1)}, bf16[1024,384]{1,0:T(8,128)(2,1)S(1)}, u32[]{:S(2)}, u32[]{:S(2)}) collective-permute-start(bf16[1024,384]{1,0:T(8,128)(2,1)S(1)} %get-tuple-element.101), channel_id=1, source_target_pairs={{0,2},{1,3},{4,0},{5,1},{8,4},{9,5},{12,8},{13,9},{14,12},{15,13},... | collective-permute-start | bytes 2359304 | tf_op jit(solution)/shard_map/ppermute | solution.py:399
  53.8 19.4 %collective-permute-start.8 = (bf16[1024,384]{1,0:T(8,128)(2,1)S(1)}, bf16[1024,384]{1,0:T(8,128)(2,1)S(1)}, u32[]{:S(2)}, u32[]{:S(2)}) collective-permute-start(bf16[1024,384]{1,0:T(8,128)(2,1)S(1)} %get-tuple-element.102), channel_id=1, source_target_pairs={{4,6},{5,7},{6,4},{7,5},{8,10},{9,11},{10,8},{11,9},{20,22},{21,23... | collective-permute-start | bytes 2359304 | tf_op jit(solution)/shard_map/ppermute | solution.py:399
  54.5 48.8 %collective-permute-start.17 = (bf16[192,4096]{1,0:T(8,128)(2,1)}, bf16[192,4096]{1,0:T(8,128)(2,1)S(1)}, u32[]{:S(2)}, u32[]{:S(2)}) collective-permute-start(bf16[192,4096]{1,0:T(8,128)(2,1)} %get-tuple-element.151), channel_id=1, source_target_pairs={{0,1},{1,0},{2,3},{3,2},{4,5},{5,4},{6,7},{7,6},{8,9},{9,8},{10,11... | collective-permute-start | bytes 4718600 | tf_op jit(solution)/shard_map/ppermute | solution.py:402
  75.1 20.1 %collective-permute-start.10 = (bf16[1024,384]{1,0:T(8,128)(2,1)S(1)}, bf16[1024,384]{1,0:T(8,128)(2,1)S(1)}, u32[]{:S(2)}, u32[]{:S(2)}) collective-permute-start(bf16[1024,384]{1,0:T(8,128)(2,1)S(1)} %get-tuple-element.117), channel_id=1, source_target_pairs={{0,4},{1,5},{4,8},{5,9},{8,12},{9,13},{12,14},{13,15},{14,10},{15,... | collective-permute-start | bytes 2359304 | tf_op jit(solution)/shard_map/ppermute | solution.py:399
  79.0 18.3 %collective-permute-start.11 = (bf16[1024,384]{1,0:T(8,128)(2,1)S(1)}, bf16[1024,384]{1,0:T(8,128)(2,1)S(1)}, u32[]{:S(2)}, u32[]{:S(2)}) collective-permute-start(bf16[1024,384]{1,0:T(8,128)(2,1)S(1)} %get-tuple-element.118), channel_id=1, source_target_pairs={{0,2},{1,3},{4,0},{5,1},{8,4},{9,5},{12,8},{13,9},{14,12},{15,13},... | collective-permute-start | bytes 2359304 | tf_op jit(solution)/shard_map/ppermute | solution.py:399
  79.0 18.3 %collective-permute-start.12 = (bf16[1024,384]{1,0:T(8,128)(2,1)S(1)}, bf16[1024,384]{1,0:T(8,128)(2,1)S(1)}, u32[]{:S(2)}, u32[]{:S(2)}) collective-permute-start(bf16[1024,384]{1,0:T(8,128)(2,1)S(1)} %get-tuple-element.119), channel_id=1, source_target_pairs={{4,6},{5,7},{6,4},{7,5},{8,10},{9,11},{10,8},{11,9},{20,22},{21,23... | collective-permute-start | bytes 2359304 | tf_op jit(solution)/shard_map/ppermute | solution.py:399
  98.1 18.3 %collective-permute-start.14 = (bf16[1024,384]{1,0:T(8,128)(2,1)S(1)}, bf16[1024,384]{1,0:T(8,128)(2,1)S(1)}, u32[]{:S(2)}, u32[]{:S(2)}) collective-permute-start(bf16[1024,384]{1,0:T(8,128)(2,1)S(1)} %get-tuple-element.142), channel_id=1, source_target_pairs={{0,4},{1,5},{4,8},{5,9},{8,12},{9,13},{12,14},{13,15},{14,10},{15,... | collective-permute-start | bytes 2359304 | tf_op jit(solution)/shard_map/ppermute | solution.py:399
  101.8 16.8 %collective-permute-start.15 = (bf16[1024,384]{1,0:T(8,128)(2,1)S(1)}, bf16[1024,384]{1,0:T(8,128)(2,1)S(1)}, u32[]{:S(2)}, u32[]{:S(2)}) collective-permute-start(bf16[1024,384]{1,0:T(8,128)(2,1)S(1)} %get-tuple-element.143), channel_id=1, source_target_pairs={{0,2},{1,3},{4,0},{5,1},{8,4},{9,5},{12,8},{13,9},{14,12},{15,13},... | collective-permute-start | bytes 2359304 | tf_op jit(solution)/shard_map/ppermute | solution.py:399
  101.8 16.8 %collective-permute-start.16 = (bf16[1024,384]{1,0:T(8,128)(2,1)S(1)}, bf16[1024,384]{1,0:T(8,128)(2,1)S(1)}, u32[]{:S(2)}, u32[]{:S(2)}) collective-permute-start(bf16[1024,384]{1,0:T(8,128)(2,1)S(1)} %get-tuple-element.144), channel_id=1, source_target_pairs={{4,6},{5,7},{6,4},{7,5},{8,10},{9,11},{10,8},{11,9},{20,22},{21,23... | collective-permute-start | bytes 2359304 | tf_op jit(solution)/shard_map/ppermute | solution.py:399
  102.5 21.1 %collective-permute-start.20 = (bf16[192,4096]{1,0:T(8,128)(2,1)S(1)}, bf16[192,4096]{1,0:T(8,128)(2,1)S(1)}, u32[]{:S(2)}, u32[]{:S(2)}) collective-permute-start(bf16[192,4096]{1,0:T(8,128)(2,1)S(1)} %get-tuple-element.161), channel_id=1, source_target_pairs={{0,1},{1,0},{2,3},{3,2},{4,5},{5,4},{6,7},{7,6},{8,9},{9,8},{10,11... | collective-permute-start | bytes 4718600 | tf_op jit(solution)/shard_map/ppermute | solution.py:402
  103.4 18.9 %collective-permute-start.22 = (f32[208,384]{1,0:T(8,128)S(1)}, f32[208,384]{1,0:T(8,128)S(1)}, u32[]{:S(2)}, u32[]{:S(2)}) collective-permute-start(f32[208,384]{1,0:T(8,128)S(1)} %get-tuple-element.148), channel_id=1, source_target_pairs={{0,1},{1,0},{2,3},{3,2},{4,5},{5,4},{6,7},{7,6},{8,9},{9,8},{10,11... | collective-permute-start | bytes 958472 | tf_op jit(solution)/shard_map/ppermute | solution.py:435
  118.6 16.8 %collective-permute-start.18 = (bf16[1024,384]{1,0:T(8,128)(2,1)S(1)}, bf16[1024,384]{1,0:T(8,128)(2,1)S(1)}, u32[]{:S(2)}, u32[]{:S(2)}) collective-permute-start(bf16[1024,384]{1,0:T(8,128)(2,1)S(1)} %collective-permute-done.14.refs_6_), channel_id=1, source_target_pairs={{0,4},{1,5},{4,8},{5,9},{8,12},{9,13},{12,14},{13,15},{14,10},{15,... | collective-permute-start | bytes 2359304 | tf_op jit(solution)/shard_map/ppermute | solution.py:399
  122.3 18.8 %collective-permute-start.19 = (bf16[1024,384]{1,0:T(8,128)(2,1)S(1)}, bf16[1024,384]{1,0:T(8,128)(2,1)S(1)}, u32[]{:S(2)}, u32[]{:S(2)}) collective-permute-start(bf16[1024,384]{1,0:T(8,128)(2,1)S(1)} %collective-permute-done.15.refs_7_), channel_id=1, source_target_pairs={{0,2},{1,3},{4,0},{5,1},{8,4},{9,5},{12,8},{13,9},{14,12},{15,13},... | collective-permute-start | bytes 2359304 | tf_op jit(solution)/shard_map/ppermute | solution.py:399
  122.4 22.1 %collective-permute-start.23 = (f32[208,384]{1,0:T(8,128)S(1)}, f32[208,384]{1,0:T(8,128)S(1)}, u32[]{:S(2)}, u32[]{:S(2)}) collective-permute-start(f32[208,384]{1,0:T(8,128)S(1)} %pad_maximum_fusion), channel_id=1, source_target_pairs={{4,0},{5,1},{8,12},{9,13},{10,14},{11,15},{6,2},{7,3},{20,16},{21,... | collective-permute-start | bytes 958472 | tf_op jit(solution)/shard_map/ppermute | solution.py:437
  141.1 4.4 %copy-start = (bf16[192,384]{1,0:T(8,128)(2,1)S(1)}, bf16[192,384]{1,0:T(8,128)(2,1)}, u32[]{:S(2)}) copy-start(bf16[192,384]{1,0:T(8,128)(2,1)} %param.6) | copy-start | bytes 442372
  143.7 1.7 %collective-permute-start.21 = (f32[208,384]{1,0:T(8,128)S(1)}, f32[208,384]{1,0:T(8,128)S(1)}, u32[]{:S(2)}, u32[]{:S(2)}) collective-permute-start(f32[208,384]{1,0:T(8,128)S(1)} %get-tuple-element.173), channel_id=1, source_target_pairs={{0,1},{1,0},{2,3},{3,2},{4,5},{5,4},{6,7},{7,6},{8,9},{9,8},{10,11... | collective-permute-start | bytes 958472 | tf_op jit(solution)/shard_map/ppermute | solution.py:438
  143.9 2.4 %copy-start.1 = (f32[192]{0:T(256)}, f32[192]{0:T(256)S(1)}, u32[]{:S(2)}) copy-start(f32[192]{0:T(256)S(1)} %reduce_sum.9) | copy-start | bytes 2308

commit v8 on v1

v8 whole, which is shorter than its diff:
```python
import functools

import jax
import jax.numpy as jnp
import numpy as np
from jax import lax
from jax.experimental import pallas as pl
from jax.experimental.pallas import tpu as pltpu
from jax.sharding import PartitionSpec as P

CORES = 2
ONES = 16
SHIPS = True
SLOTS = 1
MOST = 2
ABSORB_FROM = 3
PER_LENT = 4
EARLY = 1
REST_AT = 2
DEGREE_PARTS = 4
DEGREE_AT = 3
HELP_AT = (3, 4)
LEND_AFTER = 0
TILE = 128
SHORT = pl.CostEstimate(flops=0, bytes_accessed=1024, transcendentals=0)
VMEM_LIMIT = 40 * 1024 * 1024
LEND_LIMIT = 44 * 1024 * 1024


def chip_cycle(chips):
    wide = 1
    while (2 * wide) ** 2 <= chips:
        wide *= 2
    high = chips // wide
    if wide == 1 or high % 2 or wide * high != chips:
        return list(range(chips))
    walk = [(0, 0)]
    for i in range(high):
        line = range(1, wide)
        walk += [(i, j) for j in (line if i % 2 == 0 else reversed(line))]
    walk += [(i, 0) for i in range(high - 1, 0, -1)]
    walk = walk[:1] + walk[:0:-1]
    return [i * wide + j for i, j in walk]


def make_rounds(chips, ships):
    count = 6 if ships else chips - 1
    main = [[("own", 0)] * 4] + [[("main", r)] * 4 for r in range(1, count)]
    turns = [{"main": sources} for sources in main]
    if ships:
        main[1][3] = ("own", 1)
        main[2][0] = ("ship", 0)
        main[3][0] = ("ship", 1)
        main[3][1] = ("ch", 2)
        main[4][1] = ("ch", 3)
        for r, source in ((1, ("own", 0)), (2, ("main", 1)), (3, ("main", 2)), (4, ("main", 4))):
            turns[r]["ch"] = [source] * 4
    return turns


def make_route(chips, port, r):
    if port == "main":
        return {p: (p + 1) % chips for p in range(chips)}
    return {1: 6, 5: 2} if r == 4 else {6: 1, 2: 5}


def trace_blocks(chips, turns):
    held = {("own", s): [(p, s) for p in range(chips)] for s in range(2)}
    corner = [p % 4 == 0 for p in range(chips)]
    for k, ahead in enumerate((1, 6)):
        held["ship", k] = [((p + ahead) % chips, 0) if corner[p] else None for p in range(chips)]
    for r, turn in enumerate(turns, 1):
        for port, sources in turn.items():
            held[port, r] = [None] * chips
            for p, q in make_route(chips, port, r).items():
                source = sources[p % 4]
                held[port, r][q] = None if source[0] == "ship" else held[source][p]
    return held


def lend_kernel(sizes, first, depth, where, rows_ref, *refs):
    sems = refs[-1]
    copies = []
    for part, size in enumerate(sizes):
        for k in range(size):
            unit = sum(sizes[:part]) + k
            start = pl.multiple_of(where[first + unit] * depth, 128)
            copies.append(
                pltpu.make_async_copy(
                    rows_ref.at[:, pl.ds(start, depth)],
                    refs[part].at[:, pl.ds(k * depth, depth)],
                    sems.at[unit],
                )
            )
    for copy in copies:
        copy.start()
    for copy in copies:
        copy.wait()


def lend(where, adj_rows, sizes, first, depth):
    rows = adj_rows.shape[0]
    return pl.pallas_call(
        functools.partial(lend_kernel, sizes, first, depth),
        in_specs=[pl.BlockSpec(memory_space=pltpu.SMEM), pl.BlockSpec(memory_space=pl.ANY)],
        out_specs=[pl.BlockSpec(memory_space=pltpu.VMEM)] * len(sizes),
        out_shape=[jax.ShapeDtypeStruct((rows, size * depth), adj_rows.dtype) for size in sizes],
        scratch_shapes=[pltpu.SemaphoreType.DMA((sum(sizes),))],
        compiler_params=pltpu.CompilerParams(vmem_limit_bytes=LEND_LIMIT),
        cost_estimate=SHORT,
        name="lend",
    )(where, adj_rows)


def absorb_kernel(count, flags, rows, first, where, *refs):
    own, other, slab = (refs[k * count : (k + 1) * count] for k in range(3))
    mine_out, theirs_out = refs[-2:]
    total = None
    for k in range(count):
        ones = jnp.ones((ONES, own[k].shape[1]), own[k].dtype)
        left = jnp.concatenate([own[k][...], other[k][...], ones], axis=0)
        product = jnp.dot(left, slab[k][...], preferred_element_type=jnp.float32)
        if flags[k] is not None:
            product = jnp.where(where[flags[k]] > 0, product, 0.0)
        total = product if total is None else total + product
    mine, theirs = total[:rows], total[rows:]
    if not first:
        mine_in, theirs_in = refs[3 * count : 3 * count + 2]
        mine, theirs = mine + mine_in[...], theirs + theirs_in[...]
    mine_out[...] = mine
    theirs_out[...] = theirs


def absorb(where, adj_rows, borrowed, slabs, units, flags, sums):
    count = len(slabs)
    rows = adj_rows.shape[0]
    depth, width = slabs[0].shape

    def own(k):
        return pl.BlockSpec((rows, depth), lambda g, where: (0, where[2 + units[k]]))

    def other(k):
        return pl.BlockSpec((rows, depth), lambda g, where: (0, units[k] % PER_LENT))

    def whole(shape):
        return pl.BlockSpec(shape, lambda g, where: (0, 0))

    shapes = [(rows, width), (rows + ONES, width)]
    first = sums is None
    operands = [adj_rows] * count + [borrowed[unit // PER_LENT] for unit in units] + list(slabs)
    in_specs = [own(k) for k in range(count)] + [other(k) for k in range(count)]
    in_specs += [whole((depth, width))] * count
    if not first:
        operands += list(sums)
        in_specs += [whole(shape) for shape in shapes]
    at = 1 + 3 * count
    return pl.pallas_call(
        functools.partial(absorb_kernel, count, flags, rows, first),
        grid_spec=pltpu.PrefetchScalarGridSpec(
            num_scalar_prefetch=1,
            grid=(1,),
            in_specs=in_specs,
            out_specs=[whole(shape) for shape in shapes],
        ),
        out_shape=[jax.ShapeDtypeStruct(shape, jnp.float32) for shape in shapes],
        input_output_aliases={} if first else {at: 0, at + 1: 1},
        compiler_params=pltpu.CompilerParams(vmem_limit_bytes=VMEM_LIMIT),
        cost_estimate=SHORT,
        name="absorb",
    )(where, *operands)


def pick_kernel(choices, n_in, where, *refs):
    outs = refs[n_in:]
    for out, by_kind in zip(outs, choices):
        for source in sorted(set(by_kind), key=str):
            kinds = [kind for kind, chosen in enumerate(by_kind) if chosen == source]
            here = where[1] == kinds[0]
            for kind in kinds[1:]:
                here = here | (where[1] == kind)

            def send(out=out, source=source):
                if isinstance(source, int):
                    out[...] = refs[source][...]
                    return
                left = jnp.concatenate([refs[source[0]][...], refs[source[1]][...]], axis=0)
                for i in range(left.shape[0] // TILE):
                    for k in range(left.shape[1] // TILE):
                        out[k * TILE : (k + 1) * TILE, i * TILE : (i + 1) * TILE] = left[
                            i * TILE : (i + 1) * TILE, k * TILE : (k + 1) * TILE
                        ]

            pl.when(here)(send)


def pick(where, operands, specs, choices, shape):
    return pl.pallas_call(
        functools.partial(pick_kernel, choices, len(operands)),
        grid_spec=pltpu.PrefetchScalarGridSpec(
            num_scalar_prefetch=1,
            grid=(1,),
            in_specs=specs,
            out_specs=[pl.BlockSpec(shape.shape, lambda g, where: (0, 0))] * len(choices),
        ),
        out_shape=[shape] * len(choices),
        compiler_params=pltpu.CompilerParams(vmem_limit_bytes=VMEM_LIMIT),
        cost_estimate=SHORT,
        name="pick",
    )(where, *operands)


def help_kernel(rows, first, where, *refs):
    mine_out, theirs_out, left = refs[-3:]
    packed, slab = refs[:2]
    if first:
        mine_out[...] = jnp.zeros_like(mine_out)
        theirs_out[...] = jnp.zeros_like(theirs_out)
    else:
        mine_out[...] = refs[2][...]
        theirs_out[...] = refs[3][...]

    @pl.when(where[1] == 1)
    def _():
        depth, width = packed.shape
        for i in range(width // TILE):
            for k in range(depth // TILE):
                left[i * TILE : (i + 1) * TILE, k * TILE : (k + 1) * TILE] = packed[
                    k * TILE : (k + 1) * TILE, i * TILE : (i + 1) * TILE
                ]
        left[width:, :] = jnp.ones((ONES, depth), left.dtype)
        product = jnp.dot(left[...], slab[...], preferred_element_type=jnp.float32)
        mine_out[...] += product[:rows]
        theirs_out[...] += product[rows:]


def help_corner(where, packed, slab, rows, sums):
    depth, width = packed.shape
    shapes = [(rows, width), (rows + ONES, width)]
    first = sums is None
    operands = [packed, slab] + ([] if first else list(sums))

    def whole(shape):
        return pl.BlockSpec(shape, lambda g, where: (0, 0))

    return pl.pallas_call(
        functools.partial(help_kernel, rows, first),
        grid_spec=pltpu.PrefetchScalarGridSpec(
            num_scalar_prefetch=1,
            grid=(1,),
            in_specs=[whole((depth, width))] * 2 + ([] if first else [whole(s) for s in shapes]),
            out_specs=[whole(shape) for shape in shapes],
            scratch_shapes=[pltpu.VMEM((width + ONES, depth), packed.dtype)],
        ),
        out_shape=[jax.ShapeDtypeStruct(shape, jnp.float32) for shape in shapes],
        compiler_params=pltpu.CompilerParams(vmem_limit_bytes=VMEM_LIMIT),
        cost_estimate=SHORT,
        name="help",
    )(where, *operands)


def make_shards(n_row):
    chips = n_row // CORES
    cycle = chip_cycle(chips)
    place = {chip: k for k, chip in enumerate(cycle)}

    def walk(d):
        p = place[d // CORES]
        return p if d % CORES == 0 else chips - 1 - p

    def device(p, c):
        return cycle[p if c == 0 else chips - 1 - p] * CORES + c

    def pairs(route):
        return [(device(p, c), device(q, c)) for p, q in route.items() for c in range(CORES)]

    swap = [(d, d ^ 1) for d in range(n_row)]

    def shards(adj_rows, adj_panel, adj_tile):
        rows = adj_rows.shape[0]
        _, depth, width = adj_panel.shape
        ships = SHIPS and chips == 8 and 2 * rows == width and width % TILE == 0 and depth % TILE == 0
        turns = make_rounds(chips, ships)
        blocks = trace_blocks(chips, turns)
        rounds = len(turns)
        halves = range(CORES)

        groups = [[("own", 0)]] + [[(port, r) for port in turn] for r, turn in enumerate(turns, 1)]
        sources = [source for group in groups for source in group]
        if ships:
            sources = [("ship", 0), ("ship", 1)] + sources
        units, flags = {}, {}
        table = [[d % CORES, walk(d) % 4] for d in range(n_row)]
        for k, source in enumerate(sources):
            units[source] = [CORES * k + j for j in halves]
            for d in range(n_row):
                c = d % CORES
                p, other = blocks[source][walk(d)] or (walk(d), 0)
                owner = device(p, c) // CORES
                table[d] += [(c ^ other) * n_row + owner * CORES + (c ^ j) for j in halves]
        n_units = CORES * len(sources)
        table = [table[d] + table[d ^ 1][2:] for d in range(n_row)]
        for source in sources:
            flags[source] = None
            if source[0] == "main" and None in blocks[source]:
                flags[source] = len(table[0])
                for d in range(n_row):
                    table[d].append(int(blocks[source][walk(d)] is not None))
        me = lax.axis_index("row")
        where = jnp.asarray(np.array(table, np.int32))[me]
        core = lax.rem(me, CORES)

        def tie(values, others):
            return lax.optimization_barrier((values, others))[0]

        def exchange(value):
            return lax.ppermute(value, "row", swap)

        def depart(turn, j):
            sending = {}
            for port, chosen in turn.items():
                kinds = sorted(set(chosen))
                pieces = [(packed if source[0] == "ship" else slab)[source][j] for source in kinds]
                if len(kinds) == 1:
                    sending[port] = pieces[0]
                    continue
                specs = [pl.BlockSpec((depth, width), lambda g, where: (0, 0))] * len(pieces)
                choices = [[kinds.index(source) for source in chosen]]
                shape = jax.ShapeDtypeStruct((depth, width), adj_panel.dtype)
                sending[port] = pick(where, pieces, specs, choices, shape)[0]
            return sending

        def pack(source):
            shape = jax.ShapeDtypeStruct((depth, width), adj_panel.dtype)
            result = []
            for unit in units[source]:
                specs = [
                    pl.BlockSpec((rows, depth), lambda g, where, unit=unit: (0, where[2 + unit])),
                    pl.BlockSpec((rows, depth), lambda g, where, unit=unit: (0, unit % PER_LENT)),
                ]
                result += pick(where, [adj_rows, borrowed[unit // PER_LENT]], specs, [[(0, 1)] * 4], shape)
            return result

        here = lax.dynamic_index_in_dim(adj_panel, core, 0, keepdims=False)
        there = lax.dynamic_index_in_dim(adj_panel, 1 - core, 0, keepdims=False)
        slab = {("own", 0): [here, exchange(there)]}
        if ships:
            slab["own", 1] = [there, exchange(here)]
        sizes = [min(PER_LENT, n_units - k) for k in range(0, n_units, PER_LENT)]
        lent = lend(where, tie(adj_rows, slab["own", 0][LEND_AFTER]), sizes, 2 + n_units, depth)
        borrowed = [exchange(part) for part in lent[:EARLY]]
        packed = {("ship", k): pack(("ship", k)) for k in range(2)} if ships else {}
        sums, helped = None, None
        degree = []
        due = [(0, j) for j in halves]
        stretch = adj_rows.shape[1] // DEGREE_PARTS
        past = []
        for r in range(1, rounds + 2):
            for port in turns[r - 1] if r <= rounds else ():
                slab[port, r] = []
            for j in halves:
                at = r - 1
                if at > 0 and len(past) >= SLOTS:
                    arrived = tie([slab[port, at][j] for port in turns[at - 1]], past[-SLOTS])
                    for port, piece in zip(turns[at - 1], arrived):
                        slab[port, at][j] = piece
                if r <= rounds:
                    sending = depart(turns[r - 1], j)
                    for port, piece in sending.items():
                        slab[port, r].append(lax.ppermute(piece, "row", pairs(make_route(chips, port, r))))
                    if r == REST_AT and j == 0:
                        borrowed += [exchange(part) for part in tie(lent[EARLY:], list(sending.values()))]
                if at == 0:
                    continue
                gate = [slab[port, at][j] for port in turns[at - 1]]
                if r <= rounds:
                    gate = [gate, list(sending.values())]
                done = []
                past.append(done)
                due.append((at, j))
                if ships and at in HELP_AT:
                    beside = slab["own", 0] if at == HELP_AT[0] else slab["ch", 2]
                    helped = help_corner(where, slab["main", at][j], tie(beside[j], gate), rows, helped)
                    done.append(helped)
                    if (at, j) == (HELP_AT[1], 1):
                        back = lax.ppermute(jnp.concatenate(helped, axis=0), "row", pairs({1: 0, 5: 4}))
                if at >= ABSORB_FROM:
                    now = tie(adj_rows, gate)
                    for _ in range(MOST if r <= rounds else len(due)):
                        if due:
                            t, part = due.pop(0)
                            sums = absorb(
                                where,
                                now,
                                borrowed,
                                tie([slab[source][part] for source in groups[t]], gate),
                                [units[source][part] for source in groups[t]],
                                [flags[source] for source in groups[t]],
                                sums,
                            )
                            done.append(sums)
                if at >= DEGREE_AT and len(degree) < DEGREE_PARTS:
                    k = len(degree) * stretch
                    part = lax.slice_in_dim(tie(adj_rows, gate), k, k + stretch, axis=1)
                    degree.append(jnp.sum(part, axis=1, dtype=jnp.float32))
                    done.append(degree[-1])
        degree = sum(degree)

        mine, theirs = sums
        if ships:
            mine, theirs = mine + back[:rows], theirs + back[rows:]
        partner = exchange(theirs)
        square = mine + partner[:rows]
        col_degree = theirs[rows : rows + 1] + partner[rows : rows + 1]
        tile = adj_tile.astype(jnp.float32)
        lower = jnp.minimum(degree[:, None], col_degree)
        intersection = (square + tile) / (lower + 1.0 - tile)
        return (intersection, degree)

    return shards


def solution(mesh):
    in_specs = (
        P(("parts", "row"), None),
        P(None, ("parts", "row"), None),
        P(("parts", "row"), None),
    )
    out_specs = (P(("parts", "row"), None), P(("parts", "row")))
    return jax.shard_map(
        make_shards(mesh.shape["row"]), mesh=mesh, in_specs=in_specs, out_specs=out_specs, check_vma=False
    )
```

time: 210 us -> 137 us (0.65)
  waiting for transfers between devices: 82.7 us -> 19.9 us
  Pallas kernels: 0 us -> 55 us
  matrix products: 45.8 us -> 0 us
  local copies, waits for them, and re-layouts: 35.5 us -> 3.66 us
  starting transfers between devices: 16 us -> 44.6 us
  between operations: 16.9 us -> 1.27 us
    ppermute x16 -> x31, waiting for transfers between devices: 82.7 us -> 19.9 us  [the longest x20 14.1 us: shards(): lax.ppermute(piece, 'row', pairs(make_route(chips, port, r)))]
    pallas_call x0 -> x31, Pallas kernels: none -> 55 us  [the longest x14 34.3 us: absorb(): pl.pallas_call(functools.partial(absorb_kernel, count, flags, rows, first...]
    dot_general x32 -> x0, matrix products: 45.8 us -> none  [the longest x16 23.6 us: shards(): mine = mine + jnp.dot(own, piece, preferred_element_type=jnp.float32)]
    ppermute x16 -> x31, starting transfers between devices: 16 us -> 44.6 us  [the longest x20 41.9 us: shards(): lax.ppermute(piece, 'row', pairs(make_route(chips, port, r)))]
    unnamed x39 -> x28, local copies, waits for them, and re-layouts: 27.2 us -> 1.43 us
    dynamic_slice x8 -> x0, local copies, waits for them, and re-layouts: 5.12 us -> none  [shards(): chip = jnp.asarray(owners(step if s % 2 == 0 else -step))[me]]
    reduce_sum x16 -> x4, other arithmetic: 10.4 us -> 9.71 us  [shards(): degree.append(jnp.sum(part, axis=1, dtype=jnp.float32))]
  transfers between devices with their start and end apart: 16 -> 31, of which waited for: 7 -> 6; matrix products, arithmetic and copies ran while one was open for 18% -> 8% of each run, Pallas kernels for 0% -> 41%
where the time goes in v8:
time: 137 us; the launch traced here: 135 us
  Pallas kernels  55 us (40%)
  starting transfers between devices  44.6 us (33%)
  waiting for transfers between devices  19.9 us (15%)
  other arithmetic  10.7 us (8%)
  local copies, waits for them, and re-layouts  3.66 us (3%)
    ppermute x20, starting transfers between devices, shards(): lax.ppermute(piece, 'row', pairs(make_route(chips, port, r)))  41.9 us
    pallas_call x14, Pallas kernels, absorb(): pl.pallas_call(functools.partial(absorb_kernel, count, flags, rows, first...  34.3 us
    ppermute x20, waiting for transfers between devices, shards(): lax.ppermute(piece, 'row', pairs(make_route(chips, port, r)))  14.1 us
    pallas_call x12, Pallas kernels, pick(): pl.pallas_call(functools.partial(pick_kernel, choices, len(operands)), gr...  11.6 us
    reduce_sum x4, other arithmetic, shards(): degree.append(jnp.sum(part, axis=1, dtype=jnp.float32))  9.71 us
    pallas_call x1, Pallas kernels, lend(): pl.pallas_call(functools.partial(lend_kernel, sizes, first, depth), in_sp...  6.6 us
    ppermute x1, waiting for transfers between devices, shards(): lax.ppermute(jnp.concatenate(helped, axis=0), 'row', pairs({1: 0, 5: 4}))  4.29 us
  transfers between devices with their start and end apart: 31, of which 6 were waited for; matrix products, arithmetic and copies ran while one was open for 8% of the time, Pallas kernels for 41%

profile of v8, /device:TPU:0, one launch (start us, length us, event | category | flops | bytes accessed | tf_op | source)
XLA Modules:
  0.0 135.1 jit_solution(651402190815804427)
XLA Ops:
  0.6 1.5 %dynamic-slice_bitcast_fusion = (bf16[1024,384]{1,0:T(8,128)(2,1)S(1)}, bf16[1024,384]{1,0:T(8,128)(2,1)S(1)}) fusion(bf16[2,1024,384]{2,1,0:T(8,128)(2,1)} %param.5, s32[]{:T(128)S(6)} %select_n.12, s32[]{:T(128)S(6)} %select_n.11), kind=kLoop, calls=%fused_computation.4 | loop fusion | bytes 3145736 | tf_op jit(solution)/shard_map/jit(dynamic_index_in_dim)/squeeze | solution.py:343
  2.7 2.6 %collective-permute-start.8 = (bf16[1024,384]{1,0:T(8,128)(2,1)S(1)}, bf16[1024,384]{1,0:T(8,128)(2,1)S(1)}, u32[]{:S(2)}, u32[]{:S(2)}) collective-permute-start(bf16[1024,384]{1,0:T(8,128)(2,1)S(1)} %get-tuple-element.110.refs_1_.refs_2_), channel_id=1, source_target_pairs={{0,4},{3,7},{4,8},{7,11},{8,12},{11,15},{12,14},{15,13},{14,10},{1... | collective-permute-start | bytes 2359304 | tf_op jit(solution)/shard_map/ppermute | solution.py:369
  6.0 6.6 %lend.1 = (bf16[192,4096]{1,0:T(8,128)(2,1)S(1)}, bf16[192,4096]{1,0:T(8,128)(2,1)S(1)}, bf16[192,4096]{1,0:T(8,128)(2,1)}, bf16[192,4096]{1,0:T(8,128)(2,1)}, b...) custom-call(s32[56]{0:T(128)S(1)} %fusion.2.where, ...), custom_call_target="tpu_custom_call" | custom-call | bytes 1024 | tf_op jit(solution)/shard_map/lend/pallas_call | solution.py:103
  12.6 1.1 copy-done
  13.8 1.5 %collective-permute-start.1 = (bf16[1024,384]{1,0:T(8,128)(2,1)S(1)}, bf16[1024,384]{1,0:T(8,128)(2,1)S(1)}, u32[]{:S(2)}, u32[]{:S(2)}) collective-permute-start(bf16[1024,384]{1,0:T(8,128)(2,1)S(1)} %collective-permute-done.refs_2_.refs_1_), channel_id=1, source_target_pairs={{0,4},{3,7},{4,8},{7,11},{8,12},{11,15},{12,14},{15,13},{14,10},{1... | collective-permute-start | bytes 2359304 | tf_op jit(solution)/shard_map/ppermute | solution.py:369
  16.9 2.1 %collective-permute-start.9 = (bf16[1024,384]{1,0:T(8,128)(2,1)S(1)}, bf16[1024,384]{1,0:T(8,128)(2,1)S(1)}, u32[]{:S(2)}, u32[]{:S(2)}) collective-permute-start(bf16[1024,384]{1,0:T(8,128)(2,1)S(1)} %pick.15), channel_id=1, source_target_pairs={{0,4},{3,7},{4,8},{7,11},{8,12},{11,15},{12,14},{15,13},{14,10},{1... | collective-permute-start | bytes 2359304 | tf_op jit(solution)/shard_map/ppermute | solution.py:369
  19.0 6.9 %collective-permute-done.1.refs_0_.refs_2_ = bf16[1024,384]{1,0:T(8,128)(2,1)S(1)} collective-permute-done((bf16[1024,384]{1,0:T(8,128)(2,1)S(1)}, bf16[1024,384]{1,0:T(8,128)(2,1)S(1)}, u32[]{:S(2)}, u32[]{:S(2)}) %collective-permute-start.1) | collective-permute-done | bytes 786464 | tf_op jit(solution)/shard_map/ppermute | solution.py:369
  27.2 3.6 %collective-permute-start.3 = (bf16[1024,384]{1,0:T(8,128)(2,1)S(1)}, bf16[1024,384]{1,0:T(8,128)(2,1)S(1)}, u32[]{:S(2)}, u32[]{:S(2)}) collective-permute-start(bf16[1024,384]{1,0:T(8,128)(2,1)S(1)} %pick.12), channel_id=1, source_target_pairs={{0,4},{3,7},{4,8},{7,11},{8,12},{11,15},{12,14},{15,13},{14,10},{1... | collective-permute-start | bytes 2359304 | tf_op jit(solution)/shard_map/ppermute | solution.py:369
  30.9 3.4 %collective-permute-done.9.refs_0_.refs_4_ = bf16[1024,384]{1,0:T(8,128)(2,1)S(1)} collective-permute-done((bf16[1024,384]{1,0:T(8,128)(2,1)S(1)}, bf16[1024,384]{1,0:T(8,128)(2,1)S(1)}, u32[]{:S(2)}, u32[]{:S(2)}) %collective-permute-start.9) | collective-permute-done | bytes 786464 | tf_op jit(solution)/shard_map/ppermute | solution.py:369
  35.0 1.6 %pick.16.refs_1_ = bf16[1024,384]{1,0:T(8,128)(2,1)S(1)} custom-call(s32[56]{0:T(128)S(1)} %fusion.2.where, bf16[192,32768]{1,0:T(8,128)(2,1)} %refs_0_.21, bf16[192,4096]{1,0:T(8,128)(2,1)S(1)} %collective-permute-done.5.refs_1_), custom_call_target="tpu_custom_call" | custom-call | bytes 1024 | tf_op jit(solution)/shard_map/pick/pallas_call | solution.py:197
  37.3 2.1 %collective-permute-start.11 = (bf16[1024,384]{1,0:T(8,128)(2,1)S(1)}, bf16[1024,384]{1,0:T(8,128)(2,1)S(1)}, u32[]{:S(2)}, u32[]{:S(2)}) collective-permute-start(bf16[1024,384]{1,0:T(8,128)(2,1)S(1)} %pick.17), channel_id=1, source_target_pairs={{0,4},{3,7},{4,8},{7,11},{8,12},{11,15},{12,14},{15,13},{14,10},{1... | collective-permute-start | bytes 2359304 | tf_op jit(solution)/shard_map/ppermute | solution.py:369
  40.1 2.6 %collective-permute-done.3.refs_0_.refs_4_ = bf16[1024,384]{1,0:T(8,128)(2,1)S(1)} collective-permute-done((bf16[1024,384]{1,0:T(8,128)(2,1)S(1)}, bf16[1024,384]{1,0:T(8,128)(2,1)S(1)}, u32[]{:S(2)}, u32[]{:S(2)}) %collective-permute-start.3) | collective-permute-done | bytes 786464 | tf_op jit(solution)/shard_map/ppermute | solution.py:369
  42.7 1.6 %pick.13.refs_1_ = bf16[1024,384]{1,0:T(8,128)(2,1)S(1)} custom-call(s32[56]{0:T(128)S(1)} %fusion.2.where, bf16[192,32768]{1,0:T(8,128)(2,1)} %refs_0_.21, bf16[192,4096]{1,0:T(8,128)(2,1)S(1)} %collective-permute-done.5.refs_1_), custom_call_target="tpu_custom_call" | custom-call | bytes 1024 | tf_op jit(solution)/shard_map/pick/pallas_call | solution.py:197
  45.0 4.6 %collective-permute-start.6 = (bf16[1024,384]{1,0:T(8,128)(2,1)S(1)}, bf16[1024,384]{1,0:T(8,128)(2,1)S(1)}, u32[]{:S(2)}, u32[]{:S(2)}) collective-permute-start(bf16[1024,384]{1,0:T(8,128)(2,1)S(1)} %pick.14), channel_id=1, source_target_pairs={{0,4},{3,7},{4,8},{7,11},{8,12},{11,15},{12,14},{15,13},{14,10},{1... | collective-permute-start | bytes 2359304 | tf_op jit(solution)/shard_map/ppermute | solution.py:369
  49.6 1.6 %pick.18.refs_2_ = bf16[1024,384]{1,0:T(8,128)(2,1)S(1)} custom-call(s32[56]{0:T(128)S(1)} %fusion.2.where, bf16[192,32768]{1,0:T(8,128)(2,1)} %refs_0_.21, bf16[192,4096]{1,0:T(8,128)(2,1)S(1)} %collective-permute-done.5.refs_1_), custom_call_target="tpu_custom_call" | custom-call | bytes 1024 | tf_op jit(solution)/shard_map/pick/pallas_call | solution.py:197
  52.6 4.3 %collective-permute-start.16 = (bf16[1024,384]{1,0:T(8,128)(2,1)S(1)}, bf16[1024,384]{1,0:T(8,128)(2,1)S(1)}, u32[]{:S(2)}, u32[]{:S(2)}) collective-permute-start(bf16[1024,384]{1,0:T(8,128)(2,1)S(1)} %pick.19), channel_id=1, source_target_pairs={{0,4},{3,7},{4,8},{7,11},{8,12},{11,15},{12,14},{15,13},{14,10},{1... | collective-permute-start | bytes 2359304 | tf_op jit(solution)/shard_map/ppermute | solution.py:369
  56.9 1.6 %pick.20.refs_2_ = bf16[1024,384]{1,0:T(8,128)(2,1)S(1)} custom-call(s32[56]{0:T(128)S(1)} %fusion.2.where, bf16[192,32768]{1,0:T(8,128)(2,1)} %refs_0_.21, bf16[192,4096]{1,0:T(8,128)(2,1)S(1)} %collective-permute-done.5.refs_1_), custom_call_target="tpu_custom_call" | custom-call | bytes 1024 | tf_op jit(solution)/shard_map/pick/pallas_call | solution.py:197
  59.2 2.1 %absorb.14 = (f32[192,384]{1,0:T(8,128)S(1)}, f32[208,384]{1,0:T(8,128)S(1)}) custom-call(s32[56]{0:T(128)S(1)} %fusion.2.where, bf16[192,32768]{1,0:T(8,128)(2,1)} %refs_0_.21, bf16[192,4096]{1,0:T(8,128)(2,1)S(1)} %collective-permute-done.13.refs_1_, bf16[1024,384]{1,0:T(8,128)(2,1)S(1)} %get-tuple-element.110.refs_1_.refs_2_), custom_call_target="tpu_custom_call" | custom-call | bytes 1024 | tf_op jit(solution)/shard_map/absorb/pallas_call | solution.py:157
  61.3 2.1 %absorb.15 = (f32[192,384]{1,0:T(8,128)S(1)}, f32[208,384]{1,0:T(8,128)S(1)}) custom-call(s32[56]{0:T(128)S(1)} %fusion.2.where, bf16[192,32768]{1,0:T(8,128)(2,1)} %refs_0_.21, bf16[192,4096]{1,0:T(8,128)(2,1)S(1)} %collective-permute-done.13.refs_1_, ...), custom_call_target="tpu_custom_call", output_to_operand_aliasing={{0}: (4, {}), {1}: (5, {})} | custom-call | bytes 1024 | tf_op jit(solution)/shard_map/absorb/pallas_call | solution.py:157
  63.5 2.4 %convert_reduce_fusion.3 = f32[192]{0:T(256)S(1)} fusion(bf16[192,32768]{1,0:T(8,128)(2,1)} %refs_0_.21), kind=kLoop, calls=%fused_computation.3 | loop fusion | flops 3145536 | bytes 3146496 | tf_op jit(solution)/shard_map/reduce_sum | solution.py:404
  65.9 0.7 collective-permute-start.15
  67.3 2.4 %convert_reduce_fusion.2 = f32[192]{0:T(256)S(1)} fusion(bf16[192,32768]{1,0:T(8,128)(2,1)} %refs_0_.21), kind=kLoop, calls=%fused_computation.2 | loop fusion | flops 3145536 | bytes 3146496 | tf_op jit(solution)/shard_map/reduce_sum | solution.py:404
  69.7 2.1 %absorb.16 = (f32[192,384]{1,0:T(8,128)S(1)}, f32[208,384]{1,0:T(8,128)S(1)}) custom-call(s32[56]{0:T(128)S(1)} %fusion.2.where, bf16[192,32768]{1,0:T(8,128)(2,1)} %refs_0_.21, bf16[192,4096]{1,0:T(8,128)(2,1)S(1)} %collective-permute-done.13.refs_1_, ...), custom_call_target="tpu_custom_call", output_to_operand_aliasing={{0}: (4, {}), {1}: (5, {})} | custom-call | bytes 1024 | tf_op jit(solution)/shard_map/absorb/pallas_call | solution.py:157
  71.9 3.7 %collective-permute-start.14 = (bf16[1024,384]{1,0:T(8,128)(2,1)S(1)}, bf16[1024,384]{1,0:T(8,128)(2,1)S(1)}, u32[]{:S(2)}, u32[]{:S(2)}) collective-permute-start(bf16[1024,384]{1,0:T(8,128)(2,1)S(1)} %pick.21), channel_id=1, source_target_pairs={{0,4},{3,7},{4,8},{7,11},{8,12},{11,15},{12,14},{15,13},{14,10},{1... | collective-permute-start | bytes 2359304 | tf_op jit(solution)/shard_map/ppermute | solution.py:369
  76.3 2.1 %absorb.17 = (f32[192,384]{1,0:T(8,128)S(1)}, f32[208,384]{1,0:T(8,128)S(1)}) custom-call(s32[56]{0:T(128)S(1)} %fusion.2.where, bf16[192,32768]{1,0:T(8,128)(2,1)} %refs_0_.21, bf16[192,4096]{1,0:T(8,128)(2,1)S(1)} %collective-permute-done.13.refs_1_, ...), custom_call_target="tpu_custom_call", output_to_operand_aliasing={{0}: (4, {}), {1}: (5, {})} | custom-call | bytes 1024 | tf_op jit(solution)/shard_map/absorb/pallas_call | solution.py:157
  79.1 1.3 collective-permute-start.21
  80.4 2.4 %convert_reduce_fusion.1 = f32[192]{0:T(256)S(1)} fusion(bf16[192,32768]{1,0:T(8,128)(2,1)} %refs_0_.21), kind=kLoop, calls=%fused_computation.1 | loop fusion | flops 3145536 | bytes 3146496 | tf_op jit(solution)/shard_map/reduce_sum | solution.py:404
  82.9 0.8 collective-permute-start.22
  83.7 2.7 %absorb.18 = (f32[192,384]{1,0:T(8,128)S(1)}, f32[208,384]{1,0:T(8,128)S(1)}) custom-call(s32[56]{0:T(128)S(1)} %fusion.2.where, bf16[192,32768]{1,0:T(8,128)(2,1)} %refs_0_.21, bf16[192,32768]{1,0:T(8,128)(2,1)} %refs_0_.21, bf16[192,4096]{1,0:T(8,128)(2,1)S(1)} %collective-permute-done.18.refs_2_.refs_3_, ...), custom_call_target="tpu_custom_call", output_to_operand_aliasing={{0}: (7, {}), {1}: (8, {})} | custom-call | bytes 1024 | tf_op jit(solution)/shard_map/absorb/pallas_call | solution.py:157
  86.9 0.8 help.6
  87.7 2.7 %absorb.19 = (f32[192,384]{1,0:T(8,128)S(1)}, f32[208,384]{1,0:T(8,128)S(1)}) custom-call(s32[56]{0:T(128)S(1)} %fusion.2.where, bf16[192,32768]{1,0:T(8,128)(2,1)} %refs_0_.21, bf16[192,32768]{1,0:T(8,128)(2,1)} %refs_0_.21, bf16[192,4096]{1,0:T(8,128)(2,1)S(1)} %collective-permute-done.18.refs_2_.refs_3_, ...), custom_call_target="tpu_custom_call", output_to_operand_aliasing={{0}: (7, {}), {1}: (8, {})} | custom-call | bytes 1024 | tf_op jit(solution)/shard_map/absorb/pallas_call | solution.py:157
  91.0 4.0 %collective-permute-start.19 = (bf16[1024,384]{1,0:T(8,128)(2,1)S(1)}, bf16[1024,384]{1,0:T(8,128)(2,1)S(1)}, u32[]{:S(2)}, u32[]{:S(2)}) collective-permute-start(bf16[1024,384]{1,0:T(8,128)(2,1)S(1)} %pick.23), channel_id=1, source_target_pairs={{0,4},{3,7},{4,8},{7,11},{8,12},{11,15},{12,14},{15,13},{14,10},{1... | collective-permute-start | bytes 2359304 | tf_op jit(solution)/shard_map/ppermute | solution.py:369
  96.3 2.7 %absorb.20 = (f32[192,384]{1,0:T(8,128)S(1)}, f32[208,384]{1,0:T(8,128)S(1)}) custom-call(s32[56]{0:T(128)S(1)} %fusion.2.where, bf16[192,32768]{1,0:T(8,128)(2,1)} %refs_0_.21, bf16[192,32768]{1,0:T(8,128)(2,1)} %refs_0_.21, bf16[192,4096]{1,0:T(8,128)(2,1)S(1)} %collective-permute-done.23.refs_2_.refs_3_, ...), custom_call_target="tpu_custom_call", output_to_operand_aliasing={{0}: (7, {}), {1}: (8, {})} | custom-call | bytes 1024 | tf_op jit(solution)/shard_map/absorb/pallas_call | solution.py:157
  99.1 2.7 %absorb.21 = (f32[192,384]{1,0:T(8,128)S(1)}, f32[208,384]{1,0:T(8,128)S(1)}) custom-call(s32[56]{0:T(128)S(1)} %fusion.2.where, bf16[192,32768]{1,0:T(8,128)(2,1)} %refs_0_.21, bf16[192,32768]{1,0:T(8,128)(2,1)} %refs_0_.21, bf16[192,4096]{1,0:T(8,128)(2,1)S(1)} %collective-permute-done.23.refs_2_.refs_3_, ...), custom_call_target="tpu_custom_call", output_to_operand_aliasing={{0}: (7, {}), {1}: (8, {})} | custom-call | bytes 1024 | tf_op jit(solution)/shard_map/absorb/pallas_call | solution.py:157
  101.8 2.5 %convert_reduce_fusion = f32[192]{0:T(256)S(1)} fusion(bf16[192,32768]{1,0:T(8,128)(2,1)} %refs_0_.21), kind=kLoop, calls=%fused_computation | loop fusion | flops 3145536 | bytes 3146496 | tf_op jit(solution)/shard_map/reduce_sum | solution.py:404
  104.4 3.8 %collective-permute-start.26 = (bf16[1024,384]{1,0:T(8,128)(2,1)S(1)}, bf16[1024,384]{1,0:T(8,128)(2,1)S(1)}, u32[]{:S(2)}, u32[]{:S(2)}) collective-permute-start(bf16[1024,384]{1,0:T(8,128)(2,1)S(1)} %collective-permute-done.21.refs_4_), channel_id=1, source_target_pairs={{0,4},{3,7},{4,8},{7,11},{8,12},{11,15},{12,14},{15,13},{14,10},{1... | collective-permute-start | bytes 2359304 | tf_op jit(solution)/shard_map/ppermute | solution.py:369
  108.2 2.7 %absorb.22 = (f32[192,384]{1,0:T(8,128)S(1)}, f32[208,384]{1,0:T(8,128)S(1)}) custom-call(s32[56]{0:T(128)S(1)} %fusion.2.where, bf16[192,32768]{1,0:T(8,128)(2,1)} %refs_0_.21, bf16[192,32768]{1,0:T(8,128)(2,1)} %refs_0_.21, bf16[192,4096]{1,0:T(8,128)(2,1)S(1)} %collective-permute-done.24.refs_2_.refs_3_, ...), custom_call_target="tpu_custom_call", output_to_operand_aliasing={{0}: (7, {}), {1}: (8, {})} | custom-call | bytes 1024 | tf_op jit(solution)/shard_map/absorb/pallas_call | solution.py:157
  110.9 2.7 %absorb.23 = (f32[192,384]{1,0:T(8,128)S(1)}, f32[208,384]{1,0:T(8,128)S(1)}) custom-call(s32[56]{0:T(128)S(1)} %fusion.2.where, bf16[192,32768]{1,0:T(8,128)(2,1)} %refs_0_.21, bf16[192,32768]{1,0:T(8,128)(2,1)} %refs_0_.21, bf16[192,4096]{1,0:T(8,128)(2,1)S(1)} %collective-permute-done.24.refs_2_.refs_3_, ...), custom_call_target="tpu_custom_call", output_to_operand_aliasing={{0}: (7, {}), {1}: (8, {})} | custom-call | bytes 1024 | tf_op jit(solution)/shard_map/absorb/pallas_call | solution.py:157
  113.7 2.3 %collective-permute-start.25 = (bf16[1024,384]{1,0:T(8,128)(2,1)S(1)}, bf16[1024,384]{1,0:T(8,128)(2,1)S(1)}, u32[]{:S(2)}, u32[]{:S(2)}) collective-permute-start(bf16[1024,384]{1,0:T(8,128)(2,1)S(1)} %collective-permute-done.19.refs_4_), channel_id=1, source_target_pairs={{0,4},{3,7},{4,8},{7,11},{8,12},{11,15},{12,14},{15,13},{14,10},{1... | collective-permute-start | bytes 2359304 | tf_op jit(solution)/shard_map/ppermute | solution.py:369
  116.0 1.3 collective-permute-start.29
  117.4 2.7 %absorb.24 = (f32[192,384]{1,0:T(8,128)S(1)}, f32[208,384]{1,0:T(8,128)S(1)}) custom-call(s32[56]{0:T(128)S(1)} %fusion.2.where, bf16[192,32768]{1,0:T(8,128)(2,1)} %refs_0_.21, bf16[192,32768]{1,0:T(8,128)(2,1)} %refs_0_.21, bf16[192,4096]{1,0:T(8,128)(2,1)S(1)} %collective-permute-done.27.refs_2_.refs_3_, ...), custom_call_target="tpu_custom_call", output_to_operand_aliasing={{0}: (7, {}), {1}: (8, {})} | custom-call | bytes 1024 | tf_op jit(solution)/shard_map/absorb/pallas_call | solution.py:157
  120.1 2.7 %absorb.25 = (f32[192,384]{1,0:T(8,128)S(1)}, f32[208,384]{1,0:T(8,128)S(1)}) custom-call(s32[56]{0:T(128)S(1)} %fusion.2.where, bf16[192,32768]{1,0:T(8,128)(2,1)} %refs_0_.21, bf16[192,32768]{1,0:T(8,128)(2,1)} %refs_0_.21, bf16[192,4096]{1,0:T(8,128)(2,1)S(1)} %collective-permute-done.27.refs_2_.refs_3_, ...), custom_call_target="tpu_custom_call", output_to_operand_aliasing={{0}: (7, {}), {1}: (8, {})} | custom-call | bytes 1024 | tf_op jit(solution)/shard_map/absorb/pallas_call | solution.py:157
  122.8 2.1 %absorb.26 = (f32[192,384]{1,0:T(8,128)S(1)}, f32[208,384]{1,0:T(8,128)S(1)}) custom-call(s32[56]{0:T(128)S(1)} %fusion.2.where, bf16[192,32768]{1,0:T(8,128)(2,1)} %refs_0_.21, bf16[192,2048]{1,0:T(8,128)(2,1)S(1)} %collective-permute-done.28.refs_1_, ...), custom_call_target="tpu_custom_call", output_to_operand_aliasing={{0}: (4, {}), {1}: (5, {})} | custom-call | bytes 1024 | tf_op jit(solution)/shard_map/absorb/pallas_call | solution.py:157
  125.0 1.1 collective-permute-done.25.refs_2_
  126.1 2.1 %absorb.27 = (f32[192,384]{1,0:T(8,128)S(1)}, f32[208,384]{1,0:T(8,128)S(1)}) custom-call(s32[56]{0:T(128)S(1)} %fusion.2.where, bf16[192,32768]{1,0:T(8,128)(2,1)} %refs_0_.21, bf16[192,2048]{1,0:T(8,128)(2,1)S(1)} %collective-permute-done.28.refs_1_, ...), custom_call_target="tpu_custom_call", output_to_operand_aliasing={{0}: (4, {}), {1}: (5, {})} | custom-call | bytes 1024 | tf_op jit(solution)/shard_map/absorb/pallas_call | solution.py:157
  128.3 4.3 %collective-permute-done.29 = f32[400,384]{1,0:T(8,128)S(1)} collective-permute-done((f32[400,384]{1,0:T(8,128)S(1)}, f32[400,384]{1,0:T(8,128)S(1)}, u32[]{:S(2)}, u32[]{:S(2)}) %collective-permute-start.29) | collective-permute-done | bytes 614432 | tf_op jit(solution)/shard_map/ppermute | solution.py:385
  132.8 1.5 %collective-permute-done.30 = f32[208,384]{1,0:T(8,128)S(1)} collective-permute-done((f32[208,384]{1,0:T(8,128)S(1)}, f32[208,384]{1,0:T(8,128)S(1)}, u32[]{:S(2)}, u32[]{:S(2)}) %collective-permute-start.30) | collective-permute-done | bytes 319520 | tf_op jit(solution)/shard_map/ppermute | solution.py:316
  134.3 0.8 fusion
  (84 shorter events, 13.6 us)
Async XLA Ops:
  2.2 11.6 %collective-permute-start = (bf16[1024,384]{1,0:T(8,128)(2,1)S(1)}, bf16[1024,384]{1,0:T(8,128)(2,1)S(1)}, u32[]{:S(2)}, u32[]{:S(2)}) collective-permute-start(bf16[1024,384]{1,0:T(8,128)(2,1)S(1)} %get-tuple-element.205.refs_1_), channel_id=1, source_target_pairs={{0,1},{1,0},{2,3},{3,2},{4,5},{5,4},{6,7},{7,6},{8,9},{9,8},{10,11... | collective-permute-start | bytes 2359304 | tf_op jit(solution)/shard_map/ppermute | solution.py:316
  2.7 13.5 %collective-permute-start.8 = (bf16[1024,384]{1,0:T(8,128)(2,1)S(1)}, bf16[1024,384]{1,0:T(8,128)(2,1)S(1)}, u32[]{:S(2)}, u32[]{:S(2)}) collective-permute-start(bf16[1024,384]{1,0:T(8,128)(2,1)S(1)} %get-tuple-element.110.refs_1_.refs_2_), channel_id=1, source_target_pairs={{0,4},{3,7},{4,8},{7,11},{8,12},{11,15},{12,14},{15,13},{14,10},{1... | collective-permute-start | bytes 2359304 | tf_op jit(solution)/shard_map/ppermute | solution.py:369
  12.6 1.2 copy-start
  13.8 5.2 %copy-start.2 = (bf16[192,4096]{1,0:T(8,128)(2,1)}, bf16[192,4096]{1,0:T(8,128)(2,1)S(1)}, u32[]{:S(2)}) copy-start(bf16[192,4096]{1,0:T(8,128)(2,1)S(1)} %get-tuple-element.172) | copy-start | bytes 4718596
  13.8 13.4 %copy-start.4 = (bf16[192,2048]{1,0:T(8,128)(2,1)}, bf16[192,2048]{1,0:T(8,128)(2,1)S(1)}, u32[]{:S(2)}) copy-start(bf16[192,2048]{1,0:T(8,128)(2,1)S(1)} %get-tuple-element.195) | copy-start | bytes 2359300
  13.8 21.2 %collective-permute-start.5 = (bf16[192,4096]{1,0:T(8,128)(2,1)S(1)}, bf16[192,4096]{1,0:T(8,128)(2,1)S(1)}, u32[]{:S(2)}, u32[]{:S(2)}) collective-permute-start(bf16[192,4096]{1,0:T(8,128)(2,1)S(1)} %get-tuple-element.105), channel_id=1, source_target_pairs={{0,1},{1,0},{2,3},{3,2},{4,5},{5,4},{6,7},{7,6},{8,9},{9,8},{10,11... | collective-permute-start | bytes 4718600 | tf_op jit(solution)/shard_map/ppermute | solution.py:316
  13.8 12.0 %collective-permute-start.1 = (bf16[1024,384]{1,0:T(8,128)(2,1)S(1)}, bf16[1024,384]{1,0:T(8,128)(2,1)S(1)}, u32[]{:S(2)}, u32[]{:S(2)}) collective-permute-start(bf16[1024,384]{1,0:T(8,128)(2,1)S(1)} %collective-permute-done.refs_2_.refs_1_), channel_id=1, source_target_pairs={{0,4},{3,7},{4,8},{7,11},{8,12},{11,15},{12,14},{15,13},{14,10},{1... | collective-permute-start | bytes 2359304 | tf_op jit(solution)/shard_map/ppermute | solution.py:369
  15.3 10.5 %collective-permute-start.2 = (bf16[1024,384]{1,0:T(8,128)(2,1)S(1)}, bf16[1024,384]{1,0:T(8,128)(2,1)S(1)}, u32[]{:S(2)}, u32[]{:S(2)}) collective-permute-start(bf16[1024,384]{1,0:T(8,128)(2,1)S(1)} %get-tuple-element.110.refs_1_.refs_2_), channel_id=1, source_target_pairs={{0,1},{1,0},{2,3},{3,2},{4,5},{5,4},{6,7},{7,6},{8,9},{9,8},{10,11... | collective-permute-start | bytes 2359304 | tf_op jit(solution)/shard_map/ppermute | solution.py:316
  15.5 11.7 %collective-permute-start.10 = (bf16[1024,384]{1,0:T(8,128)(2,1)S(1)}, bf16[1024,384]{1,0:T(8,128)(2,1)S(1)}, u32[]{:S(2)}, u32[]{:S(2)}) collective-permute-start(bf16[1024,384]{1,0:T(8,128)(2,1)S(1)} %get-tuple-element.110.refs_1_.refs_2_), channel_id=1, source_target_pairs={{6,4},{5,7},{8,10},{11,9},{22,20},{21,23},{24,26},{27,25}} | collective-permute-start | bytes 2359304 | tf_op jit(solution)/shard_map/ppermute | solution.py:369
  16.9 17.4 %collective-permute-start.9 = (bf16[1024,384]{1,0:T(8,128)(2,1)S(1)}, bf16[1024,384]{1,0:T(8,128)(2,1)S(1)}, u32[]{:S(2)}, u32[]{:S(2)}) collective-permute-start(bf16[1024,384]{1,0:T(8,128)(2,1)S(1)} %pick.15), channel_id=1, source_target_pairs={{0,4},{3,7},{4,8},{7,11},{8,12},{11,15},{12,14},{15,13},{14,10},{1... | collective-permute-start | bytes 2359304 | tf_op jit(solution)/shard_map/ppermute | solution.py:369
  25.8 26.8 %collective-permute-start.13 = (bf16[192,4096]{1,0:T(8,128)(2,1)S(1)}, bf16[192,4096]{1,0:T(8,128)(2,1)S(1)}, u32[]{:S(2)}, u32[]{:S(2)}) collective-permute-start(bf16[192,4096]{1,0:T(8,128)(2,1)S(1)} %get-tuple-element.120), channel_id=1, source_target_pairs={{0,1},{1,0},{2,3},{3,2},{4,5},{5,4},{6,7},{7,6},{8,9},{9,8},{10,11... | collective-permute-start | bytes 4718600 | tf_op jit(solution)/shard_map/ppermute | solution.py:316
  25.9 13.5 %collective-permute-start.4 = (bf16[1024,384]{1,0:T(8,128)(2,1)S(1)}, bf16[1024,384]{1,0:T(8,128)(2,1)S(1)}, u32[]{:S(2)}, u32[]{:S(2)}) collective-permute-start(bf16[1024,384]{1,0:T(8,128)(2,1)S(1)} %collective-permute-done.refs_2_.refs_1_), channel_id=1, source_target_pairs={{6,4},{5,7},{8,10},{11,9},{22,20},{21,23},{24,26},{27,25}} | collective-permute-start | bytes 2359304 | tf_op jit(solution)/shard_map/ppermute | solution.py:369
  27.2 15.5 %collective-permute-start.3 = (bf16[1024,384]{1,0:T(8,128)(2,1)S(1)}, bf16[1024,384]{1,0:T(8,128)(2,1)S(1)}, u32[]{:S(2)}, u32[]{:S(2)}) collective-permute-start(bf16[1024,384]{1,0:T(8,128)(2,1)S(1)} %pick.12), channel_id=1, source_target_pairs={{0,4},{3,7},{4,8},{7,11},{8,12},{11,15},{12,14},{15,13},{14,10},{1... | collective-permute-start | bytes 2359304 | tf_op jit(solution)/shard_map/ppermute | solution.py:369
  34.3 10.7 %collective-permute-start.12 = (bf16[1024,384]{1,0:T(8,128)(2,1)S(1)}, bf16[1024,384]{1,0:T(8,128)(2,1)S(1)}, u32[]{:S(2)}, u32[]{:S(2)}) collective-permute-start(bf16[1024,384]{1,0:T(8,128)(2,1)S(1)} %collective-permute-done.8.refs_0_.refs_2_), channel_id=1, source_target_pairs={{6,4},{5,7},{8,10},{11,9},{22,20},{21,23},{24,26},{27,25}} | collective-permute-start | bytes 2359304 | tf_op jit(solution)/shard_map/ppermute | solution.py:369
  37.3 14.0 %collective-permute-start.11 = (bf16[1024,384]{1,0:T(8,128)(2,1)S(1)}, bf16[1024,384]{1,0:T(8,128)(2,1)S(1)}, u32[]{:S(2)}, u32[]{:S(2)}) collective-permute-start(bf16[1024,384]{1,0:T(8,128)(2,1)S(1)} %pick.17), channel_id=1, source_target_pairs={{0,4},{3,7},{4,8},{7,11},{8,12},{11,15},{12,14},{15,13},{14,10},{1... | collective-permute-start | bytes 2359304 | tf_op jit(solution)/shard_map/ppermute | solution.py:369
  39.4 17.6 %collective-permute-start.7 = (bf16[1024,384]{1,0:T(8,128)(2,1)S(1)}, bf16[1024,384]{1,0:T(8,128)(2,1)S(1)}, u32[]{:S(2)}, u32[]{:S(2)}) collective-permute-start(bf16[1024,384]{1,0:T(8,128)(2,1)S(1)} %collective-permute-done.1.refs_0_.refs_2_), channel_id=1, source_target_pairs={{6,4},{5,7},{8,10},{11,9},{22,20},{21,23},{24,26},{27,25}} | collective-permute-start | bytes 2359304 | tf_op jit(solution)/shard_map/ppermute | solution.py:369
  42.7 36.4 %collective-permute-start.18 = (bf16[192,4096]{1,0:T(8,128)(2,1)}, bf16[192,4096]{1,0:T(8,128)(2,1)S(1)}, u32[]{:S(2)}, u32[]{:S(2)}) collective-permute-start(bf16[192,4096]{1,0:T(8,128)(2,1)} %get-tuple-element.145), channel_id=1, source_target_pairs={{0,1},{1,0},{2,3},{3,2},{4,5},{5,4},{6,7},{7,6},{8,9},{9,8},{10,11... | collective-permute-start | bytes 4718600 | tf_op jit(solution)/shard_map/ppermute | solution.py:316
  45.0 20.9 %collective-permute-start.6 = (bf16[1024,384]{1,0:T(8,128)(2,1)S(1)}, bf16[1024,384]{1,0:T(8,128)(2,1)S(1)}, u32[]{:S(2)}, u32[]{:S(2)}) collective-permute-start(bf16[1024,384]{1,0:T(8,128)(2,1)S(1)} %pick.14), channel_id=1, source_target_pairs={{0,4},{3,7},{4,8},{7,11},{8,12},{11,15},{12,14},{15,13},{14,10},{1... | collective-permute-start | bytes 2359304 | tf_op jit(solution)/shard_map/ppermute | solution.py:369
  51.3 20.6 %collective-permute-start.17 = (bf16[1024,384]{1,0:T(8,128)(2,1)S(1)}, bf16[1024,384]{1,0:T(8,128)(2,1)S(1)}, u32[]{:S(2)}, u32[]{:S(2)}) collective-permute-start(bf16[1024,384]{1,0:T(8,128)(2,1)S(1)} %collective-permute-done.9.refs_0_.refs_4_), channel_id=1, source_target_pairs={{4,6},{7,5},{10,8},{9,11},{20,22},{23,21},{26,24},{25,27}} | collective-permute-start | bytes 2359304 | tf_op jit(solution)/shard_map/ppermute | solution.py:369
  52.6 23.0 %collective-permute-start.16 = (bf16[1024,384]{1,0:T(8,128)(2,1)S(1)}, bf16[1024,384]{1,0:T(8,128)(2,1)S(1)}, u32[]{:S(2)}, u32[]{:S(2)}) collective-permute-start(bf16[1024,384]{1,0:T(8,128)(2,1)S(1)} %pick.19), channel_id=1, source_target_pairs={{0,4},{3,7},{4,8},{7,11},{8,12},{11,15},{12,14},{15,13},{14,10},{1... | collective-permute-start | bytes 2359304 | tf_op jit(solution)/shard_map/ppermute | solution.py:369
  56.9 34.1 %collective-permute-start.23 = (bf16[192,4096]{1,0:T(8,128)(2,1)}, bf16[192,4096]{1,0:T(8,128)(2,1)S(1)}, u32[]{:S(2)}, u32[]{:S(2)}) collective-permute-start(bf16[192,4096]{1,0:T(8,128)(2,1)} %get-tuple-element.160), channel_id=1, source_target_pairs={{0,1},{1,0},{2,3},{3,2},{4,5},{5,4},{6,7},{7,6},{8,9},{9,8},{10,11... | collective-permute-start | bytes 4718600 | tf_op jit(solution)/shard_map/ppermute | solution.py:316
  65.9 16.9 %collective-permute-start.15 = (bf16[1024,384]{1,0:T(8,128)(2,1)S(1)}, bf16[1024,384]{1,0:T(8,128)(2,1)S(1)}, u32[]{:S(2)}, u32[]{:S(2)}) collective-permute-start(bf16[1024,384]{1,0:T(8,128)(2,1)S(1)} %collective-permute-done.3.refs_0_.refs_4_), channel_id=1, source_target_pairs={{4,6},{7,5},{10,8},{9,11},{20,22},{23,21},{26,24},{25,27}} | collective-permute-start | bytes 2359304 | tf_op jit(solution)/shard_map/ppermute | solution.py:369
  69.7 6.0 %copy-start.3 = (bf16[192,4096]{1,0:T(8,128)(2,1)S(1)}, bf16[192,4096]{1,0:T(8,128)(2,1)}, u32[]{:S(2)}) copy-start(bf16[192,4096]{1,0:T(8,128)(2,1)} %copy-done.2) | copy-start | bytes 4718596
  71.9 14.6 %collective-permute-start.14 = (bf16[1024,384]{1,0:T(8,128)(2,1)S(1)}, bf16[1024,384]{1,0:T(8,128)(2,1)S(1)}, u32[]{:S(2)}, u32[]{:S(2)}) collective-permute-start(bf16[1024,384]{1,0:T(8,128)(2,1)S(1)} %pick.21), channel_id=1, source_target_pairs={{0,4},{3,7},{4,8},{7,11},{8,12},{11,15},{12,14},{15,13},{14,10},{1... | collective-permute-start | bytes 2359304 | tf_op jit(solution)/shard_map/ppermute | solution.py:369
  75.6 28.7 %collective-permute-start.24 = (bf16[192,4096]{1,0:T(8,128)(2,1)S(1)}, bf16[192,4096]{1,0:T(8,128)(2,1)S(1)}, u32[]{:S(2)}, u32[]{:S(2)}) collective-permute-start(bf16[192,4096]{1,0:T(8,128)(2,1)S(1)} %copy-done.3), channel_id=1, source_target_pairs={{0,1},{1,0},{2,3},{3,2},{4,5},{5,4},{6,7},{7,6},{8,9},{9,8},{10,11... | collective-permute-start | bytes 4718600 | tf_op jit(solution)/shard_map/ppermute | solution.py:316
  79.1 15.9 %collective-permute-start.21 = (bf16[1024,384]{1,0:T(8,128)(2,1)S(1)}, bf16[1024,384]{1,0:T(8,128)(2,1)S(1)}, u32[]{:S(2)}, u32[]{:S(2)}) collective-permute-start(bf16[1024,384]{1,0:T(8,128)(2,1)S(1)} %pick.22), channel_id=1, source_target_pairs={{0,4},{3,7},{4,8},{7,11},{8,12},{11,15},{12,14},{15,13},{14,10},{1... | collective-permute-start | bytes 2359304 | tf_op jit(solution)/shard_map/ppermute | solution.py:369
  82.8 3.6 %copy-start.1 = (bf16[192,4096]{1,0:T(8,128)(2,1)S(1)}, bf16[192,4096]{1,0:T(8,128)(2,1)}, u32[]{:S(2)}) copy-start(bf16[192,4096]{1,0:T(8,128)(2,1)} %copy-done) | copy-start | bytes 4718596
  82.9 21.4 %collective-permute-start.22 = (bf16[1024,384]{1,0:T(8,128)(2,1)S(1)}, bf16[1024,384]{1,0:T(8,128)(2,1)S(1)}, u32[]{:S(2)}, u32[]{:S(2)}) collective-permute-start(bf16[1024,384]{1,0:T(8,128)(2,1)S(1)} %collective-permute-done.16.refs_1_.refs_0_.refs_4_), channel_id=1, source_target_pairs={{6,4},{5,7},{8,10},{11,9},{22,20},{21,23},{24,26},{27,25}} | collective-permute-start | bytes 2359304 | tf_op jit(solution)/shard_map/ppermute | solution.py:369
  86.5 30.9 %collective-permute-start.27 = (bf16[192,4096]{1,0:T(8,128)(2,1)S(1)}, bf16[192,4096]{1,0:T(8,128)(2,1)S(1)}, u32[]{:S(2)}, u32[]{:S(2)}) collective-permute-start(bf16[192,4096]{1,0:T(8,128)(2,1)S(1)} %copy-done.1), channel_id=1, source_target_pairs={{0,1},{1,0},{2,3},{3,2},{4,5},{5,4},{6,7},{7,6},{8,9},{9,8},{10,11... | collective-permute-start | bytes 4718600 | tf_op jit(solution)/shard_map/ppermute | solution.py:316
  91.0 22.6 %collective-permute-start.19 = (bf16[1024,384]{1,0:T(8,128)(2,1)S(1)}, bf16[1024,384]{1,0:T(8,128)(2,1)S(1)}, u32[]{:S(2)}, u32[]{:S(2)}) collective-permute-start(bf16[1024,384]{1,0:T(8,128)(2,1)S(1)} %pick.23), channel_id=1, source_target_pairs={{0,4},{3,7},{4,8},{7,11},{8,12},{11,15},{12,14},{15,13},{14,10},{1... | collective-permute-start | bytes 2359304 | tf_op jit(solution)/shard_map/ppermute | solution.py:369
  95.0 18.6 %collective-permute-start.20 = (bf16[1024,384]{1,0:T(8,128)(2,1)S(1)}, bf16[1024,384]{1,0:T(8,128)(2,1)S(1)}, u32[]{:S(2)}, u32[]{:S(2)}) collective-permute-start(bf16[1024,384]{1,0:T(8,128)(2,1)S(1)} %collective-permute-done.14.refs_1_.refs_0_.refs_4_), channel_id=1, source_target_pairs={{6,4},{5,7},{8,10},{11,9},{22,20},{21,23},{24,26},{27,25}} | collective-permute-start | bytes 2359304 | tf_op jit(solution)/shard_map/ppermute | solution.py:369
  101.8 2.5 %copy-start.5 = (bf16[192,2048]{1,0:T(8,128)(2,1)S(1)}, bf16[192,2048]{1,0:T(8,128)(2,1)}, u32[]{:S(2)}) copy-start(bf16[192,2048]{1,0:T(8,128)(2,1)} %copy-done.4) | copy-start | bytes 2359300
  104.3 18.5 %collective-permute-start.28 = (bf16[192,2048]{1,0:T(8,128)(2,1)S(1)}, bf16[192,2048]{1,0:T(8,128)(2,1)S(1)}, u32[]{:S(2)}, u32[]{:S(2)}) collective-permute-start(bf16[192,2048]{1,0:T(8,128)(2,1)S(1)} %copy-done.5), channel_id=1, source_target_pairs={{0,1},{1,0},{2,3},{3,2},{4,5},{5,4},{6,7},{7,6},{8,9},{9,8},{10,11... | collective-permute-start | bytes 2359304 | tf_op jit(solution)/shard_map/ppermute | solution.py:316
  104.4 18.4 %collective-permute-start.26 = (bf16[1024,384]{1,0:T(8,128)(2,1)S(1)}, bf16[1024,384]{1,0:T(8,128)(2,1)S(1)}, u32[]{:S(2)}, u32[]{:S(2)}) collective-permute-start(bf16[1024,384]{1,0:T(8,128)(2,1)S(1)} %collective-permute-done.21.refs_4_), channel_id=1, source_target_pairs={{0,4},{3,7},{4,8},{7,11},{8,12},{11,15},{12,14},{15,13},{14,10},{1... | collective-permute-start | bytes 2359304 | tf_op jit(solution)/shard_map/ppermute | solution.py:369
  113.7 12.5 %collective-permute-start.25 = (bf16[1024,384]{1,0:T(8,128)(2,1)S(1)}, bf16[1024,384]{1,0:T(8,128)(2,1)S(1)}, u32[]{:S(2)}, u32[]{:S(2)}) collective-permute-start(bf16[1024,384]{1,0:T(8,128)(2,1)S(1)} %collective-permute-done.19.refs_4_), channel_id=1, source_target_pairs={{0,4},{3,7},{4,8},{7,11},{8,12},{11,15},{12,14},{15,13},{14,10},{1... | collective-permute-start | bytes 2359304 | tf_op jit(solution)/shard_map/ppermute | solution.py:369
  116.0 16.5 %collective-permute-start.29 = (f32[400,384]{1,0:T(8,128)S(1)}, f32[400,384]{1,0:T(8,128)S(1)}, u32[]{:S(2)}, u32[]{:S(2)}) collective-permute-start(f32[400,384]{1,0:T(8,128)S(1)} %pad_maximum_fusion), channel_id=1, source_target_pairs={{4,0},{7,3},{10,14},{9,13},{20,16},{23,19},{26,30},{25,29}} | collective-permute-start | bytes 1843208 | tf_op jit(solution)/shard_map/ppermute | solution.py:385
  126.1 8.2 %copy-start.6 = (bf16[192,384]{1,0:T(8,128)(2,1)S(1)}, bf16[192,384]{1,0:T(8,128)(2,1)}, u32[]{:S(2)}) copy-start(bf16[192,384]{1,0:T(8,128)(2,1)} %param.6) | copy-start | bytes 442372
  132.6 1.7 %collective-permute-start.30 = (f32[208,384]{1,0:T(8,128)S(1)}, f32[208,384]{1,0:T(8,128)S(1)}, u32[]{:S(2)}, u32[]{:S(2)}) collective-permute-start(f32[208,384]{1,0:T(8,128)S(1)} %slice_add_fusion), channel_id=1, source_target_pairs={{0,1},{1,0},{2,3},{3,2},{4,5},{5,4},{6,7},{7,6},{8,9},{9,8},{10,11... | collective-permute-start | bytes 958472 | tf_op jit(solution)/shard_map/ppermute | solution.py:316
  132.7 2.4 %copy-start.7 = (f32[192]{0:T(256)}, f32[192]{0:T(256)S(1)}, u32[]{:S(2)}) copy-start(f32[192]{0:T(256)S(1)} %add_add_fusion) | copy-start | bytes 2308

commit v9 on v8

--- a/solution.py
+++ b/solution.py
@@ -18,12 +18,12 @@
 EARLY = 1
 REST_AT = 2
 DEGREE_PARTS = 4
-DEGREE_AT = 3
+DEGREE_AT = 1
 HELP_AT = (3, 4)
 LEND_AFTER = 0
 TILE = 128
 SHORT = pl.CostEstimate(flops=0, bytes_accessed=1024, transcendentals=0)
-VMEM_LIMIT = 40 * 1024 * 1024
+VMEM_LIMIT = 10 * 1024 * 1024
 LEND_LIMIT = 44 * 1024 * 1024
 
 

time: 137 us -> 131 us (0.956)
  Pallas kernels: 55 us -> 38.1 us
  waiting for transfers between devices: 19.9 us -> 27.7 us
  starting transfers between devices: 44.6 us -> 50.4 us
  other arithmetic: 10.7 us -> 6.83 us
  local copies, waits for them, and re-layouts: 3.66 us -> 5.68 us
    pallas_call x14, Pallas kernels: 34.3 us -> 20.5 us  [absorb(): pl.pallas_call(functools.partial(absorb_kernel, count, flags, rows, first...]
    ppermute x20, waiting for transfers between devices: 14.1 us -> 20.8 us  [shards(): lax.ppermute(piece, 'row', pairs(make_route(chips, port, r)))]
    ppermute x20, starting transfers between devices: 41.9 us -> 47.1 us  [shards(): lax.ppermute(piece, 'row', pairs(make_route(chips, port, r)))]
    reduce_sum x4, other arithmetic: 9.71 us -> 5.86 us  [shards(): degree.append(jnp.sum(part, axis=1, dtype=jnp.float32))]
    pallas_call x12, Pallas kernels: 11.6 us -> 8.89 us  [pick(): pl.pallas_call(functools.partial(pick_kernel, choices, len(operands)), gr...]
    pallas_call x1, Pallas kernels: 6.6 us -> 4.98 us  [lend(): pl.pallas_call(functools.partial(lend_kernel, sizes, first, depth), in_sp...]
  transfers between devices with their start and end apart: 31 -> 31, of which waited for: 6 -> 10; matrix products, arithmetic and copies ran while one was open for 8% -> 5% of each run, Pallas kernels for 41% -> 29%
where the time goes in v9:
time: 131 us; the launch traced here: 130 us
  starting transfers between devices  50.4 us (38%)
  Pallas kernels  38.1 us (29%)
  waiting for transfers between devices  27.7 us (21%)
  other arithmetic  6.83 us (5%)
  local copies, waits for them, and re-layouts  5.68 us (4%)
  between operations  1.32 us (1%)
    ppermute x20, starting transfers between devices, shards(): lax.ppermute(piece, 'row', pairs(make_route(chips, port, r)))  47.1 us
    ppermute x20, waiting for transfers between devices, shards(): lax.ppermute(piece, 'row', pairs(make_route(chips, port, r)))  20.8 us
    pallas_call x14, Pallas kernels, absorb(): pl.pallas_call(functools.partial(absorb_kernel, count, flags, rows, first...  20.5 us
    pallas_call x12, Pallas kernels, pick(): pl.pallas_call(functools.partial(pick_kernel, choices, len(operands)), gr...  8.89 us
    reduce_sum x4, other arithmetic, shards(): degree.append(jnp.sum(part, axis=1, dtype=jnp.float32))  5.86 us
    ppermute x1, waiting for transfers between devices, shards(): lax.ppermute(jnp.concatenate(helped, axis=0), 'row', pairs({1: 0, 5: 4}))  5.28 us
    pallas_call x1, Pallas kernels, lend(): pl.pallas_call(functools.partial(lend_kernel, sizes, first, depth), in_sp...  4.98 us
    pallas_call x4, Pallas kernels, help_corner(): pl.pallas_call(functools.partial(help_kernel, rows, first), grid_spec=plt...  3.64 us
  transfers between devices with their start and end apart: 31, of which 10 were waited for; matrix products, arithmetic and copies ran while one was open for 5% of the time, Pallas kernels for 29%

profile of v9, /device:TPU:0, one launch (start us, length us, event | category | flops | bytes accessed | tf_op | source)
XLA Modules:
  0.0 129.9 jit_solution(10887476486501136018)
XLA Ops:
  0.6 2.4 %dynamic-slice_bitcast_fusion = (bf16[1024,384]{1,0:T(8,128)(2,1)S(1)}, bf16[1024,384]{1,0:T(8,128)(2,1)}) fusion(bf16[2,1024,384]{2,1,0:T(8,128)(2,1)} %param.5, s32[]{:T(128)S(6)} %select_n.12, s32[]{:T(128)S(6)} %select_n.11), kind=kLoop, calls=%fused_computation.4 | loop fusion | bytes 3145736 | tf_op jit(solution)/shard_map/jit(dynamic_index_in_dim)/squeeze | solution.py:343
  3.5 2.6 %collective-permute-start.2 = (bf16[1024,384]{1,0:T(8,128)(2,1)S(1)}, bf16[1024,384]{1,0:T(8,128)(2,1)S(1)}, u32[]{:S(2)}, u32[]{:S(2)}) collective-permute-start(bf16[1024,384]{1,0:T(8,128)(2,1)S(1)} %get-tuple-element.121.refs_1_.refs_2_), channel_id=1, source_target_pairs={{0,4},{3,7},{4,8},{7,11},{8,12},{11,15},{12,14},{15,13},{14,10},{1... | collective-permute-start | bytes 2359304 | tf_op jit(solution)/shard_map/ppermute | solution.py:369
  6.8 5.0 %lend.1 = (bf16[192,4096]{1,0:T(8,128)(2,1)S(1)}, bf16[192,4096]{1,0:T(8,128)(2,1)S(1)}, bf16[192,4096]{1,0:T(8,128)(2,1)S(1)}, bf16[192,4096]{1,0:T(8,128)(2,1)...) custom-call(s32[56]{0:T(128)S(1)} %fusion.2.where, ...), custom_call_target="tpu_custom_call" | custom-call | bytes 1024 | tf_op jit(solution)/shard_map/lend/pallas_call | solution.py:103
  11.8 1.1 copy-done.2
  12.9 1.1 copy-done.4
  14.2 1.5 %collective-permute-start.1 = (bf16[1024,384]{1,0:T(8,128)(2,1)}, bf16[1024,384]{1,0:T(8,128)(2,1)S(1)}, u32[]{:S(2)}, u32[]{:S(2)}) collective-permute-start(bf16[1024,384]{1,0:T(8,128)(2,1)} %collective-permute-done.refs_2_.refs_1_), channel_id=1, source_target_pairs={{0,4},{3,7},{4,8},{7,11},{8,12},{11,15},{12,14},{15,13},{14,10},{1... | collective-permute-start | bytes 2359304 | tf_op jit(solution)/shard_map/ppermute | solution.py:369
  16.5 1.7 %pick.12 = bf16[1024,384]{1,0:T(8,128)(2,1)S(1)} custom-call(s32[56]{0:T(128)S(1)} %fusion.2.where, bf16[1024,384]{1,0:T(8,128)(2,1)S(1)} %collective-permute-done.2.refs_0_.refs_2_, bf16[1024,384]{1,0:T(8,128)(2,1)} %get-tuple-element.215.refs_1_), custom_call_target="tpu_custom_call" | custom-call | bytes 1024 | tf_op jit(solution)/shard_map/pick/pallas_call | solution.py:197
  18.3 2.1 %collective-permute-start.6 = (bf16[1024,384]{1,0:T(8,128)(2,1)S(1)}, bf16[1024,384]{1,0:T(8,128)(2,1)S(1)}, u32[]{:S(2)}, u32[]{:S(2)}) collective-permute-start(bf16[1024,384]{1,0:T(8,128)(2,1)S(1)} %pick.12), channel_id=1, source_target_pairs={{0,4},{3,7},{4,8},{7,11},{8,12},{11,15},{12,14},{15,13},{14,10},{1... | collective-permute-start | bytes 2359304 | tf_op jit(solution)/shard_map/ppermute | solution.py:369
  20.4 6.0 %collective-permute-done.1.refs_0_.refs_2_ = bf16[1024,384]{1,0:T(8,128)(2,1)S(1)} collective-permute-done((bf16[1024,384]{1,0:T(8,128)(2,1)}, bf16[1024,384]{1,0:T(8,128)(2,1)S(1)}, u32[]{:S(2)}, u32[]{:S(2)}) %collective-permute-start.1) | collective-permute-done | bytes 786464 | tf_op jit(solution)/shard_map/ppermute | solution.py:369
  26.4 2.4 %convert_reduce_fusion.3 = f32[192]{0:T(256)S(1)} fusion(bf16[192,32768]{1,0:T(8,128)(2,1)} %refs_0_.21), kind=kLoop, calls=%fused_computation.3 | loop fusion | flops 3145536 | bytes 3146496 | tf_op jit(solution)/shard_map/reduce_sum | solution.py:404
  28.8 0.7 collective-permute-start.5
  30.2 2.1 %collective-permute-start.4 = (bf16[1024,384]{1,0:T(8,128)(2,1)S(1)}, bf16[1024,384]{1,0:T(8,128)(2,1)S(1)}, u32[]{:S(2)}, u32[]{:S(2)}) collective-permute-start(bf16[1024,384]{1,0:T(8,128)(2,1)S(1)} %pick.13), channel_id=1, source_target_pairs={{0,4},{3,7},{4,8},{7,11},{8,12},{11,15},{12,14},{15,13},{14,10},{1... | collective-permute-start | bytes 2359304 | tf_op jit(solution)/shard_map/ppermute | solution.py:369
  32.3 2.4 %convert_reduce_fusion.2 = f32[192]{0:T(256)S(1)} fusion(bf16[192,32768]{1,0:T(8,128)(2,1)} %refs_0_.21), kind=kLoop, calls=%fused_computation.2 | loop fusion | flops 3145536 | bytes 3146496 | tf_op jit(solution)/shard_map/reduce_sum | solution.py:404
  36.9 4.5 %collective-permute-start.11 = (bf16[1024,384]{1,0:T(8,128)(2,1)S(1)}, bf16[1024,384]{1,0:T(8,128)(2,1)S(1)}, u32[]{:S(2)}, u32[]{:S(2)}) collective-permute-start(bf16[1024,384]{1,0:T(8,128)(2,1)S(1)} %pick.15), channel_id=1, source_target_pairs={{0,4},{3,7},{4,8},{7,11},{8,12},{11,15},{12,14},{15,13},{14,10},{1... | collective-permute-start | bytes 2359304 | tf_op jit(solution)/shard_map/ppermute | solution.py:369
  42.2 1.1 collective-permute-done.4.refs_0_.refs_4_
  43.3 1.0 collective-permute-start.18
  47.5 4.2 %collective-permute-done.11.refs_1_.refs_0_.refs_4_ = bf16[1024,384]{1,0:T(8,128)(2,1)S(1)} collective-permute-done((bf16[1024,384]{1,0:T(8,128)(2,1)S(1)}, bf16[1024,384]{1,0:T(8,128)(2,1)S(1)}, u32[]{:S(2)}, u32[]{:S(2)}) %collective-permute-start.11) | collective-permute-done | bytes 786464 | tf_op jit(solution)/shard_map/ppermute | solution.py:369
  51.7 2.7 %collective-permute-start.9 = (bf16[1024,384]{1,0:T(8,128)(2,1)S(1)}, bf16[1024,384]{1,0:T(8,128)(2,1)S(1)}, u32[]{:S(2)}, u32[]{:S(2)}) collective-permute-start(bf16[1024,384]{1,0:T(8,128)(2,1)S(1)} %pick.17), channel_id=1, source_target_pairs={{0,4},{3,7},{4,8},{7,11},{8,12},{11,15},{12,14},{15,13},{14,10},{1... | collective-permute-start | bytes 2359304 | tf_op jit(solution)/shard_map/ppermute | solution.py:369
  55.5 2.4 %collective-permute-start.16 = (bf16[1024,384]{1,0:T(8,128)(2,1)S(1)}, bf16[1024,384]{1,0:T(8,128)(2,1)S(1)}, u32[]{:S(2)}, u32[]{:S(2)}) collective-permute-start(bf16[1024,384]{1,0:T(8,128)(2,1)S(1)} %pick.19), channel_id=1, source_target_pairs={{0,4},{3,7},{4,8},{7,11},{8,12},{11,15},{12,14},{15,13},{14,10},{1... | collective-permute-start | bytes 2359304 | tf_op jit(solution)/shard_map/ppermute | solution.py:369
  59.3 1.1 absorb.14
  60.5 2.3 %absorb.15 = (f32[192,384]{1,0:T(8,128)S(1)}, f32[208,384]{1,0:T(8,128)S(1)}) custom-call(s32[56]{0:T(128)S(1)} %fusion.2.where, bf16[192,32768]{1,0:T(8,128)(2,1)S(1)} %bitcast.7, bf16[192,4096]{1,0:T(8,128)(2,1)S(1)} %collective-permute-done.13.refs_1_, ...), custom_call_target="tpu_custom_call", output_to_operand_aliasing={{0}: (4, {}), {1}: (5, {})} | custom-call | bytes 1024 | tf_op jit(solution)/shard_map/absorb/pallas_call | solution.py:157
  62.8 1.3 %collective-permute-done.9.refs_1_.refs_0_.refs_4_ = bf16[1024,384]{1,0:T(8,128)(2,1)S(1)} collective-permute-done((bf16[1024,384]{1,0:T(8,128)(2,1)S(1)}, bf16[1024,384]{1,0:T(8,128)(2,1)S(1)}, u32[]{:S(2)}, u32[]{:S(2)}) %collective-permute-start.9) | collective-permute-done | bytes 786464 | tf_op jit(solution)/shard_map/ppermute | solution.py:369
  65.4 1.1 absorb.16
  66.6 9.2 %collective-permute-start.14 = (bf16[1024,384]{1,0:T(8,128)(2,1)S(1)}, bf16[1024,384]{1,0:T(8,128)(2,1)S(1)}, u32[]{:S(2)}, u32[]{:S(2)}) collective-permute-start(bf16[1024,384]{1,0:T(8,128)(2,1)S(1)} %pick.21), channel_id=1, source_target_pairs={{0,4},{3,7},{4,8},{7,11},{8,12},{11,15},{12,14},{15,13},{14,10},{1... | collective-permute-start | bytes 2359304 | tf_op jit(solution)/shard_map/ppermute | solution.py:369
  75.9 1.7 %help.5 = (f32[192,384]{1,0:T(8,128)S(1)}, f32[208,384]{1,0:T(8,128)S(1)}) custom-call(s32[56]{0:T(128)S(1)} %fusion.2.where, bf16[1024,384]{1,0:T(8,128)(2,1)S(1)} %collective-permute-done.9.refs_1_.refs_0_.refs_4_, bf16[1024,384]{1,0:T(8,128)(2,1)} %collective-permute-done.refs_2_.refs_1_, f32[192,384]{1,0:T(8,128)S(1)} %get-tuple-element.122.refs_2_, ...), custom_call_target="tpu_custom_call" | custom-call | bytes 1024 | tf_op jit(solution)/shard_map/help/pallas_call | solution.py:245
  77.7 1.1 absorb.17
  79.5 1.3 %collective-permute-start.21 = (bf16[1024,384]{1,0:T(8,128)(2,1)S(1)}, bf16[1024,384]{1,0:T(8,128)(2,1)S(1)}, u32[]{:S(2)}, u32[]{:S(2)}) collective-permute-start(bf16[1024,384]{1,0:T(8,128)(2,1)S(1)} %pick.22), channel_id=1, source_target_pairs={{0,4},{3,7},{4,8},{7,11},{8,12},{11,15},{12,14},{15,13},{14,10},{1... | collective-permute-start | bytes 2359304 | tf_op jit(solution)/shard_map/ppermute | solution.py:369
  81.5 1.6 %absorb.18 = (f32[192,384]{1,0:T(8,128)S(1)}, f32[208,384]{1,0:T(8,128)S(1)}) custom-call(s32[56]{0:T(128)S(1)} %fusion.2.where, bf16[192,32768]{1,0:T(8,128)(2,1)S(1)} %bitcast.7, bf16[192,32768]{1,0:T(8,128)(2,1)S(1)} %bitcast.7, bf16[192,4096]{1,0:T(8,128)(2,1)S(1)} %collective-permute-done.18.refs_2_.refs_3_, ...), custom_call_target="tpu_custom_call", output_to_operand_aliasing={{0}: (7, {}), {1}: (8, {})} | custom-call | bytes 1024 | tf_op jit(solution)/shard_map/absorb/pallas_call | solution.py:157
  83.1 2.2 %collective-permute-done.14.refs_1_.refs_0_.refs_4_ = bf16[1024,384]{1,0:T(8,128)(2,1)S(1)} collective-permute-done((bf16[1024,384]{1,0:T(8,128)(2,1)S(1)}, bf16[1024,384]{1,0:T(8,128)(2,1)S(1)}, u32[]{:S(2)}, u32[]{:S(2)}) %collective-permute-start.14) | collective-permute-done | bytes 786464 | tf_op jit(solution)/shard_map/ppermute | solution.py:369
  85.4 0.8 help.6
  86.1 1.6 %absorb.19 = (f32[192,384]{1,0:T(8,128)S(1)}, f32[208,384]{1,0:T(8,128)S(1)}) custom-call(s32[56]{0:T(128)S(1)} %fusion.2.where, bf16[192,32768]{1,0:T(8,128)(2,1)S(1)} %bitcast.7, bf16[192,32768]{1,0:T(8,128)(2,1)S(1)} %bitcast.7, bf16[192,4096]{1,0:T(8,128)(2,1)S(1)} %collective-permute-done.18.refs_2_.refs_3_, ...), custom_call_target="tpu_custom_call", output_to_operand_aliasing={{0}: (7, {}), {1}: (8, {})} | custom-call | bytes 1024 | tf_op jit(solution)/shard_map/absorb/pallas_call | solution.py:157
  88.4 4.6 %collective-permute-start.19 = (bf16[1024,384]{1,0:T(8,128)(2,1)S(1)}, bf16[1024,384]{1,0:T(8,128)(2,1)S(1)}, u32[]{:S(2)}, u32[]{:S(2)}) collective-permute-start(bf16[1024,384]{1,0:T(8,128)(2,1)S(1)} %pick.23), channel_id=1, source_target_pairs={{0,4},{3,7},{4,8},{7,11},{8,12},{11,15},{12,14},{15,13},{14,10},{1... | collective-permute-start | bytes 2359304 | tf_op jit(solution)/shard_map/ppermute | solution.py:369
  93.0 0.8 collective-permute-done.21.refs_4_
  95.1 1.6 %absorb.20 = (f32[192,384]{1,0:T(8,128)S(1)}, f32[208,384]{1,0:T(8,128)S(1)}) custom-call(s32[56]{0:T(128)S(1)} %fusion.2.where, bf16[192,32768]{1,0:T(8,128)(2,1)S(1)} %bitcast.7, bf16[192,32768]{1,0:T(8,128)(2,1)S(1)} %bitcast.7, bf16[192,4096]{1,0:T(8,128)(2,1)S(1)} %collective-permute-done.23.refs_2_.refs_3_, ...), custom_call_target="tpu_custom_call", output_to_operand_aliasing={{0}: (7, {}), {1}: (8, {})} | custom-call | bytes 1024 | tf_op jit(solution)/shard_map/absorb/pallas_call | solution.py:157
  96.7 1.6 %absorb.21 = (f32[192,384]{1,0:T(8,128)S(1)}, f32[208,384]{1,0:T(8,128)S(1)}) custom-call(s32[56]{0:T(128)S(1)} %fusion.2.where, bf16[192,32768]{1,0:T(8,128)(2,1)S(1)} %bitcast.7, bf16[192,32768]{1,0:T(8,128)(2,1)S(1)} %bitcast.7, bf16[192,4096]{1,0:T(8,128)(2,1)S(1)} %collective-permute-done.23.refs_2_.refs_3_, ...), custom_call_target="tpu_custom_call", output_to_operand_aliasing={{0}: (7, {}), {1}: (8, {})} | custom-call | bytes 1024 | tf_op jit(solution)/shard_map/absorb/pallas_call | solution.py:157
  98.4 4.5 %collective-permute-start.26 = (bf16[1024,384]{1,0:T(8,128)(2,1)S(1)}, bf16[1024,384]{1,0:T(8,128)(2,1)S(1)}, u32[]{:S(2)}, u32[]{:S(2)}) collective-permute-start(bf16[1024,384]{1,0:T(8,128)(2,1)S(1)} %collective-permute-done.21.refs_4_), channel_id=1, source_target_pairs={{0,4},{3,7},{4,8},{7,11},{8,12},{11,15},{12,14},{15,13},{14,10},{1... | collective-permute-start | bytes 2359304 | tf_op jit(solution)/shard_map/ppermute | solution.py:369
  102.9 1.6 %absorb.22 = (f32[192,384]{1,0:T(8,128)S(1)}, f32[208,384]{1,0:T(8,128)S(1)}) custom-call(s32[56]{0:T(128)S(1)} %fusion.2.where, bf16[192,32768]{1,0:T(8,128)(2,1)S(1)} %bitcast.7, bf16[192,32768]{1,0:T(8,128)(2,1)S(1)} %bitcast.7, bf16[192,4096]{1,0:T(8,128)(2,1)S(1)} %collective-permute-done.24.refs_2_.refs_3_, ...), custom_call_target="tpu_custom_call", output_to_operand_aliasing={{0}: (7, {}), {1}: (8, {})} | custom-call | bytes 1024 | tf_op jit(solution)/shard_map/absorb/pallas_call | solution.py:157
  104.6 1.6 %absorb.23 = (f32[192,384]{1,0:T(8,128)S(1)}, f32[208,384]{1,0:T(8,128)S(1)}) custom-call(s32[56]{0:T(128)S(1)} %fusion.2.where, bf16[192,32768]{1,0:T(8,128)(2,1)S(1)} %bitcast.7, bf16[192,32768]{1,0:T(8,128)(2,1)S(1)} %bitcast.7, bf16[192,4096]{1,0:T(8,128)(2,1)S(1)} %collective-permute-done.24.refs_2_.refs_3_, ...), custom_call_target="tpu_custom_call", output_to_operand_aliasing={{0}: (7, {}), {1}: (8, {})} | custom-call | bytes 1024 | tf_op jit(solution)/shard_map/absorb/pallas_call | solution.py:157
  106.2 4.0 %collective-permute-start.25 = (bf16[1024,384]{1,0:T(8,128)(2,1)S(1)}, bf16[1024,384]{1,0:T(8,128)(2,1)S(1)}, u32[]{:S(2)}, u32[]{:S(2)}) collective-permute-start(bf16[1024,384]{1,0:T(8,128)(2,1)S(1)} %collective-permute-done.19.refs_4_), channel_id=1, source_target_pairs={{0,4},{3,7},{4,8},{7,11},{8,12},{11,15},{12,14},{15,13},{14,10},{1... | collective-permute-start | bytes 2359304 | tf_op jit(solution)/shard_map/ppermute | solution.py:369
  110.2 1.3 collective-permute-start.29
  111.5 1.6 %absorb.24 = (f32[192,384]{1,0:T(8,128)S(1)}, f32[208,384]{1,0:T(8,128)S(1)}) custom-call(s32[56]{0:T(128)S(1)} %fusion.2.where, bf16[192,32768]{1,0:T(8,128)(2,1)S(1)} %bitcast.7, bf16[192,32768]{1,0:T(8,128)(2,1)S(1)} %bitcast.7, bf16[192,4096]{1,0:T(8,128)(2,1)S(1)} %collective-permute-done.27.refs_2_.refs_3_, ...), custom_call_target="tpu_custom_call", output_to_operand_aliasing={{0}: (7, {}), {1}: (8, {})} | custom-call | bytes 1024 | tf_op jit(solution)/shard_map/absorb/pallas_call | solution.py:157
  113.1 1.6 %absorb.25 = (f32[192,384]{1,0:T(8,128)S(1)}, f32[208,384]{1,0:T(8,128)S(1)}) custom-call(s32[56]{0:T(128)S(1)} %fusion.2.where, bf16[192,32768]{1,0:T(8,128)(2,1)S(1)} %bitcast.7, bf16[192,32768]{1,0:T(8,128)(2,1)S(1)} %bitcast.7, bf16[192,4096]{1,0:T(8,128)(2,1)S(1)} %collective-permute-done.27.refs_2_.refs_3_, ...), custom_call_target="tpu_custom_call", output_to_operand_aliasing={{0}: (7, {}), {1}: (8, {})} | custom-call | bytes 1024 | tf_op jit(solution)/shard_map/absorb/pallas_call | solution.py:157
  114.7 1.1 absorb.26
  115.9 5.0 %collective-permute-done.25.refs_2_ = bf16[1024,384]{1,0:T(8,128)(2,1)S(1)} collective-permute-done((bf16[1024,384]{1,0:T(8,128)(2,1)S(1)}, bf16[1024,384]{1,0:T(8,128)(2,1)S(1)}, u32[]{:S(2)}, u32[]{:S(2)}) %collective-permute-start.25) | collective-permute-done | bytes 786464 | tf_op jit(solution)/shard_map/ppermute | solution.py:369
  120.9 1.1 absorb.27
  122.0 5.3 %collective-permute-done.29 = f32[400,384]{1,0:T(8,128)S(1)} collective-permute-done((f32[400,384]{1,0:T(8,128)S(1)}, f32[400,384]{1,0:T(8,128)S(1)}, u32[]{:S(2)}, u32[]{:S(2)}) %collective-permute-start.29) | collective-permute-done | bytes 614432 | tf_op jit(solution)/shard_map/ppermute | solution.py:385
  127.4 1.6 %collective-permute-done.30 = f32[208,384]{1,0:T(8,128)S(1)} collective-permute-done((f32[208,384]{1,0:T(8,128)S(1)}, f32[208,384]{1,0:T(8,128)S(1)}, u32[]{:S(2)}, u32[]{:S(2)}) %collective-permute-start.30) | collective-permute-done | bytes 319520 | tf_op jit(solution)/shard_map/ppermute | solution.py:316
  129.0 0.9 fusion
  (95 shorter events, 16.6 us)
Async XLA Ops:
  3.0 11.2 %collective-permute-start = (bf16[1024,384]{1,0:T(8,128)(2,1)}, bf16[1024,384]{1,0:T(8,128)(2,1)}, u32[]{:S(2)}, u32[]{:S(2)}) collective-permute-start(bf16[1024,384]{1,0:T(8,128)(2,1)} %get-tuple-element.215.refs_1_), channel_id=1, source_target_pairs={{0,1},{1,0},{2,3},{3,2},{4,5},{5,4},{6,7},{7,6},{8,9},{9,8},{10,11... | collective-permute-start | bytes 2359304 | tf_op jit(solution)/shard_map/ppermute | solution.py:316
  3.5 13.0 %collective-permute-start.2 = (bf16[1024,384]{1,0:T(8,128)(2,1)S(1)}, bf16[1024,384]{1,0:T(8,128)(2,1)S(1)}, u32[]{:S(2)}, u32[]{:S(2)}) collective-permute-start(bf16[1024,384]{1,0:T(8,128)(2,1)S(1)} %get-tuple-element.121.refs_1_.refs_2_), channel_id=1, source_target_pairs={{0,4},{3,7},{4,8},{7,11},{8,12},{11,15},{12,14},{15,13},{14,10},{1... | collective-permute-start | bytes 2359304 | tf_op jit(solution)/shard_map/ppermute | solution.py:369
  6.8 28.8 %slice-start = ((s8[12582912]{0:T(1024)(128)(4,1)}), s8[4194304]{0:T(1024)(128)(4,1)S(1)}, s32[]{:S(2)}) async-start(s8[12582912]{0:T(1024)(128)(4,1)} %bitcast.6), calls=%async_computation | async-start | bytes 8388608
  6.8 28.8 %slice-start.1 = ((s8[12582912]{0:T(1024)(128)(4,1)}), s8[4194304]{0:T(1024)(128)(4,1)S(1)}, s32[]{:S(2)}) async-start(s8[12582912]{0:T(1024)(128)(4,1)} %bitcast.6), calls=%async_computation.1 | async-start | bytes 8388608
  11.8 1.1 copy-start.2
  12.9 1.2 copy-start.4
  14.0 6.3 %copy-start = (bf16[192,4096]{1,0:T(8,128)(2,1)}, bf16[192,4096]{1,0:T(8,128)(2,1)S(1)}, u32[]{:S(2)}) copy-start(bf16[192,4096]{1,0:T(8,128)(2,1)S(1)} %get-tuple-element.194) | copy-start | bytes 4718596
  14.0 6.3 %copy-start.6 = (bf16[192,2048]{1,0:T(8,128)(2,1)}, bf16[192,2048]{1,0:T(8,128)(2,1)S(1)}, u32[]{:S(2)}) copy-start(bf16[192,2048]{1,0:T(8,128)(2,1)S(1)} %get-tuple-element.205) | copy-start | bytes 2359300
  14.0 21.5 %collective-permute-start.8 = (bf16[192,4096]{1,0:T(8,128)(2,1)S(1)}, bf16[192,4096]{1,0:T(8,128)(2,1)S(1)}, u32[]{:S(2)}, u32[]{:S(2)}) collective-permute-start(bf16[192,4096]{1,0:T(8,128)(2,1)S(1)} %get-tuple-element.114), channel_id=1, source_target_pairs={{0,1},{1,0},{2,3},{3,2},{4,5},{5,4},{6,7},{7,6},{8,9},{9,8},{10,11... | collective-permute-start | bytes 4718600 | tf_op jit(solution)/shard_map/ppermute | solution.py:316
  14.2 12.2 %collective-permute-start.1 = (bf16[1024,384]{1,0:T(8,128)(2,1)}, bf16[1024,384]{1,0:T(8,128)(2,1)S(1)}, u32[]{:S(2)}, u32[]{:S(2)}) collective-permute-start(bf16[1024,384]{1,0:T(8,128)(2,1)} %collective-permute-done.refs_2_.refs_1_), channel_id=1, source_target_pairs={{0,4},{3,7},{4,8},{7,11},{8,12},{11,15},{12,14},{15,13},{14,10},{1... | collective-permute-start | bytes 2359304 | tf_op jit(solution)/shard_map/ppermute | solution.py:369
  15.7 13.2 %collective-permute-start.3 = (bf16[1024,384]{1,0:T(8,128)(2,1)S(1)}, bf16[1024,384]{1,0:T(8,128)(2,1)S(1)}, u32[]{:S(2)}, u32[]{:S(2)}) collective-permute-start(bf16[1024,384]{1,0:T(8,128)(2,1)S(1)} %get-tuple-element.121.refs_1_.refs_2_), channel_id=1, source_target_pairs={{0,1},{1,0},{2,3},{3,2},{4,5},{5,4},{6,7},{7,6},{8,9},{9,8},{10,11... | collective-permute-start | bytes 2359304 | tf_op jit(solution)/shard_map/ppermute | solution.py:316
  15.8 14.3 %collective-permute-start.7 = (bf16[1024,384]{1,0:T(8,128)(2,1)S(1)}, bf16[1024,384]{1,0:T(8,128)(2,1)S(1)}, u32[]{:S(2)}, u32[]{:S(2)}) collective-permute-start(bf16[1024,384]{1,0:T(8,128)(2,1)S(1)} %get-tuple-element.121.refs_1_.refs_2_), channel_id=1, source_target_pairs={{6,4},{5,7},{8,10},{11,9},{22,20},{21,23},{24,26},{27,25}} | collective-permute-start | bytes 2359304 | tf_op jit(solution)/shard_map/ppermute | solution.py:369
  18.3 16.5 %collective-permute-start.6 = (bf16[1024,384]{1,0:T(8,128)(2,1)S(1)}, bf16[1024,384]{1,0:T(8,128)(2,1)S(1)}, u32[]{:S(2)}, u32[]{:S(2)}) collective-permute-start(bf16[1024,384]{1,0:T(8,128)(2,1)S(1)} %pick.12), channel_id=1, source_target_pairs={{0,4},{3,7},{4,8},{7,11},{8,12},{11,15},{12,14},{15,13},{14,10},{1... | collective-permute-start | bytes 2359304 | tf_op jit(solution)/shard_map/ppermute | solution.py:369
  20.4 15.2 %slice-start.2 = ((s8[12582912]{0:T(1024)(128)(4,1)}), s8[4194304]{0:T(1024)(128)(4,1)S(1)}, s32[]{:S(2)}) async-start(s8[12582912]{0:T(1024)(128)(4,1)} %bitcast.6), calls=%async_computation.2 | async-start | bytes 8388608
  26.4 29.1 %collective-permute-start.13 = (bf16[192,4096]{1,0:T(8,128)(2,1)S(1)}, bf16[192,4096]{1,0:T(8,128)(2,1)S(1)}, u32[]{:S(2)}, u32[]{:S(2)}) collective-permute-start(bf16[192,4096]{1,0:T(8,128)(2,1)S(1)} %get-tuple-element.131), channel_id=1, source_target_pairs={{0,1},{1,0},{2,3},{3,2},{4,5},{5,4},{6,7},{7,6},{8,9},{9,8},{10,11... | collective-permute-start | bytes 4718600 | tf_op jit(solution)/shard_map/ppermute | solution.py:316
  28.8 12.6 %collective-permute-start.5 = (bf16[1024,384]{1,0:T(8,128)(2,1)}, bf16[1024,384]{1,0:T(8,128)(2,1)S(1)}, u32[]{:S(2)}, u32[]{:S(2)}) collective-permute-start(bf16[1024,384]{1,0:T(8,128)(2,1)} %collective-permute-done.refs_2_.refs_1_), channel_id=1, source_target_pairs={{6,4},{5,7},{8,10},{11,9},{22,20},{21,23},{24,26},{27,25}} | collective-permute-start | bytes 2359304 | tf_op jit(solution)/shard_map/ppermute | solution.py:369
  30.2 13.1 %collective-permute-start.4 = (bf16[1024,384]{1,0:T(8,128)(2,1)S(1)}, bf16[1024,384]{1,0:T(8,128)(2,1)S(1)}, u32[]{:S(2)}, u32[]{:S(2)}) collective-permute-start(bf16[1024,384]{1,0:T(8,128)(2,1)S(1)} %pick.13), channel_id=1, source_target_pairs={{0,4},{3,7},{4,8},{7,11},{8,12},{11,15},{12,14},{15,13},{14,10},{1... | collective-permute-start | bytes 2359304 | tf_op jit(solution)/shard_map/ppermute | solution.py:369
  34.8 12.0 %collective-permute-start.12 = (bf16[1024,384]{1,0:T(8,128)(2,1)S(1)}, bf16[1024,384]{1,0:T(8,128)(2,1)S(1)}, u32[]{:S(2)}, u32[]{:S(2)}) collective-permute-start(bf16[1024,384]{1,0:T(8,128)(2,1)S(1)} %collective-permute-done.2.refs_0_.refs_2_), channel_id=1, source_target_pairs={{6,4},{5,7},{8,10},{11,9},{22,20},{21,23},{24,26},{27,25}} | collective-permute-start | bytes 2359304 | tf_op jit(solution)/shard_map/ppermute | solution.py:369
  36.9 14.8 %collective-permute-start.11 = (bf16[1024,384]{1,0:T(8,128)(2,1)S(1)}, bf16[1024,384]{1,0:T(8,128)(2,1)S(1)}, u32[]{:S(2)}, u32[]{:S(2)}) collective-permute-start(bf16[1024,384]{1,0:T(8,128)(2,1)S(1)} %pick.15), channel_id=1, source_target_pairs={{0,4},{3,7},{4,8},{7,11},{8,12},{11,15},{12,14},{15,13},{14,10},{1... | collective-permute-start | bytes 2359304 | tf_op jit(solution)/shard_map/ppermute | solution.py:369
  41.5 16.5 %collective-permute-start.10 = (bf16[1024,384]{1,0:T(8,128)(2,1)S(1)}, bf16[1024,384]{1,0:T(8,128)(2,1)S(1)}, u32[]{:S(2)}, u32[]{:S(2)}) collective-permute-start(bf16[1024,384]{1,0:T(8,128)(2,1)S(1)} %collective-permute-done.1.refs_0_.refs_2_), channel_id=1, source_target_pairs={{6,4},{5,7},{8,10},{11,9},{22,20},{21,23},{24,26},{27,25}} | collective-permute-start | bytes 2359304 | tf_op jit(solution)/shard_map/ppermute | solution.py:369
  43.3 36.2 %collective-permute-start.18 = (bf16[192,4096]{1,0:T(8,128)(2,1)S(1)}, bf16[192,4096]{1,0:T(8,128)(2,1)S(1)}, u32[]{:S(2)}, u32[]{:S(2)}) collective-permute-start(bf16[192,4096]{1,0:T(8,128)(2,1)S(1)} %get-tuple-element.155), channel_id=1, source_target_pairs={{0,1},{1,0},{2,3},{3,2},{4,5},{5,4},{6,7},{7,6},{8,9},{9,8},{10,11... | collective-permute-start | bytes 4718600 | tf_op jit(solution)/shard_map/ppermute | solution.py:316
  46.8 19.8 %collective-permute-start.17 = (bf16[1024,384]{1,0:T(8,128)(2,1)S(1)}, bf16[1024,384]{1,0:T(8,128)(2,1)S(1)}, u32[]{:S(2)}, u32[]{:S(2)}) collective-permute-start(bf16[1024,384]{1,0:T(8,128)(2,1)S(1)} %collective-permute-done.6.refs_0_.refs_4_), channel_id=1, source_target_pairs={{4,6},{7,5},{10,8},{9,11},{20,22},{23,21},{26,24},{25,27}} | collective-permute-start | bytes 2359304 | tf_op jit(solution)/shard_map/ppermute | solution.py:369
  51.7 12.4 %collective-permute-start.9 = (bf16[1024,384]{1,0:T(8,128)(2,1)S(1)}, bf16[1024,384]{1,0:T(8,128)(2,1)S(1)}, u32[]{:S(2)}, u32[]{:S(2)}) collective-permute-start(bf16[1024,384]{1,0:T(8,128)(2,1)S(1)} %pick.17), channel_id=1, source_target_pairs={{0,4},{3,7},{4,8},{7,11},{8,12},{11,15},{12,14},{15,13},{14,10},{1... | collective-permute-start | bytes 2359304 | tf_op jit(solution)/shard_map/ppermute | solution.py:369
  54.9 3.1 %copy-start.5 = (bf16[192,4096]{1,0:T(8,128)(2,1)S(1)}, bf16[192,4096]{1,0:T(8,128)(2,1)}, u32[]{:S(2)}) copy-start(bf16[192,4096]{1,0:T(8,128)(2,1)} %copy-done.4) | copy-start | bytes 4718596
  55.5 20.3 %collective-permute-start.16 = (bf16[1024,384]{1,0:T(8,128)(2,1)S(1)}, bf16[1024,384]{1,0:T(8,128)(2,1)S(1)}, u32[]{:S(2)}, u32[]{:S(2)}) collective-permute-start(bf16[1024,384]{1,0:T(8,128)(2,1)S(1)} %pick.19), channel_id=1, source_target_pairs={{0,4},{3,7},{4,8},{7,11},{8,12},{11,15},{12,14},{15,13},{14,10},{1... | collective-permute-start | bytes 2359304 | tf_op jit(solution)/shard_map/ppermute | solution.py:369
  58.0 30.4 %collective-permute-start.23 = (bf16[192,4096]{1,0:T(8,128)(2,1)S(1)}, bf16[192,4096]{1,0:T(8,128)(2,1)S(1)}, u32[]{:S(2)}, u32[]{:S(2)}) collective-permute-start(bf16[192,4096]{1,0:T(8,128)(2,1)S(1)} %copy-done.5), channel_id=1, source_target_pairs={{0,1},{1,0},{2,3},{3,2},{4,5},{5,4},{6,7},{7,6},{8,9},{9,8},{10,11... | collective-permute-start | bytes 4718600 | tf_op jit(solution)/shard_map/ppermute | solution.py:316
  64.1 16.7 %collective-permute-start.15 = (bf16[1024,384]{1,0:T(8,128)(2,1)S(1)}, bf16[1024,384]{1,0:T(8,128)(2,1)S(1)}, u32[]{:S(2)}, u32[]{:S(2)}) collective-permute-start(bf16[1024,384]{1,0:T(8,128)(2,1)S(1)} %collective-permute-done.4.refs_0_.refs_4_), channel_id=1, source_target_pairs={{4,6},{7,5},{10,8},{9,11},{20,22},{23,21},{26,24},{25,27}} | collective-permute-start | bytes 2359304 | tf_op jit(solution)/shard_map/ppermute | solution.py:369
  65.4 10.4 %copy-start.3 = (bf16[192,4096]{1,0:T(8,128)(2,1)S(1)}, bf16[192,4096]{1,0:T(8,128)(2,1)}, u32[]{:S(2)}) copy-start(bf16[192,4096]{1,0:T(8,128)(2,1)} %copy-done.2) | copy-start | bytes 4718596
  66.6 18.7 %collective-permute-start.14 = (bf16[1024,384]{1,0:T(8,128)(2,1)S(1)}, bf16[1024,384]{1,0:T(8,128)(2,1)S(1)}, u32[]{:S(2)}, u32[]{:S(2)}) collective-permute-start(bf16[1024,384]{1,0:T(8,128)(2,1)S(1)} %pick.21), channel_id=1, source_target_pairs={{0,4},{3,7},{4,8},{7,11},{8,12},{11,15},{12,14},{15,13},{14,10},{1... | collective-permute-start | bytes 2359304 | tf_op jit(solution)/shard_map/ppermute | solution.py:369
  75.9 22.5 %collective-permute-start.24 = (bf16[192,4096]{1,0:T(8,128)(2,1)S(1)}, bf16[192,4096]{1,0:T(8,128)(2,1)S(1)}, u32[]{:S(2)}, u32[]{:S(2)}) collective-permute-start(bf16[192,4096]{1,0:T(8,128)(2,1)S(1)} %copy-done.3), channel_id=1, source_target_pairs={{0,1},{1,0},{2,3},{3,2},{4,5},{5,4},{6,7},{7,6},{8,9},{9,8},{10,11... | collective-permute-start | bytes 4718600 | tf_op jit(solution)/shard_map/ppermute | solution.py:316
  79.5 5.9 %copy-start.1 = (bf16[192,4096]{1,0:T(8,128)(2,1)S(1)}, bf16[192,4096]{1,0:T(8,128)(2,1)}, u32[]{:S(2)}) copy-start(bf16[192,4096]{1,0:T(8,128)(2,1)} %copy-done) | copy-start | bytes 4718596
  79.5 14.3 %collective-permute-start.21 = (bf16[1024,384]{1,0:T(8,128)(2,1)S(1)}, bf16[1024,384]{1,0:T(8,128)(2,1)S(1)}, u32[]{:S(2)}, u32[]{:S(2)}) collective-permute-start(bf16[1024,384]{1,0:T(8,128)(2,1)S(1)} %pick.22), channel_id=1, source_target_pairs={{0,4},{3,7},{4,8},{7,11},{8,12},{11,15},{12,14},{15,13},{14,10},{1... | collective-permute-start | bytes 2359304 | tf_op jit(solution)/shard_map/ppermute | solution.py:369
  80.8 17.5 %collective-permute-start.22 = (bf16[1024,384]{1,0:T(8,128)(2,1)S(1)}, bf16[1024,384]{1,0:T(8,128)(2,1)S(1)}, u32[]{:S(2)}, u32[]{:S(2)}) collective-permute-start(bf16[1024,384]{1,0:T(8,128)(2,1)S(1)} %collective-permute-done.16.refs_1_.refs_0_.refs_4_), channel_id=1, source_target_pairs={{6,4},{5,7},{8,10},{11,9},{22,20},{21,23},{24,26},{27,25}} | collective-permute-start | bytes 2359304 | tf_op jit(solution)/shard_map/ppermute | solution.py:369
  85.3 26.1 %collective-permute-start.27 = (bf16[192,4096]{1,0:T(8,128)(2,1)S(1)}, bf16[192,4096]{1,0:T(8,128)(2,1)S(1)}, u32[]{:S(2)}, u32[]{:S(2)}) collective-permute-start(bf16[192,4096]{1,0:T(8,128)(2,1)S(1)} %copy-done.1), channel_id=1, source_target_pairs={{0,1},{1,0},{2,3},{3,2},{4,5},{5,4},{6,7},{7,6},{8,9},{9,8},{10,11... | collective-permute-start | bytes 4718600 | tf_op jit(solution)/shard_map/ppermute | solution.py:316
  88.4 17.8 %collective-permute-start.19 = (bf16[1024,384]{1,0:T(8,128)(2,1)S(1)}, bf16[1024,384]{1,0:T(8,128)(2,1)S(1)}, u32[]{:S(2)}, u32[]{:S(2)}) collective-permute-start(bf16[1024,384]{1,0:T(8,128)(2,1)S(1)} %pick.23), channel_id=1, source_target_pairs={{0,4},{3,7},{4,8},{7,11},{8,12},{11,15},{12,14},{15,13},{14,10},{1... | collective-permute-start | bytes 2359304 | tf_op jit(solution)/shard_map/ppermute | solution.py:369
  93.8 12.4 %collective-permute-start.20 = (bf16[1024,384]{1,0:T(8,128)(2,1)S(1)}, bf16[1024,384]{1,0:T(8,128)(2,1)S(1)}, u32[]{:S(2)}, u32[]{:S(2)}) collective-permute-start(bf16[1024,384]{1,0:T(8,128)(2,1)S(1)} %collective-permute-done.14.refs_1_.refs_0_.refs_4_), channel_id=1, source_target_pairs={{6,4},{5,7},{8,10},{11,9},{22,20},{21,23},{24,26},{27,25}} | collective-permute-start | bytes 2359304 | tf_op jit(solution)/shard_map/ppermute | solution.py:369
  96.7 1.6 %copy-start.7 = (bf16[192,2048]{1,0:T(8,128)(2,1)S(1)}, bf16[192,2048]{1,0:T(8,128)(2,1)}, u32[]{:S(2)}) copy-start(bf16[192,2048]{1,0:T(8,128)(2,1)} %copy-done.6) | copy-start | bytes 2359300
  98.3 16.4 %collective-permute-start.28 = (bf16[192,2048]{1,0:T(8,128)(2,1)S(1)}, bf16[192,2048]{1,0:T(8,128)(2,1)S(1)}, u32[]{:S(2)}, u32[]{:S(2)}) collective-permute-start(bf16[192,2048]{1,0:T(8,128)(2,1)S(1)} %copy-done.7), channel_id=1, source_target_pairs={{0,1},{1,0},{2,3},{3,2},{4,5},{5,4},{6,7},{7,6},{8,9},{9,8},{10,11... | collective-permute-start | bytes 2359304 | tf_op jit(solution)/shard_map/ppermute | solution.py:316
  98.4 16.3 %collective-permute-start.26 = (bf16[1024,384]{1,0:T(8,128)(2,1)S(1)}, bf16[1024,384]{1,0:T(8,128)(2,1)S(1)}, u32[]{:S(2)}, u32[]{:S(2)}) collective-permute-start(bf16[1024,384]{1,0:T(8,128)(2,1)S(1)} %collective-permute-done.21.refs_4_), channel_id=1, source_target_pairs={{0,4},{3,7},{4,8},{7,11},{8,12},{11,15},{12,14},{15,13},{14,10},{1... | collective-permute-start | bytes 2359304 | tf_op jit(solution)/shard_map/ppermute | solution.py:369
  106.2 14.7 %collective-permute-start.25 = (bf16[1024,384]{1,0:T(8,128)(2,1)S(1)}, bf16[1024,384]{1,0:T(8,128)(2,1)S(1)}, u32[]{:S(2)}, u32[]{:S(2)}) collective-permute-start(bf16[1024,384]{1,0:T(8,128)(2,1)S(1)} %collective-permute-done.19.refs_4_), channel_id=1, source_target_pairs={{0,4},{3,7},{4,8},{7,11},{8,12},{11,15},{12,14},{15,13},{14,10},{1... | collective-permute-start | bytes 2359304 | tf_op jit(solution)/shard_map/ppermute | solution.py:369
  110.2 17.1 %collective-permute-start.29 = (f32[400,384]{1,0:T(8,128)S(1)}, f32[400,384]{1,0:T(8,128)S(1)}, u32[]{:S(2)}, u32[]{:S(2)}) collective-permute-start(f32[400,384]{1,0:T(8,128)S(1)} %pad_maximum_fusion), channel_id=1, source_target_pairs={{4,0},{7,3},{10,14},{9,13},{20,16},{23,19},{26,30},{25,29}} | collective-permute-start | bytes 1843208 | tf_op jit(solution)/shard_map/ppermute | solution.py:385
  120.9 8.2 %copy-start.8 = (bf16[192,384]{1,0:T(8,128)(2,1)S(1)}, bf16[192,384]{1,0:T(8,128)(2,1)}, u32[]{:S(2)}) copy-start(bf16[192,384]{1,0:T(8,128)(2,1)} %param.6) | copy-start | bytes 442372
  127.3 1.7 %collective-permute-start.30 = (f32[208,384]{1,0:T(8,128)S(1)}, f32[208,384]{1,0:T(8,128)S(1)}, u32[]{:S(2)}, u32[]{:S(2)}) collective-permute-start(f32[208,384]{1,0:T(8,128)S(1)} %slice_add_fusion), channel_id=1, source_target_pairs={{0,1},{1,0},{2,3},{3,2},{4,5},{5,4},{6,7},{7,6},{8,9},{9,8},{10,11... | collective-permute-start | bytes 958472 | tf_op jit(solution)/shard_map/ppermute | solution.py:316
  127.4 2.5 %copy-start.9 = (f32[192]{0:T(256)}, f32[192]{0:T(256)S(1)}, u32[]{:S(2)}) copy-start(f32[192]{0:T(256)S(1)} %add_add_fusion) | copy-start | bytes 2308

commit v10 on v9

--- a/solution.py
+++ b/solution.py
@@ -12,15 +12,15 @@
 ONES = 16
 SHIPS = True
 SLOTS = 1
-MOST = 2
-ABSORB_FROM = 3
+MOST = 1
+ABSORB_FROM = 2
 PER_LENT = 4
 EARLY = 1
 REST_AT = 2
 DEGREE_PARTS = 4
 DEGREE_AT = 1
 HELP_AT = (3, 4)
-LEND_AFTER = 0
+LEND_AFTER = 1
 TILE = 128
 SHORT = pl.CostEstimate(flops=0, bytes_accessed=1024, transcendentals=0)
 VMEM_LIMIT = 10 * 1024 * 1024
@@ -51,9 +51,9 @@
         main[1][3] = ("own", 1)
         main[2][0] = ("ship", 0)
         main[3][0] = ("ship", 1)
-        main[3][1] = ("ch", 2)
-        main[4][1] = ("ch", 3)
-        for r, source in ((1, ("own", 0)), (2, ("main", 1)), (3, ("main", 2)), (4, ("main", 4))):
+        main[3][1] = ("ch", 1)
+        main[4][1] = ("ch", 2)
+        for r, source in ((0, ("own", 0)), (1, ("main", 1)), (2, ("main", 2)), (4, ("main", 4))):
             turns[r]["ch"] = [source] * 4
     return turns
 
@@ -61,7 +61,7 @@
 def make_route(chips, port, r):
     if port == "main":
         return {p: (p + 1) % chips for p in range(chips)}
-    return {1: 6, 5: 2} if r == 4 else {6: 1, 2: 5}
+    return {1: 6, 5: 2} if r == 3 else {6: 1, 2: 5}
 
 
 def trace_blocks(chips, turns):
@@ -378,7 +378,7 @@
                 past.append(done)
                 due.append((at, j))
                 if ships and at in HELP_AT:
-                    beside = slab["own", 0] if at == HELP_AT[0] else slab["ch", 2]
+                    beside = slab["own", 0] if at == HELP_AT[0] else slab["ch", 1]
                     helped = help_corner(where, slab["main", at][j], tie(beside[j], gate), rows, helped)
                     done.append(helped)
                     if (at, j) == (HELP_AT[1], 1):

time: 131 us -> 134 us (1.023)
  waiting for transfers between devices: 27.7 us -> 15.6 us
  Pallas kernels: 38.1 us -> 44.2 us
  starting transfers between devices: 50.4 us -> 55.7 us
  local copies, waits for them, and re-layouts: 5.68 us -> 8.14 us
    ppermute x20, waiting for transfers between devices: 20.8 us -> 10.5 us  [shards(): lax.ppermute(piece, 'row', pairs(make_route(chips, port, r)))]
    ppermute x20, starting transfers between devices: 47.1 us -> 52.6 us  [shards(): lax.ppermute(piece, 'row', pairs(make_route(chips, port, r)))]
    unnamed x38, local copies, waits for them, and re-layouts: 2.59 us -> 5.91 us
    pallas_call x14, Pallas kernels: 20.5 us -> 23.3 us  [absorb(): pl.pallas_call(functools.partial(absorb_kernel, count, flags, rows, first...]
    pallas_call x12, Pallas kernels: 8.89 us -> 11.1 us  [pick(): pl.pallas_call(functools.partial(pick_kernel, choices, len(operands)), gr...]
    ppermute x1, waiting for transfers between devices: 5.28 us -> 3.56 us  [shards(): lax.ppermute(jnp.concatenate(helped, axis=0), 'row', pairs({1: 0, 5: 4}))]
  transfers between devices with their start and end apart: 31 -> 31, of which waited for: 10 -> 6; matrix products, arithmetic and copies ran while one was open for 5% -> 5% of each run, Pallas kernels for 29% -> 34%
where the time goes in v10:
time: 134 us; the launch traced here: 132 us
  starting transfers between devices  55.7 us (42%)
  Pallas kernels  44.2 us (33%)
  waiting for transfers between devices  15.6 us (12%)
  local copies, waits for them, and re-layouts  8.14 us (6%)
  other arithmetic  6.84 us (5%)
  between operations  1.35 us (1%)
    ppermute x20, starting transfers between devices, shards(): lax.ppermute(piece, 'row', pairs(make_route(chips, port, r)))  52.6 us
    pallas_call x14, Pallas kernels, absorb(): pl.pallas_call(functools.partial(absorb_kernel, count, flags, rows, first...  23.3 us
    pallas_call x12, Pallas kernels, pick(): pl.pallas_call(functools.partial(pick_kernel, choices, len(operands)), gr...  11.1 us
    ppermute x20, waiting for transfers between devices, shards(): lax.ppermute(piece, 'row', pairs(make_route(chips, port, r)))  10.5 us
    unnamed x38, local copies, waits for them, and re-layouts  5.91 us
    reduce_sum x4, other arithmetic, shards(): degree.append(jnp.sum(part, axis=1, dtype=jnp.float32))  5.86 us
    pallas_call x1, Pallas kernels, lend(): pl.pallas_call(functools.partial(lend_kernel, sizes, first, depth), in_sp...  5.05 us
    pallas_call x4, Pallas kernels, help_corner(): pl.pallas_call(functools.partial(help_kernel, rows, first), grid_spec=plt...  4.77 us
  transfers between devices with their start and end apart: 31, of which 6 were waited for; matrix products, arithmetic and copies ran while one was open for 5% of the time, Pallas kernels for 34%

profile of v10, /device:TPU:0, one launch (start us, length us, event | category | flops | bytes accessed | tf_op | source)
XLA Modules:
  0.0 131.9 jit_solution(6751472603777100302)
XLA Ops:
  0.6 1.5 %dynamic-slice_bitcast_fusion = (bf16[1024,384]{1,0:T(8,128)(2,1)S(1)}, bf16[1024,384]{1,0:T(8,128)(2,1)S(1)}) fusion(bf16[2,1024,384]{2,1,0:T(8,128)(2,1)} %param.5, s32[]{:T(128)S(6)} %select_n.12, s32[]{:T(128)S(6)} %select_n.11), kind=kLoop, calls=%fused_computation.4 | loop fusion | bytes 3145736 | tf_op jit(solution)/shard_map/jit(dynamic_index_in_dim)/squeeze | solution.py:343
  2.7 0.9 copy-done
  3.6 2.6 %collective-permute-start.3 = (bf16[1024,384]{1,0:T(8,128)(2,1)S(1)}, bf16[1024,384]{1,0:T(8,128)(2,1)}, u32[]{:S(2)}, u32[]{:S(2)}) collective-permute-start(bf16[1024,384]{1,0:T(8,128)(2,1)S(1)} %get-tuple-element.135.refs_2_.refs_1_), channel_id=1, source_target_pairs={{0,4},{3,7},{4,8},{7,11},{8,12},{11,15},{12,14},{15,13},{14,10},{1... | collective-permute-start | bytes 2359304 | tf_op jit(solution)/shard_map/ppermute | solution.py:369
  6.2 1.5 %collective-permute-start.4 = (bf16[1024,384]{1,0:T(8,128)(2,1)S(1)}, bf16[1024,384]{1,0:T(8,128)(2,1)}, u32[]{:S(2)}, u32[]{:S(2)}) collective-permute-start(bf16[1024,384]{1,0:T(8,128)(2,1)S(1)} %get-tuple-element.135.refs_2_.refs_1_), channel_id=1, source_target_pairs={{6,4},{5,7},{8,10},{11,9},{22,20},{21,23},{24,26},{27,25}} | collective-permute-start | bytes 2359304 | tf_op jit(solution)/shard_map/ppermute | solution.py:369
  8.4 2.0 %collective-permute-start.1 = (bf16[1024,384]{1,0:T(8,128)(2,1)}, bf16[1024,384]{1,0:T(8,128)(2,1)}, u32[]{:S(2)}, u32[]{:S(2)}) collective-permute-start(bf16[1024,384]{1,0:T(8,128)(2,1)} %collective-permute-done.refs_2_.refs_1_), channel_id=1, source_target_pairs={{0,4},{3,7},{4,8},{7,11},{8,12},{11,15},{12,14},{15,13},{14,10},{1... | collective-permute-start | bytes 2359304 | tf_op jit(solution)/shard_map/ppermute | solution.py:369
  11.1 5.0 %lend.1 = (bf16[192,4096]{1,0:T(8,128)(2,1)S(1)}, bf16[192,4096]{1,0:T(8,128)(2,1)S(1)}, bf16[192,4096]{1,0:T(8,128)(2,1)S(1)}, bf16[192,4096]{1,0:T(8,128)(2,1)...) custom-call(s32[56]{0:T(128)S(1)} %fusion.2.where, ...), custom_call_target="tpu_custom_call" | custom-call | bytes 1024 | tf_op jit(solution)/shard_map/lend/pallas_call | solution.py:103
  16.2 1.1 copy-done.4
  17.3 1.1 copy-done.6
  18.5 1.7 %copy-done.1 = bf16[1024,384]{1,0:T(8,128)(2,1)S(1)} copy-done((bf16[1024,384]{1,0:T(8,128)(2,1)S(1)}, bf16[1024,384]{1,0:T(8,128)(2,1)}, u32[]{:S(2)}) %copy-start.1) | copy-done | bytes 786456
  20.2 1.7 %pick.12 = bf16[1024,384]{1,0:T(8,128)(2,1)S(1)} custom-call(s32[56]{0:T(128)S(1)} %fusion.2.where, bf16[1024,384]{1,0:T(8,128)(2,1)} %collective-permute-done.3.refs_0_.refs_4_, bf16[1024,384]{1,0:T(8,128)(2,1)S(1)} %copy-done.1), custom_call_target="tpu_custom_call" | custom-call | bytes 1024 | tf_op jit(solution)/shard_map/pick/pallas_call | solution.py:197
  22.5 7.5 %collective-permute-start.8 = (bf16[1024,384]{1,0:T(8,128)(2,1)S(1)}, bf16[1024,384]{1,0:T(8,128)(2,1)S(1)}, u32[]{:S(2)}, u32[]{:S(2)}) collective-permute-start(bf16[1024,384]{1,0:T(8,128)(2,1)S(1)} %pick.12), channel_id=1, source_target_pairs={{0,4},{3,7},{4,8},{7,11},{8,12},{11,15},{12,14},{15,13},{14,10},{1... | collective-permute-start | bytes 2359304 | tf_op jit(solution)/shard_map/ppermute | solution.py:369
  30.8 2.4 %convert_reduce_fusion.3 = f32[192]{0:T(256)S(1)} fusion(bf16[192,32768]{1,0:T(8,128)(2,1)} %refs_0_.21), kind=kLoop, calls=%fused_computation.3 | loop fusion | flops 3145536 | bytes 3146496 | tf_op jit(solution)/shard_map/reduce_sum | solution.py:404
  33.2 1.7 %pick.13 = bf16[1024,384]{1,0:T(8,128)(2,1)S(1)} custom-call(s32[56]{0:T(128)S(1)} %fusion.2.where, bf16[1024,384]{1,0:T(8,128)(2,1)} %collective-permute-done.1.refs_0_.refs_4_, bf16[1024,384]{1,0:T(8,128)(2,1)S(1)} %collective-permute-done.5.refs_1_), custom_call_target="tpu_custom_call" | custom-call | bytes 1024 | tf_op jit(solution)/shard_map/pick/pallas_call | solution.py:197
  35.6 4.0 %collective-permute-done.8.refs_0_.refs_4_ = bf16[1024,384]{1,0:T(8,128)(2,1)S(1)} collective-permute-done((bf16[1024,384]{1,0:T(8,128)(2,1)S(1)}, bf16[1024,384]{1,0:T(8,128)(2,1)S(1)}, u32[]{:S(2)}, u32[]{:S(2)}) %collective-permute-start.8) | collective-permute-done | bytes 786464 | tf_op jit(solution)/shard_map/ppermute | solution.py:369
  40.3 2.4 %convert_reduce_fusion.2 = f32[192]{0:T(256)S(1)} fusion(bf16[192,32768]{1,0:T(8,128)(2,1)} %refs_0_.21), kind=kLoop, calls=%fused_computation.2 | loop fusion | flops 3145536 | bytes 3146496 | tf_op jit(solution)/shard_map/reduce_sum | solution.py:404
  42.8 0.7 collective-permute-start.15
  44.9 7.0 %collective-permute-start.14 = (bf16[1024,384]{1,0:T(8,128)(2,1)S(1)}, bf16[1024,384]{1,0:T(8,128)(2,1)S(1)}, u32[]{:S(2)}, u32[]{:S(2)}) collective-permute-start(bf16[1024,384]{1,0:T(8,128)(2,1)S(1)} %pick.15), channel_id=1, source_target_pairs={{0,4},{3,7},{4,8},{7,11},{8,12},{11,15},{12,14},{15,13},{14,10},{1... | collective-permute-start | bytes 2359304 | tf_op jit(solution)/shard_map/ppermute | solution.py:369
  51.9 1.1 absorb.14
  53.6 0.7 collective-permute-start.13
  55.6 8.0 %collective-permute-start.12 = (bf16[1024,384]{1,0:T(8,128)(2,1)S(1)}, bf16[1024,384]{1,0:T(8,128)(2,1)S(1)}, u32[]{:S(2)}, u32[]{:S(2)}) collective-permute-start(bf16[1024,384]{1,0:T(8,128)(2,1)S(1)} %pick.17), channel_id=1, source_target_pairs={{0,4},{3,7},{4,8},{7,11},{8,12},{11,15},{12,14},{15,13},{14,10},{1... | collective-permute-start | bytes 2359304 | tf_op jit(solution)/shard_map/ppermute | solution.py:369
  64.8 2.3 %absorb.15 = (f32[192,384]{1,0:T(8,128)S(1)}, f32[208,384]{1,0:T(8,128)S(1)}) custom-call(s32[56]{0:T(128)S(1)} %fusion.2.where, bf16[192,32768]{1,0:T(8,128)(2,1)S(1)} %bitcast.7, bf16[192,4096]{1,0:T(8,128)(2,1)S(1)} %collective-permute-done.11.refs_1_.refs_2_, ...), custom_call_target="tpu_custom_call", output_to_operand_aliasing={{0}: (4, {}), {1}: (5, {})} | custom-call | bytes 1024 | tf_op jit(solution)/shard_map/absorb/pallas_call | solution.py:157
  67.3 1.7 %pick.19 = bf16[1024,384]{1,0:T(8,128)(2,1)S(1)} custom-call(s32[56]{0:T(128)S(1)} %fusion.2.where, bf16[1024,384]{1,0:T(8,128)(2,1)} %collective-permute-done.4.refs_0_.refs_5_.refs_1_, bf16[1024,384]{1,0:T(8,128)(2,1)S(1)} %collective-permute-done.14.refs_1_.refs_0_.refs_4_, bf16[1024,384]{1,0:T(8,128)(2,1)S(1)} %pick.18.refs_2_), custom_call_target="tpu_custom_call" | custom-call | bytes 1024 | tf_op jit(solution)/shard_map/pick/pallas_call | solution.py:197
  70.4 0.8 copy-done.5
  71.7 3.0 %absorb.16 = (f32[192,384]{1,0:T(8,128)S(1)}, f32[208,384]{1,0:T(8,128)S(1)}) custom-call(s32[56]{0:T(128)S(1)} %fusion.2.where, bf16[192,32768]{1,0:T(8,128)(2,1)S(1)} %bitcast.7, bf16[192,32768]{1,0:T(8,128)(2,1)S(1)} %bitcast.7, bf16[192,4096]{1,0:T(8,128)(2,1)S(1)} %collective-permute-done.11.refs_1_.refs_2_, ...), custom_call_target="tpu_custom_call", output_to_operand_aliasing={{0}: (7, {}), {1}: (8, {})} | custom-call | bytes 1024 | tf_op jit(solution)/shard_map/absorb/pallas_call | solution.py:157
  75.4 1.8 %collective-permute-start.17 = (bf16[1024,384]{1,0:T(8,128)(2,1)S(1)}, bf16[1024,384]{1,0:T(8,128)(2,1)S(1)}, u32[]{:S(2)}, u32[]{:S(2)}) collective-permute-start(bf16[1024,384]{1,0:T(8,128)(2,1)S(1)} %pick.21), channel_id=1, source_target_pairs={{0,4},{3,7},{4,8},{7,11},{8,12},{11,15},{12,14},{15,13},{14,10},{1... | collective-permute-start | bytes 2359304 | tf_op jit(solution)/shard_map/ppermute | solution.py:369
  77.2 1.7 %help.5 = (f32[192,384]{1,0:T(8,128)S(1)}, f32[208,384]{1,0:T(8,128)S(1)}) custom-call(s32[56]{0:T(128)S(1)} %fusion.2.where, bf16[1024,384]{1,0:T(8,128)(2,1)S(1)} %collective-permute-done.12.refs_1_.refs_0_.refs_4_, bf16[1024,384]{1,0:T(8,128)(2,1)} %collective-permute-done.refs_2_.refs_1_, f32[192,384]{1,0:T(8,128)S(1)} %get-tuple-element.136.refs_2_, ...), custom_call_target="tpu_custom_call" | custom-call | bytes 1024 | tf_op jit(solution)/shard_map/help/pallas_call | solution.py:245
  78.9 2.8 %absorb.17 = (f32[192,384]{1,0:T(8,128)S(1)}, f32[208,384]{1,0:T(8,128)S(1)}) custom-call(s32[56]{0:T(128)S(1)} %fusion.2.where, bf16[192,32768]{1,0:T(8,128)(2,1)S(1)} %bitcast.7, bf16[192,32768]{1,0:T(8,128)(2,1)S(1)} %bitcast.7, bf16[192,4096]{1,0:T(8,128)(2,1)S(1)} %collective-permute-done.11.refs_1_.refs_2_, ...), custom_call_target="tpu_custom_call", output_to_operand_aliasing={{0}: (7, {}), {1}: (8, {})} | custom-call | bytes 1024 | tf_op jit(solution)/shard_map/absorb/pallas_call | solution.py:157
  82.3 2.4 %collective-permute-start.22 = (bf16[1024,384]{1,0:T(8,128)(2,1)S(1)}, bf16[1024,384]{1,0:T(8,128)(2,1)S(1)}, u32[]{:S(2)}, u32[]{:S(2)}) collective-permute-start(bf16[1024,384]{1,0:T(8,128)(2,1)S(1)} %pick.22), channel_id=1, source_target_pairs={{0,4},{3,7},{4,8},{7,11},{8,12},{11,15},{12,14},{15,13},{14,10},{1... | collective-permute-start | bytes 2359304 | tf_op jit(solution)/shard_map/ppermute | solution.py:369
  85.4 1.9 %help.6 = (f32[192,384]{1,0:T(8,128)S(1)}, f32[208,384]{1,0:T(8,128)S(1)}) custom-call(s32[56]{0:T(128)S(1)} %fusion.2.where, bf16[1024,384]{1,0:T(8,128)(2,1)S(1)} %collective-permute-done.18.refs_1_.refs_0_.refs_2_, bf16[1024,384]{1,0:T(8,128)(2,1)} %collective-permute-done.4.refs_0_.refs_5_.refs_1_, f32[192,384]{1,0:T(8,128)S(1)} %get-tuple-element.147.refs_2_, ...), custom_call_target="tpu_custom_call" | custom-call | bytes 1024 | tf_op jit(solution)/shard_map/help/pallas_call | solution.py:245
  87.4 1.6 %absorb.18 = (f32[192,384]{1,0:T(8,128)S(1)}, f32[208,384]{1,0:T(8,128)S(1)}) custom-call(s32[56]{0:T(128)S(1)} %fusion.2.where, bf16[192,32768]{1,0:T(8,128)(2,1)S(1)} %bitcast.7, bf16[192,32768]{1,0:T(8,128)(2,1)S(1)} %bitcast.7, bf16[192,4096]{1,0:T(8,128)(2,1)S(1)} %collective-permute-done.16.refs_3_.refs_2_, ...), custom_call_target="tpu_custom_call", output_to_operand_aliasing={{0}: (7, {}), {1}: (8, {})} | custom-call | bytes 1024 | tf_op jit(solution)/shard_map/absorb/pallas_call | solution.py:157
  89.0 1.0 collective-permute-done.17.refs_1_.refs_0_.refs_2_
  90.6 2.5 %collective-permute-start.20 = (bf16[1024,384]{1,0:T(8,128)(2,1)S(1)}, bf16[1024,384]{1,0:T(8,128)(2,1)S(1)}, u32[]{:S(2)}, u32[]{:S(2)}) collective-permute-start(bf16[1024,384]{1,0:T(8,128)(2,1)S(1)} %pick.23), channel_id=1, source_target_pairs={{0,4},{3,7},{4,8},{7,11},{8,12},{11,15},{12,14},{15,13},{14,10},{1... | collective-permute-start | bytes 2359304 | tf_op jit(solution)/shard_map/ppermute | solution.py:369
  93.1 5.3 %collective-permute-done.22.refs_4_ = bf16[1024,384]{1,0:T(8,128)(2,1)S(1)} collective-permute-done((bf16[1024,384]{1,0:T(8,128)(2,1)S(1)}, bf16[1024,384]{1,0:T(8,128)(2,1)S(1)}, u32[]{:S(2)}, u32[]{:S(2)}) %collective-permute-start.22) | collective-permute-done | bytes 786464 | tf_op jit(solution)/shard_map/ppermute | solution.py:369
  99.7 1.6 %absorb.19 = (f32[192,384]{1,0:T(8,128)S(1)}, f32[208,384]{1,0:T(8,128)S(1)}) custom-call(s32[56]{0:T(128)S(1)} %fusion.2.where, bf16[192,32768]{1,0:T(8,128)(2,1)S(1)} %bitcast.7, bf16[192,32768]{1,0:T(8,128)(2,1)S(1)} %bitcast.7, bf16[192,4096]{1,0:T(8,128)(2,1)S(1)} %collective-permute-done.16.refs_3_.refs_2_, ...), custom_call_target="tpu_custom_call", output_to_operand_aliasing={{0}: (7, {}), {1}: (8, {})} | custom-call | bytes 1024 | tf_op jit(solution)/shard_map/absorb/pallas_call | solution.py:157
  101.3 3.7 %collective-permute-start.26 = (bf16[1024,384]{1,0:T(8,128)(2,1)S(1)}, bf16[1024,384]{1,0:T(8,128)(2,1)S(1)}, u32[]{:S(2)}, u32[]{:S(2)}) collective-permute-start(bf16[1024,384]{1,0:T(8,128)(2,1)S(1)} %collective-permute-done.22.refs_4_), channel_id=1, source_target_pairs={{0,4},{3,7},{4,8},{7,11},{8,12},{11,15},{12,14},{15,13},{14,10},{1... | collective-permute-start | bytes 2359304 | tf_op jit(solution)/shard_map/ppermute | solution.py:369
  105.0 1.6 %absorb.20 = (f32[192,384]{1,0:T(8,128)S(1)}, f32[208,384]{1,0:T(8,128)S(1)}) custom-call(s32[56]{0:T(128)S(1)} %fusion.2.where, bf16[192,32768]{1,0:T(8,128)(2,1)S(1)} %bitcast.7, bf16[192,32768]{1,0:T(8,128)(2,1)S(1)} %bitcast.7, bf16[192,4096]{1,0:T(8,128)(2,1)S(1)} %collective-permute-done.19.refs_3_.refs_2_, ...), custom_call_target="tpu_custom_call", output_to_operand_aliasing={{0}: (7, {}), {1}: (8, {})} | custom-call | bytes 1024 | tf_op jit(solution)/shard_map/absorb/pallas_call | solution.py:157
  106.8 7.9 %collective-permute-start.25 = (bf16[1024,384]{1,0:T(8,128)(2,1)S(1)}, bf16[1024,384]{1,0:T(8,128)(2,1)S(1)}, u32[]{:S(2)}, u32[]{:S(2)}) collective-permute-start(bf16[1024,384]{1,0:T(8,128)(2,1)S(1)} %collective-permute-done.20.refs_4_), channel_id=1, source_target_pairs={{0,4},{3,7},{4,8},{7,11},{8,12},{11,15},{12,14},{15,13},{14,10},{1... | collective-permute-start | bytes 2359304 | tf_op jit(solution)/shard_map/ppermute | solution.py:369
  114.8 1.3 collective-permute-start.29
  116.1 1.6 %absorb.21 = (f32[192,384]{1,0:T(8,128)S(1)}, f32[208,384]{1,0:T(8,128)S(1)}) custom-call(s32[56]{0:T(128)S(1)} %fusion.2.where, bf16[192,32768]{1,0:T(8,128)(2,1)S(1)} %bitcast.7, bf16[192,32768]{1,0:T(8,128)(2,1)S(1)} %bitcast.7, bf16[192,4096]{1,0:T(8,128)(2,1)S(1)} %collective-permute-done.19.refs_3_.refs_2_, ...), custom_call_target="tpu_custom_call", output_to_operand_aliasing={{0}: (7, {}), {1}: (8, {})} | custom-call | bytes 1024 | tf_op jit(solution)/shard_map/absorb/pallas_call | solution.py:157
  117.7 1.1 absorb.22
  118.9 1.2 absorb.23
  120.1 1.6 %absorb.24 = (f32[192,384]{1,0:T(8,128)S(1)}, f32[208,384]{1,0:T(8,128)S(1)}) custom-call(s32[56]{0:T(128)S(1)} %fusion.2.where, bf16[192,32768]{1,0:T(8,128)(2,1)S(1)} %bitcast.7, bf16[192,32768]{1,0:T(8,128)(2,1)S(1)} %bitcast.7, bf16[192,4096]{1,0:T(8,128)(2,1)S(1)} %collective-permute-done.27.refs_2_.refs_3_, ...), custom_call_target="tpu_custom_call", output_to_operand_aliasing={{0}: (7, {}), {1}: (8, {})} | custom-call | bytes 1024 | tf_op jit(solution)/shard_map/absorb/pallas_call | solution.py:157
  121.8 1.6 %absorb.25 = (f32[192,384]{1,0:T(8,128)S(1)}, f32[208,384]{1,0:T(8,128)S(1)}) custom-call(s32[56]{0:T(128)S(1)} %fusion.2.where, bf16[192,32768]{1,0:T(8,128)(2,1)S(1)} %bitcast.7, bf16[192,32768]{1,0:T(8,128)(2,1)S(1)} %bitcast.7, bf16[192,4096]{1,0:T(8,128)(2,1)S(1)} %collective-permute-done.27.refs_2_.refs_3_, ...), custom_call_target="tpu_custom_call", output_to_operand_aliasing={{0}: (7, {}), {1}: (8, {})} | custom-call | bytes 1024 | tf_op jit(solution)/shard_map/absorb/pallas_call | solution.py:157
  123.4 1.1 absorb.26
  124.6 1.1 absorb.27
  125.7 3.6 %collective-permute-done.29 = f32[400,384]{1,0:T(8,128)S(1)} collective-permute-done((f32[400,384]{1,0:T(8,128)S(1)}, f32[400,384]{1,0:T(8,128)S(1)}, u32[]{:S(2)}, u32[]{:S(2)}) %collective-permute-start.29) | collective-permute-done | bytes 614432 | tf_op jit(solution)/shard_map/ppermute | solution.py:385
  129.4 1.6 %collective-permute-done.30 = f32[208,384]{1,0:T(8,128)S(1)} collective-permute-done((f32[208,384]{1,0:T(8,128)S(1)}, f32[208,384]{1,0:T(8,128)S(1)}, u32[]{:S(2)}, u32[]{:S(2)}) %collective-permute-start.30) | collective-permute-done | bytes 319520 | tf_op jit(solution)/shard_map/ppermute | solution.py:316
  131.0 0.9 fusion
  (95 shorter events, 15.5 us)
Async XLA Ops:
  2.2 5.5 %collective-permute-start = (bf16[1024,384]{1,0:T(8,128)(2,1)S(1)}, bf16[1024,384]{1,0:T(8,128)(2,1)}, u32[]{:S(2)}, u32[]{:S(2)}) collective-permute-start(bf16[1024,384]{1,0:T(8,128)(2,1)S(1)} %get-tuple-element.215.refs_1_), channel_id=1, source_target_pairs={{0,1},{1,0},{2,3},{3,2},{4,5},{5,4},{6,7},{7,6},{8,9},{9,8},{10,11... | collective-permute-start | bytes 2359304 | tf_op jit(solution)/shard_map/ppermute | solution.py:316
  2.7 0.9 copy-start
  3.6 14.9 %collective-permute-start.3 = (bf16[1024,384]{1,0:T(8,128)(2,1)S(1)}, bf16[1024,384]{1,0:T(8,128)(2,1)}, u32[]{:S(2)}, u32[]{:S(2)}) collective-permute-start(bf16[1024,384]{1,0:T(8,128)(2,1)S(1)} %get-tuple-element.135.refs_2_.refs_1_), channel_id=1, source_target_pairs={{0,4},{3,7},{4,8},{7,11},{8,12},{11,15},{12,14},{15,13},{14,10},{1... | collective-permute-start | bytes 2359304 | tf_op jit(solution)/shard_map/ppermute | solution.py:369
  6.2 15.9 %collective-permute-start.4 = (bf16[1024,384]{1,0:T(8,128)(2,1)S(1)}, bf16[1024,384]{1,0:T(8,128)(2,1)}, u32[]{:S(2)}, u32[]{:S(2)}) collective-permute-start(bf16[1024,384]{1,0:T(8,128)(2,1)S(1)} %get-tuple-element.135.refs_2_.refs_1_), channel_id=1, source_target_pairs={{6,4},{5,7},{8,10},{11,9},{22,20},{21,23},{24,26},{27,25}} | collective-permute-start | bytes 2359304 | tf_op jit(solution)/shard_map/ppermute | solution.py:369
  7.7 14.8 %collective-permute-start.2 = (bf16[1024,384]{1,0:T(8,128)(2,1)}, bf16[1024,384]{1,0:T(8,128)(2,1)S(1)}, u32[]{:S(2)}, u32[]{:S(2)}) collective-permute-start(bf16[1024,384]{1,0:T(8,128)(2,1)} %collective-permute-done.refs_2_.refs_1_), channel_id=1, source_target_pairs={{6,4},{5,7},{8,10},{11,9},{22,20},{21,23},{24,26},{27,25}} | collective-permute-start | bytes 2359304 | tf_op jit(solution)/shard_map/ppermute | solution.py:369
  8.4 21.6 %collective-permute-start.1 = (bf16[1024,384]{1,0:T(8,128)(2,1)}, bf16[1024,384]{1,0:T(8,128)(2,1)}, u32[]{:S(2)}, u32[]{:S(2)}) collective-permute-start(bf16[1024,384]{1,0:T(8,128)(2,1)} %collective-permute-done.refs_2_.refs_1_), channel_id=1, source_target_pairs={{0,4},{3,7},{4,8},{7,11},{8,12},{11,15},{12,14},{15,13},{14,10},{1... | collective-permute-start | bytes 2359304 | tf_op jit(solution)/shard_map/ppermute | solution.py:369
  11.1 32.4 %slice-start = ((s8[12582912]{0:T(1024)(128)(4,1)}), s8[4194304]{0:T(1024)(128)(4,1)S(1)}, s32[]{:S(2)}) async-start(s8[12582912]{0:T(1024)(128)(4,1)} %bitcast.6), calls=%async_computation | async-start | bytes 8388608
  11.1 32.4 %slice-start.1 = ((s8[12582912]{0:T(1024)(128)(4,1)}), s8[4194304]{0:T(1024)(128)(4,1)S(1)}, s32[]{:S(2)}) async-start(s8[12582912]{0:T(1024)(128)(4,1)} %bitcast.6), calls=%async_computation.1 | async-start | bytes 8388608
  16.1 1.1 copy-start.4
  17.3 1.2 copy-start.6
  18.4 3.5 %copy-start.2 = (bf16[192,4096]{1,0:T(8,128)(2,1)}, bf16[192,4096]{1,0:T(8,128)(2,1)S(1)}, u32[]{:S(2)}) copy-start(bf16[192,4096]{1,0:T(8,128)(2,1)S(1)} %get-tuple-element.196) | copy-start | bytes 4718596
  18.4 3.5 %copy-start.8 = (bf16[192,2048]{1,0:T(8,128)(2,1)}, bf16[192,2048]{1,0:T(8,128)(2,1)S(1)}, u32[]{:S(2)}) copy-start(bf16[192,2048]{1,0:T(8,128)(2,1)S(1)} %get-tuple-element.205) | copy-start | bytes 2359300
  18.4 24.3 %collective-permute-start.10 = (bf16[192,4096]{1,0:T(8,128)(2,1)S(1)}, bf16[192,4096]{1,0:T(8,128)(2,1)S(1)}, u32[]{:S(2)}, u32[]{:S(2)}) collective-permute-start(bf16[192,4096]{1,0:T(8,128)(2,1)S(1)} %get-tuple-element.115), channel_id=1, source_target_pairs={{0,1},{1,0},{2,3},{3,2},{4,5},{5,4},{6,7},{7,6},{8,9},{9,8},{10,11... | collective-permute-start | bytes 4718600 | tf_op jit(solution)/shard_map/ppermute | solution.py:316
  18.5 1.7 %copy-start.1 = (bf16[1024,384]{1,0:T(8,128)(2,1)S(1)}, bf16[1024,384]{1,0:T(8,128)(2,1)}, u32[]{:S(2)}) copy-start(bf16[1024,384]{1,0:T(8,128)(2,1)} %copy-done) | copy-start | bytes 2359300
  22.0 21.5 %slice-start.2 = ((s8[12582912]{0:T(1024)(128)(4,1)}), s8[4194304]{0:T(1024)(128)(4,1)S(1)}, s32[]{:S(2)}) async-start(s8[12582912]{0:T(1024)(128)(4,1)} %bitcast.6), calls=%async_computation.2 | async-start | bytes 8388608
  22.0 22.9 %collective-permute-start.11 = (bf16[192,4096]{1,0:T(8,128)(2,1)S(1)}, bf16[192,4096]{1,0:T(8,128)(2,1)S(1)}, u32[]{:S(2)}, u32[]{:S(2)}) collective-permute-start(bf16[192,4096]{1,0:T(8,128)(2,1)S(1)} %get-tuple-element.123), channel_id=1, source_target_pairs={{0,1},{1,0},{2,3},{3,2},{4,5},{5,4},{6,7},{7,6},{8,9},{9,8},{10,11... | collective-permute-start | bytes 4718600 | tf_op jit(solution)/shard_map/ppermute | solution.py:316
  22.1 11.1 %collective-permute-start.5 = (bf16[1024,384]{1,0:T(8,128)(2,1)S(1)}, bf16[1024,384]{1,0:T(8,128)(2,1)S(1)}, u32[]{:S(2)}, u32[]{:S(2)}) collective-permute-start(bf16[1024,384]{1,0:T(8,128)(2,1)S(1)} %get-tuple-element.135.refs_2_.refs_1_), channel_id=1, source_target_pairs={{0,1},{1,0},{2,3},{3,2},{4,5},{5,4},{6,7},{7,6},{8,9},{9,8},{10,11... | collective-permute-start | bytes 2359304 | tf_op jit(solution)/shard_map/ppermute | solution.py:316
  22.5 17.0 %collective-permute-start.8 = (bf16[1024,384]{1,0:T(8,128)(2,1)S(1)}, bf16[1024,384]{1,0:T(8,128)(2,1)S(1)}, u32[]{:S(2)}, u32[]{:S(2)}) collective-permute-start(bf16[1024,384]{1,0:T(8,128)(2,1)S(1)} %pick.12), channel_id=1, source_target_pairs={{0,4},{3,7},{4,8},{7,11},{8,12},{11,15},{12,14},{15,13},{14,10},{1... | collective-permute-start | bytes 2359304 | tf_op jit(solution)/shard_map/ppermute | solution.py:369
  30.0 10.2 %collective-permute-start.9 = (bf16[1024,384]{1,0:T(8,128)(2,1)}, bf16[1024,384]{1,0:T(8,128)(2,1)S(1)}, u32[]{:S(2)}, u32[]{:S(2)}) collective-permute-start(bf16[1024,384]{1,0:T(8,128)(2,1)} %collective-permute-done.3.refs_0_.refs_4_), channel_id=1, source_target_pairs={{6,4},{5,7},{8,10},{11,9},{22,20},{21,23},{24,26},{27,25}} | collective-permute-start | bytes 2359304 | tf_op jit(solution)/shard_map/ppermute | solution.py:369
  34.9 18.6 %collective-permute-start.6 = (bf16[1024,384]{1,0:T(8,128)(2,1)S(1)}, bf16[1024,384]{1,0:T(8,128)(2,1)S(1)}, u32[]{:S(2)}, u32[]{:S(2)}) collective-permute-start(bf16[1024,384]{1,0:T(8,128)(2,1)S(1)} %pick.13), channel_id=1, source_target_pairs={{0,4},{3,7},{4,8},{7,11},{8,12},{11,15},{12,14},{15,13},{14,10},{1... | collective-permute-start | bytes 2359304 | tf_op jit(solution)/shard_map/ppermute | solution.py:369
  39.5 14.0 %collective-permute-start.7 = (bf16[1024,384]{1,0:T(8,128)(2,1)}, bf16[1024,384]{1,0:T(8,128)(2,1)S(1)}, u32[]{:S(2)}, u32[]{:S(2)}) collective-permute-start(bf16[1024,384]{1,0:T(8,128)(2,1)} %collective-permute-done.1.refs_0_.refs_4_), channel_id=1, source_target_pairs={{6,4},{5,7},{8,10},{11,9},{22,20},{21,23},{24,26},{27,25}} | collective-permute-start | bytes 2359304 | tf_op jit(solution)/shard_map/ppermute | solution.py:369
  40.3 30.1 %collective-permute-start.16 = (bf16[192,4096]{1,0:T(8,128)(2,1)S(1)}, bf16[192,4096]{1,0:T(8,128)(2,1)S(1)}, u32[]{:S(2)}, u32[]{:S(2)}) collective-permute-start(bf16[192,4096]{1,0:T(8,128)(2,1)S(1)} %get-tuple-element.139), channel_id=1, source_target_pairs={{0,1},{1,0},{2,3},{3,2},{4,5},{5,4},{6,7},{7,6},{8,9},{9,8},{10,11... | collective-permute-start | bytes 4718600 | tf_op jit(solution)/shard_map/ppermute | solution.py:316
  42.8 24.4 %collective-permute-start.15 = (bf16[1024,384]{1,0:T(8,128)(2,1)S(1)}, bf16[1024,384]{1,0:T(8,128)(2,1)S(1)}, u32[]{:S(2)}, u32[]{:S(2)}) collective-permute-start(bf16[1024,384]{1,0:T(8,128)(2,1)S(1)} %collective-permute-done.8.refs_0_.refs_4_), channel_id=1, source_target_pairs={{4,6},{7,5},{10,8},{9,11},{20,22},{23,21},{26,24},{25,27}} | collective-permute-start | bytes 2359304 | tf_op jit(solution)/shard_map/ppermute | solution.py:369
  44.9 22.4 %collective-permute-start.14 = (bf16[1024,384]{1,0:T(8,128)(2,1)S(1)}, bf16[1024,384]{1,0:T(8,128)(2,1)S(1)}, u32[]{:S(2)}, u32[]{:S(2)}) collective-permute-start(bf16[1024,384]{1,0:T(8,128)(2,1)S(1)} %pick.15), channel_id=1, source_target_pairs={{0,4},{3,7},{4,8},{7,11},{8,12},{11,15},{12,14},{15,13},{14,10},{1... | collective-permute-start | bytes 2359304 | tf_op jit(solution)/shard_map/ppermute | solution.py:369
  53.6 21.2 %collective-permute-start.13 = (bf16[1024,384]{1,0:T(8,128)(2,1)S(1)}, bf16[1024,384]{1,0:T(8,128)(2,1)S(1)}, u32[]{:S(2)}, u32[]{:S(2)}) collective-permute-start(bf16[1024,384]{1,0:T(8,128)(2,1)S(1)} %collective-permute-done.6.refs_0_.refs_4_), channel_id=1, source_target_pairs={{4,6},{7,5},{10,8},{9,11},{20,22},{23,21},{26,24},{25,27}} | collective-permute-start | bytes 2359304 | tf_op jit(solution)/shard_map/ppermute | solution.py:369
  55.6 19.1 %collective-permute-start.12 = (bf16[1024,384]{1,0:T(8,128)(2,1)S(1)}, bf16[1024,384]{1,0:T(8,128)(2,1)S(1)}, u32[]{:S(2)}, u32[]{:S(2)}) collective-permute-start(bf16[1024,384]{1,0:T(8,128)(2,1)S(1)} %pick.17), channel_id=1, source_target_pairs={{0,4},{3,7},{4,8},{7,11},{8,12},{11,15},{12,14},{15,13},{14,10},{1... | collective-permute-start | bytes 2359304 | tf_op jit(solution)/shard_map/ppermute | solution.py:369
  64.8 2.3 %copy-start.7 = (bf16[192,4096]{1,0:T(8,128)(2,1)S(1)}, bf16[192,4096]{1,0:T(8,128)(2,1)}, u32[]{:S(2)}) copy-start(bf16[192,4096]{1,0:T(8,128)(2,1)} %copy-done.6) | copy-start | bytes 4718596
  67.2 20.1 %collective-permute-start.19 = (bf16[192,4096]{1,0:T(8,128)(2,1)S(1)}, bf16[192,4096]{1,0:T(8,128)(2,1)S(1)}, u32[]{:S(2)}, u32[]{:S(2)}) collective-permute-start(bf16[192,4096]{1,0:T(8,128)(2,1)S(1)} %copy-done.7), channel_id=1, source_target_pairs={{0,1},{1,0},{2,3},{3,2},{4,5},{5,4},{6,7},{7,6},{8,9},{9,8},{10,11... | collective-permute-start | bytes 4718600 | tf_op jit(solution)/shard_map/ppermute | solution.py:316
  69.0 12.7 %collective-permute-start.18 = (bf16[1024,384]{1,0:T(8,128)(2,1)S(1)}, bf16[1024,384]{1,0:T(8,128)(2,1)S(1)}, u32[]{:S(2)}, u32[]{:S(2)}) collective-permute-start(bf16[1024,384]{1,0:T(8,128)(2,1)S(1)} %pick.19), channel_id=1, source_target_pairs={{0,4},{3,7},{4,8},{7,11},{8,12},{11,15},{12,14},{15,13},{14,10},{1... | collective-permute-start | bytes 2359304 | tf_op jit(solution)/shard_map/ppermute | solution.py:369
  69.8 1.4 %copy-start.5 = (bf16[192,4096]{1,0:T(8,128)(2,1)S(1)}, bf16[192,4096]{1,0:T(8,128)(2,1)}, u32[]{:S(2)}) copy-start(bf16[192,4096]{1,0:T(8,128)(2,1)} %copy-done.4) | copy-start | bytes 4718596
  71.2 33.8 %collective-permute-start.24 = (bf16[192,4096]{1,0:T(8,128)(2,1)S(1)}, bf16[192,4096]{1,0:T(8,128)(2,1)S(1)}, u32[]{:S(2)}, u32[]{:S(2)}) collective-permute-start(bf16[192,4096]{1,0:T(8,128)(2,1)S(1)} %copy-done.5), channel_id=1, source_target_pairs={{0,1},{1,0},{2,3},{3,2},{4,5},{5,4},{6,7},{7,6},{8,9},{9,8},{10,11... | collective-permute-start | bytes 4718600 | tf_op jit(solution)/shard_map/ppermute | solution.py:316
  75.4 14.6 %collective-permute-start.17 = (bf16[1024,384]{1,0:T(8,128)(2,1)S(1)}, bf16[1024,384]{1,0:T(8,128)(2,1)S(1)}, u32[]{:S(2)}, u32[]{:S(2)}) collective-permute-start(bf16[1024,384]{1,0:T(8,128)(2,1)S(1)} %pick.21), channel_id=1, source_target_pairs={{0,4},{3,7},{4,8},{7,11},{8,12},{11,15},{12,14},{15,13},{14,10},{1... | collective-permute-start | bytes 2359304 | tf_op jit(solution)/shard_map/ppermute | solution.py:369
  82.3 5.0 %copy-start.3 = (bf16[192,4096]{1,0:T(8,128)(2,1)S(1)}, bf16[192,4096]{1,0:T(8,128)(2,1)}, u32[]{:S(2)}) copy-start(bf16[192,4096]{1,0:T(8,128)(2,1)} %copy-done.2) | copy-start | bytes 4718596
  82.3 16.1 %collective-permute-start.22 = (bf16[1024,384]{1,0:T(8,128)(2,1)S(1)}, bf16[1024,384]{1,0:T(8,128)(2,1)S(1)}, u32[]{:S(2)}, u32[]{:S(2)}) collective-permute-start(bf16[1024,384]{1,0:T(8,128)(2,1)S(1)} %pick.22), channel_id=1, source_target_pairs={{0,4},{3,7},{4,8},{7,11},{8,12},{11,15},{12,14},{15,13},{14,10},{1... | collective-permute-start | bytes 2359304 | tf_op jit(solution)/shard_map/ppermute | solution.py:369
  84.7 16.6 %collective-permute-start.23 = (bf16[1024,384]{1,0:T(8,128)(2,1)S(1)}, bf16[1024,384]{1,0:T(8,128)(2,1)S(1)}, u32[]{:S(2)}, u32[]{:S(2)}) collective-permute-start(bf16[1024,384]{1,0:T(8,128)(2,1)S(1)} %collective-permute-done.18.refs_1_.refs_0_.refs_2_), channel_id=1, source_target_pairs={{6,4},{5,7},{8,10},{11,9},{22,20},{21,23},{24,26},{27,25}} | collective-permute-start | bytes 2359304 | tf_op jit(solution)/shard_map/ppermute | solution.py:369
  87.3 32.8 %collective-permute-start.27 = (bf16[192,4096]{1,0:T(8,128)(2,1)S(1)}, bf16[192,4096]{1,0:T(8,128)(2,1)S(1)}, u32[]{:S(2)}, u32[]{:S(2)}) collective-permute-start(bf16[192,4096]{1,0:T(8,128)(2,1)S(1)} %copy-done.3), channel_id=1, source_target_pairs={{0,1},{1,0},{2,3},{3,2},{4,5},{5,4},{6,7},{7,6},{8,9},{9,8},{10,11... | collective-permute-start | bytes 4718600 | tf_op jit(solution)/shard_map/ppermute | solution.py:316
  90.6 16.2 %collective-permute-start.20 = (bf16[1024,384]{1,0:T(8,128)(2,1)S(1)}, bf16[1024,384]{1,0:T(8,128)(2,1)S(1)}, u32[]{:S(2)}, u32[]{:S(2)}) collective-permute-start(bf16[1024,384]{1,0:T(8,128)(2,1)S(1)} %pick.23), channel_id=1, source_target_pairs={{0,4},{3,7},{4,8},{7,11},{8,12},{11,15},{12,14},{15,13},{14,10},{1... | collective-permute-start | bytes 2359304 | tf_op jit(solution)/shard_map/ppermute | solution.py:369
  98.4 8.4 %collective-permute-start.21 = (bf16[1024,384]{1,0:T(8,128)(2,1)S(1)}, bf16[1024,384]{1,0:T(8,128)(2,1)S(1)}, u32[]{:S(2)}, u32[]{:S(2)}) collective-permute-start(bf16[1024,384]{1,0:T(8,128)(2,1)S(1)} %collective-permute-done.17.refs_1_.refs_0_.refs_2_), channel_id=1, source_target_pairs={{6,4},{5,7},{8,10},{11,9},{22,20},{21,23},{24,26},{27,25}} | collective-permute-start | bytes 2359304 | tf_op jit(solution)/shard_map/ppermute | solution.py:369
  99.7 5.3 %copy-start.9 = (bf16[192,2048]{1,0:T(8,128)(2,1)S(1)}, bf16[192,2048]{1,0:T(8,128)(2,1)}, u32[]{:S(2)}) copy-start(bf16[192,2048]{1,0:T(8,128)(2,1)} %copy-done.8) | copy-start | bytes 2359300
  101.3 16.4 %collective-permute-start.26 = (bf16[1024,384]{1,0:T(8,128)(2,1)S(1)}, bf16[1024,384]{1,0:T(8,128)(2,1)S(1)}, u32[]{:S(2)}, u32[]{:S(2)}) collective-permute-start(bf16[1024,384]{1,0:T(8,128)(2,1)S(1)} %collective-permute-done.22.refs_4_), channel_id=1, source_target_pairs={{0,4},{3,7},{4,8},{7,11},{8,12},{11,15},{12,14},{15,13},{14,10},{1... | collective-permute-start | bytes 2359304 | tf_op jit(solution)/shard_map/ppermute | solution.py:369
  105.0 18.4 %collective-permute-start.28 = (bf16[192,2048]{1,0:T(8,128)(2,1)S(1)}, bf16[192,2048]{1,0:T(8,128)(2,1)S(1)}, u32[]{:S(2)}, u32[]{:S(2)}) collective-permute-start(bf16[192,2048]{1,0:T(8,128)(2,1)S(1)} %copy-done.9), channel_id=1, source_target_pairs={{0,1},{1,0},{2,3},{3,2},{4,5},{5,4},{6,7},{7,6},{8,9},{9,8},{10,11... | collective-permute-start | bytes 2359304 | tf_op jit(solution)/shard_map/ppermute | solution.py:316
  106.8 17.7 %collective-permute-start.25 = (bf16[1024,384]{1,0:T(8,128)(2,1)S(1)}, bf16[1024,384]{1,0:T(8,128)(2,1)S(1)}, u32[]{:S(2)}, u32[]{:S(2)}) collective-permute-start(bf16[1024,384]{1,0:T(8,128)(2,1)S(1)} %collective-permute-done.20.refs_4_), channel_id=1, source_target_pairs={{0,4},{3,7},{4,8},{7,11},{8,12},{11,15},{12,14},{15,13},{14,10},{1... | collective-permute-start | bytes 2359304 | tf_op jit(solution)/shard_map/ppermute | solution.py:369
  114.8 14.5 %collective-permute-start.29 = (f32[400,384]{1,0:T(8,128)S(1)}, f32[400,384]{1,0:T(8,128)S(1)}, u32[]{:S(2)}, u32[]{:S(2)}) collective-permute-start(f32[400,384]{1,0:T(8,128)S(1)} %pad_maximum_fusion), channel_id=1, source_target_pairs={{4,0},{7,3},{10,14},{9,13},{20,16},{23,19},{26,30},{25,29}} | collective-permute-start | bytes 1843208 | tf_op jit(solution)/shard_map/ppermute | solution.py:385
  124.6 6.5 %copy-start.10 = (bf16[192,384]{1,0:T(8,128)(2,1)S(1)}, bf16[192,384]{1,0:T(8,128)(2,1)}, u32[]{:S(2)}) copy-start(bf16[192,384]{1,0:T(8,128)(2,1)} %param.6) | copy-start | bytes 442372
  129.3 1.7 %collective-permute-start.30 = (f32[208,384]{1,0:T(8,128)S(1)}, f32[208,384]{1,0:T(8,128)S(1)}, u32[]{:S(2)}, u32[]{:S(2)}) collective-permute-start(f32[208,384]{1,0:T(8,128)S(1)} %slice_add_fusion), channel_id=1, source_target_pairs={{0,1},{1,0},{2,3},{3,2},{4,5},{5,4},{6,7},{7,6},{8,9},{9,8},{10,11... | collective-permute-start | bytes 958472 | tf_op jit(solution)/shard_map/ppermute | solution.py:316
  129.4 2.5 %copy-start.11 = (f32[192]{0:T(256)}, f32[192]{0:T(256)S(1)}, u32[]{:S(2)}) copy-start(f32[192]{0:T(256)S(1)} %add_add_fusion) | copy-start | bytes 2308

commit v11 on v10

--- a/solution.py
+++ b/solution.py
@@ -10,15 +10,15 @@
 
 CORES = 2
 ONES = 16
-SHIPS = True
+SHIPS = False
 SLOTS = 1
-MOST = 1
-ABSORB_FROM = 2
+MOST = 2
+ABSORB_FROM = 3
 PER_LENT = 4
 EARLY = 1
 REST_AT = 2
 DEGREE_PARTS = 4
-DEGREE_AT = 1
+DEGREE_AT = 2
 HELP_AT = (3, 4)
 LEND_AFTER = 1
 TILE = 128

time: 134 us -> 129 us (0.963); the launches traced: 132 us -> 129 us
  waiting for transfers between devices: 15.6 us -> 66.1 us
  starting transfers between devices: 55.7 us -> 30.6 us
  Pallas kernels: 44.2 us -> 25.4 us
  local copies, waits for them, and re-layouts: 8.14 us -> 2.5 us
  other arithmetic: 6.84 us -> 2.96 us
    ppermute x20 -> x14, waiting for transfers between devices: 10.5 us -> 64.5 us  [shards(): lax.ppermute(piece, 'row', pairs(make_route(chips, port, r)))]
    ppermute x20 -> x14, starting transfers between devices: 52.6 us -> 29.9 us  [shards(): lax.ppermute(piece, 'row', pairs(make_route(chips, port, r)))]
    pallas_call x16 -> x0, Pallas kernels: 15.9 us -> none  [the longest x12 11.1 us: pick(): pl.pallas_call(functools.partial(pick_kernel, choices, len(operands)), gr...]
    unnamed x38 -> x18, local copies, waits for them, and re-layouts: 5.91 us -> 0.28 us
    reduce_sum x4, other arithmetic: 5.86 us -> 2.08 us  [shards(): degree.append(jnp.sum(part, axis=1, dtype=jnp.float32))]
    ppermute x1 -> x0, waiting for transfers between devices: 3.56 us -> none  [shards(): lax.ppermute(jnp.concatenate(helped, axis=0), 'row', pairs({1: 0, 5: 4}))]
    pallas_call x14 -> x16, Pallas kernels: 23.3 us -> 21.7 us  [absorb(): pl.pallas_call(functools.partial(absorb_kernel, count, flags, rows, first...]
    pallas_call x1, Pallas kernels: 5.05 us -> 3.69 us  [lend(): pl.pallas_call(functools.partial(lend_kernel, sizes, first, depth), in_sp...]
  transfers between devices with their start and end apart: 31 -> 20, of which waited for: 6 -> 15; matrix products, arithmetic and copies ran while one was open for 5% -> 2% of each run, Pallas kernels for 34% -> 19%
where the time goes in v11:
time: 129 us
  waiting for transfers between devices  66.1 us (51%)
  starting transfers between devices  30.6 us (24%)
  Pallas kernels  25.4 us (20%)
  other arithmetic  2.96 us (2%)
  local copies, waits for them, and re-layouts  2.5 us (2%)
    ppermute x14, waiting for transfers between devices, shards(): lax.ppermute(piece, 'row', pairs(make_route(chips, port, r)))  64.5 us
    ppermute x14, starting transfers between devices, shards(): lax.ppermute(piece, 'row', pairs(make_route(chips, port, r)))  29.9 us
    pallas_call x16, Pallas kernels, absorb(): pl.pallas_call(functools.partial(absorb_kernel, count, flags, rows, first...  21.7 us
    pallas_call x1, Pallas kernels, lend(): pl.pallas_call(functools.partial(lend_kernel, sizes, first, depth), in_sp...  3.69 us
  transfers between devices with their start and end apart: 20, of which 15 were waited for; matrix products, arithmetic and copies ran while one was open for 2% of the time, Pallas kernels for 19%

profile of v11, /device:TPU:0, one launch (start us, length us, event | category | flops | bytes accessed | tf_op | source)
XLA Modules:
  0.0 128.5 jit_solution(14475702618490017663)
XLA Ops:
  0.6 1.5 %dynamic-slice_bitcast_fusion = (bf16[1024,384]{1,0:T(8,128)(2,1)S(1)}, bf16[1024,384]{1,0:T(8,128)(2,1)S(1)}) fusion(bf16[2,1024,384]{2,1,0:T(8,128)(2,1)} %param.5, s32[]{:T(128)S(6)} %select_n.12, s32[]{:T(128)S(6)} %select_n.11), kind=kLoop, calls=%fused_computation.4 | loop fusion | bytes 3145736 | tf_op jit(solution)/shard_map/jit(dynamic_index_in_dim)/squeeze | solution.py:343
  2.7 2.6 %collective-permute-start.3 = (bf16[1024,384]{1,0:T(8,128)(2,1)S(1)}, bf16[1024,384]{1,0:T(8,128)(2,1)}, u32[]{:S(2)}, u32[]{:S(2)}) collective-permute-start(bf16[1024,384]{1,0:T(8,128)(2,1)S(1)} %get-tuple-element.88.refs_2_), channel_id=1, source_target_pairs={{0,4},{3,7},{4,8},{7,11},{8,12},{11,15},{12,14},{15,13},{14,10},{1... | collective-permute-start | bytes 2359304 | tf_op jit(solution)/shard_map/ppermute | solution.py:369
  5.3 2.3 %collective-permute-start.1 = (bf16[1024,384]{1,0:T(8,128)(2,1)}, bf16[1024,384]{1,0:T(8,128)(2,1)}, u32[]{:S(2)}, u32[]{:S(2)}) collective-permute-start(bf16[1024,384]{1,0:T(8,128)(2,1)} %collective-permute-done.refs_2_), channel_id=1, source_target_pairs={{0,4},{3,7},{4,8},{7,11},{8,12},{11,15},{12,14},{15,13},{14,10},{1... | collective-permute-start | bytes 2359304 | tf_op jit(solution)/shard_map/ppermute | solution.py:369
  7.7 7.7 %collective-permute-done.3.refs_2_ = bf16[1024,384]{1,0:T(8,128)(2,1)} collective-permute-done((bf16[1024,384]{1,0:T(8,128)(2,1)S(1)}, bf16[1024,384]{1,0:T(8,128)(2,1)}, u32[]{:S(2)}, u32[]{:S(2)}) %collective-permute-start.3) | collective-permute-done | bytes 786464 | tf_op jit(solution)/shard_map/ppermute | solution.py:369
  15.4 2.1 %collective-permute-start.4 = (bf16[1024,384]{1,0:T(8,128)(2,1)}, bf16[1024,384]{1,0:T(8,128)(2,1)S(1)}, u32[]{:S(2)}, u32[]{:S(2)}) collective-permute-start(bf16[1024,384]{1,0:T(8,128)(2,1)} %collective-permute-done.3.refs_2_), channel_id=1, source_target_pairs={{0,4},{3,7},{4,8},{7,11},{8,12},{11,15},{12,14},{15,13},{14,10},{1... | collective-permute-start | bytes 2359304 | tf_op jit(solution)/shard_map/ppermute | solution.py:369
  18.1 3.7 %lend.1 = (bf16[192,4096]{1,0:T(8,128)(2,1)S(1)}, bf16[192,4096]{1,0:T(8,128)(2,1)S(1)}, bf16[192,4096]{1,0:T(8,128)(2,1)S(1)}, bf16[192,4096]{1,0:T(8,128)(2,1)S(1)}) custom-call(s32[34]{0:T(128)S(1)} %fusion.2.where, bf16[192,32768]{1,0:T(8,128)(2,1)} %refs_0_.15), custom_call_target="tpu_custom_call" | custom-call | bytes 1024 | tf_op jit(solution)/shard_map/lend/pallas_call | solution.py:103
  21.9 1.9 %collective-permute-done.1.refs_2_ = bf16[1024,384]{1,0:T(8,128)(2,1)} collective-permute-done((bf16[1024,384]{1,0:T(8,128)(2,1)}, bf16[1024,384]{1,0:T(8,128)(2,1)}, u32[]{:S(2)}, u32[]{:S(2)}) %collective-permute-start.1) | collective-permute-done | bytes 786464 | tf_op jit(solution)/shard_map/ppermute | solution.py:369
  23.8 2.1 %collective-permute-start.2 = (bf16[1024,384]{1,0:T(8,128)(2,1)}, bf16[1024,384]{1,0:T(8,128)(2,1)S(1)}, u32[]{:S(2)}, u32[]{:S(2)}) collective-permute-start(bf16[1024,384]{1,0:T(8,128)(2,1)} %collective-permute-done.1.refs_2_), channel_id=1, source_target_pairs={{0,4},{3,7},{4,8},{7,11},{8,12},{11,15},{12,14},{15,13},{14,10},{1... | collective-permute-start | bytes 2359304 | tf_op jit(solution)/shard_map/ppermute | solution.py:369
  25.9 6.2 %collective-permute-done.4.refs_2_ = bf16[1024,384]{1,0:T(8,128)(2,1)S(1)} collective-permute-done((bf16[1024,384]{1,0:T(8,128)(2,1)}, bf16[1024,384]{1,0:T(8,128)(2,1)S(1)}, u32[]{:S(2)}, u32[]{:S(2)}) %collective-permute-start.4) | collective-permute-done | bytes 786464 | tf_op jit(solution)/shard_map/ppermute | solution.py:369
  32.1 2.1 %collective-permute-start.6 = (bf16[1024,384]{1,0:T(8,128)(2,1)S(1)}, bf16[1024,384]{1,0:T(8,128)(2,1)S(1)}, u32[]{:S(2)}, u32[]{:S(2)}) collective-permute-start(bf16[1024,384]{1,0:T(8,128)(2,1)S(1)} %collective-permute-done.4.refs_2_), channel_id=1, source_target_pairs={{0,4},{3,7},{4,8},{7,11},{8,12},{11,15},{12,14},{15,13},{14,10},{1... | collective-permute-start | bytes 2359304 | tf_op jit(solution)/shard_map/ppermute | solution.py:369
  34.7 5.8 %collective-permute-done.2.refs_2_ = bf16[1024,384]{1,0:T(8,128)(2,1)S(1)} collective-permute-done((bf16[1024,384]{1,0:T(8,128)(2,1)}, bf16[1024,384]{1,0:T(8,128)(2,1)S(1)}, u32[]{:S(2)}, u32[]{:S(2)}) %collective-permute-start.2) | collective-permute-done | bytes 786464 | tf_op jit(solution)/shard_map/ppermute | solution.py:369
  40.5 2.1 %collective-permute-start.5 = (bf16[1024,384]{1,0:T(8,128)(2,1)S(1)}, bf16[1024,384]{1,0:T(8,128)(2,1)S(1)}, u32[]{:S(2)}, u32[]{:S(2)}) collective-permute-start(bf16[1024,384]{1,0:T(8,128)(2,1)S(1)} %collective-permute-done.2.refs_2_), channel_id=1, source_target_pairs={{0,4},{3,7},{4,8},{7,11},{8,12},{11,15},{12,14},{15,13},{14,10},{1... | collective-permute-start | bytes 2359304 | tf_op jit(solution)/shard_map/ppermute | solution.py:369
  43.1 5.8 %collective-permute-done.6.refs_2_ = bf16[1024,384]{1,0:T(8,128)(2,1)S(1)} collective-permute-done((bf16[1024,384]{1,0:T(8,128)(2,1)S(1)}, bf16[1024,384]{1,0:T(8,128)(2,1)S(1)}, u32[]{:S(2)}, u32[]{:S(2)}) %collective-permute-start.6) | collective-permute-done | bytes 786464 | tf_op jit(solution)/shard_map/ppermute | solution.py:369
  49.0 2.1 %collective-permute-start.9 = (bf16[1024,384]{1,0:T(8,128)(2,1)S(1)}, bf16[1024,384]{1,0:T(8,128)(2,1)S(1)}, u32[]{:S(2)}, u32[]{:S(2)}) collective-permute-start(bf16[1024,384]{1,0:T(8,128)(2,1)S(1)} %collective-permute-done.6.refs_2_), channel_id=1, source_target_pairs={{0,4},{3,7},{4,8},{7,11},{8,12},{11,15},{12,14},{15,13},{14,10},{1... | collective-permute-start | bytes 2359304 | tf_op jit(solution)/shard_map/ppermute | solution.py:369
  51.6 1.1 absorb.16
  52.7 2.3 %absorb.17 = (f32[192,384]{1,0:T(8,128)S(1)}, f32[208,384]{1,0:T(8,128)S(1)}) custom-call(s32[34]{0:T(128)S(1)} %fusion.2.where, bf16[192,32768]{1,0:T(8,128)(2,1)S(1)} %copy-done, bf16[192,4096]{1,0:T(8,128)(2,1)S(1)} %collective-permute-done.7.refs_1_, ...), custom_call_target="tpu_custom_call", output_to_operand_aliasing={{0}: (4, {}), {1}: (5, {})} | custom-call | bytes 1024 | tf_op jit(solution)/shard_map/absorb/pallas_call | solution.py:157
  55.1 2.3 %collective-permute-done.5.refs_2_ = bf16[1024,384]{1,0:T(8,128)(2,1)S(1)} collective-permute-done((bf16[1024,384]{1,0:T(8,128)(2,1)S(1)}, bf16[1024,384]{1,0:T(8,128)(2,1)S(1)}, u32[]{:S(2)}, u32[]{:S(2)}) %collective-permute-start.5) | collective-permute-done | bytes 786464 | tf_op jit(solution)/shard_map/ppermute | solution.py:369
  57.4 2.1 %collective-permute-start.8 = (bf16[1024,384]{1,0:T(8,128)(2,1)S(1)}, bf16[1024,384]{1,0:T(8,128)(2,1)S(1)}, u32[]{:S(2)}, u32[]{:S(2)}) collective-permute-start(bf16[1024,384]{1,0:T(8,128)(2,1)S(1)} %collective-permute-done.5.refs_2_), channel_id=1, source_target_pairs={{0,4},{3,7},{4,8},{7,11},{8,12},{11,15},{12,14},{15,13},{14,10},{1... | collective-permute-start | bytes 2359304 | tf_op jit(solution)/shard_map/ppermute | solution.py:369
  59.5 2.3 %absorb.18 = (f32[192,384]{1,0:T(8,128)S(1)}, f32[208,384]{1,0:T(8,128)S(1)}) custom-call(s32[34]{0:T(128)S(1)} %fusion.2.where, bf16[192,32768]{1,0:T(8,128)(2,1)S(1)} %copy-done, bf16[192,4096]{1,0:T(8,128)(2,1)S(1)} %collective-permute-done.7.refs_1_, ...), custom_call_target="tpu_custom_call", output_to_operand_aliasing={{0}: (4, {}), {1}: (5, {})} | custom-call | bytes 1024 | tf_op jit(solution)/shard_map/absorb/pallas_call | solution.py:157
  61.8 2.3 %absorb.19 = (f32[192,384]{1,0:T(8,128)S(1)}, f32[208,384]{1,0:T(8,128)S(1)}) custom-call(s32[34]{0:T(128)S(1)} %fusion.2.where, bf16[192,32768]{1,0:T(8,128)(2,1)S(1)} %copy-done, bf16[192,4096]{1,0:T(8,128)(2,1)S(1)} %collective-permute-done.7.refs_1_, ...), custom_call_target="tpu_custom_call", output_to_operand_aliasing={{0}: (4, {}), {1}: (5, {})} | custom-call | bytes 1024 | tf_op jit(solution)/shard_map/absorb/pallas_call | solution.py:157
  64.7 1.1 collective-permute-done.9.refs_2_
  65.8 2.1 %collective-permute-start.12 = (bf16[1024,384]{1,0:T(8,128)(2,1)S(1)}, bf16[1024,384]{1,0:T(8,128)(2,1)S(1)}, u32[]{:S(2)}, u32[]{:S(2)}) collective-permute-start(bf16[1024,384]{1,0:T(8,128)(2,1)S(1)} %collective-permute-done.9.refs_2_), channel_id=1, source_target_pairs={{0,4},{3,7},{4,8},{7,11},{8,12},{11,15},{12,14},{15,13},{14,10},{1... | collective-permute-start | bytes 2359304 | tf_op jit(solution)/shard_map/ppermute | solution.py:369
  67.9 1.1 absorb.20
  69.1 1.1 absorb.21
  70.2 4.0 %collective-permute-done.8.refs_2_ = bf16[1024,384]{1,0:T(8,128)(2,1)S(1)} collective-permute-done((bf16[1024,384]{1,0:T(8,128)(2,1)S(1)}, bf16[1024,384]{1,0:T(8,128)(2,1)S(1)}, u32[]{:S(2)}, u32[]{:S(2)}) %collective-permute-start.8) | collective-permute-done | bytes 786464 | tf_op jit(solution)/shard_map/ppermute | solution.py:369
  74.2 2.1 %collective-permute-start.11 = (bf16[1024,384]{1,0:T(8,128)(2,1)S(1)}, bf16[1024,384]{1,0:T(8,128)(2,1)S(1)}, u32[]{:S(2)}, u32[]{:S(2)}) collective-permute-start(bf16[1024,384]{1,0:T(8,128)(2,1)S(1)} %collective-permute-done.8.refs_2_), channel_id=1, source_target_pairs={{0,4},{3,7},{4,8},{7,11},{8,12},{11,15},{12,14},{15,13},{14,10},{1... | collective-permute-start | bytes 2359304 | tf_op jit(solution)/shard_map/ppermute | solution.py:369
  76.3 1.1 absorb.22
  77.5 1.1 absorb.23
  78.7 4.0 %collective-permute-done.12.refs_2_ = bf16[1024,384]{1,0:T(8,128)(2,1)S(1)} collective-permute-done((bf16[1024,384]{1,0:T(8,128)(2,1)S(1)}, bf16[1024,384]{1,0:T(8,128)(2,1)S(1)}, u32[]{:S(2)}, u32[]{:S(2)}) %collective-permute-start.12) | collective-permute-done | bytes 786464 | tf_op jit(solution)/shard_map/ppermute | solution.py:369
  82.7 2.1 %collective-permute-start.15 = (bf16[1024,384]{1,0:T(8,128)(2,1)S(1)}, bf16[1024,384]{1,0:T(8,128)(2,1)S(1)}, u32[]{:S(2)}, u32[]{:S(2)}) collective-permute-start(bf16[1024,384]{1,0:T(8,128)(2,1)S(1)} %collective-permute-done.12.refs_2_), channel_id=1, source_target_pairs={{0,4},{3,7},{4,8},{7,11},{8,12},{11,15},{12,14},{15,13},{14,10},{1... | collective-permute-start | bytes 2359304 | tf_op jit(solution)/shard_map/ppermute | solution.py:369
  84.7 1.1 absorb.24
  85.9 1.1 absorb.25
  87.1 4.0 %collective-permute-done.11.refs_2_ = bf16[1024,384]{1,0:T(8,128)(2,1)S(1)} collective-permute-done((bf16[1024,384]{1,0:T(8,128)(2,1)S(1)}, bf16[1024,384]{1,0:T(8,128)(2,1)S(1)}, u32[]{:S(2)}, u32[]{:S(2)}) %collective-permute-start.11) | collective-permute-done | bytes 786464 | tf_op jit(solution)/shard_map/ppermute | solution.py:369
  91.1 2.1 %collective-permute-start.14 = (bf16[1024,384]{1,0:T(8,128)(2,1)S(1)}, bf16[1024,384]{1,0:T(8,128)(2,1)S(1)}, u32[]{:S(2)}, u32[]{:S(2)}) collective-permute-start(bf16[1024,384]{1,0:T(8,128)(2,1)S(1)} %collective-permute-done.11.refs_2_), channel_id=1, source_target_pairs={{0,4},{3,7},{4,8},{7,11},{8,12},{11,15},{12,14},{15,13},{14,10},{1... | collective-permute-start | bytes 2359304 | tf_op jit(solution)/shard_map/ppermute | solution.py:369
  93.2 1.1 absorb.26
  94.4 1.1 absorb.27
  95.5 4.0 %collective-permute-done.15.refs_2_ = bf16[1024,384]{1,0:T(8,128)(2,1)S(1)} collective-permute-done((bf16[1024,384]{1,0:T(8,128)(2,1)S(1)}, bf16[1024,384]{1,0:T(8,128)(2,1)S(1)}, u32[]{:S(2)}, u32[]{:S(2)}) %collective-permute-start.15) | collective-permute-done | bytes 786464 | tf_op jit(solution)/shard_map/ppermute | solution.py:369
  99.5 2.1 %collective-permute-start.18 = (bf16[1024,384]{1,0:T(8,128)(2,1)S(1)}, bf16[1024,384]{1,0:T(8,128)(2,1)S(1)}, u32[]{:S(2)}, u32[]{:S(2)}) collective-permute-start(bf16[1024,384]{1,0:T(8,128)(2,1)S(1)} %collective-permute-done.15.refs_2_), channel_id=1, source_target_pairs={{0,4},{3,7},{4,8},{7,11},{8,12},{11,15},{12,14},{15,13},{14,10},{1... | collective-permute-start | bytes 2359304 | tf_op jit(solution)/shard_map/ppermute | solution.py:369
  101.6 1.1 absorb.28
  102.7 5.2 %collective-permute-done.14.refs_2_ = bf16[1024,384]{1,0:T(8,128)(2,1)S(1)} collective-permute-done((bf16[1024,384]{1,0:T(8,128)(2,1)S(1)}, bf16[1024,384]{1,0:T(8,128)(2,1)S(1)}, u32[]{:S(2)}, u32[]{:S(2)}) %collective-permute-start.14) | collective-permute-done | bytes 786464 | tf_op jit(solution)/shard_map/ppermute | solution.py:369
  107.9 2.1 %collective-permute-start.17 = (bf16[1024,384]{1,0:T(8,128)(2,1)S(1)}, bf16[1024,384]{1,0:T(8,128)(2,1)S(1)}, u32[]{:S(2)}, u32[]{:S(2)}) collective-permute-start(bf16[1024,384]{1,0:T(8,128)(2,1)S(1)} %collective-permute-done.14.refs_2_), channel_id=1, source_target_pairs={{0,4},{3,7},{4,8},{7,11},{8,12},{11,15},{12,14},{15,13},{14,10},{1... | collective-permute-start | bytes 2359304 | tf_op jit(solution)/shard_map/ppermute | solution.py:369
  110.0 1.1 absorb.29
  111.2 5.2 %collective-permute-done.18.refs_2_ = bf16[1024,384]{1,0:T(8,128)(2,1)S(1)} collective-permute-done((bf16[1024,384]{1,0:T(8,128)(2,1)S(1)}, bf16[1024,384]{1,0:T(8,128)(2,1)S(1)}, u32[]{:S(2)}, u32[]{:S(2)}) %collective-permute-start.18) | collective-permute-done | bytes 786464 | tf_op jit(solution)/shard_map/ppermute | solution.py:369
  116.4 1.1 absorb.30
  117.5 7.3 %collective-permute-done.17.refs_2_ = bf16[1024,384]{1,0:T(8,128)(2,1)S(1)} collective-permute-done((bf16[1024,384]{1,0:T(8,128)(2,1)S(1)}, bf16[1024,384]{1,0:T(8,128)(2,1)S(1)}, u32[]{:S(2)}, u32[]{:S(2)}) %collective-permute-start.17) | collective-permute-done | bytes 786464 | tf_op jit(solution)/shard_map/ppermute | solution.py:369
  124.8 1.1 absorb.31
  126.0 1.6 %collective-permute-done.19 = f32[208,384]{1,0:T(8,128)S(1)} collective-permute-done((f32[208,384]{1,0:T(8,128)S(1)}, f32[208,384]{1,0:T(8,128)S(1)}, u32[]{:S(2)}, u32[]{:S(2)}) %collective-permute-start.19) | collective-permute-done | bytes 319520 | tf_op jit(solution)/shard_map/ppermute | solution.py:316
  127.6 0.9 fusion
  (36 shorter events, 3.8 us)
Async XLA Ops:
  2.2 3.2 %collective-permute-start = (bf16[1024,384]{1,0:T(8,128)(2,1)S(1)}, bf16[1024,384]{1,0:T(8,128)(2,1)}, u32[]{:S(2)}, u32[]{:S(2)}) collective-permute-start(bf16[1024,384]{1,0:T(8,128)(2,1)S(1)} %get-tuple-element.161), channel_id=1, source_target_pairs={{0,1},{1,0},{2,3},{3,2},{4,5},{5,4},{6,7},{7,6},{8,9},{9,8},{10,11... | collective-permute-start | bytes 2359304 | tf_op jit(solution)/shard_map/ppermute | solution.py:316
  2.7 12.7 %collective-permute-start.3 = (bf16[1024,384]{1,0:T(8,128)(2,1)S(1)}, bf16[1024,384]{1,0:T(8,128)(2,1)}, u32[]{:S(2)}, u32[]{:S(2)}) collective-permute-start(bf16[1024,384]{1,0:T(8,128)(2,1)S(1)} %get-tuple-element.88.refs_2_), channel_id=1, source_target_pairs={{0,4},{3,7},{4,8},{7,11},{8,12},{11,15},{12,14},{15,13},{14,10},{1... | collective-permute-start | bytes 2359304 | tf_op jit(solution)/shard_map/ppermute | solution.py:369
  5.3 18.4 %collective-permute-start.1 = (bf16[1024,384]{1,0:T(8,128)(2,1)}, bf16[1024,384]{1,0:T(8,128)(2,1)}, u32[]{:S(2)}, u32[]{:S(2)}) collective-permute-start(bf16[1024,384]{1,0:T(8,128)(2,1)} %collective-permute-done.refs_2_), channel_id=1, source_target_pairs={{0,4},{3,7},{4,8},{7,11},{8,12},{11,15},{12,14},{15,13},{14,10},{1... | collective-permute-start | bytes 2359304 | tf_op jit(solution)/shard_map/ppermute | solution.py:369
  15.4 16.7 %collective-permute-start.4 = (bf16[1024,384]{1,0:T(8,128)(2,1)}, bf16[1024,384]{1,0:T(8,128)(2,1)S(1)}, u32[]{:S(2)}, u32[]{:S(2)}) collective-permute-start(bf16[1024,384]{1,0:T(8,128)(2,1)} %collective-permute-done.3.refs_2_), channel_id=1, source_target_pairs={{0,4},{3,7},{4,8},{7,11},{8,12},{11,15},{12,14},{15,13},{14,10},{1... | collective-permute-start | bytes 2359304 | tf_op jit(solution)/shard_map/ppermute | solution.py:369
  18.1 16.1 %copy-start = (bf16[192,32768]{1,0:T(8,128)(2,1)S(1)}, bf16[192,32768]{1,0:T(8,128)(2,1)}, u32[]{:S(2)}) copy-start(bf16[192,32768]{1,0:T(8,128)(2,1)} %refs_0_.15) | copy-start | bytes 37748740
  21.8 29.7 %collective-permute-start.7 = (bf16[192,4096]{1,0:T(8,128)(2,1)S(1)}, bf16[192,4096]{1,0:T(8,128)(2,1)S(1)}, u32[]{:S(2)}, u32[]{:S(2)}) collective-permute-start(bf16[192,4096]{1,0:T(8,128)(2,1)S(1)} %get-tuple-element.87), channel_id=1, source_target_pairs={{0,1},{1,0},{2,3},{3,2},{4,5},{5,4},{6,7},{7,6},{8,9},{9,8},{10,11... | collective-permute-start | bytes 4718600 | tf_op jit(solution)/shard_map/ppermute | solution.py:316
  23.8 16.7 %collective-permute-start.2 = (bf16[1024,384]{1,0:T(8,128)(2,1)}, bf16[1024,384]{1,0:T(8,128)(2,1)S(1)}, u32[]{:S(2)}, u32[]{:S(2)}) collective-permute-start(bf16[1024,384]{1,0:T(8,128)(2,1)} %collective-permute-done.1.refs_2_), channel_id=1, source_target_pairs={{0,4},{3,7},{4,8},{7,11},{8,12},{11,15},{12,14},{15,13},{14,10},{1... | collective-permute-start | bytes 2359304 | tf_op jit(solution)/shard_map/ppermute | solution.py:369
  32.1 16.9 %collective-permute-start.6 = (bf16[1024,384]{1,0:T(8,128)(2,1)S(1)}, bf16[1024,384]{1,0:T(8,128)(2,1)S(1)}, u32[]{:S(2)}, u32[]{:S(2)}) collective-permute-start(bf16[1024,384]{1,0:T(8,128)(2,1)S(1)} %collective-permute-done.4.refs_2_), channel_id=1, source_target_pairs={{0,4},{3,7},{4,8},{7,11},{8,12},{11,15},{12,14},{15,13},{14,10},{1... | collective-permute-start | bytes 2359304 | tf_op jit(solution)/shard_map/ppermute | solution.py:369
  34.2 33.7 %collective-permute-start.10 = (bf16[192,4096]{1,0:T(8,128)(2,1)S(1)}, bf16[192,4096]{1,0:T(8,128)(2,1)S(1)}, u32[]{:S(2)}, u32[]{:S(2)}) collective-permute-start(bf16[192,4096]{1,0:T(8,128)(2,1)S(1)} %get-tuple-element.107), channel_id=1, source_target_pairs={{0,1},{1,0},{2,3},{3,2},{4,5},{5,4},{6,7},{7,6},{8,9},{9,8},{10,11... | collective-permute-start | bytes 4718600 | tf_op jit(solution)/shard_map/ppermute | solution.py:316
  40.5 16.9 %collective-permute-start.5 = (bf16[1024,384]{1,0:T(8,128)(2,1)S(1)}, bf16[1024,384]{1,0:T(8,128)(2,1)S(1)}, u32[]{:S(2)}, u32[]{:S(2)}) collective-permute-start(bf16[1024,384]{1,0:T(8,128)(2,1)S(1)} %collective-permute-done.2.refs_2_), channel_id=1, source_target_pairs={{0,4},{3,7},{4,8},{7,11},{8,12},{11,15},{12,14},{15,13},{14,10},{1... | collective-permute-start | bytes 2359304 | tf_op jit(solution)/shard_map/ppermute | solution.py:369
  42.6 42.1 %collective-permute-start.13 = (bf16[192,4096]{1,0:T(8,128)(2,1)S(1)}, bf16[192,4096]{1,0:T(8,128)(2,1)S(1)}, u32[]{:S(2)}, u32[]{:S(2)}) collective-permute-start(bf16[192,4096]{1,0:T(8,128)(2,1)S(1)} %get-tuple-element.124), channel_id=1, source_target_pairs={{0,1},{1,0},{2,3},{3,2},{4,5},{5,4},{6,7},{7,6},{8,9},{9,8},{10,11... | collective-permute-start | bytes 4718600 | tf_op jit(solution)/shard_map/ppermute | solution.py:316
  49.0 16.9 %collective-permute-start.9 = (bf16[1024,384]{1,0:T(8,128)(2,1)S(1)}, bf16[1024,384]{1,0:T(8,128)(2,1)S(1)}, u32[]{:S(2)}, u32[]{:S(2)}) collective-permute-start(bf16[1024,384]{1,0:T(8,128)(2,1)S(1)} %collective-permute-done.6.refs_2_), channel_id=1, source_target_pairs={{0,4},{3,7},{4,8},{7,11},{8,12},{11,15},{12,14},{15,13},{14,10},{1... | collective-permute-start | bytes 2359304 | tf_op jit(solution)/shard_map/ppermute | solution.py:369
  57.4 16.9 %collective-permute-start.8 = (bf16[1024,384]{1,0:T(8,128)(2,1)S(1)}, bf16[1024,384]{1,0:T(8,128)(2,1)S(1)}, u32[]{:S(2)}, u32[]{:S(2)}) collective-permute-start(bf16[1024,384]{1,0:T(8,128)(2,1)S(1)} %collective-permute-done.5.refs_2_), channel_id=1, source_target_pairs={{0,4},{3,7},{4,8},{7,11},{8,12},{11,15},{12,14},{15,13},{14,10},{1... | collective-permute-start | bytes 2359304 | tf_op jit(solution)/shard_map/ppermute | solution.py:369
  65.8 16.9 %collective-permute-start.12 = (bf16[1024,384]{1,0:T(8,128)(2,1)S(1)}, bf16[1024,384]{1,0:T(8,128)(2,1)S(1)}, u32[]{:S(2)}, u32[]{:S(2)}) collective-permute-start(bf16[1024,384]{1,0:T(8,128)(2,1)S(1)} %collective-permute-done.9.refs_2_), channel_id=1, source_target_pairs={{0,4},{3,7},{4,8},{7,11},{8,12},{11,15},{12,14},{15,13},{14,10},{1... | collective-permute-start | bytes 2359304 | tf_op jit(solution)/shard_map/ppermute | solution.py:369
  74.2 16.9 %collective-permute-start.11 = (bf16[1024,384]{1,0:T(8,128)(2,1)S(1)}, bf16[1024,384]{1,0:T(8,128)(2,1)S(1)}, u32[]{:S(2)}, u32[]{:S(2)}) collective-permute-start(bf16[1024,384]{1,0:T(8,128)(2,1)S(1)} %collective-permute-done.8.refs_2_), channel_id=1, source_target_pairs={{0,4},{3,7},{4,8},{7,11},{8,12},{11,15},{12,14},{15,13},{14,10},{1... | collective-permute-start | bytes 2359304 | tf_op jit(solution)/shard_map/ppermute | solution.py:369
  76.3 25.3 %collective-permute-start.16 = (bf16[192,4096]{1,0:T(8,128)(2,1)S(1)}, bf16[192,4096]{1,0:T(8,128)(2,1)S(1)}, u32[]{:S(2)}, u32[]{:S(2)}) collective-permute-start(bf16[192,4096]{1,0:T(8,128)(2,1)S(1)} %get-tuple-element.141), channel_id=1, source_target_pairs={{0,1},{1,0},{2,3},{3,2},{4,5},{5,4},{6,7},{7,6},{8,9},{9,8},{10,11... | collective-permute-start | bytes 4718600 | tf_op jit(solution)/shard_map/ppermute | solution.py:316
  82.7 16.9 %collective-permute-start.15 = (bf16[1024,384]{1,0:T(8,128)(2,1)S(1)}, bf16[1024,384]{1,0:T(8,128)(2,1)S(1)}, u32[]{:S(2)}, u32[]{:S(2)}) collective-permute-start(bf16[1024,384]{1,0:T(8,128)(2,1)S(1)} %collective-permute-done.12.refs_2_), channel_id=1, source_target_pairs={{0,4},{3,7},{4,8},{7,11},{8,12},{11,15},{12,14},{15,13},{14,10},{1... | collective-permute-start | bytes 2359304 | tf_op jit(solution)/shard_map/ppermute | solution.py:369
  91.1 16.9 %collective-permute-start.14 = (bf16[1024,384]{1,0:T(8,128)(2,1)S(1)}, bf16[1024,384]{1,0:T(8,128)(2,1)S(1)}, u32[]{:S(2)}, u32[]{:S(2)}) collective-permute-start(bf16[1024,384]{1,0:T(8,128)(2,1)S(1)} %collective-permute-done.11.refs_2_), channel_id=1, source_target_pairs={{0,4},{3,7},{4,8},{7,11},{8,12},{11,15},{12,14},{15,13},{14,10},{1... | collective-permute-start | bytes 2359304 | tf_op jit(solution)/shard_map/ppermute | solution.py:369
  99.5 16.9 %collective-permute-start.18 = (bf16[1024,384]{1,0:T(8,128)(2,1)S(1)}, bf16[1024,384]{1,0:T(8,128)(2,1)S(1)}, u32[]{:S(2)}, u32[]{:S(2)}) collective-permute-start(bf16[1024,384]{1,0:T(8,128)(2,1)S(1)} %collective-permute-done.15.refs_2_), channel_id=1, source_target_pairs={{0,4},{3,7},{4,8},{7,11},{8,12},{11,15},{12,14},{15,13},{14,10},{1... | collective-permute-start | bytes 2359304 | tf_op jit(solution)/shard_map/ppermute | solution.py:369
  107.9 16.9 %collective-permute-start.17 = (bf16[1024,384]{1,0:T(8,128)(2,1)S(1)}, bf16[1024,384]{1,0:T(8,128)(2,1)S(1)}, u32[]{:S(2)}, u32[]{:S(2)}) collective-permute-start(bf16[1024,384]{1,0:T(8,128)(2,1)S(1)} %collective-permute-done.14.refs_2_), channel_id=1, source_target_pairs={{0,4},{3,7},{4,8},{7,11},{8,12},{11,15},{12,14},{15,13},{14,10},{1... | collective-permute-start | bytes 2359304 | tf_op jit(solution)/shard_map/ppermute | solution.py:369
  124.8 2.9 %copy-start.1 = (bf16[192,384]{1,0:T(8,128)(2,1)S(1)}, bf16[192,384]{1,0:T(8,128)(2,1)}, u32[]{:S(2)}) copy-start(bf16[192,384]{1,0:T(8,128)(2,1)} %param.6) | copy-start | bytes 442372
  125.9 1.7 %collective-permute-start.19 = (f32[208,384]{1,0:T(8,128)S(1)}, f32[208,384]{1,0:T(8,128)S(1)}, u32[]{:S(2)}, u32[]{:S(2)}) collective-permute-start(f32[208,384]{1,0:T(8,128)S(1)} %get-tuple-element.159), channel_id=1, source_target_pairs={{0,1},{1,0},{2,3},{3,2},{4,5},{5,4},{6,7},{7,6},{8,9},{9,8},{10,11... | collective-permute-start | bytes 958472 | tf_op jit(solution)/shard_map/ppermute | solution.py:316
  126.0 2.5 %copy-start.2 = (f32[192]{0:T(256)}, f32[192]{0:T(256)S(1)}, u32[]{:S(2)}) copy-start(f32[192]{0:T(256)S(1)} %add_add_fusion) | copy-start | bytes 2308

commit v12 on v11

--- a/solution.py
+++ b/solution.py
@@ -131,16 +131,16 @@
     theirs_out[...] = theirs
 
 
-def absorb(where, adj_rows, borrowed, slabs, units, flags, sums):
+def absorb(where, adj_rows, borrowed, slabs, units, flags, sums, cuts=1, cut=0):
     count = len(slabs)
     rows = adj_rows.shape[0]
     depth, width = slabs[0].shape
 
     def own(k):
-        return pl.BlockSpec((rows, depth), lambda g, where: (0, where[2 + units[k]]))
+        return pl.BlockSpec((rows, depth), lambda g, where: (0, where[2 + units[k]] * cuts + cut))
 
     def other(k):
-        return pl.BlockSpec((rows, depth), lambda g, where: (0, units[k] % PER_LENT))
+        return pl.BlockSpec((rows, depth), lambda g, where: (0, units[k] % PER_LENT * cuts + cut))
 
     def whole(shape):
         return pl.BlockSpec(shape, lambda g, where: (0, 0))
@@ -283,6 +283,7 @@
         blocks = trace_blocks(chips, turns)
         rounds = len(turns)
         halves = range(CORES)
+        cuts = 2 if depth % 256 == 0 and not ships else 1
 
         groups = [[("own", 0)]] + [[(port, r) for port in turn] for r, turn in enumerate(turns, 1)]
         sources = [source for group in groups for source in group]
@@ -359,12 +360,20 @@
                 slab[port, r] = []
             for j in halves:
                 at = r - 1
-                if at > 0 and len(past) >= SLOTS:
+                if at > 0 and r <= rounds and len(past) >= SLOTS:
                     arrived = tie([slab[port, at][j] for port in turns[at - 1]], past[-SLOTS])
                     for port, piece in zip(turns[at - 1], arrived):
                         slab[port, at][j] = piece
                 if r <= rounds:
                     sending = depart(turns[r - 1], j)
+                    if r == rounds and j == 1 and cuts > 1:
+                        piece, size = sending["main"], depth // cuts
+                        last = [
+                            lax.ppermute(piece[k * size : (k + 1) * size], "row", pairs(make_route(chips, "main", r)))
+                            for k in range(cuts)
+                        ]
+                        slab["main", r].append(last)
+                        sending = {}
                     for port, piece in sending.items():
                         slab[port, r].append(lax.ppermute(piece, "row", pairs(make_route(chips, port, r))))
                     if r == REST_AT and j == 0:
@@ -372,6 +381,8 @@
                 if at == 0:
                     continue
                 gate = [slab[port, at][j] for port in turns[at - 1]]
+                if isinstance(gate[0], list):
+                    gate = [gate[0][0]]
                 if r <= rounds:
                     gate = [gate, list(sending.values())]
                 done = []
@@ -388,6 +399,12 @@
                     for _ in range(MOST if r <= rounds else len(due)):
                         if due:
                             t, part = due.pop(0)
+                            if isinstance(slab[groups[t][0]][part], list):
+                                unit = units[groups[t][0]][part]
+                                for k, piece in enumerate(last):
+                                    rows_now = adj_rows
+                                    sums = absorb(where, rows_now, borrowed, [piece], [unit], [None], sums, cuts, k)
+                                continue
                             sums = absorb(
                                 where,
                                 now,

time: 129 us -> 129 us (level)
  waiting for transfers between devices: 66.1 us -> 63.5 us
  starting transfers between devices: 30.6 us -> 32.2 us
    ppermute x14 -> x13, waiting for transfers between devices: 64.5 us -> 56.7 us  [shards(): lax.ppermute(piece, 'row', pairs(make_route(chips, port, r)))]
    ppermute x0 -> x2, waiting for transfers between devices: none -> 5.2 us  [shards(): lax.ppermute(piece[k * size:(k + 1) * size], 'row', pairs(make_route(chip...]
    ppermute x0 -> x2, starting transfers between devices: none -> 3.71 us  [shards(): lax.ppermute(piece[k * size:(k + 1) * size], 'row', pairs(make_route(chip...]
    ppermute x14 -> x13, starting transfers between devices: 29.9 us -> 27.8 us  [shards(): lax.ppermute(piece, 'row', pairs(make_route(chips, port, r)))]
    pallas_call x16 -> x17, Pallas kernels: 21.7 us -> 22.5 us  [absorb(): pl.pallas_call(functools.partial(absorb_kernel, count, flags, rows, first...]
  transfers between devices with their start and end apart: 20 -> 21, of which waited for: 15 -> 16; matrix products, arithmetic and copies ran while one was open for 2% -> 2% of each run, Pallas kernels for 19% -> 20%
where the time goes in v12:
time: 129 us; the launch traced here: 128 us
  waiting for transfers between devices  63.5 us (49%)
  starting transfers between devices  32.2 us (25%)
  Pallas kernels  26.2 us (20%)
  other arithmetic  2.96 us (2%)
  local copies, waits for them, and re-layouts  2.58 us (2%)
    ppermute x13, waiting for transfers between devices, shards(): lax.ppermute(piece, 'row', pairs(make_route(chips, port, r)))  56.7 us
    ppermute x13, starting transfers between devices, shards(): lax.ppermute(piece, 'row', pairs(make_route(chips, port, r)))  27.8 us
    pallas_call x17, Pallas kernels, absorb(): pl.pallas_call(functools.partial(absorb_kernel, count, flags, rows, first...  22.5 us
    ppermute x2, waiting for transfers between devices, shards(): lax.ppermute(piece[k * size:(k + 1) * size], 'row', pairs(make_route(chip...  5.2 us
    ppermute x2, starting transfers between devices, shards(): lax.ppermute(piece[k * size:(k + 1) * size], 'row', pairs(make_route(chip...  3.71 us
    pallas_call x1, Pallas kernels, lend(): pl.pallas_call(functools.partial(lend_kernel, sizes, first, depth), in_sp...  3.69 us
  transfers between devices with their start and end apart: 21, of which 16 were waited for; matrix products, arithmetic and copies ran while one was open for 2% of the time, Pallas kernels for 20%

profile of v12, /device:TPU:0, one launch (start us, length us, event | category | flops | bytes accessed | tf_op | source)
XLA Modules:
  0.0 128.3 jit_solution(11239428723417385120)
XLA Ops:
  0.6 1.5 %dynamic-slice_bitcast_fusion = (bf16[1024,384]{1,0:T(8,128)(2,1)S(1)}, bf16[1024,384]{1,0:T(8,128)(2,1)S(1)}) fusion(bf16[2,1024,384]{2,1,0:T(8,128)(2,1)} %param.5, s32[]{:T(128)S(6)} %select_n.12, s32[]{:T(128)S(6)} %select_n.11), kind=kLoop, calls=%fused_computation.4 | loop fusion | bytes 3145736 | tf_op jit(solution)/shard_map/jit(dynamic_index_in_dim)/squeeze | solution.py:344
  2.7 2.6 %collective-permute-start.1 = (bf16[1024,384]{1,0:T(8,128)(2,1)S(1)}, bf16[1024,384]{1,0:T(8,128)(2,1)}, u32[]{:S(2)}, u32[]{:S(2)}) collective-permute-start(bf16[1024,384]{1,0:T(8,128)(2,1)S(1)} %get-tuple-element.90.refs_2_), channel_id=1, source_target_pairs={{0,4},{3,7},{4,8},{7,11},{8,12},{11,15},{12,14},{15,13},{14,10},{1... | collective-permute-start | bytes 2359304 | tf_op jit(solution)/shard_map/ppermute | solution.py:378
  5.3 2.3 %collective-permute-start.3 = (bf16[1024,384]{1,0:T(8,128)(2,1)}, bf16[1024,384]{1,0:T(8,128)(2,1)}, u32[]{:S(2)}, u32[]{:S(2)}) collective-permute-start(bf16[1024,384]{1,0:T(8,128)(2,1)} %collective-permute-done.refs_2_), channel_id=1, source_target_pairs={{0,4},{3,7},{4,8},{7,11},{8,12},{11,15},{12,14},{15,13},{14,10},{1... | collective-permute-start | bytes 2359304 | tf_op jit(solution)/shard_map/ppermute | solution.py:378
  7.7 7.7 %collective-permute-done.1.refs_2_ = bf16[1024,384]{1,0:T(8,128)(2,1)} collective-permute-done((bf16[1024,384]{1,0:T(8,128)(2,1)S(1)}, bf16[1024,384]{1,0:T(8,128)(2,1)}, u32[]{:S(2)}, u32[]{:S(2)}) %collective-permute-start.1) | collective-permute-done | bytes 786464 | tf_op jit(solution)/shard_map/ppermute | solution.py:378
  15.4 2.1 %collective-permute-start.5 = (bf16[1024,384]{1,0:T(8,128)(2,1)}, bf16[1024,384]{1,0:T(8,128)(2,1)S(1)}, u32[]{:S(2)}, u32[]{:S(2)}) collective-permute-start(bf16[1024,384]{1,0:T(8,128)(2,1)} %collective-permute-done.1.refs_2_), channel_id=1, source_target_pairs={{0,4},{3,7},{4,8},{7,11},{8,12},{11,15},{12,14},{15,13},{14,10},{1... | collective-permute-start | bytes 2359304 | tf_op jit(solution)/shard_map/ppermute | solution.py:378
  18.1 3.7 %lend.1 = (bf16[192,4096]{1,0:T(8,128)(2,1)S(1)}, bf16[192,4096]{1,0:T(8,128)(2,1)S(1)}, bf16[192,4096]{1,0:T(8,128)(2,1)S(1)}, bf16[192,4096]{1,0:T(8,128)(2,1)S(1)}) custom-call(s32[34]{0:T(128)S(1)} %fusion.2.where, bf16[192,32768]{1,0:T(8,128)(2,1)} %refs_0_.18), custom_call_target="tpu_custom_call" | custom-call | bytes 1024 | tf_op jit(solution)/shard_map/lend/pallas_call | solution.py:103
  21.9 1.9 %collective-permute-done.3.refs_2_ = bf16[1024,384]{1,0:T(8,128)(2,1)} collective-permute-done((bf16[1024,384]{1,0:T(8,128)(2,1)}, bf16[1024,384]{1,0:T(8,128)(2,1)}, u32[]{:S(2)}, u32[]{:S(2)}) %collective-permute-start.3) | collective-permute-done | bytes 786464 | tf_op jit(solution)/shard_map/ppermute | solution.py:378
  23.8 2.1 %collective-permute-start.4 = (bf16[1024,384]{1,0:T(8,128)(2,1)}, bf16[1024,384]{1,0:T(8,128)(2,1)S(1)}, u32[]{:S(2)}, u32[]{:S(2)}) collective-permute-start(bf16[1024,384]{1,0:T(8,128)(2,1)} %collective-permute-done.3.refs_2_), channel_id=1, source_target_pairs={{0,4},{3,7},{4,8},{7,11},{8,12},{11,15},{12,14},{15,13},{14,10},{1... | collective-permute-start | bytes 2359304 | tf_op jit(solution)/shard_map/ppermute | solution.py:378
  25.9 6.2 %collective-permute-done.5.refs_2_ = bf16[1024,384]{1,0:T(8,128)(2,1)S(1)} collective-permute-done((bf16[1024,384]{1,0:T(8,128)(2,1)}, bf16[1024,384]{1,0:T(8,128)(2,1)S(1)}, u32[]{:S(2)}, u32[]{:S(2)}) %collective-permute-start.5) | collective-permute-done | bytes 786464 | tf_op jit(solution)/shard_map/ppermute | solution.py:378
  32.1 2.1 %collective-permute-start.7 = (bf16[1024,384]{1,0:T(8,128)(2,1)S(1)}, bf16[1024,384]{1,0:T(8,128)(2,1)S(1)}, u32[]{:S(2)}, u32[]{:S(2)}) collective-permute-start(bf16[1024,384]{1,0:T(8,128)(2,1)S(1)} %collective-permute-done.5.refs_2_), channel_id=1, source_target_pairs={{0,4},{3,7},{4,8},{7,11},{8,12},{11,15},{12,14},{15,13},{14,10},{1... | collective-permute-start | bytes 2359304 | tf_op jit(solution)/shard_map/ppermute | solution.py:378
  34.7 5.8 %collective-permute-done.4.refs_2_ = bf16[1024,384]{1,0:T(8,128)(2,1)S(1)} collective-permute-done((bf16[1024,384]{1,0:T(8,128)(2,1)}, bf16[1024,384]{1,0:T(8,128)(2,1)S(1)}, u32[]{:S(2)}, u32[]{:S(2)}) %collective-permute-start.4) | collective-permute-done | bytes 786464 | tf_op jit(solution)/shard_map/ppermute | solution.py:378
  40.5 2.1 %collective-permute-start.6 = (bf16[1024,384]{1,0:T(8,128)(2,1)S(1)}, bf16[1024,384]{1,0:T(8,128)(2,1)S(1)}, u32[]{:S(2)}, u32[]{:S(2)}) collective-permute-start(bf16[1024,384]{1,0:T(8,128)(2,1)S(1)} %collective-permute-done.4.refs_2_), channel_id=1, source_target_pairs={{0,4},{3,7},{4,8},{7,11},{8,12},{11,15},{12,14},{15,13},{14,10},{1... | collective-permute-start | bytes 2359304 | tf_op jit(solution)/shard_map/ppermute | solution.py:378
  43.1 5.8 %collective-permute-done.7.refs_2_ = bf16[1024,384]{1,0:T(8,128)(2,1)S(1)} collective-permute-done((bf16[1024,384]{1,0:T(8,128)(2,1)S(1)}, bf16[1024,384]{1,0:T(8,128)(2,1)S(1)}, u32[]{:S(2)}, u32[]{:S(2)}) %collective-permute-start.7) | collective-permute-done | bytes 786464 | tf_op jit(solution)/shard_map/ppermute | solution.py:378
  49.0 2.1 %collective-permute-start.10 = (bf16[1024,384]{1,0:T(8,128)(2,1)S(1)}, bf16[1024,384]{1,0:T(8,128)(2,1)S(1)}, u32[]{:S(2)}, u32[]{:S(2)}) collective-permute-start(bf16[1024,384]{1,0:T(8,128)(2,1)S(1)} %collective-permute-done.7.refs_2_), channel_id=1, source_target_pairs={{0,4},{3,7},{4,8},{7,11},{8,12},{11,15},{12,14},{15,13},{14,10},{1... | collective-permute-start | bytes 2359304 | tf_op jit(solution)/shard_map/ppermute | solution.py:378
  51.6 1.1 absorb.17
  52.7 2.3 %absorb.18 = (f32[192,384]{1,0:T(8,128)S(1)}, f32[208,384]{1,0:T(8,128)S(1)}) custom-call(s32[34]{0:T(128)S(1)} %fusion.2.where, bf16[192,32768]{1,0:T(8,128)(2,1)S(1)} %copy-done, bf16[192,4096]{1,0:T(8,128)(2,1)S(1)} %collective-permute-done.8.refs_1_, ...), custom_call_target="tpu_custom_call", output_to_operand_aliasing={{0}: (4, {}), {1}: (5, {})} | custom-call | bytes 1024 | tf_op jit(solution)/shard_map/absorb/pallas_call | solution.py:157
  55.1 2.3 %collective-permute-done.6.refs_2_ = bf16[1024,384]{1,0:T(8,128)(2,1)S(1)} collective-permute-done((bf16[1024,384]{1,0:T(8,128)(2,1)S(1)}, bf16[1024,384]{1,0:T(8,128)(2,1)S(1)}, u32[]{:S(2)}, u32[]{:S(2)}) %collective-permute-start.6) | collective-permute-done | bytes 786464 | tf_op jit(solution)/shard_map/ppermute | solution.py:378
  57.4 2.1 %collective-permute-start.9 = (bf16[1024,384]{1,0:T(8,128)(2,1)S(1)}, bf16[1024,384]{1,0:T(8,128)(2,1)S(1)}, u32[]{:S(2)}, u32[]{:S(2)}) collective-permute-start(bf16[1024,384]{1,0:T(8,128)(2,1)S(1)} %collective-permute-done.6.refs_2_), channel_id=1, source_target_pairs={{0,4},{3,7},{4,8},{7,11},{8,12},{11,15},{12,14},{15,13},{14,10},{1... | collective-permute-start | bytes 2359304 | tf_op jit(solution)/shard_map/ppermute | solution.py:378
  59.5 2.3 %absorb.19 = (f32[192,384]{1,0:T(8,128)S(1)}, f32[208,384]{1,0:T(8,128)S(1)}) custom-call(s32[34]{0:T(128)S(1)} %fusion.2.where, bf16[192,32768]{1,0:T(8,128)(2,1)S(1)} %copy-done, bf16[192,4096]{1,0:T(8,128)(2,1)S(1)} %collective-permute-done.8.refs_1_, ...), custom_call_target="tpu_custom_call", output_to_operand_aliasing={{0}: (4, {}), {1}: (5, {})} | custom-call | bytes 1024 | tf_op jit(solution)/shard_map/absorb/pallas_call | solution.py:157
  61.8 2.3 %absorb.20 = (f32[192,384]{1,0:T(8,128)S(1)}, f32[208,384]{1,0:T(8,128)S(1)}) custom-call(s32[34]{0:T(128)S(1)} %fusion.2.where, bf16[192,32768]{1,0:T(8,128)(2,1)S(1)} %copy-done, bf16[192,4096]{1,0:T(8,128)(2,1)S(1)} %collective-permute-done.8.refs_1_, ...), custom_call_target="tpu_custom_call", output_to_operand_aliasing={{0}: (4, {}), {1}: (5, {})} | custom-call | bytes 1024 | tf_op jit(solution)/shard_map/absorb/pallas_call | solution.py:157
  64.7 1.1 collective-permute-done.10.refs_2_
  65.8 2.1 %collective-permute-start.13 = (bf16[1024,384]{1,0:T(8,128)(2,1)S(1)}, bf16[1024,384]{1,0:T(8,128)(2,1)S(1)}, u32[]{:S(2)}, u32[]{:S(2)}) collective-permute-start(bf16[1024,384]{1,0:T(8,128)(2,1)S(1)} %collective-permute-done.10.refs_2_), channel_id=1, source_target_pairs={{0,4},{3,7},{4,8},{7,11},{8,12},{11,15},{12,14},{15,13},{14,10},{1... | collective-permute-start | bytes 2359304 | tf_op jit(solution)/shard_map/ppermute | solution.py:378
  67.9 1.1 absorb.21
  69.1 1.1 absorb.22
  70.2 4.0 %collective-permute-done.9.refs_2_ = bf16[1024,384]{1,0:T(8,128)(2,1)S(1)} collective-permute-done((bf16[1024,384]{1,0:T(8,128)(2,1)S(1)}, bf16[1024,384]{1,0:T(8,128)(2,1)S(1)}, u32[]{:S(2)}, u32[]{:S(2)}) %collective-permute-start.9) | collective-permute-done | bytes 786464 | tf_op jit(solution)/shard_map/ppermute | solution.py:378
  74.2 2.1 %collective-permute-start.12 = (bf16[1024,384]{1,0:T(8,128)(2,1)S(1)}, bf16[1024,384]{1,0:T(8,128)(2,1)S(1)}, u32[]{:S(2)}, u32[]{:S(2)}) collective-permute-start(bf16[1024,384]{1,0:T(8,128)(2,1)S(1)} %collective-permute-done.9.refs_2_), channel_id=1, source_target_pairs={{0,4},{3,7},{4,8},{7,11},{8,12},{11,15},{12,14},{15,13},{14,10},{1... | collective-permute-start | bytes 2359304 | tf_op jit(solution)/shard_map/ppermute | solution.py:378
  76.3 1.1 absorb.23
  77.5 1.1 absorb.24
  78.7 4.0 %collective-permute-done.13.refs_2_ = bf16[1024,384]{1,0:T(8,128)(2,1)S(1)} collective-permute-done((bf16[1024,384]{1,0:T(8,128)(2,1)S(1)}, bf16[1024,384]{1,0:T(8,128)(2,1)S(1)}, u32[]{:S(2)}, u32[]{:S(2)}) %collective-permute-start.13) | collective-permute-done | bytes 786464 | tf_op jit(solution)/shard_map/ppermute | solution.py:378
  82.7 2.1 %collective-permute-start.16 = (bf16[1024,384]{1,0:T(8,128)(2,1)S(1)}, bf16[1024,384]{1,0:T(8,128)(2,1)S(1)}, u32[]{:S(2)}, u32[]{:S(2)}) collective-permute-start(bf16[1024,384]{1,0:T(8,128)(2,1)S(1)} %collective-permute-done.13.refs_2_), channel_id=1, source_target_pairs={{0,4},{3,7},{4,8},{7,11},{8,12},{11,15},{12,14},{15,13},{14,10},{1... | collective-permute-start | bytes 2359304 | tf_op jit(solution)/shard_map/ppermute | solution.py:378
  84.7 1.1 absorb.25
  85.9 1.1 absorb.26
  87.1 4.0 %collective-permute-done.12.refs_2_ = bf16[1024,384]{1,0:T(8,128)(2,1)S(1)} collective-permute-done((bf16[1024,384]{1,0:T(8,128)(2,1)S(1)}, bf16[1024,384]{1,0:T(8,128)(2,1)S(1)}, u32[]{:S(2)}, u32[]{:S(2)}) %collective-permute-start.12) | collective-permute-done | bytes 786464 | tf_op jit(solution)/shard_map/ppermute | solution.py:378
  91.1 2.1 %collective-permute-start.15 = (bf16[1024,384]{1,0:T(8,128)(2,1)S(1)}, bf16[1024,384]{1,0:T(8,128)(2,1)S(1)}, u32[]{:S(2)}, u32[]{:S(2)}) collective-permute-start(bf16[1024,384]{1,0:T(8,128)(2,1)S(1)} %collective-permute-done.12.refs_2_), channel_id=1, source_target_pairs={{0,4},{3,7},{4,8},{7,11},{8,12},{11,15},{12,14},{15,13},{14,10},{1... | collective-permute-start | bytes 2359304 | tf_op jit(solution)/shard_map/ppermute | solution.py:378
  93.2 1.1 absorb.27
  94.4 1.1 absorb.28
  95.5 4.0 %collective-permute-done.16.refs_2_ = bf16[1024,384]{1,0:T(8,128)(2,1)S(1)} collective-permute-done((bf16[1024,384]{1,0:T(8,128)(2,1)S(1)}, bf16[1024,384]{1,0:T(8,128)(2,1)S(1)}, u32[]{:S(2)}, u32[]{:S(2)}) %collective-permute-start.16) | collective-permute-done | bytes 786464 | tf_op jit(solution)/shard_map/ppermute | solution.py:378
  99.5 2.1 %collective-permute-start.19 = (bf16[1024,384]{1,0:T(8,128)(2,1)S(1)}, bf16[1024,384]{1,0:T(8,128)(2,1)S(1)}, u32[]{:S(2)}, u32[]{:S(2)}) collective-permute-start(bf16[1024,384]{1,0:T(8,128)(2,1)S(1)} %collective-permute-done.16.refs_2_), channel_id=1, source_target_pairs={{0,4},{3,7},{4,8},{7,11},{8,12},{11,15},{12,14},{15,13},{14,10},{1... | collective-permute-start | bytes 2359304 | tf_op jit(solution)/shard_map/ppermute | solution.py:378
  101.6 1.1 absorb.29
  102.7 5.2 %collective-permute-done.15.refs_2_ = bf16[1024,384]{1,0:T(8,128)(2,1)S(1)} collective-permute-done((bf16[1024,384]{1,0:T(8,128)(2,1)S(1)}, bf16[1024,384]{1,0:T(8,128)(2,1)S(1)}, u32[]{:S(2)}, u32[]{:S(2)}) %collective-permute-start.15) | collective-permute-done | bytes 786464 | tf_op jit(solution)/shard_map/ppermute | solution.py:378
  108.0 2.1 %collective-permute-start.18 = (bf16[512,384]{1,0:T(8,128)(2,1)S(1)}, bf16[512,384]{1,0:T(8,128)(2,1)S(1)}, u32[]{:S(2)}, u32[]{:S(2)}) collective-permute-start(bf16[512,384]{1,0:T(8,128)(2,1)S(1)} %get-tuple-element.158), channel_id=1, source_target_pairs={{0,4},{3,7},{4,8},{7,11},{8,12},{11,15},{12,14},{15,13},{14,10},{1... | collective-permute-start | bytes 1179656 | tf_op jit(solution)/shard_map/ppermute | solution.py:372
  110.2 1.6 %collective-permute-start.17 = (bf16[512,384]{1,0:T(8,128)(2,1)S(1)}, bf16[512,384]{1,0:T(8,128)(2,1)S(1)}, u32[]{:S(2)}, u32[]{:S(2)}) collective-permute-start(bf16[512,384]{1,0:T(8,128)(2,1)S(1)} %get-tuple-element.159), channel_id=1, source_target_pairs={{0,4},{3,7},{4,8},{7,11},{8,12},{11,15},{12,14},{15,13},{14,10},{1... | collective-permute-start | bytes 1179656 | tf_op jit(solution)/shard_map/ppermute | solution.py:372
  111.7 4.6 %collective-permute-done.19.refs_2_ = bf16[1024,384]{1,0:T(8,128)(2,1)S(1)} collective-permute-done((bf16[1024,384]{1,0:T(8,128)(2,1)S(1)}, bf16[1024,384]{1,0:T(8,128)(2,1)S(1)}, u32[]{:S(2)}, u32[]{:S(2)}) %collective-permute-start.19) | collective-permute-done | bytes 786464 | tf_op jit(solution)/shard_map/ppermute | solution.py:378
  116.4 1.1 absorb.30
  117.5 1.1 absorb.31
  118.7 1.9 %collective-permute-done.18.refs_2_ = bf16[512,384]{1,0:T(8,128)(2,1)S(1)} collective-permute-done((bf16[512,384]{1,0:T(8,128)(2,1)S(1)}, bf16[512,384]{1,0:T(8,128)(2,1)S(1)}, u32[]{:S(2)}, u32[]{:S(2)}) %collective-permute-start.18) | collective-permute-done | bytes 393248 | tf_op jit(solution)/shard_map/ppermute | solution.py:372
  121.5 3.3 %collective-permute-done.17.refs_2_ = bf16[512,384]{1,0:T(8,128)(2,1)S(1)} collective-permute-done((bf16[512,384]{1,0:T(8,128)(2,1)S(1)}, bf16[512,384]{1,0:T(8,128)(2,1)S(1)}, u32[]{:S(2)}, u32[]{:S(2)}) %collective-permute-start.17) | collective-permute-done | bytes 393248 | tf_op jit(solution)/shard_map/ppermute | solution.py:372
  125.8 1.6 %collective-permute-done.20 = f32[208,384]{1,0:T(8,128)S(1)} collective-permute-done((f32[208,384]{1,0:T(8,128)S(1)}, f32[208,384]{1,0:T(8,128)S(1)}, u32[]{:S(2)}, u32[]{:S(2)}) %collective-permute-start.20) | collective-permute-done | bytes 319520 | tf_op jit(solution)/shard_map/ppermute | solution.py:317
  (40 shorter events, 6.5 us)
Async XLA Ops:
  2.2 3.2 %collective-permute-start = (bf16[1024,384]{1,0:T(8,128)(2,1)S(1)}, bf16[1024,384]{1,0:T(8,128)(2,1)}, u32[]{:S(2)}, u32[]{:S(2)}) collective-permute-start(bf16[1024,384]{1,0:T(8,128)(2,1)S(1)} %get-tuple-element.157), channel_id=1, source_target_pairs={{0,1},{1,0},{2,3},{3,2},{4,5},{5,4},{6,7},{7,6},{8,9},{9,8},{10,11... | collective-permute-start | bytes 2359304 | tf_op jit(solution)/shard_map/ppermute | solution.py:317
  2.7 12.7 %collective-permute-start.1 = (bf16[1024,384]{1,0:T(8,128)(2,1)S(1)}, bf16[1024,384]{1,0:T(8,128)(2,1)}, u32[]{:S(2)}, u32[]{:S(2)}) collective-permute-start(bf16[1024,384]{1,0:T(8,128)(2,1)S(1)} %get-tuple-element.90.refs_2_), channel_id=1, source_target_pairs={{0,4},{3,7},{4,8},{7,11},{8,12},{11,15},{12,14},{15,13},{14,10},{1... | collective-permute-start | bytes 2359304 | tf_op jit(solution)/shard_map/ppermute | solution.py:378
  5.3 18.4 %collective-permute-start.3 = (bf16[1024,384]{1,0:T(8,128)(2,1)}, bf16[1024,384]{1,0:T(8,128)(2,1)}, u32[]{:S(2)}, u32[]{:S(2)}) collective-permute-start(bf16[1024,384]{1,0:T(8,128)(2,1)} %collective-permute-done.refs_2_), channel_id=1, source_target_pairs={{0,4},{3,7},{4,8},{7,11},{8,12},{11,15},{12,14},{15,13},{14,10},{1... | collective-permute-start | bytes 2359304 | tf_op jit(solution)/shard_map/ppermute | solution.py:378
  15.4 16.7 %collective-permute-start.5 = (bf16[1024,384]{1,0:T(8,128)(2,1)}, bf16[1024,384]{1,0:T(8,128)(2,1)S(1)}, u32[]{:S(2)}, u32[]{:S(2)}) collective-permute-start(bf16[1024,384]{1,0:T(8,128)(2,1)} %collective-permute-done.1.refs_2_), channel_id=1, source_target_pairs={{0,4},{3,7},{4,8},{7,11},{8,12},{11,15},{12,14},{15,13},{14,10},{1... | collective-permute-start | bytes 2359304 | tf_op jit(solution)/shard_map/ppermute | solution.py:378
  18.1 16.1 %copy-start = (bf16[192,32768]{1,0:T(8,128)(2,1)S(1)}, bf16[192,32768]{1,0:T(8,128)(2,1)}, u32[]{:S(2)}) copy-start(bf16[192,32768]{1,0:T(8,128)(2,1)} %refs_0_.18) | copy-start | bytes 37748740
  21.8 29.7 %collective-permute-start.8 = (bf16[192,4096]{1,0:T(8,128)(2,1)S(1)}, bf16[192,4096]{1,0:T(8,128)(2,1)S(1)}, u32[]{:S(2)}, u32[]{:S(2)}) collective-permute-start(bf16[192,4096]{1,0:T(8,128)(2,1)S(1)} %get-tuple-element.89), channel_id=1, source_target_pairs={{0,1},{1,0},{2,3},{3,2},{4,5},{5,4},{6,7},{7,6},{8,9},{9,8},{10,11... | collective-permute-start | bytes 4718600 | tf_op jit(solution)/shard_map/ppermute | solution.py:317
  23.8 16.7 %collective-permute-start.4 = (bf16[1024,384]{1,0:T(8,128)(2,1)}, bf16[1024,384]{1,0:T(8,128)(2,1)S(1)}, u32[]{:S(2)}, u32[]{:S(2)}) collective-permute-start(bf16[1024,384]{1,0:T(8,128)(2,1)} %collective-permute-done.3.refs_2_), channel_id=1, source_target_pairs={{0,4},{3,7},{4,8},{7,11},{8,12},{11,15},{12,14},{15,13},{14,10},{1... | collective-permute-start | bytes 2359304 | tf_op jit(solution)/shard_map/ppermute | solution.py:378
  32.1 16.9 %collective-permute-start.7 = (bf16[1024,384]{1,0:T(8,128)(2,1)S(1)}, bf16[1024,384]{1,0:T(8,128)(2,1)S(1)}, u32[]{:S(2)}, u32[]{:S(2)}) collective-permute-start(bf16[1024,384]{1,0:T(8,128)(2,1)S(1)} %collective-permute-done.5.refs_2_), channel_id=1, source_target_pairs={{0,4},{3,7},{4,8},{7,11},{8,12},{11,15},{12,14},{15,13},{14,10},{1... | collective-permute-start | bytes 2359304 | tf_op jit(solution)/shard_map/ppermute | solution.py:378
  34.2 33.7 %collective-permute-start.11 = (bf16[192,4096]{1,0:T(8,128)(2,1)S(1)}, bf16[192,4096]{1,0:T(8,128)(2,1)S(1)}, u32[]{:S(2)}, u32[]{:S(2)}) collective-permute-start(bf16[192,4096]{1,0:T(8,128)(2,1)S(1)} %get-tuple-element.106), channel_id=1, source_target_pairs={{0,1},{1,0},{2,3},{3,2},{4,5},{5,4},{6,7},{7,6},{8,9},{9,8},{10,11... | collective-permute-start | bytes 4718600 | tf_op jit(solution)/shard_map/ppermute | solution.py:317
  40.5 16.9 %collective-permute-start.6 = (bf16[1024,384]{1,0:T(8,128)(2,1)S(1)}, bf16[1024,384]{1,0:T(8,128)(2,1)S(1)}, u32[]{:S(2)}, u32[]{:S(2)}) collective-permute-start(bf16[1024,384]{1,0:T(8,128)(2,1)S(1)} %collective-permute-done.4.refs_2_), channel_id=1, source_target_pairs={{0,4},{3,7},{4,8},{7,11},{8,12},{11,15},{12,14},{15,13},{14,10},{1... | collective-permute-start | bytes 2359304 | tf_op jit(solution)/shard_map/ppermute | solution.py:378
  42.6 42.1 %collective-permute-start.14 = (bf16[192,4096]{1,0:T(8,128)(2,1)S(1)}, bf16[192,4096]{1,0:T(8,128)(2,1)S(1)}, u32[]{:S(2)}, u32[]{:S(2)}) collective-permute-start(bf16[192,4096]{1,0:T(8,128)(2,1)S(1)} %get-tuple-element.123), channel_id=1, source_target_pairs={{0,1},{1,0},{2,3},{3,2},{4,5},{5,4},{6,7},{7,6},{8,9},{9,8},{10,11... | collective-permute-start | bytes 4718600 | tf_op jit(solution)/shard_map/ppermute | solution.py:317
  49.0 16.9 %collective-permute-start.10 = (bf16[1024,384]{1,0:T(8,128)(2,1)S(1)}, bf16[1024,384]{1,0:T(8,128)(2,1)S(1)}, u32[]{:S(2)}, u32[]{:S(2)}) collective-permute-start(bf16[1024,384]{1,0:T(8,128)(2,1)S(1)} %collective-permute-done.7.refs_2_), channel_id=1, source_target_pairs={{0,4},{3,7},{4,8},{7,11},{8,12},{11,15},{12,14},{15,13},{14,10},{1... | collective-permute-start | bytes 2359304 | tf_op jit(solution)/shard_map/ppermute | solution.py:378
  57.4 16.9 %collective-permute-start.9 = (bf16[1024,384]{1,0:T(8,128)(2,1)S(1)}, bf16[1024,384]{1,0:T(8,128)(2,1)S(1)}, u32[]{:S(2)}, u32[]{:S(2)}) collective-permute-start(bf16[1024,384]{1,0:T(8,128)(2,1)S(1)} %collective-permute-done.6.refs_2_), channel_id=1, source_target_pairs={{0,4},{3,7},{4,8},{7,11},{8,12},{11,15},{12,14},{15,13},{14,10},{1... | collective-permute-start | bytes 2359304 | tf_op jit(solution)/shard_map/ppermute | solution.py:378
  65.8 16.9 %collective-permute-start.13 = (bf16[1024,384]{1,0:T(8,128)(2,1)S(1)}, bf16[1024,384]{1,0:T(8,128)(2,1)S(1)}, u32[]{:S(2)}, u32[]{:S(2)}) collective-permute-start(bf16[1024,384]{1,0:T(8,128)(2,1)S(1)} %collective-permute-done.10.refs_2_), channel_id=1, source_target_pairs={{0,4},{3,7},{4,8},{7,11},{8,12},{11,15},{12,14},{15,13},{14,10},{1... | collective-permute-start | bytes 2359304 | tf_op jit(solution)/shard_map/ppermute | solution.py:378
  74.2 16.9 %collective-permute-start.12 = (bf16[1024,384]{1,0:T(8,128)(2,1)S(1)}, bf16[1024,384]{1,0:T(8,128)(2,1)S(1)}, u32[]{:S(2)}, u32[]{:S(2)}) collective-permute-start(bf16[1024,384]{1,0:T(8,128)(2,1)S(1)} %collective-permute-done.9.refs_2_), channel_id=1, source_target_pairs={{0,4},{3,7},{4,8},{7,11},{8,12},{11,15},{12,14},{15,13},{14,10},{1... | collective-permute-start | bytes 2359304 | tf_op jit(solution)/shard_map/ppermute | solution.py:378
  76.3 25.3 %collective-permute-start.2 = (bf16[192,4096]{1,0:T(8,128)(2,1)S(1)}, bf16[192,4096]{1,0:T(8,128)(2,1)S(1)}, u32[]{:S(2)}, u32[]{:S(2)}) collective-permute-start(bf16[192,4096]{1,0:T(8,128)(2,1)S(1)} %get-tuple-element.83), channel_id=1, source_target_pairs={{0,1},{1,0},{2,3},{3,2},{4,5},{5,4},{6,7},{7,6},{8,9},{9,8},{10,11... | collective-permute-start | bytes 4718600 | tf_op jit(solution)/shard_map/ppermute | solution.py:317
  82.7 16.9 %collective-permute-start.16 = (bf16[1024,384]{1,0:T(8,128)(2,1)S(1)}, bf16[1024,384]{1,0:T(8,128)(2,1)S(1)}, u32[]{:S(2)}, u32[]{:S(2)}) collective-permute-start(bf16[1024,384]{1,0:T(8,128)(2,1)S(1)} %collective-permute-done.13.refs_2_), channel_id=1, source_target_pairs={{0,4},{3,7},{4,8},{7,11},{8,12},{11,15},{12,14},{15,13},{14,10},{1... | collective-permute-start | bytes 2359304 | tf_op jit(solution)/shard_map/ppermute | solution.py:378
  91.1 16.9 %collective-permute-start.15 = (bf16[1024,384]{1,0:T(8,128)(2,1)S(1)}, bf16[1024,384]{1,0:T(8,128)(2,1)S(1)}, u32[]{:S(2)}, u32[]{:S(2)}) collective-permute-start(bf16[1024,384]{1,0:T(8,128)(2,1)S(1)} %collective-permute-done.12.refs_2_), channel_id=1, source_target_pairs={{0,4},{3,7},{4,8},{7,11},{8,12},{11,15},{12,14},{15,13},{14,10},{1... | collective-permute-start | bytes 2359304 | tf_op jit(solution)/shard_map/ppermute | solution.py:378
  99.5 16.9 %collective-permute-start.19 = (bf16[1024,384]{1,0:T(8,128)(2,1)S(1)}, bf16[1024,384]{1,0:T(8,128)(2,1)S(1)}, u32[]{:S(2)}, u32[]{:S(2)}) collective-permute-start(bf16[1024,384]{1,0:T(8,128)(2,1)S(1)} %collective-permute-done.16.refs_2_), channel_id=1, source_target_pairs={{0,4},{3,7},{4,8},{7,11},{8,12},{11,15},{12,14},{15,13},{14,10},{1... | collective-permute-start | bytes 2359304 | tf_op jit(solution)/shard_map/ppermute | solution.py:378
  108.0 12.6 %collective-permute-start.18 = (bf16[512,384]{1,0:T(8,128)(2,1)S(1)}, bf16[512,384]{1,0:T(8,128)(2,1)S(1)}, u32[]{:S(2)}, u32[]{:S(2)}) collective-permute-start(bf16[512,384]{1,0:T(8,128)(2,1)S(1)} %get-tuple-element.158), channel_id=1, source_target_pairs={{0,4},{3,7},{4,8},{7,11},{8,12},{11,15},{12,14},{15,13},{14,10},{1... | collective-permute-start | bytes 1179656 | tf_op jit(solution)/shard_map/ppermute | solution.py:372
  110.2 14.6 %collective-permute-start.17 = (bf16[512,384]{1,0:T(8,128)(2,1)S(1)}, bf16[512,384]{1,0:T(8,128)(2,1)S(1)}, u32[]{:S(2)}, u32[]{:S(2)}) collective-permute-start(bf16[512,384]{1,0:T(8,128)(2,1)S(1)} %get-tuple-element.159), channel_id=1, source_target_pairs={{0,4},{3,7},{4,8},{7,11},{8,12},{11,15},{12,14},{15,13},{14,10},{1... | collective-permute-start | bytes 1179656 | tf_op jit(solution)/shard_map/ppermute | solution.py:372
  124.8 2.6 %copy-start.1 = (bf16[192,384]{1,0:T(8,128)(2,1)S(1)}, bf16[192,384]{1,0:T(8,128)(2,1)}, u32[]{:S(2)}) copy-start(bf16[192,384]{1,0:T(8,128)(2,1)} %param.6) | copy-start | bytes 442372
  125.7 1.7 %collective-permute-start.20 = (f32[208,384]{1,0:T(8,128)S(1)}, f32[208,384]{1,0:T(8,128)S(1)}, u32[]{:S(2)}, u32[]{:S(2)}) collective-permute-start(f32[208,384]{1,0:T(8,128)S(1)} %get-tuple-element.155), channel_id=1, source_target_pairs={{0,1},{1,0},{2,3},{3,2},{4,5},{5,4},{6,7},{7,6},{8,9},{9,8},{10,11... | collective-permute-start | bytes 958472 | tf_op jit(solution)/shard_map/ppermute | solution.py:317
  125.8 2.5 %copy-start.2 = (f32[192]{0:T(256)}, f32[192]{0:T(256)S(1)}, u32[]{:S(2)}) copy-start(f32[192]{0:T(256)S(1)} %add_add_fusion) | copy-start | bytes 2308

commit v13 on v11

--- a/solution.py
+++ b/solution.py
@@ -14,7 +14,7 @@
 SLOTS = 1
 MOST = 2
 ABSORB_FROM = 3
-PER_LENT = 4
+PER_LENT = 8
 EARLY = 1
 REST_AT = 2
 DEGREE_PARTS = 4

time: 129 us -> 136 us (1.054)
  waiting for transfers between devices: 66.1 us -> 76.3 us
  Pallas kernels: 25.4 us -> 22.4 us
    ppermute x14, waiting for transfers between devices: 64.5 us -> 73.3 us  [shards(): lax.ppermute(piece, 'row', pairs(make_route(chips, port, r)))]
    pallas_call x16, Pallas kernels: 21.7 us -> 18.2 us  [absorb(): pl.pallas_call(functools.partial(absorb_kernel, count, flags, rows, first...]
    ppermute x6 -> x4, waiting for transfers between devices: 1.59 us -> 3.01 us  [exchange(): return lax.ppermute(value, 'row', swap)]
  transfers between devices with their start and end apart: 20 -> 18, of which waited for: 15 -> 16; matrix products, arithmetic and copies ran while one was open for 2% -> 2% of each run, Pallas kernels for 19% -> 13%
where the time goes in v13:
time: 136 us
  waiting for transfers between devices  76.3 us (56%)
  starting transfers between devices  30.2 us (22%)
  Pallas kernels  22.4 us (16%)
  local copies, waits for them, and re-layouts  3.38 us (2%)
  other arithmetic  2.96 us (2%)
    ppermute x14, waiting for transfers between devices, shards(): lax.ppermute(piece, 'row', pairs(make_route(chips, port, r)))  73.3 us
    ppermute x14, starting transfers between devices, shards(): lax.ppermute(piece, 'row', pairs(make_route(chips, port, r)))  29.2 us
    pallas_call x16, Pallas kernels, absorb(): pl.pallas_call(functools.partial(absorb_kernel, count, flags, rows, first...  18.2 us
    pallas_call x1, Pallas kernels, lend(): pl.pallas_call(functools.partial(lend_kernel, sizes, first, depth), in_sp...  4.22 us
    ppermute x4, waiting for transfers between devices, exchange(): return lax.ppermute(value, 'row', swap)  3.01 us
  transfers between devices with their start and end apart: 18, of which 16 were waited for; matrix products, arithmetic and copies ran while one was open for 2% of the time, Pallas kernels for 13%

profile of v13, /device:TPU:0, one launch (start us, length us, event | category | flops | bytes accessed | tf_op | source)
XLA Modules:
  0.0 136.2 jit_solution(8949248277005326718)
XLA Ops:
  0.6 2.4 %dynamic-slice_bitcast_fusion = (bf16[1024,384]{1,0:T(8,128)(2,1)S(1)}, bf16[1024,384]{1,0:T(8,128)(2,1)}) fusion(bf16[2,1024,384]{2,1,0:T(8,128)(2,1)} %param.5, s32[]{:T(128)S(6)} %select_n.12, s32[]{:T(128)S(6)} %select_n.11), kind=kLoop, calls=%fused_computation.4 | loop fusion | bytes 3145736 | tf_op jit(solution)/shard_map/jit(dynamic_index_in_dim)/squeeze | solution.py:343
  4.2 1.4 %collective-permute-done.refs_2_ = bf16[1024,384]{1,0:T(8,128)(2,1)S(1)} collective-permute-done((bf16[1024,384]{1,0:T(8,128)(2,1)}, bf16[1024,384]{1,0:T(8,128)(2,1)S(1)}, u32[]{:S(2)}, u32[]{:S(2)}) %collective-permute-start) | collective-permute-done | bytes 786464 | tf_op jit(solution)/shard_map/ppermute | solution.py:316
  5.6 4.2 %lend.1 = (bf16[192,8192]{1,0:T(8,128)(2,1)S(1)}, bf16[192,8192]{1,0:T(8,128)(2,1)S(1)}) custom-call(s32[34]{0:T(128)S(1)} %fusion.2.where, bf16[192,32768]{1,0:T(8,128)(2,1)} %refs_0_.15), custom_call_target="tpu_custom_call" | custom-call | bytes 1024 | tf_op jit(solution)/shard_map/lend/pallas_call | solution.py:103
  10.3 2.7 %collective-permute-start.3 = (bf16[1024,384]{1,0:T(8,128)(2,1)S(1)}, bf16[1024,384]{1,0:T(8,128)(2,1)S(1)}, u32[]{:S(2)}, u32[]{:S(2)}) collective-permute-start(bf16[1024,384]{1,0:T(8,128)(2,1)S(1)} %get-tuple-element.84.refs_2_), channel_id=1, source_target_pairs={{0,4},{3,7},{4,8},{7,11},{8,12},{11,15},{12,14},{15,13},{14,10},{1... | collective-permute-start | bytes 2359304 | tf_op jit(solution)/shard_map/ppermute | solution.py:369
  13.0 1.6 %collective-permute-start.1 = (bf16[1024,384]{1,0:T(8,128)(2,1)S(1)}, bf16[1024,384]{1,0:T(8,128)(2,1)S(1)}, u32[]{:S(2)}, u32[]{:S(2)}) collective-permute-start(bf16[1024,384]{1,0:T(8,128)(2,1)S(1)} %collective-permute-done.refs_2_), channel_id=1, source_target_pairs={{0,4},{3,7},{4,8},{7,11},{8,12},{11,15},{12,14},{15,13},{14,10},{1... | collective-permute-start | bytes 2359304 | tf_op jit(solution)/shard_map/ppermute | solution.py:369
  14.6 8.3 %collective-permute-done.3.refs_2_ = bf16[1024,384]{1,0:T(8,128)(2,1)S(1)} collective-permute-done((bf16[1024,384]{1,0:T(8,128)(2,1)S(1)}, bf16[1024,384]{1,0:T(8,128)(2,1)S(1)}, u32[]{:S(2)}, u32[]{:S(2)}) %collective-permute-start.3) | collective-permute-done | bytes 786464 | tf_op jit(solution)/shard_map/ppermute | solution.py:369
  22.9 2.1 %collective-permute-start.4 = (bf16[1024,384]{1,0:T(8,128)(2,1)S(1)}, bf16[1024,384]{1,0:T(8,128)(2,1)S(1)}, u32[]{:S(2)}, u32[]{:S(2)}) collective-permute-start(bf16[1024,384]{1,0:T(8,128)(2,1)S(1)} %collective-permute-done.3.refs_2_), channel_id=1, source_target_pairs={{0,4},{3,7},{4,8},{7,11},{8,12},{11,15},{12,14},{15,13},{14,10},{1... | collective-permute-start | bytes 2359304 | tf_op jit(solution)/shard_map/ppermute | solution.py:369
  25.0 6.3 %collective-permute-done.1.refs_2_ = bf16[1024,384]{1,0:T(8,128)(2,1)S(1)} collective-permute-done((bf16[1024,384]{1,0:T(8,128)(2,1)S(1)}, bf16[1024,384]{1,0:T(8,128)(2,1)S(1)}, u32[]{:S(2)}, u32[]{:S(2)}) %collective-permute-start.1) | collective-permute-done | bytes 786464 | tf_op jit(solution)/shard_map/ppermute | solution.py:369
  31.3 2.1 %collective-permute-start.2 = (bf16[1024,384]{1,0:T(8,128)(2,1)S(1)}, bf16[1024,384]{1,0:T(8,128)(2,1)S(1)}, u32[]{:S(2)}, u32[]{:S(2)}) collective-permute-start(bf16[1024,384]{1,0:T(8,128)(2,1)S(1)} %collective-permute-done.1.refs_2_), channel_id=1, source_target_pairs={{0,4},{3,7},{4,8},{7,11},{8,12},{11,15},{12,14},{15,13},{14,10},{1... | collective-permute-start | bytes 2359304 | tf_op jit(solution)/shard_map/ppermute | solution.py:369
  33.4 6.3 %collective-permute-done.4.refs_2_ = bf16[1024,384]{1,0:T(8,128)(2,1)S(1)} collective-permute-done((bf16[1024,384]{1,0:T(8,128)(2,1)S(1)}, bf16[1024,384]{1,0:T(8,128)(2,1)S(1)}, u32[]{:S(2)}, u32[]{:S(2)}) %collective-permute-start.4) | collective-permute-done | bytes 786464 | tf_op jit(solution)/shard_map/ppermute | solution.py:369
  39.8 2.1 %collective-permute-start.6 = (bf16[1024,384]{1,0:T(8,128)(2,1)S(1)}, bf16[1024,384]{1,0:T(8,128)(2,1)S(1)}, u32[]{:S(2)}, u32[]{:S(2)}) collective-permute-start(bf16[1024,384]{1,0:T(8,128)(2,1)S(1)} %collective-permute-done.4.refs_2_), channel_id=1, source_target_pairs={{0,4},{3,7},{4,8},{7,11},{8,12},{11,15},{12,14},{15,13},{14,10},{1... | collective-permute-start | bytes 2359304 | tf_op jit(solution)/shard_map/ppermute | solution.py:369
  42.4 5.8 %collective-permute-done.2.refs_2_ = bf16[1024,384]{1,0:T(8,128)(2,1)S(1)} collective-permute-done((bf16[1024,384]{1,0:T(8,128)(2,1)S(1)}, bf16[1024,384]{1,0:T(8,128)(2,1)S(1)}, u32[]{:S(2)}, u32[]{:S(2)}) %collective-permute-start.2) | collective-permute-done | bytes 786464 | tf_op jit(solution)/shard_map/ppermute | solution.py:369
  48.2 2.1 %collective-permute-start.5 = (bf16[1024,384]{1,0:T(8,128)(2,1)S(1)}, bf16[1024,384]{1,0:T(8,128)(2,1)S(1)}, u32[]{:S(2)}, u32[]{:S(2)}) collective-permute-start(bf16[1024,384]{1,0:T(8,128)(2,1)S(1)} %collective-permute-done.2.refs_2_), channel_id=1, source_target_pairs={{0,4},{3,7},{4,8},{7,11},{8,12},{11,15},{12,14},{15,13},{14,10},{1... | collective-permute-start | bytes 2359304 | tf_op jit(solution)/shard_map/ppermute | solution.py:369
  50.8 5.8 %collective-permute-done.6.refs_2_ = bf16[1024,384]{1,0:T(8,128)(2,1)S(1)} collective-permute-done((bf16[1024,384]{1,0:T(8,128)(2,1)S(1)}, bf16[1024,384]{1,0:T(8,128)(2,1)S(1)}, u32[]{:S(2)}, u32[]{:S(2)}) %collective-permute-start.6) | collective-permute-done | bytes 786464 | tf_op jit(solution)/shard_map/ppermute | solution.py:369
  56.6 2.1 %collective-permute-start.9 = (bf16[1024,384]{1,0:T(8,128)(2,1)S(1)}, bf16[1024,384]{1,0:T(8,128)(2,1)S(1)}, u32[]{:S(2)}, u32[]{:S(2)}) collective-permute-start(bf16[1024,384]{1,0:T(8,128)(2,1)S(1)} %collective-permute-done.6.refs_2_), channel_id=1, source_target_pairs={{0,4},{3,7},{4,8},{7,11},{8,12},{11,15},{12,14},{15,13},{14,10},{1... | collective-permute-start | bytes 2359304 | tf_op jit(solution)/shard_map/ppermute | solution.py:369
  59.2 1.1 absorb.16
  60.4 1.1 absorb.17
  61.6 3.5 %collective-permute-done.5.refs_2_ = bf16[1024,384]{1,0:T(8,128)(2,1)S(1)} collective-permute-done((bf16[1024,384]{1,0:T(8,128)(2,1)S(1)}, bf16[1024,384]{1,0:T(8,128)(2,1)S(1)}, u32[]{:S(2)}, u32[]{:S(2)}) %collective-permute-start.5) | collective-permute-done | bytes 786464 | tf_op jit(solution)/shard_map/ppermute | solution.py:369
  65.0 2.1 %collective-permute-start.8 = (bf16[1024,384]{1,0:T(8,128)(2,1)S(1)}, bf16[1024,384]{1,0:T(8,128)(2,1)S(1)}, u32[]{:S(2)}, u32[]{:S(2)}) collective-permute-start(bf16[1024,384]{1,0:T(8,128)(2,1)S(1)} %collective-permute-done.5.refs_2_), channel_id=1, source_target_pairs={{0,4},{3,7},{4,8},{7,11},{8,12},{11,15},{12,14},{15,13},{14,10},{1... | collective-permute-start | bytes 2359304 | tf_op jit(solution)/shard_map/ppermute | solution.py:369
  67.1 1.1 absorb.18
  68.3 1.1 absorb.19
  70.0 3.5 %collective-permute-done.9.refs_2_ = bf16[1024,384]{1,0:T(8,128)(2,1)S(1)} collective-permute-done((bf16[1024,384]{1,0:T(8,128)(2,1)S(1)}, bf16[1024,384]{1,0:T(8,128)(2,1)S(1)}, u32[]{:S(2)}, u32[]{:S(2)}) %collective-permute-start.9) | collective-permute-done | bytes 786464 | tf_op jit(solution)/shard_map/ppermute | solution.py:369
  73.5 2.1 %collective-permute-start.11 = (bf16[1024,384]{1,0:T(8,128)(2,1)S(1)}, bf16[1024,384]{1,0:T(8,128)(2,1)S(1)}, u32[]{:S(2)}, u32[]{:S(2)}) collective-permute-start(bf16[1024,384]{1,0:T(8,128)(2,1)S(1)} %collective-permute-done.9.refs_2_), channel_id=1, source_target_pairs={{0,4},{3,7},{4,8},{7,11},{8,12},{11,15},{12,14},{15,13},{14,10},{1... | collective-permute-start | bytes 2359304 | tf_op jit(solution)/shard_map/ppermute | solution.py:369
  75.6 1.1 absorb.20
  76.8 1.1 absorb.21
  77.9 4.0 %collective-permute-done.8.refs_2_ = bf16[1024,384]{1,0:T(8,128)(2,1)S(1)} collective-permute-done((bf16[1024,384]{1,0:T(8,128)(2,1)S(1)}, bf16[1024,384]{1,0:T(8,128)(2,1)S(1)}, u32[]{:S(2)}, u32[]{:S(2)}) %collective-permute-start.8) | collective-permute-done | bytes 786464 | tf_op jit(solution)/shard_map/ppermute | solution.py:369
  81.9 2.1 %collective-permute-start.10 = (bf16[1024,384]{1,0:T(8,128)(2,1)S(1)}, bf16[1024,384]{1,0:T(8,128)(2,1)S(1)}, u32[]{:S(2)}, u32[]{:S(2)}) collective-permute-start(bf16[1024,384]{1,0:T(8,128)(2,1)S(1)} %collective-permute-done.8.refs_2_), channel_id=1, source_target_pairs={{0,4},{3,7},{4,8},{7,11},{8,12},{11,15},{12,14},{15,13},{14,10},{1... | collective-permute-start | bytes 2359304 | tf_op jit(solution)/shard_map/ppermute | solution.py:369
  84.0 1.1 absorb.22
  85.2 1.1 absorb.23
  86.3 4.0 %collective-permute-done.11.refs_2_ = bf16[1024,384]{1,0:T(8,128)(2,1)S(1)} collective-permute-done((bf16[1024,384]{1,0:T(8,128)(2,1)S(1)}, bf16[1024,384]{1,0:T(8,128)(2,1)S(1)}, u32[]{:S(2)}, u32[]{:S(2)}) %collective-permute-start.11) | collective-permute-done | bytes 786464 | tf_op jit(solution)/shard_map/ppermute | solution.py:369
  90.3 2.1 %collective-permute-start.14 = (bf16[1024,384]{1,0:T(8,128)(2,1)S(1)}, bf16[1024,384]{1,0:T(8,128)(2,1)S(1)}, u32[]{:S(2)}, u32[]{:S(2)}) collective-permute-start(bf16[1024,384]{1,0:T(8,128)(2,1)S(1)} %collective-permute-done.11.refs_2_), channel_id=1, source_target_pairs={{0,4},{3,7},{4,8},{7,11},{8,12},{11,15},{12,14},{15,13},{14,10},{1... | collective-permute-start | bytes 2359304 | tf_op jit(solution)/shard_map/ppermute | solution.py:369
  92.4 1.1 absorb.24
  93.6 1.1 absorb.25
  94.8 4.0 %collective-permute-done.10.refs_2_ = bf16[1024,384]{1,0:T(8,128)(2,1)S(1)} collective-permute-done((bf16[1024,384]{1,0:T(8,128)(2,1)S(1)}, bf16[1024,384]{1,0:T(8,128)(2,1)S(1)}, u32[]{:S(2)}, u32[]{:S(2)}) %collective-permute-start.10) | collective-permute-done | bytes 786464 | tf_op jit(solution)/shard_map/ppermute | solution.py:369
  98.8 2.1 %collective-permute-start.13 = (bf16[1024,384]{1,0:T(8,128)(2,1)S(1)}, bf16[1024,384]{1,0:T(8,128)(2,1)S(1)}, u32[]{:S(2)}, u32[]{:S(2)}) collective-permute-start(bf16[1024,384]{1,0:T(8,128)(2,1)S(1)} %collective-permute-done.10.refs_2_), channel_id=1, source_target_pairs={{0,4},{3,7},{4,8},{7,11},{8,12},{11,15},{12,14},{15,13},{14,10},{1... | collective-permute-start | bytes 2359304 | tf_op jit(solution)/shard_map/ppermute | solution.py:369
  100.8 1.1 absorb.26
  102.0 1.1 absorb.27
  103.2 4.0 %collective-permute-done.14.refs_2_ = bf16[1024,384]{1,0:T(8,128)(2,1)S(1)} collective-permute-done((bf16[1024,384]{1,0:T(8,128)(2,1)S(1)}, bf16[1024,384]{1,0:T(8,128)(2,1)S(1)}, u32[]{:S(2)}, u32[]{:S(2)}) %collective-permute-start.14) | collective-permute-done | bytes 786464 | tf_op jit(solution)/shard_map/ppermute | solution.py:369
  107.2 2.1 %collective-permute-start.16 = (bf16[1024,384]{1,0:T(8,128)(2,1)S(1)}, bf16[1024,384]{1,0:T(8,128)(2,1)S(1)}, u32[]{:S(2)}, u32[]{:S(2)}) collective-permute-start(bf16[1024,384]{1,0:T(8,128)(2,1)S(1)} %collective-permute-done.14.refs_2_), channel_id=1, source_target_pairs={{0,4},{3,7},{4,8},{7,11},{8,12},{11,15},{12,14},{15,13},{14,10},{1... | collective-permute-start | bytes 2359304 | tf_op jit(solution)/shard_map/ppermute | solution.py:369
  109.3 1.1 absorb.28
  110.4 5.2 %collective-permute-done.13.refs_2_ = bf16[1024,384]{1,0:T(8,128)(2,1)S(1)} collective-permute-done((bf16[1024,384]{1,0:T(8,128)(2,1)S(1)}, bf16[1024,384]{1,0:T(8,128)(2,1)S(1)}, u32[]{:S(2)}, u32[]{:S(2)}) %collective-permute-start.13) | collective-permute-done | bytes 786464 | tf_op jit(solution)/shard_map/ppermute | solution.py:369
  115.6 2.1 %collective-permute-start.15 = (bf16[1024,384]{1,0:T(8,128)(2,1)S(1)}, bf16[1024,384]{1,0:T(8,128)(2,1)S(1)}, u32[]{:S(2)}, u32[]{:S(2)}) collective-permute-start(bf16[1024,384]{1,0:T(8,128)(2,1)S(1)} %collective-permute-done.13.refs_2_), channel_id=1, source_target_pairs={{0,4},{3,7},{4,8},{7,11},{8,12},{11,15},{12,14},{15,13},{14,10},{1... | collective-permute-start | bytes 2359304 | tf_op jit(solution)/shard_map/ppermute | solution.py:369
  117.7 1.1 absorb.29
  118.8 5.2 %collective-permute-done.16.refs_2_ = bf16[1024,384]{1,0:T(8,128)(2,1)S(1)} collective-permute-done((bf16[1024,384]{1,0:T(8,128)(2,1)S(1)}, bf16[1024,384]{1,0:T(8,128)(2,1)S(1)}, u32[]{:S(2)}, u32[]{:S(2)}) %collective-permute-start.16) | collective-permute-done | bytes 786464 | tf_op jit(solution)/shard_map/ppermute | solution.py:369
  124.0 1.1 absorb.30
  125.2 7.3 %collective-permute-done.15.refs_2_ = bf16[1024,384]{1,0:T(8,128)(2,1)S(1)} collective-permute-done((bf16[1024,384]{1,0:T(8,128)(2,1)S(1)}, bf16[1024,384]{1,0:T(8,128)(2,1)S(1)}, u32[]{:S(2)}, u32[]{:S(2)}) %collective-permute-start.15) | collective-permute-done | bytes 786464 | tf_op jit(solution)/shard_map/ppermute | solution.py:369
  132.5 1.1 absorb.31
  133.7 1.6 %collective-permute-done.17 = f32[208,384]{1,0:T(8,128)S(1)} collective-permute-done((f32[208,384]{1,0:T(8,128)S(1)}, f32[208,384]{1,0:T(8,128)S(1)}, u32[]{:S(2)}, u32[]{:S(2)}) %collective-permute-start.17) | collective-permute-done | bytes 319520 | tf_op jit(solution)/shard_map/ppermute | solution.py:316
  (32 shorter events, 4.9 us)
Async XLA Ops:
  3.1 2.6 %collective-permute-start = (bf16[1024,384]{1,0:T(8,128)(2,1)}, bf16[1024,384]{1,0:T(8,128)(2,1)S(1)}, u32[]{:S(2)}, u32[]{:S(2)}) collective-permute-start(bf16[1024,384]{1,0:T(8,128)(2,1)} %get-tuple-element.153), channel_id=1, source_target_pairs={{0,1},{1,0},{2,3},{3,2},{4,5},{5,4},{6,7},{7,6},{8,9},{9,8},{10,11... | collective-permute-start | bytes 2359304 | tf_op jit(solution)/shard_map/ppermute | solution.py:316
  4.2 37.7 %copy-start = (bf16[192,32768]{1,0:T(8,128)(2,1)S(1)}, bf16[192,32768]{1,0:T(8,128)(2,1)}, u32[]{:S(2)}) copy-start(bf16[192,32768]{1,0:T(8,128)(2,1)} %refs_0_.15) | copy-start | bytes 37748740
  9.9 49.4 %collective-permute-start.7 = (bf16[192,8192]{1,0:T(8,128)(2,1)S(1)}, bf16[192,8192]{1,0:T(8,128)(2,1)S(1)}, u32[]{:S(2)}, u32[]{:S(2)}) collective-permute-start(bf16[192,8192]{1,0:T(8,128)(2,1)S(1)} %get-tuple-element.83), channel_id=1, source_target_pairs={{0,1},{1,0},{2,3},{3,2},{4,5},{5,4},{6,7},{7,6},{8,9},{9,8},{10,11... | collective-permute-start | bytes 9437192 | tf_op jit(solution)/shard_map/ppermute | solution.py:316
  10.3 12.6 %collective-permute-start.3 = (bf16[1024,384]{1,0:T(8,128)(2,1)S(1)}, bf16[1024,384]{1,0:T(8,128)(2,1)S(1)}, u32[]{:S(2)}, u32[]{:S(2)}) collective-permute-start(bf16[1024,384]{1,0:T(8,128)(2,1)S(1)} %get-tuple-element.84.refs_2_), channel_id=1, source_target_pairs={{0,4},{3,7},{4,8},{7,11},{8,12},{11,15},{12,14},{15,13},{14,10},{1... | collective-permute-start | bytes 2359304 | tf_op jit(solution)/shard_map/ppermute | solution.py:369
  13.0 18.3 %collective-permute-start.1 = (bf16[1024,384]{1,0:T(8,128)(2,1)S(1)}, bf16[1024,384]{1,0:T(8,128)(2,1)S(1)}, u32[]{:S(2)}, u32[]{:S(2)}) collective-permute-start(bf16[1024,384]{1,0:T(8,128)(2,1)S(1)} %collective-permute-done.refs_2_), channel_id=1, source_target_pairs={{0,4},{3,7},{4,8},{7,11},{8,12},{11,15},{12,14},{15,13},{14,10},{1... | collective-permute-start | bytes 2359304 | tf_op jit(solution)/shard_map/ppermute | solution.py:369
  22.9 16.9 %collective-permute-start.4 = (bf16[1024,384]{1,0:T(8,128)(2,1)S(1)}, bf16[1024,384]{1,0:T(8,128)(2,1)S(1)}, u32[]{:S(2)}, u32[]{:S(2)}) collective-permute-start(bf16[1024,384]{1,0:T(8,128)(2,1)S(1)} %collective-permute-done.3.refs_2_), channel_id=1, source_target_pairs={{0,4},{3,7},{4,8},{7,11},{8,12},{11,15},{12,14},{15,13},{14,10},{1... | collective-permute-start | bytes 2359304 | tf_op jit(solution)/shard_map/ppermute | solution.py:369
  31.3 16.9 %collective-permute-start.2 = (bf16[1024,384]{1,0:T(8,128)(2,1)S(1)}, bf16[1024,384]{1,0:T(8,128)(2,1)S(1)}, u32[]{:S(2)}, u32[]{:S(2)}) collective-permute-start(bf16[1024,384]{1,0:T(8,128)(2,1)S(1)} %collective-permute-done.1.refs_2_), channel_id=1, source_target_pairs={{0,4},{3,7},{4,8},{7,11},{8,12},{11,15},{12,14},{15,13},{14,10},{1... | collective-permute-start | bytes 2359304 | tf_op jit(solution)/shard_map/ppermute | solution.py:369
  33.4 59.0 %collective-permute-start.12 = (bf16[192,8192]{1,0:T(8,128)(2,1)S(1)}, bf16[192,8192]{1,0:T(8,128)(2,1)S(1)}, u32[]{:S(2)}, u32[]{:S(2)}) collective-permute-start(bf16[192,8192]{1,0:T(8,128)(2,1)S(1)} %get-tuple-element.117), channel_id=1, source_target_pairs={{0,1},{1,0},{2,3},{3,2},{4,5},{5,4},{6,7},{7,6},{8,9},{9,8},{10,11... | collective-permute-start | bytes 9437192 | tf_op jit(solution)/shard_map/ppermute | solution.py:316
  39.8 16.9 %collective-permute-start.6 = (bf16[1024,384]{1,0:T(8,128)(2,1)S(1)}, bf16[1024,384]{1,0:T(8,128)(2,1)S(1)}, u32[]{:S(2)}, u32[]{:S(2)}) collective-permute-start(bf16[1024,384]{1,0:T(8,128)(2,1)S(1)} %collective-permute-done.4.refs_2_), channel_id=1, source_target_pairs={{0,4},{3,7},{4,8},{7,11},{8,12},{11,15},{12,14},{15,13},{14,10},{1... | collective-permute-start | bytes 2359304 | tf_op jit(solution)/shard_map/ppermute | solution.py:369
  48.2 16.9 %collective-permute-start.5 = (bf16[1024,384]{1,0:T(8,128)(2,1)S(1)}, bf16[1024,384]{1,0:T(8,128)(2,1)S(1)}, u32[]{:S(2)}, u32[]{:S(2)}) collective-permute-start(bf16[1024,384]{1,0:T(8,128)(2,1)S(1)} %collective-permute-done.2.refs_2_), channel_id=1, source_target_pairs={{0,4},{3,7},{4,8},{7,11},{8,12},{11,15},{12,14},{15,13},{14,10},{1... | collective-permute-start | bytes 2359304 | tf_op jit(solution)/shard_map/ppermute | solution.py:369
  56.6 16.9 %collective-permute-start.9 = (bf16[1024,384]{1,0:T(8,128)(2,1)S(1)}, bf16[1024,384]{1,0:T(8,128)(2,1)S(1)}, u32[]{:S(2)}, u32[]{:S(2)}) collective-permute-start(bf16[1024,384]{1,0:T(8,128)(2,1)S(1)} %collective-permute-done.6.refs_2_), channel_id=1, source_target_pairs={{0,4},{3,7},{4,8},{7,11},{8,12},{11,15},{12,14},{15,13},{14,10},{1... | collective-permute-start | bytes 2359304 | tf_op jit(solution)/shard_map/ppermute | solution.py:369
  65.0 16.9 %collective-permute-start.8 = (bf16[1024,384]{1,0:T(8,128)(2,1)S(1)}, bf16[1024,384]{1,0:T(8,128)(2,1)S(1)}, u32[]{:S(2)}, u32[]{:S(2)}) collective-permute-start(bf16[1024,384]{1,0:T(8,128)(2,1)S(1)} %collective-permute-done.5.refs_2_), channel_id=1, source_target_pairs={{0,4},{3,7},{4,8},{7,11},{8,12},{11,15},{12,14},{15,13},{14,10},{1... | collective-permute-start | bytes 2359304 | tf_op jit(solution)/shard_map/ppermute | solution.py:369
  73.5 16.9 %collective-permute-start.11 = (bf16[1024,384]{1,0:T(8,128)(2,1)S(1)}, bf16[1024,384]{1,0:T(8,128)(2,1)S(1)}, u32[]{:S(2)}, u32[]{:S(2)}) collective-permute-start(bf16[1024,384]{1,0:T(8,128)(2,1)S(1)} %collective-permute-done.9.refs_2_), channel_id=1, source_target_pairs={{0,4},{3,7},{4,8},{7,11},{8,12},{11,15},{12,14},{15,13},{14,10},{1... | collective-permute-start | bytes 2359304 | tf_op jit(solution)/shard_map/ppermute | solution.py:369
  81.9 16.9 %collective-permute-start.10 = (bf16[1024,384]{1,0:T(8,128)(2,1)S(1)}, bf16[1024,384]{1,0:T(8,128)(2,1)S(1)}, u32[]{:S(2)}, u32[]{:S(2)}) collective-permute-start(bf16[1024,384]{1,0:T(8,128)(2,1)S(1)} %collective-permute-done.8.refs_2_), channel_id=1, source_target_pairs={{0,4},{3,7},{4,8},{7,11},{8,12},{11,15},{12,14},{15,13},{14,10},{1... | collective-permute-start | bytes 2359304 | tf_op jit(solution)/shard_map/ppermute | solution.py:369
  90.3 16.9 %collective-permute-start.14 = (bf16[1024,384]{1,0:T(8,128)(2,1)S(1)}, bf16[1024,384]{1,0:T(8,128)(2,1)S(1)}, u32[]{:S(2)}, u32[]{:S(2)}) collective-permute-start(bf16[1024,384]{1,0:T(8,128)(2,1)S(1)} %collective-permute-done.11.refs_2_), channel_id=1, source_target_pairs={{0,4},{3,7},{4,8},{7,11},{8,12},{11,15},{12,14},{15,13},{14,10},{1... | collective-permute-start | bytes 2359304 | tf_op jit(solution)/shard_map/ppermute | solution.py:369
  98.8 16.9 %collective-permute-start.13 = (bf16[1024,384]{1,0:T(8,128)(2,1)S(1)}, bf16[1024,384]{1,0:T(8,128)(2,1)S(1)}, u32[]{:S(2)}, u32[]{:S(2)}) collective-permute-start(bf16[1024,384]{1,0:T(8,128)(2,1)S(1)} %collective-permute-done.10.refs_2_), channel_id=1, source_target_pairs={{0,4},{3,7},{4,8},{7,11},{8,12},{11,15},{12,14},{15,13},{14,10},{1... | collective-permute-start | bytes 2359304 | tf_op jit(solution)/shard_map/ppermute | solution.py:369
  107.2 16.9 %collective-permute-start.16 = (bf16[1024,384]{1,0:T(8,128)(2,1)S(1)}, bf16[1024,384]{1,0:T(8,128)(2,1)S(1)}, u32[]{:S(2)}, u32[]{:S(2)}) collective-permute-start(bf16[1024,384]{1,0:T(8,128)(2,1)S(1)} %collective-permute-done.14.refs_2_), channel_id=1, source_target_pairs={{0,4},{3,7},{4,8},{7,11},{8,12},{11,15},{12,14},{15,13},{14,10},{1... | collective-permute-start | bytes 2359304 | tf_op jit(solution)/shard_map/ppermute | solution.py:369
  115.6 16.9 %collective-permute-start.15 = (bf16[1024,384]{1,0:T(8,128)(2,1)S(1)}, bf16[1024,384]{1,0:T(8,128)(2,1)S(1)}, u32[]{:S(2)}, u32[]{:S(2)}) collective-permute-start(bf16[1024,384]{1,0:T(8,128)(2,1)S(1)} %collective-permute-done.13.refs_2_), channel_id=1, source_target_pairs={{0,4},{3,7},{4,8},{7,11},{8,12},{11,15},{12,14},{15,13},{14,10},{1... | collective-permute-start | bytes 2359304 | tf_op jit(solution)/shard_map/ppermute | solution.py:369
  132.5 2.9 %copy-start.1 = (bf16[192,384]{1,0:T(8,128)(2,1)S(1)}, bf16[192,384]{1,0:T(8,128)(2,1)}, u32[]{:S(2)}) copy-start(bf16[192,384]{1,0:T(8,128)(2,1)} %param.6) | copy-start | bytes 442372
  133.6 1.7 %collective-permute-start.17 = (f32[208,384]{1,0:T(8,128)S(1)}, f32[208,384]{1,0:T(8,128)S(1)}, u32[]{:S(2)}, u32[]{:S(2)}) collective-permute-start(f32[208,384]{1,0:T(8,128)S(1)} %get-tuple-element.151), channel_id=1, source_target_pairs={{0,1},{1,0},{2,3},{3,2},{4,5},{5,4},{6,7},{7,6},{8,9},{9,8},{10,11... | collective-permute-start | bytes 958472 | tf_op jit(solution)/shard_map/ppermute | solution.py:316
  133.7 2.5 %copy-start.2 = (f32[192]{0:T(256)}, f32[192]{0:T(256)S(1)}, u32[]{:S(2)}) copy-start(f32[192]{0:T(256)S(1)} %add_add_fusion) | copy-start | bytes 2308
